TPU v7x, 32 devices: a whole 2x2x4 slice. The times are simulated.
32 devices in a mesh: depth: 2 (over core), scan: 16 (over z, y, x).
Axes of the slice: x: 2, y: 2, z: 4, core: 2. Of those that a mesh axis runs over, the one named last changes fastest.
Arguments:
- objects: float32 [6, 2, 2048, 256], P('depth', None, 'scan')
- probe: float32 [2, 128, 128], replicated, may hold values from -6 to 6
- row_offsets: int32 [32], P('scan'), may hold values from 0 to 2048, as said below
- col_offsets: int32 [32], P('scan'), may hold values from 0 to 128, as said below
- intensity: float32 [32, 128, 128], P('scan'), may hold values from 0.1 to 4
Outputs:
- object_grad: float32 [6, 2, 2048, 256], P('depth', None, 'scan')
- probe_grad: float32 [2, 128, 128], P(None, 'depth')
Inputs may be any that keep to these rules, and one draw needn't show every extreme that they name: `row_offsets`: position i is measured by scan index i // 2; its row offset lies from (i // 2) * 128 to (i // 2 + 1) * 128, both ends included, and on every scan index one of its positions has the upper end. `col_offsets`: some position has column offset 0 and some has the largest.
All inputs are finite; a program needn't handle non-finite values.
Results may differ from a plain program's by a relative error of at most 0.0003.
Values sent between devices are 32-bit elements; how exact they have to be, the bound alone decides.
No kernel may reach another device: no remote copies, remote signals or barrier semaphores. Data moves between devices by JAX's collectives and lax.ppermute only.
A program may use at most 64 MiB of HBM per device.

v0:
```python
import math

import jax
import jax.numpy as jnp
from jax import lax
from jax.sharding import PartitionSpec as P

PROPAGATION = 0.5


def from_behind(block, axis, distance):
    devices = range(lax.axis_size(axis))
    route = [((i - distance) % len(devices), i) for i in devices]
    return lax.ppermute(block, axis, route)


def passed_along(block, axis, distance):
    devices = range(lax.axis_size(axis))
    route = [(i - distance, i) for i in devices if i - distance in devices]
    return lax.ppermute(block, axis, route)


def broadcast(x, axis, root):
    mine = lax.axis_index(axis) == root
    return lax.psum(jnp.where(mine, x, jnp.zeros_like(x)), axis)


def matmul_high(left_side, right_side):
    return jnp.matmul(left_side, right_side, precision=lax.Precision.HIGHEST)


def dft_tables(window_width):
    grid_index = jnp.arange(window_width, dtype=jnp.int32)
    phase_steps = grid_index[:, None] * grid_index[None, :] % window_width
    turn_angle = phase_steps.astype(jnp.float32) * (2.0 * math.pi / window_width)
    norm_scale = 1.0 / math.sqrt(window_width)
    return (jnp.cos(turn_angle) * norm_scale, jnp.sin(turn_angle) * norm_scale)


def chirp_factors(window_width):
    grid_index = jnp.arange(window_width, dtype=jnp.int32)
    frequency = jnp.where(grid_index < window_width // 2, grid_index, grid_index - window_width)
    squared = frequency[:, None] ** 2 + frequency[None, :] ** 2
    phase_angle = squared.astype(jnp.float32) * (PROPAGATION * math.pi / window_width)
    return (jnp.cos(phase_angle), jnp.sin(phase_angle))


def transform(real_part, imag_part, tables, direction):
    cos_table, sin_table = tables
    mid_real = matmul_high(cos_table, real_part) + direction * matmul_high(sin_table, imag_part)
    mid_imag = matmul_high(cos_table, imag_part) - direction * matmul_high(sin_table, real_part)
    out_real = matmul_high(mid_real, cos_table) + direction * matmul_high(mid_imag, sin_table)
    out_imag = matmul_high(mid_imag, cos_table) - direction * matmul_high(mid_real, sin_table)
    return (out_real, out_imag)


def propagate(real_part, imag_part, tables, chirp_table, direction):
    chirp_cos, chirp_sin = chirp_table
    spec_real, spec_imag = transform(real_part, imag_part, tables, 1.0)
    next_real = spec_real * chirp_cos + direction * spec_imag * chirp_sin
    next_imag = spec_imag * chirp_cos - direction * spec_real * chirp_sin
    return transform(next_real, next_imag, tables, -1.0)


def forward_section(wave, patches, tables, chirp_table):
    wave_real, wave_imag = (wave[0], wave[1])
    inputs = []
    for layer_index in range(patches.shape[0]):
        inputs.append(jnp.stack([wave_real, wave_imag]))
        obj_real, obj_imag = (patches[layer_index, 0], patches[layer_index, 1])
        exit_real = wave_real * obj_real - wave_imag * obj_imag
        exit_imag = wave_real * obj_imag + wave_imag * obj_real
        wave_real, wave_imag = propagate(exit_real, exit_imag, tables, chirp_table, 1.0)
    return (jnp.stack([wave_real, wave_imag]), jnp.stack(inputs))


def backward_section(gradient, patches, inputs, tables, chirp_table):
    grad_real, grad_imag = (gradient[0], gradient[1])
    patch_grads = [None] * patches.shape[0]
    for layer_index in reversed(range(patches.shape[0])):
        chi_real, chi_imag = propagate(grad_real, grad_imag, tables, chirp_table, -1.0)
        psi_real, psi_imag = (inputs[layer_index, 0], inputs[layer_index, 1])
        patch_grads[layer_index] = jnp.stack(
            [psi_real * chi_real + psi_imag * chi_imag, psi_real * chi_imag - psi_imag * chi_real]
        )
        obj_real, obj_imag = (patches[layer_index, 0], patches[layer_index, 1])
        grad_real = obj_real * chi_real + obj_imag * chi_imag
        grad_imag = obj_real * chi_imag - obj_imag * chi_real
    return (jnp.stack([grad_real, grad_imag]), jnp.stack(patch_grads))


def far_field(exit_wave, measured, tables):
    far_real, far_imag = transform(exit_wave[0], exit_wave[1], tables, 1.0)
    misfit = far_real * far_real + far_imag * far_imag - measured
    back_real, back_imag = transform(2.0 * misfit * far_real, 2.0 * misfit * far_imag, tables, -1.0)
    return jnp.stack([back_real, back_imag])


def body(objects, probe, row_offsets, col_offsets, intensity):
    slab_count = objects.shape[0]
    tile_rows = objects.shape[2]
    window_width = probe.shape[-1]
    wave_count = row_offsets.shape[0]
    depth_count = lax.axis_size("depth")
    depth_index = lax.axis_index("depth")
    scan_index = lax.axis_index("scan")
    first_section = depth_index == 0
    last_section = depth_index == depth_count - 1
    tables = dft_tables(window_width)
    chirp_table = chirp_factors(window_width)
    local_rows = row_offsets - scan_index * tile_rows
    window_shape = (slab_count, 2, window_width, window_width)
    probe_rows = window_width // depth_count
    row_start = depth_index * probe_rows
    below_rows = from_behind(objects, "scan", -1)
    extended = jnp.concatenate([objects, below_rows], axis=2)

    def window_at(wave_index):
        return lax.dynamic_slice(
            extended, (0, 0, local_rows[wave_index], col_offsets[wave_index]), window_shape
        )

    def add_window(accum, wave_index, update):
        corner = (0, 0, local_rows[wave_index], col_offsets[wave_index])
        return lax.dynamic_update_slice(
            accum, lax.dynamic_slice(accum, corner, window_shape) + update, corner
        )

    accum_start = jnp.zeros(extended.shape, jnp.float32)
    empty_wave = jnp.zeros((2, window_width, window_width), jnp.float32)
    stored_start = jnp.zeros((wave_count,) + window_shape, jnp.float32)
    exits_start = jnp.zeros((wave_count, 2, window_width, window_width), jnp.float32)
    probe_start = jnp.zeros(probe.shape, jnp.float32)

    def forward_step(step_index, loop_state):
        outgoing, stored, exits = loop_state
        arriving = passed_along(outgoing, "depth", 1)
        arriving = jnp.where(first_section, probe, arriving)
        wave_index = step_index - depth_index
        active_step = (wave_index >= 0) & (wave_index < wave_count)
        chosen = jnp.clip(wave_index, 0, wave_count - 1)

        def forward_run_section(operand):
            leaving, inputs = forward_section(arriving, window_at(chosen), tables, chirp_table)
            return (
                leaving,
                lax.dynamic_update_index_in_dim(stored, inputs, chosen, 0),
                lax.dynamic_update_index_in_dim(exits, leaving, chosen, 0),
            )

        def forward_pass_along(operand):
            return (empty_wave, stored, exits)

        return lax.cond(active_step, forward_run_section, forward_pass_along, 0)

    outgoing, stored, exits = lax.fori_loop(
        0, wave_count + depth_count - 1, forward_step, (empty_wave, stored_start, exits_start)
    )

    def backward_step(step_index, loop_state):
        outgoing, accum, probe_part = loop_state
        arriving = passed_along(outgoing, "depth", -1)
        wave_index = step_index - (depth_count - 1 - depth_index)
        active_step = (wave_index >= 0) & (wave_index < wave_count)
        chosen = jnp.clip(wave_index, 0, wave_count - 1)

        def backward_run_section(operand):

            def from_detector(inner):
                return far_field(exits[chosen], intensity[chosen], tables)

            def from_next(inner):
                return arriving

            incoming = lax.cond(last_section, from_detector, from_next, 0)
            leaving, patch_grads = backward_section(
                incoming, window_at(chosen), stored[chosen], tables, chirp_table
            )
            return (
                leaving,
                add_window(accum, chosen, patch_grads),
                probe_part + jnp.where(first_section, leaving, 0.0),
            )

        def backward_pass_along(operand):
            return (empty_wave, accum, probe_part)

        return lax.cond(active_step, backward_run_section, backward_pass_along, 0)

    outgoing, accum, probe_part = lax.fori_loop(
        0, wave_count + depth_count - 1, backward_step, (empty_wave, accum_start, probe_start)
    )
    spill_rows = accum[:, :, tile_rows:, :]
    arrived = from_behind(spill_rows, "scan", 1)
    object_grad = accum[:, :, :tile_rows, :].at[:, :, :window_width, :].add(arrived)
    scan_total = lax.psum(probe_part, "scan")
    spread = broadcast(scan_total, "depth", 0)
    probe_grad = lax.dynamic_slice_in_dim(spread, row_start, probe_rows, 1)
    return (object_grad, probe_grad)


def solution(mesh):
    in_specs = (P("depth", None, "scan", None), P(), P("scan"), P("scan"), P("scan", None, None))
    out_specs = (P("depth", None, "scan", None), P(None, "depth", None))
    return jax.shard_map(body, mesh=mesh, in_specs=in_specs, out_specs=out_specs, check_vma=False)
```

profile of v0, /device:TPU:0, one launch (start us, length us, event | category | flops | bytes accessed | tf_op | source)
XLA Modules:
  0.0 375.8 jit_solution(359723907400930990)
XLA Ops:
  7.2 7.0 %collective-permute-start.2 = (f32[3,2,128,256]{3,2,1,0:T(8,128)}, f32[3,2,128,256]{3,2,1,0:T(8,128)S(1)}, u32[]{:S(2)}, u32[]{:S(2)}) collective-permute-start(f32[3,2,128,256]{3,2,1,0:T(8,128)} %param.19), channel_id=1, source_target_pairs={{1,0},{2,1},{3,2},{4,3},{5,4},{6,5},{7,6},{8,7},{9,8},{10,9},{11,1... | collective-permute-start | bytes 2359304 | tf_op jit(solution)/shard_map/ppermute | solution.py:14
  14.2 2.1 constant_dynamic-update-slice_fusion.1
  16.4 15.0 %collective-permute-done.2 = f32[3,2,128,256]{3,2,1,0:T(8,128)S(1)} collective-permute-done((f32[3,2,128,256]{3,2,1,0:T(8,128)}, f32[3,2,128,256]{3,2,1,0:T(8,128)S(1)}, u32[]{:S(2)}, u32[]{:S(2)}) %collective-permute-start.2) | collective-permute-done | bytes 786464 | tf_op jit(solution)/shard_map/ppermute | solution.py:14
  31.3 1.0 constant_dynamic-update-slice_fusion
  32.3 0.7 broadcast.107.clone.1
  33.1 56.9 %while.44 = (s32[]{:T(128)}, f32[2,128,128]{2,1,0:T(8,128)}, f32[2,3,2,128,128]{4,3,2,1,0:T(8,128)S(1)}, f32[2,2,128,128]{3,2,1,0:T(8,128)S(1)}, s32[]{:T(128)},...) while((s32[]{:T(128)}, f32[2,128,128]{2,1,0:T(8,128)}, ...), condition=%wide.region_3.4_spmd.clone.clone.clone, body=%wide.region_0.3_spmd.clone.clone.clone.sunk | while | flops 1209778176 | bytes 16319556 | solution.py:156
  33.1 1.3 collective-permute-start
  34.5 1.1 collective-permute-done
  35.6 23.9 %conditional.12 = (f32[2,128,128]{2,1,0:T(8,128)}, f32[2,3,2,128,128]{4,3,2,1,0:T(8,128)S(1)}, f32[2,2,128,128]{3,2,1,0:T(8,128)S(1)}) conditional(s32[]{:T(128)} %convert_element_type.355, (f32[2,3,2,128,128]{4,3,2,1,0:T(8,128)S(1)}, f32[2,2,128,128]{3,2,1,0:T(8,128)S(1)}) %tuple.295, (pred[]{:T(512)}, f32[2,128,128]{2,1,0:T(8,128)S(1)}, ...), branch_computations={%region_1.1_spmd, %region_2.2_spmd.clone} | conditional | flops 1209499648 | bytes 15597781 | solution.py:154
  38.1 0.6 dynamic_slice.38
  41.1 1.1 multiply_add_fusion.5
  47.0 1.3 multiply_add_fusion.3
  52.7 1.3 multiply_add_fusion.1
  58.7 0.7 bitcast_dynamic-update-slice_fusion
  59.5 1.3 collective-permute-start
  60.9 1.1 collective-permute-done
  61.9 23.8 %conditional.12 = (f32[2,128,128]{2,1,0:T(8,128)}, f32[2,3,2,128,128]{4,3,2,1,0:T(8,128)S(1)}, f32[2,2,128,128]{3,2,1,0:T(8,128)S(1)}) conditional(s32[]{:T(128)} %convert_element_type.355, (f32[2,3,2,128,128]{4,3,2,1,0:T(8,128)S(1)}, f32[2,2,128,128]{3,2,1,0:T(8,128)S(1)}) %tuple.295, (pred[]{:T(512)}, f32[2,128,128]{2,1,0:T(8,128)S(1)}, ...), branch_computations={%region_1.1_spmd, %region_2.2_spmd.clone} | conditional | flops 1209499648 | bytes 15597781 | solution.py:154
  64.5 0.6 dynamic_slice.38
  67.5 1.1 multiply_add_fusion.5
  73.4 1.3 multiply_add_fusion.3
  79.1 1.3 multiply_add_fusion.1
  85.1 0.7 bitcast_dynamic-update-slice_fusion
  85.8 2.3 collective-permute-start
  88.2 1.1 collective-permute-done
  89.3 0.7 conditional.12
  89.3 0.7 broadcast.97
  90.0 0.7 broadcast.107
  90.8 146.6 %while.45 = (s32[]{:T(128)}, f32[2,128,128]{2,1,0:T(8,128)}, f32[3,2,256,256]{3,2,1,0:T(8,128)S(1)}, f32[2,128,128]{2,1,0:T(8,128)S(1)}, s32[]{:T(128)}, /*index...) while((s32[]{:T(128)}, f32[2,128,128]{2,1,0:T(8,128)}, ...), condition=%wide.region_9.10_spmd.clone.clone.clone, body=%wide.region_4.9_spmd.clone.clone.clone.sunk | while | flops 1613299712 | bytes 24380844 | solution.py:190
  91.0 1.3 collective-permute-start.1
  92.4 24.5 %collective-permute-done.1 = f32[2,128,128]{2,1,0:T(8,128)S(1)} collective-permute-done((f32[2,128,128]{2,1,0:T(8,128)}, f32[2,128,128]{2,1,0:T(8,128)S(1)}, u32[]{:S(2)}, u32[]{:S(2)}) %collective-permute-start.1) | collective-permute-done | bytes 131104 | tf_op jit(solution)/shard_map/while/body/eval_jaxpr/ppermute | solution.py:20
  116.8 0.7 copy-done.2
  117.5 0.7 conditional.13
  117.5 0.7 broadcast.99
  118.2 1.3 collective-permute-start.1
  119.6 40.6 %collective-permute-done.1 = f32[2,128,128]{2,1,0:T(8,128)S(1)} collective-permute-done((f32[2,128,128]{2,1,0:T(8,128)}, f32[2,128,128]{2,1,0:T(8,128)S(1)}, u32[]{:S(2)}, u32[]{:S(2)}) %collective-permute-start.1) | collective-permute-done | bytes 131104 | tf_op jit(solution)/shard_map/while/body/eval_jaxpr/ppermute | solution.py:20
  160.1 0.7 copy-done.2
  160.8 36.2 %conditional.13 = (f32[2,128,128]{2,1,0:T(8,128)}, f32[3,2,256,256]{3,2,1,0:T(8,128)S(1)}, f32[2,128,128]{2,1,0:T(8,128)S(1)}) conditional(s32[]{:T(128)} %convert_element_type.357, (f32[3,2,256,256]{3,2,1,0:T(8,128)S(1)}, f32[2,128,128]{2,1,0:T(8,128)S(1)}) %tuple.299, (s32[]{:T(128)}, s32[2]{0:T(128)S(1)}, s32[2]{0:T(128)S(1)}, ...), branch_computations={%region_5.5_spmd, %region_6.8_spmd.clone} | conditional | flops 1613021184 | bytes 23134704 | solution.py:188
  160.8 0.7 dynamic_slice.42
  163.5 0.7 dynamic_slice.41
  167.2 0.9 conditional.9
  167.2 0.9 slice_bitcast_fusion
  172.5 1.3 multiply_add_fusion.9
  178.2 1.3 multiply_add_fusion.7
  184.2 1.1 add_bitcast_fusion.3
  185.4 0.7 select_add_fusion
  186.3 10.7 %dynamic_update_slice.13 = f32[3,2,256,256]{3,2,1,0:T(8,128)S(1)} dynamic-update-slice(f32[3,2,256,256]{3,2,1,0:T(8,128)S(1)} %get-tuple-element.1886, f32[3,2,128,128]{3,2,1,0:T(8,128)S(1)} %maximum_add_fusion, s32[]{:T(128)} %constant.156.clone.1, s32[]{:T(128)} %constant.156.clone.1, s32[]{:T(128)S(6)} %select_n.387, s32[]{:T(128)S(6)} %select_n.388) | dynamic-update-slice | bytes 786436 | tf_op jit(solution)/shard_map/while/body/eval_jaxpr/cond/branch_1_fun/dynamic_update_slice | solution.py:125
  197.0 1.3 collective-permute-start.1
  198.4 3.5 collective-permute-done.1
  201.9 0.7 copy-done.2
  202.6 34.8 %conditional.13 = (f32[2,128,128]{2,1,0:T(8,128)}, f32[3,2,256,256]{3,2,1,0:T(8,128)S(1)}, f32[2,128,128]{2,1,0:T(8,128)S(1)}) conditional(s32[]{:T(128)} %convert_element_type.357, (f32[3,2,256,256]{3,2,1,0:T(8,128)S(1)}, f32[2,128,128]{2,1,0:T(8,128)S(1)}) %tuple.299, (s32[]{:T(128)}, s32[2]{0:T(128)S(1)}, s32[2]{0:T(128)S(1)}, ...), branch_computations={%region_5.5_spmd, %region_6.8_spmd.clone} | conditional | flops 1613021184 | bytes 23134704 | solution.py:188
  202.6 0.7 dynamic_slice.42
  205.3 0.7 dynamic_slice.41
  209.0 0.9 conditional.9
  209.0 0.9 slice_bitcast_fusion
  214.3 1.3 multiply_add_fusion.9
  220.0 1.3 multiply_add_fusion.7
  226.0 1.1 add_bitcast_fusion.3
  227.1 0.7 select_add_fusion
  228.0 9.3 %dynamic_update_slice.13 = f32[3,2,256,256]{3,2,1,0:T(8,128)S(1)} dynamic-update-slice(f32[3,2,256,256]{3,2,1,0:T(8,128)S(1)} %get-tuple-element.1886, f32[3,2,128,128]{3,2,1,0:T(8,128)S(1)} %maximum_add_fusion, s32[]{:T(128)} %constant.156.clone.1, s32[]{:T(128)} %constant.156.clone.1, s32[]{:T(128)S(6)} %select_n.387, s32[]{:T(128)S(6)} %select_n.388) | dynamic-update-slice | bytes 786436 | tf_op jit(solution)/shard_map/while/body/eval_jaxpr/cond/branch_1_fun/dynamic_update_slice | solution.py:125
  238.1 107.4 %all-reduce.3.cloned.1.call-done = f32[2,128,128]{2,1,0:T(8,128)} async-done(((f32[2,128,128]{2,1,0:T(8,128)}), f32[2,128,128]{2,1,0:T(8,128)}) %all-reduce.3.cloned.1.call-update) | async-done | bytes 131088 | tf_op jit(solution)/shard_map/psum | solution.py:196
  345.4 1.6 broadcast_select_fusion.1
  347.0 18.3 %all-reduce.5.cloned.1.call-done = f32[2,128,128]{2,1,0:T(8,128)} async-done(((f32[2,128,128]{2,1,0:T(8,128)}), f32[2,128,128]{2,1,0:T(8,128)}) %all-reduce.5.cloned.1.call-update) | async-done | bytes 131088 | tf_op jit(solution)/shard_map/psum | solution.py:25
  365.3 1.5 constant_dynamic-slice_fusion
  366.8 2.2 slice_add_fusion
  (254 shorter events, 59.5 us)
Async XLA Ops:
  7.2 9.2 %copy-start.4 = (s32[2]{0:T(128)S(1)}, s32[2]{0:T(128)}, u32[]{:S(2)}) copy-start(s32[2]{0:T(128)} %param.21) | copy-start | bytes 28
  7.2 338.3 %all-reduce.3.cloned.1.call-start = ((), (), s32[]{:S(2)}) async-start(), calls=%async_computation | async-start | bytes 262144 | tf_op jit(solution)/shard_map/psum | solution.py:196
  7.2 24.1 %collective-permute-start.2 = (f32[3,2,128,256]{3,2,1,0:T(8,128)}, f32[3,2,128,256]{3,2,1,0:T(8,128)S(1)}, u32[]{:S(2)}, u32[]{:S(2)}) collective-permute-start(f32[3,2,128,256]{3,2,1,0:T(8,128)} %param.19), channel_id=1, source_target_pairs={{1,0},{2,1},{3,2},{4,3},{5,4},{6,5},{7,6},{8,7},{9,8},{10,9},{11,1... | collective-permute-start | bytes 2359304 | tf_op jit(solution)/shard_map/ppermute | solution.py:14
  16.3 16.7 %copy-start.1 = (f32[2,128,128]{2,1,0:T(8,128)S(1)}, f32[2,128,128]{2,1,0:T(8,128)}, u32[]{:S(2)}) copy-start(f32[2,128,128]{2,1,0:T(8,128)} %param.20) | copy-start | bytes 393220
  16.4 16.7 %copy-start.5 = (s32[2]{0:T(128)S(1)}, s32[2]{0:T(128)}, u32[]{:S(2)}) copy-start(s32[2]{0:T(128)} %param.22) | copy-start | bytes 28
  33.1 2.5 collective-permute-start
  59.5 2.5 collective-permute-start
  85.8 3.5 collective-permute-start
  91.0 25.9 %collective-permute-start.1 = (f32[2,128,128]{2,1,0:T(8,128)}, f32[2,128,128]{2,1,0:T(8,128)S(1)}, u32[]{:S(2)}, u32[]{:S(2)}) collective-permute-start(f32[2,128,128]{2,1,0:T(8,128)} %get-tuple-element.2270), channel_id=1, source_target_pairs={{16,0},{17,1},{18,2},{19,3},{20,4},{21,5},{22,6},{23,7},{24,8},{25... | collective-permute-start | bytes 393224 | tf_op jit(solution)/shard_map/while/body/eval_jaxpr/ppermute | solution.py:20
  116.8 0.7 copy-start.2
  118.2 41.9 %collective-permute-start.1 = (f32[2,128,128]{2,1,0:T(8,128)}, f32[2,128,128]{2,1,0:T(8,128)S(1)}, u32[]{:S(2)}, u32[]{:S(2)}) collective-permute-start(f32[2,128,128]{2,1,0:T(8,128)} %get-tuple-element.2270), channel_id=1, source_target_pairs={{16,0},{17,1},{18,2},{19,3},{20,4},{21,5},{22,6},{23,7},{24,8},{25... | collective-permute-start | bytes 393224 | tf_op jit(solution)/shard_map/while/body/eval_jaxpr/ppermute | solution.py:20
  160.1 0.7 copy-start.2
  197.0 4.9 %collective-permute-start.1 = (f32[2,128,128]{2,1,0:T(8,128)}, f32[2,128,128]{2,1,0:T(8,128)S(1)}, u32[]{:S(2)}, u32[]{:S(2)}) collective-permute-start(f32[2,128,128]{2,1,0:T(8,128)} %get-tuple-element.2270), channel_id=1, source_target_pairs={{16,0},{17,1},{18,2},{19,3},{20,4},{21,5},{22,6},{23,7},{24,8},{25... | collective-permute-start | bytes 393224 | tf_op jit(solution)/shard_map/while/body/eval_jaxpr/ppermute | solution.py:20
  201.9 0.7 copy-start.2
  237.3 0.7 copy-start
  237.4 129.4 %collective-permute-start.3 = (f32[3,2,128,256]{3,2,1,0:T(8,128)S(1)}, f32[3,2,128,256]{3,2,1,0:T(8,128)}, u32[]{:S(2)}, u32[]{:S(2)}) collective-permute-start(f32[3,2,128,256]{3,2,1,0:T(8,128)S(1)} %slice.116), channel_id=1, source_target_pairs={{15,0},{0,1},{1,2},{2,3},{3,4},{4,5},{5,6},{6,7},{7,8},{8,9},{9,10... | collective-permute-start | bytes 2359304 | tf_op jit(solution)/shard_map/ppermute | solution.py:14
  238.0 127.3 %all-reduce.5.cloned.1.call-start = ((), (), s32[]{:S(2)}) async-start(), calls=%async_computation.1 | async-start | bytes 262144 | tf_op jit(solution)/shard_map/psum | solution.py:25
Sparse Core Ops, SparseCore 0:
  238.1 107.2 all-reduce.2
  348.3 16.9 all-reduce.4
where the time goes:
time: 378 us; the launch traced here: 376 us
  waiting for transfers between devices  212 us (56%)
  matrix products  62.7 us (17%)
  local copies, waits for them, and re-layouts  38.7 us (10%)
  loops' own time  18.3 us (5%)
  starting transfers between devices  15.9 us (4%)
  between operations  14.1 us (4%)
  other arithmetic  13.8 us (4%)
    psum x1, waiting for transfers between devices, body(): scan_total = lax.psum(probe_part, 'scan')  107 us
    ppermute x6, waiting for transfers between devices, passed_along(): return lax.ppermute(block, axis, route)  71.7 us
    dot_general x192, matrix products, matmul_high(): return jnp.matmul(left_side, right_side, precision=lax.Precision.HIGHEST)  62.7 us
    dynamic_update_slice x2, local copies, waits for them, and re-layouts, add_window(): lax.dynamic_update_slice(accum, lax.dynamic_slice(accum, corner, window_s...  20 us
    psum x1, waiting for transfers between devices, broadcast(): return lax.psum(jnp.where(mine, x, jnp.zeros_like(x)), axis)  18.3 us
    ppermute x2, waiting for transfers between devices, from_behind(): return lax.ppermute(block, axis, route)  15 us
    another operation x3, loops' own time, backward_step(): return lax.cond(active_step, backward_run_section, backward_pass_along, 0)  9.2 us
    ppermute x6, starting transfers between devices, passed_along(): return lax.ppermute(block, axis, route)  8.75 us
  transfers between devices with their start and end apart: 10, of which 9 were waited for; matrix products, arithmetic and copies ran while one was open for 2% of the time, Pallas kernels for 0%

commit v1 on v0

v1 whole, which is shorter than its diff:
```python
import math

import jax
import jax.numpy as jnp
import ml_dtypes
import numpy as np
from jax import lax
from jax.experimental import pallas as pl
from jax.experimental.pallas import tpu as pltpu
from jax.sharding import PartitionSpec as P

PROPAGATION = 0.5
VMEM_LIMIT = 48 * 1024 * 1024


def block_form(matrix):
    return np.block([[matrix.real, -matrix.imag], [matrix.imag, matrix.real]])


def constant_tables(width):
    grid = np.arange(width)
    frequency = np.where(grid < width // 2, grid, grid - width)
    dft = np.exp(-2j * np.pi * ((grid[:, None] * grid[None, :]) % width) / width) / math.sqrt(width)
    chirp = np.exp(-1j * PROPAGATION * np.pi * frequency.astype(np.float64) ** 2 / width)
    step = dft.conj() @ (chirp[:, None] * dft)
    step = 0.5 * (step + step.T)
    full = np.stack([block_form(m) for m in (step, step.conj(), dft, dft.conj())])
    high = full.astype(np.float32).astype(ml_dtypes.bfloat16)
    low = (full - high.astype(np.float64)).astype(np.float32).astype(ml_dtypes.bfloat16)
    return np.stack([high, low], axis=1)


def halves(x):
    high = x.astype(jnp.bfloat16)
    return high, (x - high.astype(jnp.float32)).astype(jnp.bfloat16)


def dot(a, b):
    return jnp.dot(a, b, preferred_element_type=jnp.float32)


def times_right(x, high, low):
    x_high, x_low = halves(x)
    return dot(x_high, high) + (dot(x_low, high) + dot(x_high, low))


def times_left(high, low, x):
    x_high, x_low = halves(x)
    return dot(high, x_high) + (dot(high, x_low) + dot(low, x_high))


def both_sides(re, im, tables, which):
    n = re.shape[0]
    y = times_right(jnp.concatenate([re, im], axis=1), tables[which ^ 1, 0], tables[which ^ 1, 1])
    y = jnp.concatenate([y[:, :n], y[:, n:]], axis=0)
    z = times_left(tables[which, 0], tables[which, 1], y)
    return z[:n], z[n:]


def cut_kernel(scal, obj, mine, other, halo):
    slab, _, rows, cols = obj.shape
    width = mine.shape[-1]
    for s in range(slab):
        for p in range(2):
            tile = obj[s, p]
            for k, out in enumerate((mine, other, halo)):
                row, col = scal[2 * k], scal[2 * k + 1]
                part = pltpu.roll(tile, lax.rem(cols - col, cols), 1)[:, :width]
                out[s, p] = pltpu.roll(part, lax.rem(rows - row, rows), 0)


def wave_kernel(depth_count, scal, tables, probe, measured, *rest):
    own_parts = rest[:depth_count]
    halo_parts = rest[depth_count : 2 * depth_count]
    grads = rest[2 * depth_count : 3 * depth_count]
    probe_parts = rest[3 * depth_count : 4 * depth_count]
    layers, waves = rest[4 * depth_count :]
    slab = own_parts[0].shape[0]
    n = probe.shape[-1]
    count = slab * depth_count
    split, depth = scal[0], scal[1]
    inside = lax.broadcasted_iota(jnp.int32, (n, n), 0) < n - split
    for j in range(depth_count):
        base = lax.rem(depth - j + depth_count, depth_count) * slab
        for s in range(slab):
            layers[base + s] = own_parts[j][s]
    for q in range(depth_count):
        for s in range(slab):
            for p in range(2):
                layers[q * slab + s, p] = jnp.where(inside, layers[q * slab + s, p], halo_parts[q][s, p])

    def enter(s, re, im):
        waves[s, 0] = re
        waves[s, 1] = im
        o_re, o_im = layers[s, 0], layers[s, 1]
        return re * o_re - im * o_im, re * o_im + im * o_re

    def forward(s, wave):
        return both_sides(*enter(s, *wave), tables, 0)

    wave = lax.fori_loop(0, count - 1, forward, (probe[0], probe[1]), unroll=True if count <= 8 else 1)
    far_re, far_im = both_sides(*enter(count - 1, *wave), tables, 2)
    misfit = 2.0 * (far_re * far_re + far_im * far_im - measured[...])
    chi = both_sides(misfit * far_re, misfit * far_im, tables, 3)

    def leave(s, chi_re, chi_im):
        w_re, w_im = waves[s, 0], waves[s, 1]
        o_re, o_im = layers[s, 0], layers[s, 1]
        waves[s, 0] = w_re * chi_re + w_im * chi_im
        waves[s, 1] = w_re * chi_im - w_im * chi_re
        return o_re * chi_re + o_im * chi_im, o_re * chi_im - o_im * chi_re

    def backward(t, chi):
        return both_sides(*leave(count - 1 - t, *chi), tables, 1)

    chi = lax.fori_loop(0, count - 1, backward, chi, unroll=True if count <= 8 else 1)
    grad = leave(0, *chi)
    for j in range(depth_count):
        base = lax.rem(depth + j, depth_count) * slab
        for s in range(slab):
            grads[j][s] = waves[base + s]
    rows = n // depth_count
    waves[0, 0] = jnp.where(depth < 2, grad[0], 0.0)
    waves[0, 1] = jnp.where(depth < 2, grad[1], 0.0)
    for j in range(depth_count):
        start = pl.multiple_of(lax.rem(depth + j, depth_count) * rows, rows)
        for p in range(2):
            probe_parts[j][p] = waves[0, p, pl.ds(start, rows), :]


def place_kernel(scal, *refs):
    *parts, out = refs
    slab, _, rows, cols = out.shape
    width = parts[0].shape[-1]
    row_index = lax.broadcasted_iota(jnp.int32, (rows, width), 0)
    blank = jnp.zeros((rows, cols - width), jnp.float32)
    masks = [(row_index >= scal[4 * k + 2]) & (row_index < scal[4 * k + 3]) for k in range(len(parts))]
    for s in range(slab):
        for p in range(2):
            total = None
            for k, part in enumerate(parts):
                x = pltpu.roll(part[s, p], scal[4 * k], 0)
                x = jnp.where(masks[k], x, 0.0)
                x = pltpu.roll(jnp.concatenate([x, blank], axis=1), scal[4 * k + 1], 1)
                total = x if total is None else total + x
            out[s, p] = total


def call(kernel, name, scalars, arrays, outs, scratch=()):
    vmem = pl.BlockSpec(memory_space=pltpu.VMEM)
    moved = sum(math.prod(x.shape) * x.dtype.itemsize for x in (*arrays, *outs))
    return pl.pallas_call(
        kernel,
        name=name,
        out_shape=outs,
        in_specs=[pl.BlockSpec(memory_space=pltpu.SMEM)] + [vmem] * len(arrays),
        out_specs=[vmem] * len(outs),
        scratch_shapes=scratch,
        compiler_params=pltpu.CompilerParams(vmem_limit_bytes=VMEM_LIMIT),
        cost_estimate=pl.CostEstimate(flops=moved, bytes_accessed=moved, transcendentals=0),
    )(scalars, *arrays)


def total_over(x, axis):
    count = lax.axis_size(axis)
    if count & (count - 1):
        return lax.psum(x, axis)
    step = 1
    while step < count:
        x = x + lax.ppermute(x, axis, [(i, i ^ step) for i in range(count)])
        step *= 2
    return x


def body(objects, probe, row_offsets, col_offsets, intensity):
    slab, _, tile_rows, cols = objects.shape
    n = probe.shape[-1]
    depth_count, scan_count = lax.axis_size("depth"), lax.axis_size("scan")
    depth, scan = lax.axis_index("depth"), lax.axis_index("scan")
    f32 = jnp.float32
    ahead = [(i, (i + 1) % scan_count) for i in range(scan_count)]

    local = row_offsets - scan * tile_rows
    second = local[1] == tile_rows
    row_b = jnp.where(second, local[0], local[1])
    col_b = jnp.where(second, col_offsets[0], col_offsets[1])
    col_a = jnp.where(second, col_offsets[1], col_offsets[0])
    sent = lax.ppermute(jnp.stack([col_a, row_b, col_b]), "scan", ahead)
    col_a, row_p, col_p = sent[0], sent[1], sent[2]
    measured_a = lax.ppermute(jnp.where(second, intensity[1], intensity[0]), "scan", ahead)
    measured_b = jnp.where(second, intensity[0], intensity[1])

    on_a = depth == 0
    zero = jnp.zeros_like(col_a)
    row_mine, col_mine = jnp.where(on_a, zero, row_b), jnp.where(on_a, col_a, col_b)
    row_other, col_other = jnp.where(on_a, row_b, zero), jnp.where(on_a, col_b, col_a)
    window = jax.ShapeDtypeStruct((slab, 2, n, n), f32)
    mine, other, halo = call(
        cut_kernel,
        "cut",
        jnp.stack([row_mine, col_mine, row_other, col_other, row_p, col_p]),
        [objects],
        [window] * 3,
    )

    own = [mine]
    for j in range(1, depth_count):
        target = lax.rem(depth + j, depth_count)
        payload = other if depth_count == 2 else jnp.where((target == 0) | (depth == 0), other, mine)
        route = [((t - j) % depth_count, t) for t in (0, 1)]
        own.append(lax.ppermute(payload, "depth", route))

    def across(x, source, target, shift):
        route = [(source * scan_count + i, target * scan_count + (i + shift) % scan_count) for i in range(scan_count)]
        return lax.ppermute(x, ("depth", "scan"), route)

    halos = [across(halo, q, 1, -1) for q in range(depth_count)]

    split = jnp.where(on_a, zero, row_b)
    measured = jnp.where(on_a, measured_a, measured_b)
    tables = jnp.asarray(constant_tables(n))
    parts = call(
        lambda *refs: wave_kernel(depth_count, *refs),
        "wave",
        jnp.stack([split, depth]),
        [tables, probe, measured, *own, *halos],
        [window] * depth_count + [jax.ShapeDtypeStruct((2, n // depth_count, n), f32)] * depth_count,
        [pltpu.VMEM((slab * depth_count, 2, n, n), f32)] * 2,
    )
    grads, probe_parts = parts[:depth_count], parts[depth_count:]

    back = [grads[0]]
    probe_grad = probe_parts[0]
    for j in range(1, depth_count):
        back.append(lax.ppermute(grads[j], "depth", [(t, (t + j) % depth_count) for t in (0, 1)]))
        probe_grad = probe_grad + lax.ppermute(
            probe_parts[j], "depth", [(t, (t + j) % depth_count) for t in range(depth_count)]
        )
    spill = [across(grads[(q - 1) % depth_count], 1, q, 1) for q in range(depth_count)]
    arrived = spill[0]
    for q in range(1, depth_count):
        arrived = jnp.where(depth == q, spill[q], arrived)

    where_to = []
    for j in range(depth_count):
        is_a = depth == j
        is_b = lax.rem(depth + depth_count - 1, depth_count) == j
        row = jnp.where(is_a, zero, row_b)
        col = jnp.where(is_a, col_a, col_b)
        first = jnp.where(is_a, zero, row_b)
        last = jnp.where(is_a | is_b, zero + tile_rows, zero)
        where_to += [lax.rem(row, tile_rows), col, first, last]
    where_to += [lax.rem(row_p, tile_rows), col_p, zero, row_p]
    (object_grad,) = call(
        place_kernel,
        "place",
        jnp.stack(where_to),
        [*back, arrived],
        [jax.ShapeDtypeStruct(objects.shape, f32)],
    )
    return object_grad, total_over(probe_grad, "scan")


def solution(mesh):
    in_specs = (P("depth", None, "scan", None), P(), P("scan"), P("scan"), P("scan", None, None))
    out_specs = (P("depth", None, "scan", None), P(None, "depth", None))
    return jax.shard_map(body, mesh=mesh, in_specs=in_specs, out_specs=out_specs, check_vma=False)
```

time: 378 us -> 74.7 us (0.20)
  waiting for transfers between devices: 212 us -> 25.2 us
  matrix products: 62.7 us -> 0 us
  local copies, waits for them, and re-layouts: 38.7 us -> 5.22 us
  loops' own time: 18.3 us -> 0 us
  other arithmetic: 13.8 us -> 3.4 us
  Pallas kernels: 0 us -> 9.74 us
  starting transfers between devices: 15.9 us -> 21.5 us
  between operations: 14.1 us -> 9.19 us
    psum x2 -> x0, waiting for transfers between devices: 126 us -> none  [the longest x1 107 us: body(): scan_total = lax.psum(probe_part, 'scan')]
    dot_general x192 -> x0, matrix products: 62.7 us -> none  [matmul_high(): return jnp.matmul(left_side, right_side, precision=lax.Precision.HIGHEST)]
    ppermute x8 -> x13, waiting for transfers between devices: 86.7 us -> 25.2 us  [the longest x4 11.3 us: total_over(): x = x + lax.ppermute(x, axis, [(i, i ^ step) for i in range(count)])]
    dynamic_update_slice x2 -> x0, local copies, waits for them, and re-layouts: 20 us -> none  [add_window(): lax.dynamic_update_slice(accum, lax.dynamic_slice(accum, corner, window_s...]
    another operation x10 -> x0, loops' own time: 18.3 us -> none  [the longest x3 9.2 us: backward_step(): return lax.cond(active_step, backward_run_section, backward_pass_along, 0)]
    pallas_call x0 -> x3, Pallas kernels: none -> 9.74 us  [call(): pl.pallas_call(kernel, name=name, out_shape=outs, in_specs=[pl.BlockSpec(...]
    dynamic_slice x9 -> x0, local copies, waits for them, and re-layouts: 6.48 us -> none  [the longest x4 2.52 us: window_at(): local_rows[wave_index]]
    ppermute x8 -> x13, starting transfers between devices: 15.8 us -> 21.5 us  [the longest x4 9.53 us: total_over(): x = x + lax.ppermute(x, axis, [(i, i ^ step) for i in range(count)])]
  transfers between devices with their start and end apart: 10 -> 13, of which waited for: 9 -> 7; matrix products, arithmetic and copies ran while one was open for 2% -> 5% of each run, Pallas kernels for 0% -> 0%
where the time goes in v1:
time: 74.7 us; the launch traced here: 74.2 us
  waiting for transfers between devices  25.2 us (34%)
  starting transfers between devices  21.5 us (29%)
  Pallas kernels  9.74 us (13%)
  between operations  9.19 us (12%)
  local copies, waits for them, and re-layouts  5.22 us (7%)
  other arithmetic  3.4 us (5%)
    ppermute x4, waiting for transfers between devices, total_over(): x = x + lax.ppermute(x, axis, [(i, i ^ step) for i in range(count)])  11.3 us
    pallas_call x3, Pallas kernels, call(): pl.pallas_call(kernel, name=name, out_shape=outs, in_specs=[pl.BlockSpec(...  9.74 us
    ppermute x4, starting transfers between devices, total_over(): x = x + lax.ppermute(x, axis, [(i, i ^ step) for i in range(count)])  9.53 us
    ppermute x1, waiting for transfers between devices, body(): lax.ppermute(jnp.where(second, intensity[1], intensity[0]), 'scan', ahead)  7.42 us
    ppermute x4, starting transfers between devices, across(): return lax.ppermute(x, ('depth', 'scan'), route)  7.28 us
    ppermute x1, waiting for transfers between devices, body(): sent = lax.ppermute(jnp.stack([col_a, row_b, col_b]), 'scan', ahead)  5.51 us
    ppermute x1, starting transfers between devices, body(): sent = lax.ppermute(jnp.stack([col_a, row_b, col_b]), 'scan', ahead)  2.94 us
  transfers between devices with their start and end apart: 13, of which 7 were waited for; matrix products, arithmetic and copies ran while one was open for 5% of the time, Pallas kernels for 0%

profile of v1, /device:TPU:0, one launch (start us, length us, event | category | flops | bytes accessed | tf_op | source)
XLA Modules:
  0.0 74.2 jit_solution(8025381987179314622)
XLA Ops:
  0.6 0.0 copy-start
  0.6 0.7 %broadcast_subtract_fusion = s32[2]{0:T(128)S(1)} fusion(s32[2]{0:T(128)} %param.8, s32[]{:T(128)S(6)} %mul.3), kind=kLoop, calls=%fused_computation.5 | loop fusion | flops 2 | bytes 20 | tf_op jit(solution)/shard_map/sub | solution.py:183
  1.4 0.6 fusion.2
  2.6 1.3 %fusion.1 = (s32[1]{0:T(128)}, s32[1]{0:T(128)}) fusion(s32[2]{0:T(128)} %param.9), kind=kLoop, calls=%fused_computation.7 | loop fusion | bytes 16 | tf_op jit(solution)/shard_map/slice | solution.py:187
  7.8 0.1 pad_add_fusion
  7.8 2.9 %collective-permute-start = (s32[3]{0:T(128)S(1)}, s32[3]{0:T(128)S(1)}, u32[]{:S(2)}, u32[]{:S(2)}) collective-permute-start(s32[3]{0:T(128)S(1)} %pad_add_fusion), channel_id=1, source_target_pairs={{0,1},{1,2},{2,3},{3,4},{4,5},{5,6},{6,7},{7,8},{8,9},{9,10},{10,1... | collective-permute-start | bytes 44 | tf_op jit(solution)/shard_map/ppermute | solution.py:188
  10.8 5.5 %collective-permute-done = s32[3]{0:T(128)S(1)} collective-permute-done((s32[3]{0:T(128)S(1)}, s32[3]{0:T(128)S(1)}, u32[]{:S(2)}, u32[]{:S(2)}) %collective-permute-start) | collective-permute-done | bytes 44 | tf_op jit(solution)/shard_map/ppermute | solution.py:188
  16.3 0.7 fusion
  18.3 0.1 slice.44
  18.4 0.1 stack.78.scal
  18.5 0.0 copy-start.1
  18.5 1.1 %copy-done.1 = f32[3,2,128,256]{3,2,1,0:T(8,128)S(1)} copy-done((f32[3,2,128,256]{3,2,1,0:T(8,128)S(1)}, f32[3,2,128,256]{3,2,1,0:T(8,128)}, u32[]{:S(2)}) %copy-start.1) | copy-done | bytes 786456
  19.6 1.2 %cut.1 = (f32[3,2,128,128]{3,2,1,0:T(8,128)S(1)}, f32[3,2,128,128]{3,2,1,0:T(8,128)S(1)}, f32[3,2,128,128]{3,2,1,0:T(8,128)S(1)}) custom-call(s32[6]{0:T(128)S(1)} %stack.78.scal, f32[3,2,128,256]{3,2,1,0:T(8,128)S(1)} %copy-done.1), custom_call_target="tpu_custom_call" | custom-call | flops 1966080 | bytes 1966080 | tf_op jit(solution)/shard_map/cut/pallas_call | solution.py:152
  20.9 0.7 collective-permute-start.4
  21.6 4.6 %collective-permute-start.3 = (f32[3,2,128,128]{3,2,1,0:T(8,128)S(1)}, f32[3,2,128,128]{3,2,1,0:T(8,128)S(1)}, u32[]{:S(2)}, u32[]{:S(2)}) collective-permute-start(f32[3,2,128,128]{3,2,1,0:T(8,128)S(1)} %get-tuple-element.11), channel_id=1, source_target_pairs={{0,31},{1,16},{2,17},{3,18},{4,19},{5,20},{6,21},{7,22},{8,23},{9,... | collective-permute-start | bytes 1179656 | tf_op jit(solution)/shard_map/ppermute | solution.py:215
  26.2 0.1 collective-permute-start.2
  26.3 0.9 %select_bitcast_fusion = f32[128,128]{1,0:T(8,128)S(1)} fusion(f32[2,128,128]{2,1,0:T(8,128)} %param.10, pred[]{:T(512)S(6)} %eq.18), kind=kLoop, calls=%fused_computation.2 | loop fusion | flops 16384 | bytes 196609 | tf_op jit(solution)/shard_map/jit(_where)/select_n | solution.py:190
  27.2 0.6 collective-permute-start.1
  27.8 0.1 pad_add_fusion.1.refs_0_
  27.9 0.0 copy-start.2
  27.9 7.4 %collective-permute-done.1 = f32[128,128]{1,0:T(8,128)S(1)} collective-permute-done((f32[128,128]{1,0:T(8,128)S(1)}, f32[128,128]{1,0:T(8,128)S(1)}, u32[]{:S(2)}, u32[]{:S(2)}) %collective-permute-start.1) | collective-permute-done | bytes 65568 | tf_op jit(solution)/shard_map/ppermute | solution.py:190
  35.3 0.9 %bitcast_select_fusion.refs_3_ = f32[128,128]{1,0:T(8,128)S(1)} fusion(f32[128,128]{1,0:T(8,128)S(1)} %collective-permute-done.1, f32[2,128,128]{2,1,0:T(8,128)} %param.10, pred[]{:T(512)S(6)} %eq.18, pred[]{:T(512)S(6)} %eq.17), kind=kLoop, calls=%fused_computation.1 | loop fusion | flops 32768 | bytes 262146 | tf_op jit(solution)/shard_map/jit(_where)/select_n | solution.py:220
  36.2 0.0 collective-permute-done.2.refs_5_
  36.2 0.0 collective-permute-done.4.refs_7_
  36.2 0.0 collective-permute-done.3.refs_6_
  36.2 0.0 copy-done
  36.2 0.0 copy-done.2
  36.2 6.3 %wave.1 = (f32[3,2,128,128]{3,2,1,0:T(8,128)S(1)}, f32[3,2,128,128]{3,2,1,0:T(8,128)S(1)}, f32[2,64,128]{2,1,0:T(8,128)S(1)}, f32[2,64,128]{2,1,0:T(8,128)S(1)}) custom-call(s32[2]{0:T(128)S(1)} %pad_add_fusion.1.refs_0_, bf16[4,2,256,256]{3,2,1,0:T(8,128)(2,1)S(1)} %copy-done, f32[2,128,128]{2,1,0:T(8,128)S(1)} %copy-done.2, ...), custom_call_target="tpu_custom_call" | custom-call | flops 3735552 | bytes 3735552 | tf_op jit(solution)/shard_map/wave/pallas_call | solution.py:152
  42.6 0.7 collective-permute-start.6
  43.2 1.3 %collective-permute-start.7 = (f32[3,2,128,128]{3,2,1,0:T(8,128)S(1)}, f32[3,2,128,128]{3,2,1,0:T(8,128)S(1)}, u32[]{:S(2)}, u32[]{:S(2)}) collective-permute-start(f32[3,2,128,128]{3,2,1,0:T(8,128)S(1)} %get-tuple-element.13), channel_id=1, source_target_pairs={{16,1},{17,2},{18,3},{19,4},{20,5},{21,6},{22,7},{23,8},{24,9},{25... | collective-permute-start | bytes 1179656 | tf_op jit(solution)/shard_map/ppermute | solution.py:215
  44.5 1.1 %collective-permute-start.8 = (f32[2,64,128]{2,1,0:T(8,128)S(1)}, f32[2,64,128]{2,1,0:T(8,128)S(1)}, u32[]{:S(2)}, u32[]{:S(2)}) collective-permute-start(f32[2,64,128]{2,1,0:T(8,128)S(1)} %get-tuple-element.15), channel_id=1, source_target_pairs={{0,16},{16,0},{1,17},{17,1},{2,18},{18,2},{3,19},{19,3},{4,20},{20... | collective-permute-start | bytes 196616 | tf_op jit(solution)/shard_map/ppermute | solution.py:236
  45.6 0.9 %collective-permute-done.8 = f32[2,64,128]{2,1,0:T(8,128)S(1)} collective-permute-done((f32[2,64,128]{2,1,0:T(8,128)S(1)}, f32[2,64,128]{2,1,0:T(8,128)S(1)}, u32[]{:S(2)}, u32[]{:S(2)}) %collective-permute-start.8) | collective-permute-done | bytes 65568 | tf_op jit(solution)/shard_map/ppermute | solution.py:236
  46.5 1.6 %collective-permute-start.9 = (f32[2,64,128]{2,1,0:T(8,128)S(1)}, f32[2,64,128]{2,1,0:T(8,128)S(1)}, u32[]{:S(2)}, u32[]{:S(2)}) collective-permute-start(f32[2,64,128]{2,1,0:T(8,128)S(1)} %add.20), channel_id=1, source_target_pairs={{0,1},{1,0},{2,3},{3,2},{4,5},{5,4},{6,7},{7,6},{8,9},{9,8},{10,11... | collective-permute-start | bytes 196616 | tf_op jit(solution)/shard_map/ppermute | solution.py:170
  48.1 3.5 %collective-permute-done.9 = f32[2,64,128]{2,1,0:T(8,128)S(1)} collective-permute-done((f32[2,64,128]{2,1,0:T(8,128)S(1)}, f32[2,64,128]{2,1,0:T(8,128)S(1)}, u32[]{:S(2)}, u32[]{:S(2)}) %collective-permute-start.9) | collective-permute-done | bytes 65568 | tf_op jit(solution)/shard_map/ppermute | solution.py:170
  51.6 7.7 %collective-permute-start.10 = (f32[2,64,128]{2,1,0:T(8,128)S(1)}, f32[2,64,128]{2,1,0:T(8,128)S(1)}, u32[]{:S(2)}, u32[]{:S(2)}) collective-permute-start(f32[2,64,128]{2,1,0:T(8,128)S(1)} %add.21), channel_id=1, source_target_pairs={{0,2},{1,3},{2,0},{3,1},{4,6},{5,7},{6,4},{7,5},{8,10},{9,11},{10,... | collective-permute-start | bytes 196616 | tf_op jit(solution)/shard_map/ppermute | solution.py:170
  59.4 0.0 collective-permute-start.5
  59.4 2.2 %collective-permute-done.10 = f32[2,64,128]{2,1,0:T(8,128)S(1)} collective-permute-done((f32[2,64,128]{2,1,0:T(8,128)S(1)}, f32[2,64,128]{2,1,0:T(8,128)S(1)}, u32[]{:S(2)}, u32[]{:S(2)}) %collective-permute-start.10) | collective-permute-done | bytes 65568 | tf_op jit(solution)/shard_map/ppermute | solution.py:170
  61.6 0.1 collective-permute-start.11
  61.7 4.3 %collective-permute-done.11 = f32[2,64,128]{2,1,0:T(8,128)S(1)} collective-permute-done((f32[2,64,128]{2,1,0:T(8,128)S(1)}, f32[2,64,128]{2,1,0:T(8,128)S(1)}, u32[]{:S(2)}, u32[]{:S(2)}) %collective-permute-start.11) | collective-permute-done | bytes 65568 | tf_op jit(solution)/shard_map/ppermute | solution.py:170
  66.0 0.1 collective-permute-start.12
  68.6 1.3 %stack.73.scal = s32[12]{0:T(128)S(1)} concatenate(s32[1]{0:T(128)} %bitcast.2, s32[1]{0:T(128)} %bitcast.9, s32[1]{0:T(128)} %bitcast.10, s32[1]{0:T(128)} %bitcast.11, s32[1]{0:T(128)} %bitcast.12, s32[1]{0:T(128)} %bitcast.13, s32[1]{0:T(128)} %bitcast.14, s32[1]{0:T(128)} %bitcast.15, s32[1]{0:T(128)} %bitcast.17, s32[1]{0:T(128)} %get-tuple-element.16, s32[1]{0:T(128)} %constant.30.clone.1, ...), dimensions={0} | concatenate | bytes 96 | tf_op jit(solution)/shard_map/stack | solution.py:257
  70.0 1.4 %collective-permute-done.12 = f32[2,64,128]{2,1,0:T(8,128)S(1)} collective-permute-done((f32[2,64,128]{2,1,0:T(8,128)S(1)}, f32[2,64,128]{2,1,0:T(8,128)S(1)}, u32[]{:S(2)}, u32[]{:S(2)}) %collective-permute-start.12) | collective-permute-done | bytes 65568 | tf_op jit(solution)/shard_map/ppermute | solution.py:170
  71.3 0.6 add.24
  72.0 0.0 collective-permute-done.6
  72.0 0.0 collective-permute-done.7
  72.0 0.1 broadcast_select_fusion.refs_2_
  72.0 0.0 collective-permute-done.5.refs_1_
  72.0 2.2 %place.1 = f32[3,2,128,256]{3,2,1,0:T(8,128)} custom-call(s32[12]{0:T(128)S(1)} %stack.73.scal, f32[3,2,128,128]{3,2,1,0:T(8,128)S(1)} %get-tuple-element.12.refs_0_, f32[3,2,128,128]{3,2,1,0:T(8,128)S(1)} %collective-permute-done.5.refs_1_, f32[3,2,128,128]{3,2,1,0:T(8,128)S(1)} %broadcast_select_fusion.refs_2_), custom_call_target="tpu_custom_call" | custom-call | flops 1966080 | bytes 1966080 | tf_op jit(solution)/shard_map/place/pallas_call | solution.py:152
  (4 shorter events, 0.0 us)
Async XLA Ops:
  0.6 35.6 %copy-start = (bf16[4,2,256,256]{3,2,1,0:T(8,128)(2,1)S(1)}, bf16[4,2,256,256]{3,2,1,0:T(8,128)(2,1)}, u32[]{:S(2)}) copy-start(bf16[4,2,256,256]{3,2,1,0:T(8,128)(2,1)} %constant.31.clone.refs_1_) | copy-start | bytes 3145732
  7.8 8.5 %collective-permute-start = (s32[3]{0:T(128)S(1)}, s32[3]{0:T(128)S(1)}, u32[]{:S(2)}, u32[]{:S(2)}) collective-permute-start(s32[3]{0:T(128)S(1)} %pad_add_fusion), channel_id=1, source_target_pairs={{0,1},{1,2},{2,3},{3,4},{4,5},{5,6},{6,7},{7,8},{8,9},{9,10},{10,1... | collective-permute-start | bytes 44 | tf_op jit(solution)/shard_map/ppermute | solution.py:188
  18.5 1.1 %copy-start.1 = (f32[3,2,128,256]{3,2,1,0:T(8,128)S(1)}, f32[3,2,128,256]{3,2,1,0:T(8,128)}, u32[]{:S(2)}) copy-start(f32[3,2,128,256]{3,2,1,0:T(8,128)} %obj.1) | copy-start | bytes 2359300
  20.9 15.3 %collective-permute-start.4 = (f32[3,2,128,128]{3,2,1,0:T(8,128)S(1)}, f32[3,2,128,128]{3,2,1,0:T(8,128)S(1)}, u32[]{:S(2)}, u32[]{:S(2)}) collective-permute-start(f32[3,2,128,128]{3,2,1,0:T(8,128)S(1)} %get-tuple-element.11), channel_id=1, source_target_pairs={{16,31},{17,16},{18,17},{19,18},{20,19},{21,20},{22,21},{23,22},{2... | collective-permute-start | bytes 1179656 | tf_op jit(solution)/shard_map/ppermute | solution.py:215
  21.6 14.6 %collective-permute-start.3 = (f32[3,2,128,128]{3,2,1,0:T(8,128)S(1)}, f32[3,2,128,128]{3,2,1,0:T(8,128)S(1)}, u32[]{:S(2)}, u32[]{:S(2)}) collective-permute-start(f32[3,2,128,128]{3,2,1,0:T(8,128)S(1)} %get-tuple-element.11), channel_id=1, source_target_pairs={{0,31},{1,16},{2,17},{3,18},{4,19},{5,20},{6,21},{7,22},{8,23},{9,... | collective-permute-start | bytes 1179656 | tf_op jit(solution)/shard_map/ppermute | solution.py:215
  26.2 10.0 %collective-permute-start.2 = (f32[3,2,128,128]{3,2,1,0:T(8,128)S(1)}, f32[3,2,128,128]{3,2,1,0:T(8,128)S(1)}, u32[]{:S(2)}, u32[]{:S(2)}) collective-permute-start(f32[3,2,128,128]{3,2,1,0:T(8,128)S(1)} %get-tuple-element.10), channel_id=1, source_target_pairs={{16,0},{0,16},{17,1},{1,17},{18,2},{2,18},{19,3},{3,19},{20,4},{4,... | collective-permute-start | bytes 1179656 | tf_op jit(solution)/shard_map/ppermute | solution.py:211
  27.2 8.1 %collective-permute-start.1 = (f32[128,128]{1,0:T(8,128)S(1)}, f32[128,128]{1,0:T(8,128)S(1)}, u32[]{:S(2)}, u32[]{:S(2)}) collective-permute-start(f32[128,128]{1,0:T(8,128)S(1)} %select_bitcast_fusion), channel_id=1, source_target_pairs={{0,1},{1,2},{2,3},{3,4},{4,5},{5,6},{6,7},{7,8},{8,9},{9,10},{10,1... | collective-permute-start | bytes 196616 | tf_op jit(solution)/shard_map/ppermute | solution.py:190
  27.9 8.4 %copy-start.2 = (f32[2,128,128]{2,1,0:T(8,128)S(1)}, f32[2,128,128]{2,1,0:T(8,128)}, u32[]{:S(2)}) copy-start(f32[2,128,128]{2,1,0:T(8,128)} %refs_2_.1) | copy-start | bytes 393220
  42.6 29.4 %collective-permute-start.6 = (f32[3,2,128,128]{3,2,1,0:T(8,128)S(1)}, f32[3,2,128,128]{3,2,1,0:T(8,128)S(1)}, u32[]{:S(2)}, u32[]{:S(2)}) collective-permute-start(f32[3,2,128,128]{3,2,1,0:T(8,128)S(1)} %get-tuple-element.12.refs_0_), channel_id=1, source_target_pairs={{16,17},{17,18},{18,19},{19,20},{20,21},{21,22},{22,23},{23,24},{2... | collective-permute-start | bytes 1179656 | tf_op jit(solution)/shard_map/ppermute | solution.py:215
  43.2 28.7 %collective-permute-start.7 = (f32[3,2,128,128]{3,2,1,0:T(8,128)S(1)}, f32[3,2,128,128]{3,2,1,0:T(8,128)S(1)}, u32[]{:S(2)}, u32[]{:S(2)}) collective-permute-start(f32[3,2,128,128]{3,2,1,0:T(8,128)S(1)} %get-tuple-element.13), channel_id=1, source_target_pairs={{16,1},{17,2},{18,3},{19,4},{20,5},{21,6},{22,7},{23,8},{24,9},{25... | collective-permute-start | bytes 1179656 | tf_op jit(solution)/shard_map/ppermute | solution.py:215
  44.5 2.0 %collective-permute-start.8 = (f32[2,64,128]{2,1,0:T(8,128)S(1)}, f32[2,64,128]{2,1,0:T(8,128)S(1)}, u32[]{:S(2)}, u32[]{:S(2)}) collective-permute-start(f32[2,64,128]{2,1,0:T(8,128)S(1)} %get-tuple-element.15), channel_id=1, source_target_pairs={{0,16},{16,0},{1,17},{17,1},{2,18},{18,2},{3,19},{19,3},{4,20},{20... | collective-permute-start | bytes 196616 | tf_op jit(solution)/shard_map/ppermute | solution.py:236
  46.5 5.1 %collective-permute-start.9 = (f32[2,64,128]{2,1,0:T(8,128)S(1)}, f32[2,64,128]{2,1,0:T(8,128)S(1)}, u32[]{:S(2)}, u32[]{:S(2)}) collective-permute-start(f32[2,64,128]{2,1,0:T(8,128)S(1)} %add.20), channel_id=1, source_target_pairs={{0,1},{1,0},{2,3},{3,2},{4,5},{5,4},{6,7},{7,6},{8,9},{9,8},{10,11... | collective-permute-start | bytes 196616 | tf_op jit(solution)/shard_map/ppermute | solution.py:170
  51.6 10.0 %collective-permute-start.10 = (f32[2,64,128]{2,1,0:T(8,128)S(1)}, f32[2,64,128]{2,1,0:T(8,128)S(1)}, u32[]{:S(2)}, u32[]{:S(2)}) collective-permute-start(f32[2,64,128]{2,1,0:T(8,128)S(1)} %add.21), channel_id=1, source_target_pairs={{0,2},{1,3},{2,0},{3,1},{4,6},{5,7},{6,4},{7,5},{8,10},{9,11},{10,... | collective-permute-start | bytes 196616 | tf_op jit(solution)/shard_map/ppermute | solution.py:170
  59.4 12.7 %collective-permute-start.5 = (f32[3,2,128,128]{3,2,1,0:T(8,128)S(1)}, f32[3,2,128,128]{3,2,1,0:T(8,128)S(1)}, u32[]{:S(2)}, u32[]{:S(2)}) collective-permute-start(f32[3,2,128,128]{3,2,1,0:T(8,128)S(1)} %get-tuple-element.13), channel_id=1, source_target_pairs={{0,16},{16,0},{1,17},{17,1},{2,18},{18,2},{3,19},{19,3},{4,20},{20... | collective-permute-start | bytes 1179656 | tf_op jit(solution)/shard_map/ppermute | solution.py:235
  61.6 4.3 %collective-permute-start.11 = (f32[2,64,128]{2,1,0:T(8,128)S(1)}, f32[2,64,128]{2,1,0:T(8,128)S(1)}, u32[]{:S(2)}, u32[]{:S(2)}) collective-permute-start(f32[2,64,128]{2,1,0:T(8,128)S(1)} %add.22), channel_id=1, source_target_pairs={{0,4},{1,5},{2,6},{3,7},{4,0},{5,1},{6,2},{7,3},{8,12},{9,13},{10,... | collective-permute-start | bytes 196616 | tf_op jit(solution)/shard_map/ppermute | solution.py:170
  66.0 5.4 %collective-permute-start.12 = (f32[2,64,128]{2,1,0:T(8,128)S(1)}, f32[2,64,128]{2,1,0:T(8,128)S(1)}, u32[]{:S(2)}, u32[]{:S(2)}) collective-permute-start(f32[2,64,128]{2,1,0:T(8,128)S(1)} %add.23), channel_id=1, source_target_pairs={{0,8},{1,9},{2,10},{3,11},{4,12},{5,13},{6,14},{7,15},{8,0},{9,1},... | collective-permute-start | bytes 196616 | tf_op jit(solution)/shard_map/ppermute | solution.py:170

commit v2 on v1

v2 whole, which is shorter than its diff:
```python
import math

import jax
import jax.numpy as jnp
import ml_dtypes
import numpy as np
from jax import lax
from jax.experimental import pallas as pl
from jax.experimental.pallas import tpu as pltpu
from jax.sharding import PartitionSpec as P

PROPAGATION = 0.5
VMEM_LIMIT = 48 * 1024 * 1024


def block_form(matrix):
    return np.block([[matrix.real, -matrix.imag], [matrix.imag, matrix.real]])


def constant_tables(width):
    grid = np.arange(width)
    frequency = np.where(grid < width // 2, grid, grid - width)
    dft = np.exp(-2j * np.pi * ((grid[:, None] * grid[None, :]) % width) / width) / math.sqrt(width)
    chirp = np.exp(-1j * PROPAGATION * np.pi * frequency.astype(np.float64) ** 2 / width)
    step = dft.conj() @ (chirp[:, None] * dft)
    step = 0.5 * (step + step.T)
    full = np.stack([block_form(m) for m in (step, step.conj(), dft, dft.conj())])
    high = full.astype(np.float32).astype(ml_dtypes.bfloat16)
    low = (full - high.astype(np.float64)).astype(np.float32).astype(ml_dtypes.bfloat16)
    return np.stack([high, low], axis=1)


def halves(x):
    high = x.astype(jnp.bfloat16)
    return high, (x - high.astype(jnp.float32)).astype(jnp.bfloat16)


def dot(a, b):
    return jnp.dot(a, b, preferred_element_type=jnp.float32)


def times_right(x, high, low):
    x_high, x_low = halves(x)
    return dot(x_high, high) + (dot(x_low, high) + dot(x_high, low))


def times_left(high, low, x):
    x_high, x_low = halves(x)
    return dot(high, x_high) + (dot(high, x_low) + dot(low, x_high))


def both_sides(re, im, tables, which):
    n = re.shape[0]
    y = times_right(jnp.concatenate([re, im], axis=1), tables[which ^ 1, 0], tables[which ^ 1, 1])
    y = jnp.concatenate([y[:, :n], y[:, n:]], axis=0)
    z = times_left(tables[which, 0], tables[which, 1], y)
    return z[:n], z[n:]


def share(rows, cols, tile_rows, chips_back):
    count = lax.axis_size("scan")
    base = lax.rem(lax.axis_index("scan") + count - chips_back, count) * tile_rows
    second = rows[1] - base == tile_rows
    a = jnp.where(second, 1, 0)
    return a, cols[a], rows[1 - a] - base, cols[1 - a]


def cut_kernel(rows_own, cols_own, rows_prev, cols_prev, obj, mine, other, halo):
    slab, _, rows, cols = obj.shape
    width = mine.shape[-1]
    on_a = lax.axis_index("depth") == 0
    _, _, row_b, col_b = share(rows_own, cols_own, rows, 0)
    _, col_a, row_p, col_p = share(rows_prev, cols_prev, rows, 1)
    row_mine, col_mine = jnp.where(on_a, 0, row_b), jnp.where(on_a, col_a, col_b)
    row_other, col_other = jnp.where(on_a, row_b, 0), jnp.where(on_a, col_b, col_a)
    corners = ((mine, row_mine, col_mine), (other, row_other, col_other), (halo, row_p, col_p))
    for s in range(slab):
        for p in range(2):
            tile = obj[s, p]
            for out, row, col in corners:
                part = pltpu.roll(tile, lax.rem(cols - col, cols), 1)[:, :width]
                out[s, p] = pltpu.roll(part, lax.rem(rows - row, rows), 0)


def wave_kernel(depth_count, rows_own, cols_own, rows_prev, cols_prev, tables, probe, near, far, *rest):
    own_parts = rest[:depth_count]
    halo_parts = rest[depth_count : 2 * depth_count]
    grads = rest[2 * depth_count : 3 * depth_count]
    probe_grad, layers, waves = rest[3 * depth_count :]
    slab = own_parts[0].shape[0]
    n = probe.shape[-1]
    count = slab * depth_count
    depth = lax.axis_index("depth")
    on_a = depth == 0
    a_own, _, row_b, _ = share(rows_own, cols_own, n, 0)
    a_prev, _, _, _ = share(rows_prev, cols_prev, n, 1)
    measured = jnp.where(on_a, far[a_prev], near[1 - a_own])
    split = jnp.where(on_a, 0, row_b)
    inside = lax.broadcasted_iota(jnp.int32, (n, n), 0) < n - split
    for j in range(depth_count):
        base = lax.rem(depth - j + depth_count, depth_count) * slab
        for s in range(slab):
            layers[base + s] = own_parts[j][s]
    for q in range(depth_count):
        for s in range(slab):
            for p in range(2):
                layers[q * slab + s, p] = jnp.where(inside, layers[q * slab + s, p], halo_parts[q][s, p])

    def enter(s, re, im):
        waves[s, 0] = re
        waves[s, 1] = im
        o_re, o_im = layers[s, 0], layers[s, 1]
        return re * o_re - im * o_im, re * o_im + im * o_re

    def forward(s, wave):
        return both_sides(*enter(s, *wave), tables, 0)

    wave = lax.fori_loop(0, count - 1, forward, (probe[0], probe[1]), unroll=True if count <= 8 else 1)
    far_re, far_im = both_sides(*enter(count - 1, *wave), tables, 2)
    misfit = 2.0 * (far_re * far_re + far_im * far_im - measured)
    chi = both_sides(misfit * far_re, misfit * far_im, tables, 3)

    def leave(s, chi_re, chi_im):
        w_re, w_im = waves[s, 0], waves[s, 1]
        o_re, o_im = layers[s, 0], layers[s, 1]
        waves[s, 0] = w_re * chi_re + w_im * chi_im
        waves[s, 1] = w_re * chi_im - w_im * chi_re
        return o_re * chi_re + o_im * chi_im, o_re * chi_im - o_im * chi_re

    def backward(t, chi):
        return both_sides(*leave(count - 1 - t, *chi), tables, 1)

    chi = lax.fori_loop(0, count - 1, backward, chi, unroll=True if count <= 8 else 1)
    grad = leave(0, *chi)
    for j in range(depth_count):
        base = lax.rem(depth + j, depth_count) * slab
        for s in range(slab):
            grads[j][s] = waves[base + s]
    rows = n // depth_count
    for k in range(depth_count):
        for p in range(2):
            probe_grad[k, p] = jnp.where(depth < 2, grad[p][k * rows : (k + 1) * rows], 0.0)


def place_kernel(depth_count, rows_own, cols_own, rows_prev, cols_prev, *refs):
    *parts, out = refs
    slab, _, rows, cols = out.shape
    width = parts[0].shape[-1]
    depth = lax.axis_index("depth")
    _, _, row_b, col_b = share(rows_own, cols_own, rows, 0)
    _, col_a, row_p, col_p = share(rows_prev, cols_prev, rows, 1)
    row_index = lax.broadcasted_iota(jnp.int32, (rows, width), 0)
    blank = jnp.zeros((rows, cols - width), jnp.float32)
    corners = []
    for j in range(depth_count):
        is_a = depth == j
        is_b = lax.rem(depth + depth_count - 1, depth_count) == j
        row = jnp.where(is_a, 0, row_b)
        last = jnp.where(is_a | is_b, rows, 0)
        corners.append((row, jnp.where(is_a, col_a, col_b), row, last))
    corners.append((row_p, col_p, 0, row_p))
    masks = [(row_index >= first) & (row_index < last) for _, _, first, last in corners]
    for s in range(slab):
        for p in range(2):
            total = None
            for (row, col, _, _), mask, part in zip(corners, masks, parts):
                x = jnp.where(mask, pltpu.roll(part[s, p], lax.rem(row, rows), 0), 0.0)
                x = pltpu.roll(jnp.concatenate([x, blank], axis=1), col, 1)
                total = x if total is None else total + x
            out[s, p] = total


def call(kernel, name, scalars, arrays, outs, scratch=()):
    vmem = pl.BlockSpec(memory_space=pltpu.VMEM)
    moved = sum(math.prod(x.shape) * x.dtype.itemsize for x in (*arrays, *outs))
    return pl.pallas_call(
        kernel,
        name=name,
        out_shape=outs,
        in_specs=[pl.BlockSpec(memory_space=pltpu.SMEM)] * len(scalars) + [vmem] * len(arrays),
        out_specs=[vmem] * len(outs),
        scratch_shapes=scratch,
        compiler_params=pltpu.CompilerParams(vmem_limit_bytes=VMEM_LIMIT),
        cost_estimate=pl.CostEstimate(flops=moved, bytes_accessed=moved, transcendentals=0),
    )(*scalars, *arrays)


def total_over(blocks):
    depth_count, _, rows, n = blocks.shape
    scan_count = lax.axis_size("scan")
    if (2 * rows) % (8 * scan_count) == 0:
        piece = 2 * rows // scan_count
        pieces = blocks.reshape(depth_count * scan_count, piece, n)
        pieces = lax.all_to_all(pieces, ("depth", "scan"), 0, 0, tiled=True)
        summed = jnp.broadcast_to(jnp.sum(pieces, axis=0), (scan_count, piece, n))
        return lax.all_to_all(summed, "scan", 0, 0, tiled=True).reshape(2, rows, n)
    block = lax.psum_scatter(blocks, "depth", scatter_dimension=0)
    if scan_count & (scan_count - 1):
        return lax.psum(block, "scan")
    step = 1
    while step < scan_count:
        block = block + lax.ppermute(block, "scan", [(i, i ^ step) for i in range(scan_count)])
        step *= 2
    return block


def body(objects, probe, row_offsets, col_offsets, intensity):
    slab = objects.shape[0]
    n = probe.shape[-1]
    depth_count, scan_count = lax.axis_size("depth"), lax.axis_size("scan")
    depth = lax.axis_index("depth")
    f32 = jnp.float32

    def across(x, source, target, shift):
        route = [(source * scan_count + i, target * scan_count + (i + shift) % scan_count) for i in range(scan_count)]
        return lax.ppermute(x, ("depth", "scan"), route)

    ahead = [(i, (i + 1) % scan_count) for i in range(scan_count)]
    rows_prev = lax.ppermute(row_offsets, "scan", ahead)
    cols_prev = lax.ppermute(col_offsets, "scan", ahead)
    far = across(intensity, 0, 0, 1)
    offsets = [row_offsets, col_offsets, rows_prev, cols_prev]

    window = jax.ShapeDtypeStruct((slab, 2, n, n), f32)
    mine, other, halo = call(cut_kernel, "cut", offsets, [objects], [window] * 3)

    own = [mine]
    for j in range(1, depth_count):
        target = lax.rem(depth + j, depth_count)
        payload = other if depth_count == 2 else jnp.where((target == 0) | (depth == 0), other, mine)
        route = [((t - j) % depth_count, t) for t in (0, 1)]
        own.append(lax.ppermute(payload, "depth", route))
    halos = [across(halo, q, 1, -1) for q in range(depth_count)]

    tables = jnp.asarray(constant_tables(n))
    *grads, probe_blocks = call(
        lambda *refs: wave_kernel(depth_count, *refs),
        "wave",
        offsets,
        [tables, probe, intensity, far, *own, *halos],
        [window] * depth_count + [jax.ShapeDtypeStruct((depth_count, 2, n // depth_count, n), f32)],
        [pltpu.VMEM((slab * depth_count, 2, n, n), f32)] * 2,
    )
    probe_grad = total_over(probe_blocks)

    back = [grads[0]]
    for j in range(1, depth_count):
        back.append(lax.ppermute(grads[j], "depth", [(t, (t + j) % depth_count) for t in (0, 1)]))
    spill = [across(grads[(q - 1) % depth_count], 1, q, 1) for q in range(depth_count)]
    arrived = spill[0]
    for q in range(1, depth_count):
        arrived = jnp.where(depth == q, spill[q], arrived)
    (object_grad,) = call(
        lambda *refs: place_kernel(depth_count, *refs),
        "place",
        offsets,
        [*back, arrived],
        [jax.ShapeDtypeStruct(objects.shape, f32)],
    )
    return object_grad, probe_grad


def solution(mesh):
    in_specs = (P("depth", None, "scan", None), P(), P("scan"), P("scan"), P("scan", None, None))
    out_specs = (P("depth", None, "scan", None), P(None, "depth", None))
    return jax.shard_map(body, mesh=mesh, in_specs=in_specs, out_specs=out_specs, check_vma=False)
```

time: 74.7 us -> 70.7 us (0.946)
  between operations: 9.19 us -> 0.75 us
  waiting for transfers between devices: 25.2 us -> 31.2 us
  other arithmetic: 3.4 us -> 0.08 us
  Pallas kernels: 9.74 us -> 10.6 us
    ppermute x7 -> x2, waiting for transfers between devices: 25.2 us -> 5.78 us  [the longest x1 4.16 us: body(): rows_prev = lax.ppermute(row_offsets, 'scan', ahead)]
    all_to_all x0 -> x2, waiting for transfers between devices: none -> 18 us  [the longest x1 10.5 us: total_over(): pieces = lax.all_to_all(pieces, ('depth', 'scan'), 0, 0, tiled=True)]
    all_to_all x0 -> x2, starting transfers between devices: none -> 10.1 us  [the longest x1 6.56 us: total_over(): pieces = lax.all_to_all(pieces, ('depth', 'scan'), 0, 0, tiled=True)]
    ppermute x7 -> x2, starting transfers between devices: 14.2 us -> 4.48 us  [the longest x1 2.99 us: body(): rows_prev = lax.ppermute(row_offsets, 'scan', ahead)]
    ppermute x4 -> x5, waiting for transfers between devices: 0.01 us -> 7.36 us  [across(): return lax.ppermute(x, ('depth', 'scan'), route)]
    unnamed x6 -> x17, local copies, waits for them, and re-layouts: 1.14 us -> 4.9 us
    slice x4 -> x0, local copies, waits for them, and re-layouts: 2.65 us -> none  [the longest x1 1.33 us: body(): col_a = jnp.where(second, col_offsets[1], col_offsets[0])]
    select_n x2 -> x0, other arithmetic: 1.77 us -> none  [the longest x1 0.89 us: body(): measured = jnp.where(on_a, measured_a, measured_b)]
  transfers between devices with their start and end apart: 13 -> 11, of which waited for: 7 -> 5; matrix products, arithmetic and copies ran while one was open for 5% -> 1% of each run, Pallas kernels for 0% -> 0%
where the time goes in v2:
time: 70.7 us; the launch traced here: 70.3 us
  waiting for transfers between devices  31.2 us (44%)
  starting transfers between devices  22.1 us (31%)
  Pallas kernels  10.6 us (15%)
  local copies, waits for them, and re-layouts  5.53 us (8%)
  between operations  0.75 us (1%)
    pallas_call x3, Pallas kernels, call(): pl.pallas_call(kernel, name=name, out_shape=outs, in_specs=[pl.BlockSpec(...  10.6 us
    all_to_all x1, waiting for transfers between devices, total_over(): pieces = lax.all_to_all(pieces, ('depth', 'scan'), 0, 0, tiled=True)  10.5 us
    all_to_all x1, waiting for transfers between devices, total_over(): return lax.all_to_all(summed, 'scan', 0, 0, tiled=True).reshape(2, rows, n)  7.5 us
    ppermute x5, waiting for transfers between devices, across(): return lax.ppermute(x, ('depth', 'scan'), route)  7.36 us
    ppermute x5, starting transfers between devices, across(): return lax.ppermute(x, ('depth', 'scan'), route)  7.06 us
    all_to_all x1, starting transfers between devices, total_over(): pieces = lax.all_to_all(pieces, ('depth', 'scan'), 0, 0, tiled=True)  6.56 us
    unnamed x17, local copies, waits for them, and re-layouts  4.9 us
    ppermute x1, waiting for transfers between devices, body(): rows_prev = lax.ppermute(row_offsets, 'scan', ahead)  4.16 us
  transfers between devices with their start and end apart: 11, of which 5 were waited for; matrix products, arithmetic and copies ran while one was open for 1% of the time, Pallas kernels for 0%

profile of v2, /device:TPU:0, one launch (start us, length us, event | category | flops | bytes accessed | tf_op | source)
XLA Modules:
  0.0 70.3 jit_solution(9750067971182919628)
XLA Ops:
  0.6 3.0 %collective-permute-start = (s32[2]{0:T(128)}, s32[2]{0:T(128)S(1)}, u32[]{:S(2)}, u32[]{:S(2)}) collective-permute-start(s32[2]{0:T(128)} %refs_0_.3), channel_id=1, source_target_pairs={{0,1},{1,2},{2,3},{3,4},{4,5},{5,6},{6,7},{7,8},{8,9},{9,10},{10,1... | collective-permute-start | bytes 32 | tf_op jit(solution)/shard_map/ppermute | solution.py:219
  3.6 1.5 %collective-permute-start.1 = (s32[2]{0:T(128)}, s32[2]{0:T(128)S(1)}, u32[]{:S(2)}, u32[]{:S(2)}) collective-permute-start(s32[2]{0:T(128)} %refs_1_.3), channel_id=1, source_target_pairs={{0,1},{1,2},{2,3},{3,4},{4,5},{5,6},{6,7},{7,8},{8,9},{9,10},{10,1... | collective-permute-start | bytes 32 | tf_op jit(solution)/shard_map/ppermute | solution.py:220
  5.1 4.2 %collective-permute-done.rows_prev.refs_2_ = s32[2]{0:T(128)S(1)} collective-permute-done((s32[2]{0:T(128)}, s32[2]{0:T(128)S(1)}, u32[]{:S(2)}, u32[]{:S(2)}) %collective-permute-start) | collective-permute-done | bytes 40 | tf_op jit(solution)/shard_map/ppermute | solution.py:219
  9.3 1.6 %collective-permute-done.1.cols_prev.refs_3_ = s32[2]{0:T(128)S(1)} collective-permute-done((s32[2]{0:T(128)}, s32[2]{0:T(128)S(1)}, u32[]{:S(2)}, u32[]{:S(2)}) %collective-permute-start.1) | collective-permute-done | bytes 40 | tf_op jit(solution)/shard_map/ppermute | solution.py:220
  10.9 0.0 copy-start.1
  10.9 1.1 %copy-done.1 = f32[3,2,128,256]{3,2,1,0:T(8,128)S(1)} copy-done((f32[3,2,128,256]{3,2,1,0:T(8,128)S(1)}, f32[3,2,128,256]{3,2,1,0:T(8,128)}, u32[]{:S(2)}) %copy-start.1) | copy-done | bytes 786456
  12.0 0.0 copy-start.4
  12.0 0.7 copy-done.4
  12.7 0.0 copy-start.6
  12.7 0.7 copy-done.6
  13.3 0.0 copy-start.3
  13.3 0.0 copy-start.2
  13.3 1.4 %cut.1 = (f32[3,2,128,128]{3,2,1,0:T(8,128)S(1)}, f32[3,2,128,128]{3,2,1,0:T(8,128)S(1)}, f32[3,2,128,128]{3,2,1,0:T(8,128)S(1)}) custom-call(s32[2]{0:T(128)S(1)} %copy-done.4, s32[2]{0:T(128)S(1)} %copy-done.6, s32[2]{0:T(128)S(1)} %collective-permute-done.rows_prev.refs_2_, s32[2]{0:T(128)S(1)} %collective-permute-done.1.cols_prev.refs_3_, ...), custom_call_target="tpu_custom_call" | custom-call | flops 1966080 | bytes 1966080 | tf_op jit(solution)/shard_map/cut/pallas_call | solution.py:176
  14.7 1.3 %collective-permute-start.4 = (f32[3,2,128,128]{3,2,1,0:T(8,128)S(1)}, f32[3,2,128,128]{3,2,1,0:T(8,128)S(1)}, u32[]{:S(2)}, u32[]{:S(2)}) collective-permute-start(f32[3,2,128,128]{3,2,1,0:T(8,128)S(1)} %get-tuple-element.10), channel_id=1, source_target_pairs={{0,31},{1,16},{2,17},{3,18},{4,19},{5,20},{6,21},{7,22},{8,23},{9,... | collective-permute-start | bytes 1179656 | tf_op jit(solution)/shard_map/ppermute | solution.py:216
  16.1 0.7 collective-permute-start.5
  16.8 0.2 collective-permute-start.3
  17.0 0.0 copy-done.3
  17.0 3.1 %collective-permute-start.2 = (f32[2,128,128]{2,1,0:T(8,128)S(1)}, f32[2,128,128]{2,1,0:T(8,128)S(1)}, u32[]{:S(2)}, u32[]{:S(2)}) collective-permute-start(f32[2,128,128]{2,1,0:T(8,128)S(1)} %copy-done.3), channel_id=1, source_target_pairs={{0,1},{1,2},{2,3},{3,4},{4,5},{5,6},{6,7},{7,8},{8,9},{9,10},{10,1... | collective-permute-start | bytes 393224 | tf_op jit(solution)/shard_map/ppermute | solution.py:216
  20.1 7.3 %collective-permute-done.2.refs_7_ = f32[2,128,128]{2,1,0:T(8,128)S(1)} collective-permute-done((f32[2,128,128]{2,1,0:T(8,128)S(1)}, f32[2,128,128]{2,1,0:T(8,128)S(1)}, u32[]{:S(2)}, u32[]{:S(2)}) %collective-permute-start.2) | collective-permute-done | bytes 131104 | tf_op jit(solution)/shard_map/ppermute | solution.py:216
  27.4 0.0 collective-permute-done.4.refs_10_
  27.4 0.0 collective-permute-done.5.refs_11_
  27.4 0.0 collective-permute-done.3.refs_9_
  27.4 0.0 copy-done.2
  27.5 0.0 copy-start
  27.5 1.2 %copy-done = bf16[4,2,256,256]{3,2,1,0:T(8,128)(2,1)S(1)} copy-done((bf16[4,2,256,256]{3,2,1,0:T(8,128)(2,1)S(1)}, bf16[4,2,256,256]{3,2,1,0:T(8,128)(2,1)}, u32[]{:S(2)}) %copy-start) | copy-done | bytes 1048600
  28.7 6.9 %wave.1 = (f32[3,2,128,128]{3,2,1,0:T(8,128)S(1)}, f32[3,2,128,128]{3,2,1,0:T(8,128)S(1)}, f32[2,2,64,128]{3,2,1,0:T(8,128)}) custom-call(s32[2]{0:T(128)S(1)} %copy-done.4, s32[2]{0:T(128)S(1)} %copy-done.6, s32[2]{0:T(128)S(1)} %collective-permute-done.rows_prev.refs_2_, s32[2]{0:T(128)S(1)} %collective-permute-done.1.cols_prev.refs_3_, ...), custom_call_target="tpu_custom_call" | custom-call | flops 3932160 | bytes 3932160 | tf_op jit(solution)/shard_map/wave/pallas_call | solution.py:176
  35.6 0.7 collective-permute-start.7
  36.3 1.3 %collective-permute-start.8 = (f32[3,2,128,128]{3,2,1,0:T(8,128)S(1)}, f32[3,2,128,128]{3,2,1,0:T(8,128)S(1)}, u32[]{:S(2)}, u32[]{:S(2)}) collective-permute-start(f32[3,2,128,128]{3,2,1,0:T(8,128)S(1)} %get-tuple-element.12), channel_id=1, source_target_pairs={{16,1},{17,2},{18,3},{19,4},{20,5},{21,6},{22,7},{23,8},{24,9},{25... | collective-permute-start | bytes 1179656 | tf_op jit(solution)/shard_map/ppermute | solution.py:216
  37.6 6.6 %all-to-all-start = ((f32[32,8,128]{2,1,0:T(8,128)}), f32[32,8,128]{2,1,0:T(8,128)S(1)}, u32[]{:S(2)}, u32[]{:S(2)}) async-start(f32[32,8,128]{2,1,0:T(8,128)} %bitcast), calls=%async_computation | async-start | bytes 262144 | tf_op jit(solution)/shard_map/all_to_all | solution.py:194
  44.2 0.3 collective-permute-start.6
  44.5 10.5 %all-to-all-done = f32[32,8,128]{2,1,0:T(8,128)S(1)} async-done(((f32[32,8,128]{2,1,0:T(8,128)}), f32[32,8,128]{2,1,0:T(8,128)S(1)}, u32[]{:S(2)}, u32[]{:S(2)}) %all-to-all-start) | async-done | bytes 131104 | tf_op jit(solution)/shard_map/all_to_all | solution.py:194
  55.0 0.6 broadcast_in_dim.3
  55.7 3.5 %all-to-all-start.1 = ((f32[16,8,128]{2,1,0:T(8,128)}), f32[16,8,128]{2,1,0:T(8,128)S(1)}, u32[]{:S(2)}, u32[]{:S(2)}) async-start(f32[16,8,128]{2,1,0:T(8,128)} %broadcast_in_dim.3), calls=%async_computation.1 | async-start | bytes 131072 | tf_op jit(solution)/shard_map/all_to_all | solution.py:196
  59.2 7.5 %all-to-all-done.1 = f32[16,8,128]{2,1,0:T(8,128)S(1)} async-done(((f32[16,8,128]{2,1,0:T(8,128)}), f32[16,8,128]{2,1,0:T(8,128)S(1)}, u32[]{:S(2)}, u32[]{:S(2)}) %all-to-all-start.1) | async-done | bytes 65568 | tf_op jit(solution)/shard_map/all_to_all | solution.py:196
  66.7 0.0 copy-start.5
  66.7 0.0 copy-start.7
  66.7 0.0 collective-permute-done.7
  66.7 0.0 collective-permute-done.8
  66.8 0.0 collective-permute-done.6.refs_5_
  66.8 0.6 copy-done.5
  67.3 0.0 copy-done.7
  67.4 2.3 %place.1 = f32[3,2,128,256]{3,2,1,0:T(8,128)} custom-call(s32[2]{0:T(128)S(1)} %copy-done.5, s32[2]{0:T(128)S(1)} %copy-done.7, s32[2]{0:T(128)S(1)} %collective-permute-done.rows_prev.refs_2_, s32[2]{0:T(128)S(1)} %collective-permute-done.1.cols_prev.refs_3_, f32[3,2,128,128]{3,2,1,0:T(8,128)S(1)} %get-tuple-element.11.refs_4_, ...), custom_call_target="tpu_custom_call" | custom-call | flops 1966080 | bytes 1966080 | tf_op jit(solution)/shard_map/place/pallas_call | solution.py:176
  69.6 0.6 copy.9
  (2 shorter events, 0.1 us)
Async XLA Ops:
  0.6 8.6 %collective-permute-start = (s32[2]{0:T(128)}, s32[2]{0:T(128)S(1)}, u32[]{:S(2)}, u32[]{:S(2)}) collective-permute-start(s32[2]{0:T(128)} %refs_0_.3), channel_id=1, source_target_pairs={{0,1},{1,2},{2,3},{3,4},{4,5},{5,6},{6,7},{7,8},{8,9},{9,10},{10,1... | collective-permute-start | bytes 32 | tf_op jit(solution)/shard_map/ppermute | solution.py:219
  3.6 7.3 %collective-permute-start.1 = (s32[2]{0:T(128)}, s32[2]{0:T(128)S(1)}, u32[]{:S(2)}, u32[]{:S(2)}) collective-permute-start(s32[2]{0:T(128)} %refs_1_.3), channel_id=1, source_target_pairs={{0,1},{1,2},{2,3},{3,4},{4,5},{5,6},{6,7},{7,8},{8,9},{9,10},{10,1... | collective-permute-start | bytes 32 | tf_op jit(solution)/shard_map/ppermute | solution.py:220
  10.9 1.1 %copy-start.1 = (f32[3,2,128,256]{3,2,1,0:T(8,128)S(1)}, f32[3,2,128,256]{3,2,1,0:T(8,128)}, u32[]{:S(2)}) copy-start(f32[3,2,128,256]{3,2,1,0:T(8,128)} %obj.1) | copy-start | bytes 2359300
  12.0 0.7 copy-start.4
  12.7 0.7 copy-start.6
  13.3 3.7 %copy-start.3 = (f32[2,128,128]{2,1,0:T(8,128)S(1)}, f32[2,128,128]{2,1,0:T(8,128)}, u32[]{:S(2)}) copy-start(f32[2,128,128]{2,1,0:T(8,128)} %refs_6_.1) | copy-start | bytes 393220
  13.3 14.1 %copy-start.2 = (f32[2,128,128]{2,1,0:T(8,128)S(1)}, f32[2,128,128]{2,1,0:T(8,128)}, u32[]{:S(2)}) copy-start(f32[2,128,128]{2,1,0:T(8,128)} %refs_5_.1) | copy-start | bytes 393220
  14.7 12.7 %collective-permute-start.4 = (f32[3,2,128,128]{3,2,1,0:T(8,128)S(1)}, f32[3,2,128,128]{3,2,1,0:T(8,128)S(1)}, u32[]{:S(2)}, u32[]{:S(2)}) collective-permute-start(f32[3,2,128,128]{3,2,1,0:T(8,128)S(1)} %get-tuple-element.10), channel_id=1, source_target_pairs={{0,31},{1,16},{2,17},{3,18},{4,19},{5,20},{6,21},{7,22},{8,23},{9,... | collective-permute-start | bytes 1179656 | tf_op jit(solution)/shard_map/ppermute | solution.py:216
  16.1 11.4 %collective-permute-start.5 = (f32[3,2,128,128]{3,2,1,0:T(8,128)S(1)}, f32[3,2,128,128]{3,2,1,0:T(8,128)S(1)}, u32[]{:S(2)}, u32[]{:S(2)}) collective-permute-start(f32[3,2,128,128]{3,2,1,0:T(8,128)S(1)} %get-tuple-element.10), channel_id=1, source_target_pairs={{16,31},{17,16},{18,17},{19,18},{20,19},{21,20},{22,21},{23,22},{2... | collective-permute-start | bytes 1179656 | tf_op jit(solution)/shard_map/ppermute | solution.py:216
  16.8 10.7 %collective-permute-start.3 = (f32[3,2,128,128]{3,2,1,0:T(8,128)S(1)}, f32[3,2,128,128]{3,2,1,0:T(8,128)S(1)}, u32[]{:S(2)}, u32[]{:S(2)}) collective-permute-start(f32[3,2,128,128]{3,2,1,0:T(8,128)S(1)} %get-tuple-element.9), channel_id=1, source_target_pairs={{16,0},{0,16},{17,1},{1,17},{18,2},{2,18},{19,3},{3,19},{20,4},{4,... | collective-permute-start | bytes 1179656 | tf_op jit(solution)/shard_map/ppermute | solution.py:232
  17.0 10.4 %collective-permute-start.2 = (f32[2,128,128]{2,1,0:T(8,128)S(1)}, f32[2,128,128]{2,1,0:T(8,128)S(1)}, u32[]{:S(2)}, u32[]{:S(2)}) collective-permute-start(f32[2,128,128]{2,1,0:T(8,128)S(1)} %copy-done.3), channel_id=1, source_target_pairs={{0,1},{1,2},{2,3},{3,4},{4,5},{5,6},{6,7},{7,8},{8,9},{9,10},{10,1... | collective-permute-start | bytes 393224 | tf_op jit(solution)/shard_map/ppermute | solution.py:216
  27.5 1.2 %copy-start = (bf16[4,2,256,256]{3,2,1,0:T(8,128)(2,1)S(1)}, bf16[4,2,256,256]{3,2,1,0:T(8,128)(2,1)}, u32[]{:S(2)}) copy-start(bf16[4,2,256,256]{3,2,1,0:T(8,128)(2,1)} %constant.12.clone.refs_4_) | copy-start | bytes 3145732
  35.6 31.1 %collective-permute-start.7 = (f32[3,2,128,128]{3,2,1,0:T(8,128)S(1)}, f32[3,2,128,128]{3,2,1,0:T(8,128)S(1)}, u32[]{:S(2)}, u32[]{:S(2)}) collective-permute-start(f32[3,2,128,128]{3,2,1,0:T(8,128)S(1)} %get-tuple-element.11.refs_4_), channel_id=1, source_target_pairs={{16,17},{17,18},{18,19},{19,20},{20,21},{21,22},{22,23},{23,24},{2... | collective-permute-start | bytes 1179656 | tf_op jit(solution)/shard_map/ppermute | solution.py:216
  36.3 30.4 %collective-permute-start.8 = (f32[3,2,128,128]{3,2,1,0:T(8,128)S(1)}, f32[3,2,128,128]{3,2,1,0:T(8,128)S(1)}, u32[]{:S(2)}, u32[]{:S(2)}) collective-permute-start(f32[3,2,128,128]{3,2,1,0:T(8,128)S(1)} %get-tuple-element.12), channel_id=1, source_target_pairs={{16,1},{17,2},{18,3},{19,4},{20,5},{21,6},{22,7},{23,8},{24,9},{25... | collective-permute-start | bytes 1179656 | tf_op jit(solution)/shard_map/ppermute | solution.py:216
  37.6 17.4 %all-to-all-start = ((f32[32,8,128]{2,1,0:T(8,128)}), f32[32,8,128]{2,1,0:T(8,128)S(1)}, u32[]{:S(2)}, u32[]{:S(2)}) async-start(f32[32,8,128]{2,1,0:T(8,128)} %bitcast), calls=%async_computation | async-start | bytes 262144 | tf_op jit(solution)/shard_map/all_to_all | solution.py:194
  44.2 22.6 %collective-permute-start.6 = (f32[3,2,128,128]{3,2,1,0:T(8,128)S(1)}, f32[3,2,128,128]{3,2,1,0:T(8,128)S(1)}, u32[]{:S(2)}, u32[]{:S(2)}) collective-permute-start(f32[3,2,128,128]{3,2,1,0:T(8,128)S(1)} %get-tuple-element.12), channel_id=1, source_target_pairs={{0,16},{16,0},{1,17},{17,1},{2,18},{18,2},{3,19},{19,3},{4,20},{20... | collective-permute-start | bytes 1179656 | tf_op jit(solution)/shard_map/ppermute | solution.py:248
  55.7 11.0 %all-to-all-start.1 = ((f32[16,8,128]{2,1,0:T(8,128)}), f32[16,8,128]{2,1,0:T(8,128)S(1)}, u32[]{:S(2)}, u32[]{:S(2)}) async-start(f32[16,8,128]{2,1,0:T(8,128)} %broadcast_in_dim.3), calls=%async_computation.1 | async-start | bytes 131072 | tf_op jit(solution)/shard_map/all_to_all | solution.py:196
  66.7 0.7 copy-start.5
  66.7 0.7 copy-start.7

commit v3 on v2

--- a/solution.py
+++ b/solution.py
@@ -57,43 +57,47 @@
     return z[:n], z[n:]
 
 
-def share(rows, cols, tile_rows, chips_back):
+def share(offsets, tile_rows, chips_back):
     count = lax.axis_size("scan")
     base = lax.rem(lax.axis_index("scan") + count - chips_back, count) * tile_rows
-    second = rows[1] - base == tile_rows
+    second = offsets[1] - base == tile_rows
     a = jnp.where(second, 1, 0)
-    return a, cols[a], rows[1 - a] - base, cols[1 - a]
-
-
-def cut_kernel(rows_own, cols_own, rows_prev, cols_prev, obj, mine, other, halo):
+    return a, offsets[2 + a], offsets[1 - a] - base, offsets[3 - a]
+
+
+def cut(tile, row, col, width):
+    rows, cols = tile.shape
+    part = pltpu.roll(tile, lax.rem(cols - col, cols), 1)[:, :width]
+    return pltpu.roll(part, lax.rem(rows - row, rows), 0)
+
+
+def cut_kernel(offsets, offsets_prev, obj, mine, other):
     slab, _, rows, cols = obj.shape
     width = mine.shape[-1]
     on_a = lax.axis_index("depth") == 0
-    _, _, row_b, col_b = share(rows_own, cols_own, rows, 0)
-    _, col_a, row_p, col_p = share(rows_prev, cols_prev, rows, 1)
+    _, _, row_b, col_b = share(offsets, rows, 0)
+    _, col_a, _, _ = share(offsets_prev, rows, 1)
     row_mine, col_mine = jnp.where(on_a, 0, row_b), jnp.where(on_a, col_a, col_b)
     row_other, col_other = jnp.where(on_a, row_b, 0), jnp.where(on_a, col_b, col_a)
-    corners = ((mine, row_mine, col_mine), (other, row_other, col_other), (halo, row_p, col_p))
     for s in range(slab):
         for p in range(2):
-            tile = obj[s, p]
-            for out, row, col in corners:
-                part = pltpu.roll(tile, lax.rem(cols - col, cols), 1)[:, :width]
-                out[s, p] = pltpu.roll(part, lax.rem(rows - row, rows), 0)
-
-
-def wave_kernel(depth_count, rows_own, cols_own, rows_prev, cols_prev, tables, probe, near, far, *rest):
+            mine[s, p] = cut(obj[s, p], row_mine, col_mine, width)
+            other[s, p] = cut(obj[s, p], row_other, col_other, width)
+
+
+def wave_kernel(depth_count, offsets, offsets_prev, tables, probe, near, far, *rest):
     own_parts = rest[:depth_count]
     halo_parts = rest[depth_count : 2 * depth_count]
     grads = rest[2 * depth_count : 3 * depth_count]
-    probe_grad, layers, waves = rest[3 * depth_count :]
+    probe_parts = rest[3 * depth_count : 4 * depth_count]
+    layers, waves = rest[4 * depth_count :]
     slab = own_parts[0].shape[0]
     n = probe.shape[-1]
     count = slab * depth_count
     depth = lax.axis_index("depth")
     on_a = depth == 0
-    a_own, _, row_b, _ = share(rows_own, cols_own, n, 0)
-    a_prev, _, _, _ = share(rows_prev, cols_prev, n, 1)
+    a_own, _, row_b, col_b = share(offsets, n, 0)
+    a_prev, _, _, _ = share(offsets_prev, n, 1)
     measured = jnp.where(on_a, far[a_prev], near[1 - a_own])
     split = jnp.where(on_a, 0, row_b)
     inside = lax.broadcasted_iota(jnp.int32, (n, n), 0) < n - split
@@ -104,7 +108,8 @@
     for q in range(depth_count):
         for s in range(slab):
             for p in range(2):
-                layers[q * slab + s, p] = jnp.where(inside, layers[q * slab + s, p], halo_parts[q][s, p])
+                below = cut(halo_parts[q][s, p], row_b, col_b, n)
+                layers[q * slab + s, p] = jnp.where(inside, layers[q * slab + s, p], below)
 
     def enter(s, re, im):
         waves[s, 0] = re
@@ -137,18 +142,21 @@
         for s in range(slab):
             grads[j][s] = waves[base + s]
     rows = n // depth_count
-    for k in range(depth_count):
+    waves[0, 0] = jnp.where(depth < 2, grad[0], 0.0)
+    waves[0, 1] = jnp.where(depth < 2, grad[1], 0.0)
+    for j in range(depth_count):
+        start = pl.multiple_of(lax.rem(depth + j, depth_count) * rows, rows)
         for p in range(2):
-            probe_grad[k, p] = jnp.where(depth < 2, grad[p][k * rows : (k + 1) * rows], 0.0)
-
-
-def place_kernel(depth_count, rows_own, cols_own, rows_prev, cols_prev, *refs):
-    *parts, out = refs
+            probe_parts[j][p] = waves[0, p, pl.ds(start, rows), :]
+
+
+def place_kernel(depth_count, offsets, offsets_prev, *refs):
+    parts, spills, out = refs[:depth_count], refs[depth_count:-1], refs[-1]
     slab, _, rows, cols = out.shape
     width = parts[0].shape[-1]
     depth = lax.axis_index("depth")
-    _, _, row_b, col_b = share(rows_own, cols_own, rows, 0)
-    _, col_a, row_p, col_p = share(rows_prev, cols_prev, rows, 1)
+    _, _, row_b, col_b = share(offsets, rows, 0)
+    _, col_a, row_p, col_p = share(offsets_prev, rows, 1)
     row_index = lax.broadcasted_iota(jnp.int32, (rows, width), 0)
     blank = jnp.zeros((rows, cols - width), jnp.float32)
     corners = []
@@ -158,15 +166,20 @@
         row = jnp.where(is_a, 0, row_b)
         last = jnp.where(is_a | is_b, rows, 0)
         corners.append((row, jnp.where(is_a, col_a, col_b), row, last))
-    corners.append((row_p, col_p, 0, row_p))
     masks = [(row_index >= first) & (row_index < last) for _, _, first, last in corners]
+
+    def placed(x, row, col, mask):
+        x = jnp.where(mask, pltpu.roll(x, lax.rem(row, rows), 0), 0.0)
+        return pltpu.roll(jnp.concatenate([x, blank], axis=1), col, 1)
+
     for s in range(slab):
         for p in range(2):
-            total = None
+            x = spills[0][s, p]
+            for q in range(1, depth_count):
+                x = jnp.where(depth == q, spills[q][s, p], x)
+            total = placed(x, row_p, col_p, row_index < row_p)
             for (row, col, _, _), mask, part in zip(corners, masks, parts):
-                x = jnp.where(mask, pltpu.roll(part[s, p], lax.rem(row, rows), 0), 0.0)
-                x = pltpu.roll(jnp.concatenate([x, blank], axis=1), col, 1)
-                total = x if total is None else total + x
+                total = total + placed(part[s, p], row, col, mask)
             out[s, p] = total
 
 
@@ -185,23 +198,15 @@
     )(*scalars, *arrays)
 
 
-def total_over(blocks):
-    depth_count, _, rows, n = blocks.shape
-    scan_count = lax.axis_size("scan")
-    if (2 * rows) % (8 * scan_count) == 0:
-        piece = 2 * rows // scan_count
-        pieces = blocks.reshape(depth_count * scan_count, piece, n)
-        pieces = lax.all_to_all(pieces, ("depth", "scan"), 0, 0, tiled=True)
-        summed = jnp.broadcast_to(jnp.sum(pieces, axis=0), (scan_count, piece, n))
-        return lax.all_to_all(summed, "scan", 0, 0, tiled=True).reshape(2, rows, n)
-    block = lax.psum_scatter(blocks, "depth", scatter_dimension=0)
-    if scan_count & (scan_count - 1):
-        return lax.psum(block, "scan")
+def total_over_scan(x):
+    count = lax.axis_size("scan")
+    if count & (count - 1):
+        return lax.psum(x, "scan")
     step = 1
-    while step < scan_count:
-        block = block + lax.ppermute(block, "scan", [(i, i ^ step) for i in range(scan_count)])
+    while step < count:
+        x = x + lax.ppermute(x, "scan", [(i, i ^ step) for i in range(count)])
         step *= 2
-    return block
+    return x
 
 
 def body(objects, probe, row_offsets, col_offsets, intensity):
@@ -215,14 +220,14 @@
         route = [(source * scan_count + i, target * scan_count + (i + shift) % scan_count) for i in range(scan_count)]
         return lax.ppermute(x, ("depth", "scan"), route)
 
-    ahead = [(i, (i + 1) % scan_count) for i in range(scan_count)]
-    rows_prev = lax.ppermute(row_offsets, "scan", ahead)
-    cols_prev = lax.ppermute(col_offsets, "scan", ahead)
+    halos = [across(objects, q, 1, -1) for q in range(depth_count)]
+    offsets = jnp.concatenate([row_offsets, col_offsets])
+    offsets_prev = lax.ppermute(offsets, "scan", [(i, (i + 1) % scan_count) for i in range(scan_count)])
     far = across(intensity, 0, 0, 1)
-    offsets = [row_offsets, col_offsets, rows_prev, cols_prev]
+    offsets = [offsets, offsets_prev]
 
     window = jax.ShapeDtypeStruct((slab, 2, n, n), f32)
-    mine, other, halo = call(cut_kernel, "cut", offsets, [objects], [window] * 3)
+    mine, other = call(cut_kernel, "cut", offsets, [objects], [window] * 2)
 
     own = [mine]
     for j in range(1, depth_count):
@@ -230,31 +235,32 @@
         payload = other if depth_count == 2 else jnp.where((target == 0) | (depth == 0), other, mine)
         route = [((t - j) % depth_count, t) for t in (0, 1)]
         own.append(lax.ppermute(payload, "depth", route))
-    halos = [across(halo, q, 1, -1) for q in range(depth_count)]
 
     tables = jnp.asarray(constant_tables(n))
-    *grads, probe_blocks = call(
+    parts = call(
         lambda *refs: wave_kernel(depth_count, *refs),
         "wave",
         offsets,
         [tables, probe, intensity, far, *own, *halos],
-        [window] * depth_count + [jax.ShapeDtypeStruct((depth_count, 2, n // depth_count, n), f32)],
+        [window] * depth_count + [jax.ShapeDtypeStruct((2, n // depth_count, n), f32)] * depth_count,
         [pltpu.VMEM((slab * depth_count, 2, n, n), f32)] * 2,
     )
-    probe_grad = total_over(probe_blocks)
+    grads, probe_parts = parts[:depth_count], parts[depth_count:]
 
     back = [grads[0]]
+    probe_grad = probe_parts[0]
     for j in range(1, depth_count):
         back.append(lax.ppermute(grads[j], "depth", [(t, (t + j) % depth_count) for t in (0, 1)]))
+        probe_grad = probe_grad + lax.ppermute(
+            probe_parts[j], "depth", [(t, (t + j) % depth_count) for t in range(depth_count)]
+        )
+    probe_grad = total_over_scan(probe_grad)
     spill = [across(grads[(q - 1) % depth_count], 1, q, 1) for q in range(depth_count)]
-    arrived = spill[0]
-    for q in range(1, depth_count):
-        arrived = jnp.where(depth == q, spill[q], arrived)
     (object_grad,) = call(
         lambda *refs: place_kernel(depth_count, *refs),
         "place",
         offsets,
-        [*back, arrived],
+        [*back, *spill],
         [jax.ShapeDtypeStruct(objects.shape, f32)],
     )
     return object_grad, probe_grad

time: 70.7 us -> 71.8 us (1.016)
  waiting for transfers between devices: 31.2 us -> 34.5 us
  local copies, waits for them, and re-layouts: 5.53 us -> 2.36 us
  other arithmetic: 0.08 us -> 1.42 us
    ppermute x2 -> x6, waiting for transfers between devices: 5.78 us -> 25.5 us  [the longest x4 18.6 us: total_over_scan(): x = x + lax.ppermute(x, 'scan', [(i, i ^ step) for i in range(count)])]
    all_to_all x2 -> x0, waiting for transfers between devices: 18 us -> none  [the longest x1 10.5 us: total_over(): pieces = lax.all_to_all(pieces, ('depth', 'scan'), 0, 0, tiled=True)]
    ppermute x5, starting transfers between devices: 7.06 us -> 18.2 us  [across(): return lax.ppermute(x, ('depth', 'scan'), route)]
    all_to_all x2 -> x0, starting transfers between devices: 10.1 us -> none  [the longest x1 6.56 us: total_over(): pieces = lax.all_to_all(pieces, ('depth', 'scan'), 0, 0, tiled=True)]
    unnamed x17 -> x8, local copies, waits for them, and re-layouts: 4.9 us -> 2.36 us
    ppermute x5, waiting for transfers between devices: 7.36 us -> 8.94 us  [across(): return lax.ppermute(x, ('depth', 'scan'), route)]
    concatenate x0 -> x1, other arithmetic: none -> 0.75 us  [body(): offsets = jnp.concatenate([row_offsets, col_offsets])]
    ppermute x2 -> x6, starting transfers between devices: 4.48 us -> 4.16 us  [the longest x4 2.17 us: total_over_scan(): x = x + lax.ppermute(x, 'scan', [(i, i ^ step) for i in range(count)])]
  transfers between devices with their start and end apart: 11 -> 13, of which waited for: 5 -> 7; matrix products, arithmetic and copies ran while one was open for 1% -> 2% of each run, Pallas kernels for 0% -> 1%
where the time goes in v3:
time: 71.8 us; the launch traced here: 71.5 us
  waiting for transfers between devices  34.5 us (48%)
  starting transfers between devices  22.5 us (31%)
  Pallas kernels  9.99 us (14%)
  local copies, waits for them, and re-layouts  2.36 us (3%)
  other arithmetic  1.42 us (2%)
  between operations  0.76 us (1%)
    ppermute x4, waiting for transfers between devices, total_over_scan(): x = x + lax.ppermute(x, 'scan', [(i, i ^ step) for i in range(count)])  18.6 us
    ppermute x5, starting transfers between devices, across(): return lax.ppermute(x, ('depth', 'scan'), route)  18.2 us
    pallas_call x3, Pallas kernels, call(): pl.pallas_call(kernel, name=name, out_shape=outs, in_specs=[pl.BlockSpec(...  9.99 us
    ppermute x5, waiting for transfers between devices, across(): return lax.ppermute(x, ('depth', 'scan'), route)  8.94 us
    ppermute x1, waiting for transfers between devices, body(): lax.ppermute(offsets, 'scan', [(i, (i + 1) % scan_count) for i in range(s...  5.65 us
    unnamed x8, local copies, waits for them, and re-layouts  2.36 us
    ppermute x4, starting transfers between devices, total_over_scan(): x = x + lax.ppermute(x, 'scan', [(i, i ^ step) for i in range(count)])  2.17 us
    ppermute x1, starting transfers between devices, body(): lax.ppermute(offsets, 'scan', [(i, (i + 1) % scan_count) for i in range(s...  1.49 us
  transfers between devices with their start and end apart: 13, of which 7 were waited for; matrix products, arithmetic and copies ran while one was open for 2% of the time, Pallas kernels for 1%

profile of v3, /device:TPU:0, one launch (start us, length us, event | category | flops | bytes accessed | tf_op | source)
XLA Modules:
  0.0 71.5 jit_solution(14531423356007587271)
XLA Ops:
  0.6 0.7 collective-permute-start.4
  1.3 9.8 %collective-permute-start.3 = (f32[3,2,128,256]{3,2,1,0:T(8,128)}, f32[3,2,128,256]{3,2,1,0:T(8,128)S(1)}, u32[]{:S(2)}, u32[]{:S(2)}) collective-permute-start(f32[3,2,128,256]{3,2,1,0:T(8,128)} %obj.1), channel_id=1, source_target_pairs={{0,31},{1,16},{2,17},{3,18},{4,19},{5,20},{6,21},{7,22},{8,23},{9,... | collective-permute-start | bytes 2359304 | tf_op jit(solution)/shard_map/ppermute | solution.py:221
  11.1 0.7 %pad_add_fusion.offsets.refs_0_ = s32[4]{0:T(128)S(1)} fusion(s32[2]{0:T(128)} %param.9, s32[2]{0:T(128)} %param.8), kind=kLoop, calls=%fused_computation | loop fusion | flops 4 | bytes 32 | tf_op jit(solution)/shard_map/concatenate | solution.py:224
  11.9 1.5 %collective-permute-start = (s32[4]{0:T(128)S(1)}, s32[4]{0:T(128)S(1)}, u32[]{:S(2)}, u32[]{:S(2)}) collective-permute-start(s32[4]{0:T(128)S(1)} %pad_add_fusion.offsets.refs_0_), channel_id=1, source_target_pairs={{0,1},{1,2},{2,3},{3,4},{4,5},{5,6},{6,7},{7,8},{8,9},{9,10},{10,1... | collective-permute-start | bytes 56 | tf_op jit(solution)/shard_map/ppermute | solution.py:225
  13.4 5.6 %collective-permute-done.offsets_prev.refs_1_ = s32[4]{0:T(128)S(1)} collective-permute-done((s32[4]{0:T(128)S(1)}, s32[4]{0:T(128)S(1)}, u32[]{:S(2)}, u32[]{:S(2)}) %collective-permute-start) | collective-permute-done | bytes 48 | tf_op jit(solution)/shard_map/ppermute | solution.py:225
  19.0 0.0 copy-start.1
  19.0 1.1 %copy-done.1 = f32[3,2,128,256]{3,2,1,0:T(8,128)S(1)} copy-done((f32[3,2,128,256]{3,2,1,0:T(8,128)S(1)}, f32[3,2,128,256]{3,2,1,0:T(8,128)}, u32[]{:S(2)}) %copy-start.1) | copy-done | bytes 786456
  20.2 0.0 copy-start.3
  20.2 0.0 copy-start.2
  20.2 1.0 %cut.1 = (f32[3,2,128,128]{3,2,1,0:T(8,128)S(1)}, f32[3,2,128,128]{3,2,1,0:T(8,128)S(1)}) custom-call(s32[4]{0:T(128)S(1)} %pad_add_fusion.offsets.refs_0_, s32[4]{0:T(128)S(1)} %collective-permute-done.offsets_prev.refs_1_, f32[3,2,128,256]{3,2,1,0:T(8,128)S(1)} %copy-done.1), custom_call_target="tpu_custom_call" | custom-call | flops 1572864 | bytes 1572864 | tf_op jit(solution)/shard_map/cut/pallas_call | solution.py:189
  21.2 0.1 collective-permute-start.2
  21.3 0.0 copy-done.3
  21.3 5.8 %collective-permute-start.1 = (f32[2,128,128]{2,1,0:T(8,128)S(1)}, f32[2,128,128]{2,1,0:T(8,128)S(1)}, u32[]{:S(2)}, u32[]{:S(2)}) collective-permute-start(f32[2,128,128]{2,1,0:T(8,128)S(1)} %copy-done.3), channel_id=1, source_target_pairs={{0,1},{1,2},{2,3},{3,4},{4,5},{5,6},{6,7},{7,8},{8,9},{9,10},{10,1... | collective-permute-start | bytes 393224 | tf_op jit(solution)/shard_map/ppermute | solution.py:221
  27.1 8.9 %collective-permute-done.1.refs_5_ = f32[2,128,128]{2,1,0:T(8,128)S(1)} collective-permute-done((f32[2,128,128]{2,1,0:T(8,128)S(1)}, f32[2,128,128]{2,1,0:T(8,128)S(1)}, u32[]{:S(2)}, u32[]{:S(2)}) %collective-permute-start.1) | collective-permute-done | bytes 131104 | tf_op jit(solution)/shard_map/ppermute | solution.py:221
  36.0 0.0 collective-permute-done.2.refs_7_
  36.0 0.0 collective-permute-done.4.refs_9_
  36.0 0.0 collective-permute-done.3.refs_8_
  36.0 0.0 copy-done.2
  36.0 0.0 copy-start
  36.0 1.2 %copy-done = bf16[4,2,256,256]{3,2,1,0:T(8,128)(2,1)S(1)} copy-done((bf16[4,2,256,256]{3,2,1,0:T(8,128)(2,1)S(1)}, bf16[4,2,256,256]{3,2,1,0:T(8,128)(2,1)}, u32[]{:S(2)}) %copy-start) | copy-done | bytes 1048600
  37.3 6.7 %wave.1 = (f32[3,2,128,128]{3,2,1,0:T(8,128)S(1)}, f32[3,2,128,128]{3,2,1,0:T(8,128)S(1)}, f32[2,64,128]{2,1,0:T(8,128)S(1)}, f32[2,64,128]{2,1,0:T(8,128)S(1)}) custom-call(s32[4]{0:T(128)S(1)} %pad_add_fusion.offsets.refs_0_, s32[4]{0:T(128)S(1)} %collective-permute-done.offsets_prev.refs_1_, bf16[4,2,256,256]{3,2,1,0:T(8,128)(2,1)S(1)} %copy-done, ...), custom_call_target="tpu_custom_call" | custom-call | flops 4718592 | bytes 4718592 | tf_op jit(solution)/shard_map/wave/pallas_call | solution.py:189
  43.9 0.7 collective-permute-start.7
  44.6 1.3 %collective-permute-start.6 = (f32[3,2,128,128]{3,2,1,0:T(8,128)S(1)}, f32[3,2,128,128]{3,2,1,0:T(8,128)S(1)}, u32[]{:S(2)}, u32[]{:S(2)}) collective-permute-start(f32[3,2,128,128]{3,2,1,0:T(8,128)S(1)} %get-tuple-element.11), channel_id=1, source_target_pairs={{16,1},{17,2},{18,3},{19,4},{20,5},{21,6},{22,7},{23,8},{24,9},{25... | collective-permute-start | bytes 1179656 | tf_op jit(solution)/shard_map/ppermute | solution.py:221
  45.9 0.1 collective-permute-start.5
  46.0 0.5 collective-permute-start.8
  46.5 1.3 %collective-permute-done.8 = f32[2,64,128]{2,1,0:T(8,128)S(1)} collective-permute-done((f32[2,64,128]{2,1,0:T(8,128)S(1)}, f32[2,64,128]{2,1,0:T(8,128)S(1)}, u32[]{:S(2)}, u32[]{:S(2)}) %collective-permute-start.8) | collective-permute-done | bytes 65568 | tf_op jit(solution)/shard_map/ppermute | solution.py:254
  47.8 0.6 collective-permute-start.9
  48.4 4.5 %collective-permute-done.9 = f32[2,64,128]{2,1,0:T(8,128)S(1)} collective-permute-done((f32[2,64,128]{2,1,0:T(8,128)S(1)}, f32[2,64,128]{2,1,0:T(8,128)S(1)}, u32[]{:S(2)}, u32[]{:S(2)}) %collective-permute-start.9) | collective-permute-done | bytes 65568 | tf_op jit(solution)/shard_map/ppermute | solution.py:207
  52.9 0.1 collective-permute-start.10
  53.0 5.7 %collective-permute-done.10 = f32[2,64,128]{2,1,0:T(8,128)S(1)} collective-permute-done((f32[2,64,128]{2,1,0:T(8,128)S(1)}, f32[2,64,128]{2,1,0:T(8,128)S(1)}, u32[]{:S(2)}, u32[]{:S(2)}) %collective-permute-start.10) | collective-permute-done | bytes 65568 | tf_op jit(solution)/shard_map/ppermute | solution.py:207
  58.7 0.2 collective-permute-start.11
  58.9 4.1 %collective-permute-done.11 = f32[2,64,128]{2,1,0:T(8,128)S(1)} collective-permute-done((f32[2,64,128]{2,1,0:T(8,128)S(1)}, f32[2,64,128]{2,1,0:T(8,128)S(1)}, u32[]{:S(2)}, u32[]{:S(2)}) %collective-permute-start.11) | collective-permute-done | bytes 65568 | tf_op jit(solution)/shard_map/ppermute | solution.py:207
  63.1 1.2 %collective-permute-start.12 = (f32[2,64,128]{2,1,0:T(8,128)S(1)}, f32[2,64,128]{2,1,0:T(8,128)S(1)}, u32[]{:S(2)}, u32[]{:S(2)}) collective-permute-start(f32[2,64,128]{2,1,0:T(8,128)S(1)} %add.18), channel_id=1, source_target_pairs={{0,8},{1,9},{2,10},{3,11},{4,12},{5,13},{6,14},{7,15},{8,0},{9,1},... | collective-permute-start | bytes 196616 | tf_op jit(solution)/shard_map/ppermute | solution.py:207
  64.3 4.3 %collective-permute-done.12 = f32[2,64,128]{2,1,0:T(8,128)S(1)} collective-permute-done((f32[2,64,128]{2,1,0:T(8,128)S(1)}, f32[2,64,128]{2,1,0:T(8,128)S(1)}, u32[]{:S(2)}, u32[]{:S(2)}) %collective-permute-start.12) | collective-permute-done | bytes 65568 | tf_op jit(solution)/shard_map/ppermute | solution.py:207
  68.6 0.6 add.19
  69.2 0.0 collective-permute-done.7.refs_5_
  69.2 0.0 collective-permute-done.6.refs_4_
  69.2 0.0 collective-permute-done.5.refs_3_
  69.2 2.3 %place.1 = f32[3,2,128,256]{3,2,1,0:T(8,128)} custom-call(s32[4]{0:T(128)S(1)} %pad_add_fusion.offsets.refs_0_, s32[4]{0:T(128)S(1)} %collective-permute-done.offsets_prev.refs_1_, f32[3,2,128,128]{3,2,1,0:T(8,128)S(1)} %get-tuple-element.10.refs_2_, f32[3,2,128,128]{3,2,1,0:T(8,128)S(1)} %collective-permute-done.5.refs_3_, ...), custom_call_target="tpu_custom_call" | custom-call | flops 2359296 | bytes 2359296 | tf_op jit(solution)/shard_map/place/pallas_call | solution.py:189
  (4 shorter events, 0.0 us)
Async XLA Ops:
  0.6 35.4 %collective-permute-start.4 = (f32[3,2,128,256]{3,2,1,0:T(8,128)}, f32[3,2,128,256]{3,2,1,0:T(8,128)S(1)}, u32[]{:S(2)}, u32[]{:S(2)}) collective-permute-start(f32[3,2,128,256]{3,2,1,0:T(8,128)} %obj.1), channel_id=1, source_target_pairs={{16,31},{17,16},{18,17},{19,18},{20,19},{21,20},{22,21},{23,22},{2... | collective-permute-start | bytes 2359304 | tf_op jit(solution)/shard_map/ppermute | solution.py:221
  1.3 34.7 %collective-permute-start.3 = (f32[3,2,128,256]{3,2,1,0:T(8,128)}, f32[3,2,128,256]{3,2,1,0:T(8,128)S(1)}, u32[]{:S(2)}, u32[]{:S(2)}) collective-permute-start(f32[3,2,128,256]{3,2,1,0:T(8,128)} %obj.1), channel_id=1, source_target_pairs={{0,31},{1,16},{2,17},{3,18},{4,19},{5,20},{6,21},{7,22},{8,23},{9,... | collective-permute-start | bytes 2359304 | tf_op jit(solution)/shard_map/ppermute | solution.py:221
  11.9 7.1 %collective-permute-start = (s32[4]{0:T(128)S(1)}, s32[4]{0:T(128)S(1)}, u32[]{:S(2)}, u32[]{:S(2)}) collective-permute-start(s32[4]{0:T(128)S(1)} %pad_add_fusion.offsets.refs_0_), channel_id=1, source_target_pairs={{0,1},{1,2},{2,3},{3,4},{4,5},{5,6},{6,7},{7,8},{8,9},{9,10},{10,1... | collective-permute-start | bytes 56 | tf_op jit(solution)/shard_map/ppermute | solution.py:225
  19.0 1.1 %copy-start.1 = (f32[3,2,128,256]{3,2,1,0:T(8,128)S(1)}, f32[3,2,128,256]{3,2,1,0:T(8,128)}, u32[]{:S(2)}) copy-start(f32[3,2,128,256]{3,2,1,0:T(8,128)} %obj.1) | copy-start | bytes 2359300
  20.2 1.1 %copy-start.3 = (f32[2,128,128]{2,1,0:T(8,128)S(1)}, f32[2,128,128]{2,1,0:T(8,128)}, u32[]{:S(2)}) copy-start(f32[2,128,128]{2,1,0:T(8,128)} %refs_4_.1) | copy-start | bytes 393220
  20.2 15.9 %copy-start.2 = (f32[2,128,128]{2,1,0:T(8,128)S(1)}, f32[2,128,128]{2,1,0:T(8,128)}, u32[]{:S(2)}) copy-start(f32[2,128,128]{2,1,0:T(8,128)} %refs_3_.1) | copy-start | bytes 393220
  21.2 14.8 %collective-permute-start.2 = (f32[3,2,128,128]{3,2,1,0:T(8,128)S(1)}, f32[3,2,128,128]{3,2,1,0:T(8,128)S(1)}, u32[]{:S(2)}, u32[]{:S(2)}) collective-permute-start(f32[3,2,128,128]{3,2,1,0:T(8,128)S(1)} %get-tuple-element.9), channel_id=1, source_target_pairs={{16,0},{0,16},{17,1},{1,17},{18,2},{2,18},{19,3},{3,19},{20,4},{4,... | collective-permute-start | bytes 1179656 | tf_op jit(solution)/shard_map/ppermute | solution.py:237
  21.3 14.7 %collective-permute-start.1 = (f32[2,128,128]{2,1,0:T(8,128)S(1)}, f32[2,128,128]{2,1,0:T(8,128)S(1)}, u32[]{:S(2)}, u32[]{:S(2)}) collective-permute-start(f32[2,128,128]{2,1,0:T(8,128)S(1)} %copy-done.3), channel_id=1, source_target_pairs={{0,1},{1,2},{2,3},{3,4},{4,5},{5,6},{6,7},{7,8},{8,9},{9,10},{10,1... | collective-permute-start | bytes 393224 | tf_op jit(solution)/shard_map/ppermute | solution.py:221
  36.0 1.2 %copy-start = (bf16[4,2,256,256]{3,2,1,0:T(8,128)(2,1)S(1)}, bf16[4,2,256,256]{3,2,1,0:T(8,128)(2,1)}, u32[]{:S(2)}) copy-start(bf16[4,2,256,256]{3,2,1,0:T(8,128)(2,1)} %constant.2.clone.refs_2_) | copy-start | bytes 3145732
  43.9 25.3 %collective-permute-start.7 = (f32[3,2,128,128]{3,2,1,0:T(8,128)S(1)}, f32[3,2,128,128]{3,2,1,0:T(8,128)S(1)}, u32[]{:S(2)}, u32[]{:S(2)}) collective-permute-start(f32[3,2,128,128]{3,2,1,0:T(8,128)S(1)} %get-tuple-element.10.refs_2_), channel_id=1, source_target_pairs={{16,17},{17,18},{18,19},{19,20},{20,21},{21,22},{22,23},{23,24},{2... | collective-permute-start | bytes 1179656 | tf_op jit(solution)/shard_map/ppermute | solution.py:221
  44.6 24.6 %collective-permute-start.6 = (f32[3,2,128,128]{3,2,1,0:T(8,128)S(1)}, f32[3,2,128,128]{3,2,1,0:T(8,128)S(1)}, u32[]{:S(2)}, u32[]{:S(2)}) collective-permute-start(f32[3,2,128,128]{3,2,1,0:T(8,128)S(1)} %get-tuple-element.11), channel_id=1, source_target_pairs={{16,1},{17,2},{18,3},{19,4},{20,5},{21,6},{22,7},{23,8},{24,9},{25... | collective-permute-start | bytes 1179656 | tf_op jit(solution)/shard_map/ppermute | solution.py:221
  45.9 23.3 %collective-permute-start.5 = (f32[3,2,128,128]{3,2,1,0:T(8,128)S(1)}, f32[3,2,128,128]{3,2,1,0:T(8,128)S(1)}, u32[]{:S(2)}, u32[]{:S(2)}) collective-permute-start(f32[3,2,128,128]{3,2,1,0:T(8,128)S(1)} %get-tuple-element.11), channel_id=1, source_target_pairs={{0,16},{16,0},{1,17},{17,1},{2,18},{18,2},{3,19},{19,3},{4,20},{20... | collective-permute-start | bytes 1179656 | tf_op jit(solution)/shard_map/ppermute | solution.py:253
  46.0 1.8 %collective-permute-start.8 = (f32[2,64,128]{2,1,0:T(8,128)S(1)}, f32[2,64,128]{2,1,0:T(8,128)S(1)}, u32[]{:S(2)}, u32[]{:S(2)}) collective-permute-start(f32[2,64,128]{2,1,0:T(8,128)S(1)} %get-tuple-element.13), channel_id=1, source_target_pairs={{0,16},{16,0},{1,17},{17,1},{2,18},{18,2},{3,19},{19,3},{4,20},{20... | collective-permute-start | bytes 196616 | tf_op jit(solution)/shard_map/ppermute | solution.py:254
  47.8 5.1 %collective-permute-start.9 = (f32[2,64,128]{2,1,0:T(8,128)S(1)}, f32[2,64,128]{2,1,0:T(8,128)S(1)}, u32[]{:S(2)}, u32[]{:S(2)}) collective-permute-start(f32[2,64,128]{2,1,0:T(8,128)S(1)} %add.15), channel_id=1, source_target_pairs={{0,1},{1,0},{2,3},{3,2},{4,5},{5,4},{6,7},{7,6},{8,9},{9,8},{10,11... | collective-permute-start | bytes 196616 | tf_op jit(solution)/shard_map/ppermute | solution.py:207
  52.9 5.8 %collective-permute-start.10 = (f32[2,64,128]{2,1,0:T(8,128)S(1)}, f32[2,64,128]{2,1,0:T(8,128)S(1)}, u32[]{:S(2)}, u32[]{:S(2)}) collective-permute-start(f32[2,64,128]{2,1,0:T(8,128)S(1)} %add.16), channel_id=1, source_target_pairs={{0,2},{1,3},{2,0},{3,1},{4,6},{5,7},{6,4},{7,5},{8,10},{9,11},{10,... | collective-permute-start | bytes 196616 | tf_op jit(solution)/shard_map/ppermute | solution.py:207
  58.7 4.3 %collective-permute-start.11 = (f32[2,64,128]{2,1,0:T(8,128)S(1)}, f32[2,64,128]{2,1,0:T(8,128)S(1)}, u32[]{:S(2)}, u32[]{:S(2)}) collective-permute-start(f32[2,64,128]{2,1,0:T(8,128)S(1)} %add.17), channel_id=1, source_target_pairs={{0,4},{1,5},{2,6},{3,7},{4,0},{5,1},{6,2},{7,3},{8,12},{9,13},{10,... | collective-permute-start | bytes 196616 | tf_op jit(solution)/shard_map/ppermute | solution.py:207
  63.1 5.5 %collective-permute-start.12 = (f32[2,64,128]{2,1,0:T(8,128)S(1)}, f32[2,64,128]{2,1,0:T(8,128)S(1)}, u32[]{:S(2)}, u32[]{:S(2)}) collective-permute-start(f32[2,64,128]{2,1,0:T(8,128)S(1)} %add.18), channel_id=1, source_target_pairs={{0,8},{1,9},{2,10},{3,11},{4,12},{5,13},{6,14},{7,15},{8,0},{9,1},... | collective-permute-start | bytes 196616 | tf_op jit(solution)/shard_map/ppermute | solution.py:207

commit v4 on v3

--- a/solution.py
+++ b/solution.py
@@ -71,45 +71,56 @@
     return pltpu.roll(part, lax.rem(rows - row, rows), 0)
 
 
-def cut_kernel(offsets, offsets_prev, obj, mine, other):
-    slab, _, rows, cols = obj.shape
-    width = mine.shape[-1]
+def own_kernel(offsets, objects, intensity, probe, tiles, window_b, measured_b, measured_a, start):
+    slab, _, rows, _ = objects.shape
+    a, _, row_b, col_b = share(offsets, rows, 0)
+    measured_a[...] = intensity[a]
+    measured_b[...] = intensity[1 - a]
+    start[...] = probe[...]
+    for s in range(slab):
+        for p in range(2):
+            tile = objects[s, p]
+            tiles[s, p] = tile
+            window_b[s, p] = cut(tile, row_b, col_b, window_b.shape[-1])
+
+
+def prev_kernel(offsets_prev, tiles, window_b, window_a, halo, other):
+    slab, _, rows, _ = tiles.shape
+    width = halo.shape[-1]
+    _, col_a, row_p, col_p = share(offsets_prev, rows, 1)
     on_a = lax.axis_index("depth") == 0
-    _, _, row_b, col_b = share(offsets, rows, 0)
-    _, col_a, _, _ = share(offsets_prev, rows, 1)
-    row_mine, col_mine = jnp.where(on_a, 0, row_b), jnp.where(on_a, col_a, col_b)
-    row_other, col_other = jnp.where(on_a, row_b, 0), jnp.where(on_a, col_b, col_a)
-    for s in range(slab):
-        for p in range(2):
-            mine[s, p] = cut(obj[s, p], row_mine, col_mine, width)
-            other[s, p] = cut(obj[s, p], row_other, col_other, width)
-
-
-def wave_kernel(depth_count, offsets, offsets_prev, tables, probe, near, far, *rest):
-    own_parts = rest[:depth_count]
-    halo_parts = rest[depth_count : 2 * depth_count]
-    grads = rest[2 * depth_count : 3 * depth_count]
-    probe_parts = rest[3 * depth_count : 4 * depth_count]
-    layers, waves = rest[4 * depth_count :]
-    slab = own_parts[0].shape[0]
+    for s in range(slab):
+        for p in range(2):
+            halo[s, p] = cut(tiles[s, p], row_p, col_p, width)
+            window = cut(tiles[s, p], 0, col_a, width)
+            window_a[s, p] = window
+            other[s, p] = jnp.where(on_a, window_b[s, p], window)
+
+
+def wave_kernel(depth_count, offsets, tables, probe, near, far, window_a, window_b, *rest):
+    others, rest = rest[: depth_count - 1], rest[depth_count - 1 :]
+    halos, rest = rest[:depth_count], rest[depth_count:]
+    grads, probe_parts = rest[:depth_count], rest[depth_count : 2 * depth_count]
+    layers, waves = rest[2 * depth_count :]
+    slab = window_a.shape[0]
     n = probe.shape[-1]
     count = slab * depth_count
     depth = lax.axis_index("depth")
     on_a = depth == 0
-    a_own, _, row_b, col_b = share(offsets, n, 0)
-    a_prev, _, _, _ = share(offsets_prev, n, 1)
-    measured = jnp.where(on_a, far[a_prev], near[1 - a_own])
+    _, _, row_b, _ = share(offsets, n, 0)
     split = jnp.where(on_a, 0, row_b)
     inside = lax.broadcasted_iota(jnp.int32, (n, n), 0) < n - split
-    for j in range(depth_count):
+    for s in range(slab):
+        for p in range(2):
+            layers[depth * slab + s, p] = jnp.where(on_a, window_a[s, p], window_b[s, p])
+    for j in range(1, depth_count):
         base = lax.rem(depth - j + depth_count, depth_count) * slab
         for s in range(slab):
-            layers[base + s] = own_parts[j][s]
+            layers[base + s] = others[j - 1][s]
     for q in range(depth_count):
         for s in range(slab):
             for p in range(2):
-                below = cut(halo_parts[q][s, p], row_b, col_b, n)
-                layers[q * slab + s, p] = jnp.where(inside, layers[q * slab + s, p], below)
+                layers[q * slab + s, p] = jnp.where(inside, layers[q * slab + s, p], halos[q][s, p])
 
     def enter(s, re, im):
         waves[s, 0] = re
@@ -122,6 +133,7 @@
 
     wave = lax.fori_loop(0, count - 1, forward, (probe[0], probe[1]), unroll=True if count <= 8 else 1)
     far_re, far_im = both_sides(*enter(count - 1, *wave), tables, 2)
+    measured = jnp.where(on_a, far[...], near[...])
     misfit = 2.0 * (far_re * far_re + far_im * far_im - measured)
     chi = both_sides(misfit * far_re, misfit * far_im, tables, 3)
 
@@ -150,40 +162,68 @@
             probe_parts[j][p] = waves[0, p, pl.ds(start, rows), :]
 
 
+def placed(x, row, col, mask, cols):
+    x = jnp.where(mask, pltpu.roll(x, lax.rem(row, x.shape[0]), 0), 0.0)
+    blank = jnp.zeros((x.shape[0], cols - x.shape[1]), x.dtype)
+    return pltpu.roll(jnp.concatenate([x, blank], axis=1), col, 1)
+
+
 def place_kernel(depth_count, offsets, offsets_prev, *refs):
-    parts, spills, out = refs[:depth_count], refs[depth_count:-1], refs[-1]
+    *parts, out = refs
     slab, _, rows, cols = out.shape
-    width = parts[0].shape[-1]
     depth = lax.axis_index("depth")
     _, _, row_b, col_b = share(offsets, rows, 0)
-    _, col_a, row_p, col_p = share(offsets_prev, rows, 1)
-    row_index = lax.broadcasted_iota(jnp.int32, (rows, width), 0)
-    blank = jnp.zeros((rows, cols - width), jnp.float32)
+    _, col_a, _, _ = share(offsets_prev, rows, 1)
+    row_index = lax.broadcasted_iota(jnp.int32, (rows, parts[0].shape[-1]), 0)
     corners = []
     for j in range(depth_count):
         is_a = depth == j
         is_b = lax.rem(depth + depth_count - 1, depth_count) == j
         row = jnp.where(is_a, 0, row_b)
         last = jnp.where(is_a | is_b, rows, 0)
-        corners.append((row, jnp.where(is_a, col_a, col_b), row, last))
-    masks = [(row_index >= first) & (row_index < last) for _, _, first, last in corners]
-
-    def placed(x, row, col, mask):
-        x = jnp.where(mask, pltpu.roll(x, lax.rem(row, rows), 0), 0.0)
-        return pltpu.roll(jnp.concatenate([x, blank], axis=1), col, 1)
-
+        corners.append((row, jnp.where(is_a, col_a, col_b), (row_index >= row) & (row_index < last)))
+    for s in range(slab):
+        for p in range(2):
+            total = None
+            for (row, col, mask), part in zip(corners, parts):
+                x = placed(part[s, p], row, col, mask, cols)
+                total = x if total is None else total + x
+            out[s, p] = total
+
+
+def spill_kernel(depth_count, offsets_prev, *refs):
+    before, *spills, out = refs
+    slab, _, rows, cols = out.shape
+    depth = lax.axis_index("depth")
+    _, _, row_p, col_p = share(offsets_prev, rows, 1)
+    mask = lax.broadcasted_iota(jnp.int32, (rows, spills[0].shape[-1]), 0) < row_p
     for s in range(slab):
         for p in range(2):
             x = spills[0][s, p]
             for q in range(1, depth_count):
                 x = jnp.where(depth == q, spills[q][s, p], x)
-            total = placed(x, row_p, col_p, row_index < row_p)
-            for (row, col, _, _), mask, part in zip(corners, masks, parts):
-                total = total + placed(part[s, p], row, col, mask)
-            out[s, p] = total
-
-
-def call(kernel, name, scalars, arrays, outs, scratch=()):
+            out[s, p] = before[s, p] + placed(x, row_p, col_p, mask, cols)
+
+
+def add_kernel(count, *refs):
+    a, b = refs[:2]
+    refs[2 + count][...] = a[...] + b[...]
+
+
+def add_then(a, b, later):
+    vmem, anywhere = pl.BlockSpec(memory_space=pltpu.VMEM), pl.BlockSpec(memory_space=pl.ANY)
+    out = pl.pallas_call(
+        lambda *refs: add_kernel(len(later), *refs),
+        name="add_then",
+        out_shape=[jax.ShapeDtypeStruct(x.shape, x.dtype) for x in (a, *later)],
+        in_specs=[vmem] * 2 + [anywhere] * len(later),
+        out_specs=[vmem] + [anywhere] * len(later),
+        input_output_aliases={2 + i: 1 + i for i in range(len(later))},
+    )(a, b, *later)
+    return out[0], out[1:]
+
+
+def call(kernel, name, scalars, arrays, outs, scratch=(), work=10**9):
     vmem = pl.BlockSpec(memory_space=pltpu.VMEM)
     moved = sum(math.prod(x.shape) * x.dtype.itemsize for x in (*arrays, *outs))
     return pl.pallas_call(
@@ -194,19 +234,18 @@
         out_specs=[vmem] * len(outs),
         scratch_shapes=scratch,
         compiler_params=pltpu.CompilerParams(vmem_limit_bytes=VMEM_LIMIT),
-        cost_estimate=pl.CostEstimate(flops=moved, bytes_accessed=moved, transcendentals=0),
+        cost_estimate=pl.CostEstimate(flops=work, bytes_accessed=moved, transcendentals=0),
     )(*scalars, *arrays)
 
 
-def total_over_scan(x):
-    count = lax.axis_size("scan")
-    if count & (count - 1):
-        return lax.psum(x, "scan")
-    step = 1
-    while step < count:
-        x = x + lax.ppermute(x, "scan", [(i, i ^ step) for i in range(count)])
-        step *= 2
-    return x
+def sum_round(x, level):
+    depth_count, scan_count = lax.axis_size("depth"), lax.axis_size("scan")
+    levels = scan_count.bit_length() - 1
+    route = []
+    for d in range(depth_count):
+        step = 1 << ((level + (d % 2) * (levels // 2)) % levels)
+        route += [(d * scan_count + i, d * scan_count + (i ^ step)) for i in range(scan_count)]
+    return lax.ppermute(x, ("depth", "scan"), route)
 
 
 def body(objects, probe, row_offsets, col_offsets, intensity):
@@ -220,49 +259,71 @@
         route = [(source * scan_count + i, target * scan_count + (i + shift) % scan_count) for i in range(scan_count)]
         return lax.ppermute(x, ("depth", "scan"), route)
 
-    halos = [across(objects, q, 1, -1) for q in range(depth_count)]
     offsets = jnp.concatenate([row_offsets, col_offsets])
     offsets_prev = lax.ppermute(offsets, "scan", [(i, (i + 1) % scan_count) for i in range(scan_count)])
-    far = across(intensity, 0, 0, 1)
-    offsets = [offsets, offsets_prev]
-
     window = jax.ShapeDtypeStruct((slab, 2, n, n), f32)
-    mine, other = call(cut_kernel, "cut", offsets, [objects], [window] * 2)
-
-    own = [mine]
+    plane = jax.ShapeDtypeStruct((n, n), f32)
+    whole = jax.ShapeDtypeStruct(objects.shape, f32)
+    tiles, window_b, near, passed, start = call(
+        own_kernel,
+        "own",
+        [offsets],
+        [objects, intensity, probe],
+        [whole, window, plane, plane, jax.ShapeDtypeStruct(probe.shape, f32)],
+    )
+    far = across(passed, 0, 0, 1)
+    window_a, halo, other = call(prev_kernel, "prev", [offsets_prev], [tiles, window_b], [window] * 3)
+    halos = [across(halo, q, 1, -1) for q in range(depth_count)]
+
+    others = []
     for j in range(1, depth_count):
         target = lax.rem(depth + j, depth_count)
-        payload = other if depth_count == 2 else jnp.where((target == 0) | (depth == 0), other, mine)
+        payload = other if depth_count == 2 else jnp.where(target == 0, window_a, window_b)
         route = [((t - j) % depth_count, t) for t in (0, 1)]
-        own.append(lax.ppermute(payload, "depth", route))
+        others.append(lax.ppermute(payload, "depth", route))
 
     tables = jnp.asarray(constant_tables(n))
+    count = slab * depth_count
     parts = call(
         lambda *refs: wave_kernel(depth_count, *refs),
         "wave",
-        offsets,
-        [tables, probe, intensity, far, *own, *halos],
+        [offsets],
+        [tables, start, near, far, window_a, window_b, *others, *halos],
         [window] * depth_count + [jax.ShapeDtypeStruct((2, n // depth_count, n), f32)] * depth_count,
-        [pltpu.VMEM((slab * depth_count, 2, n, n), f32)] * 2,
+        [pltpu.VMEM((count, 2, n, n), f32)] * 2,
+        work=5 * 10**9,
     )
     grads, probe_parts = parts[:depth_count], parts[depth_count:]
 
-    back = [grads[0]]
     probe_grad = probe_parts[0]
     for j in range(1, depth_count):
-        back.append(lax.ppermute(grads[j], "depth", [(t, (t + j) % depth_count) for t in (0, 1)]))
         probe_grad = probe_grad + lax.ppermute(
             probe_parts[j], "depth", [(t, (t + j) % depth_count) for t in range(depth_count)]
         )
-    probe_grad = total_over_scan(probe_grad)
+    rounds = scan_count.bit_length() - 1
+    paired = scan_count == 1 << rounds and rounds > 2
+    if paired:
+        probe_grad, grads = add_then(probe_grad, sum_round(probe_grad, 0), grads)
+        for level in range(1, rounds - 2):
+            probe_grad = probe_grad + sum_round(probe_grad, level)
+    else:
+        probe_grad = lax.psum(probe_grad, "scan")
+
     spill = [across(grads[(q - 1) % depth_count], 1, q, 1) for q in range(depth_count)]
+    back = [grads[0]]
+    for j in range(1, depth_count):
+        back.append(lax.ppermute(grads[j], "depth", [(t, (t + j) % depth_count) for t in (0, 1)]))
     (object_grad,) = call(
-        lambda *refs: place_kernel(depth_count, *refs),
-        "place",
-        offsets,
-        [*back, *spill],
-        [jax.ShapeDtypeStruct(objects.shape, f32)],
+        lambda *refs: place_kernel(depth_count, *refs), "place", [offsets, offsets_prev], back, [whole], work=2 * 10**9
     )
+    if paired:
+        probe_grad, (object_grad,) = add_then(probe_grad, sum_round(probe_grad, rounds - 2), [object_grad])
+        last = sum_round(probe_grad, rounds - 1)
+    (object_grad,) = call(
+        lambda *refs: spill_kernel(depth_count, *refs), "spill", [offsets_prev], [object_grad, *spill], [whole]
+    )
+    if paired:
+        probe_grad, (object_grad,) = add_then(probe_grad, last, [object_grad])
     return object_grad, probe_grad
 
 

time: 71.8 us -> 73.5 us (1.024)
  the two profiles are of different devices: /device:TPU:0 before, /device:TPU:9 now
where the time goes in v4:
time: 73.5 us; the launch traced here: 72.9 us
  starting transfers between devices  33 us (45%)
  Pallas kernels  15.6 us (21%)
  waiting for transfers between devices  12.6 us (17%)
  local copies, waits for them, and re-layouts  9.35 us (13%)
  other arithmetic  1.61 us (2%)
  between operations  0.8 us (1%)
    ppermute x4, starting transfers between devices, sum_round(): return lax.ppermute(x, ('depth', 'scan'), route)  19.4 us
    pallas_call x5, Pallas kernels, call(): pl.pallas_call(kernel, name=name, out_shape=outs, in_specs=[pl.BlockSpec(...  11.1 us
    ppermute x5, starting transfers between devices, across(): return lax.ppermute(x, ('depth', 'scan'), route)  9.6 us
    unnamed x28, local copies, waits for them, and re-layouts  9.35 us
    ppermute x5, waiting for transfers between devices, across(): return lax.ppermute(x, ('depth', 'scan'), route)  7.4 us
    pallas_call x3, Pallas kernels, add_then(): pl.pallas_call(lambda *refs: add_kernel(len(later), *refs), name='add_the...  4.51 us
    ppermute x4, waiting for transfers between devices, sum_round(): return lax.ppermute(x, ('depth', 'scan'), route)  4.26 us
    ppermute x1, starting transfers between devices, body(): lax.ppermute(probe_parts[j], 'depth', [(t, (t + j) % depth_count) for t i...  1.69 us
  transfers between devices with their start and end apart: 13, of which 6 were waited for; matrix products, arithmetic and copies ran while one was open for 1% of the time, Pallas kernels for 7%

profile of v4, /device:TPU:9, one launch (start us, length us, event | category | flops | bytes accessed | tf_op | source)
XLA Modules:
  0.0 72.9 jit_solution(2747538504745709916)
XLA Ops:
  0.6 0.7 %pad_add_fusion.offsets.refs_0_ = s32[4]{0:T(128)S(1)} fusion(s32[2]{0:T(128)} %param.9, s32[2]{0:T(128)} %param.8), kind=kLoop, calls=%fused_computation | loop fusion | flops 4 | bytes 32 | tf_op jit(solution)/shard_map/concatenate | solution.py:262
  1.4 1.2 %collective-permute-start.1 = (s32[4]{0:T(128)S(1)}, s32[4]{0:T(128)S(1)}, u32[]{:S(2)}, u32[]{:S(2)}) collective-permute-start(s32[4]{0:T(128)S(1)} %pad_add_fusion.offsets.refs_0_), channel_id=1, source_target_pairs={{0,1},{1,2},{2,3},{3,4},{4,5},{5,6},{6,7},{7,8},{8,9},{9,10},{10,1... | collective-permute-start | bytes 56 | tf_op jit(solution)/shard_map/ppermute | solution.py:263
  2.6 0.0 copy-start.5
  2.6 1.1 %copy-done.5 = f32[3,2,128,256]{3,2,1,0:T(8,128)S(1)} copy-done((f32[3,2,128,256]{3,2,1,0:T(8,128)S(1)}, f32[3,2,128,256]{3,2,1,0:T(8,128)}, u32[]{:S(2)}) %copy-start.5) | copy-done | bytes 786456
  3.7 0.0 copy-start.6
  3.7 0.9 %copy-done.6 = f32[2,128,128]{2,1,0:T(8,128)S(1)} copy-done((f32[2,128,128]{2,1,0:T(8,128)S(1)}, f32[2,128,128]{2,1,0:T(8,128)}, u32[]{:S(2)}) %copy-start.6) | copy-done | bytes 131096
  4.6 0.0 copy-start.7
  4.6 0.9 %copy-done.7 = f32[2,128,128]{2,1,0:T(8,128)S(1)} copy-done((f32[2,128,128]{2,1,0:T(8,128)S(1)}, f32[2,128,128]{2,1,0:T(8,128)}, u32[]{:S(2)}) %copy-start.7) | copy-done | bytes 131096
  5.5 0.8 %own.1 = (f32[3,2,128,256]{3,2,1,0:T(8,128)S(1)}, f32[3,2,128,128]{3,2,1,0:T(8,128)S(1)}, f32[128,128]{1,0:T(8,128)S(1)}, f32[128,128]{1,0:T(8,128)S(1)}, f32[2,128,128]{2,1,0:T(8,128)S(1)}) custom-call(s32[4]{0:T(128)S(1)} %pad_add_fusion.offsets.refs_0_, f32[3,2,128,256]{3,2,1,0:T(8,128)S(1)} %copy-done.5, f32[2,128,128]{2,1,0:T(8,128)S(1)} %copy-done.6, ...), custom_call_target="tpu_custom_call" | custom-call | flops 1000000000 | bytes 2490368 | tf_op jit(solution)/shard_map/own/pallas_call | solution.py:229
  6.4 0.0 collective-permute-done.1.offsets_prev.refs_1_.refs_0_
  6.4 0.0 copy-start.8
  6.4 1.0 %prev.1 = (f32[3,2,128,128]{3,2,1,0:T(8,128)S(1)}, f32[3,2,128,128]{3,2,1,0:T(8,128)S(1)}, f32[3,2,128,128]{3,2,1,0:T(8,128)S(1)}) custom-call(s32[4]{0:T(128)S(1)} %collective-permute-done.1.offsets_prev.refs_1_.refs_0_, f32[3,2,128,256]{3,2,1,0:T(8,128)S(1)} %get-tuple-element.24.tiles, f32[3,2,128,128]{3,2,1,0:T(8,128)S(1)} %get-tuple-element.25.window_b.refs_6_), custom_call_target="tpu_custom_call" | custom-call | flops 1000000000 | bytes 2359296 | tf_op jit(solution)/shard_map/prev/pallas_call | solution.py:229
  7.4 1.1 %collective-permute-start.2 = (f32[3,2,128,128]{3,2,1,0:T(8,128)S(1)}, f32[3,2,128,128]{3,2,1,0:T(8,128)S(1)}, u32[]{:S(2)}, u32[]{:S(2)}) collective-permute-start(f32[3,2,128,128]{3,2,1,0:T(8,128)S(1)} %get-tuple-element.27), channel_id=1, source_target_pairs={{16,0},{0,16},{17,1},{1,17},{18,2},{2,18},{19,3},{3,19},{20,4},{4,... | collective-permute-start | bytes 1179656 | tf_op jit(solution)/shard_map/ppermute | solution.py:283
  8.5 3.9 %collective-permute-start.4 = (f32[3,2,128,128]{3,2,1,0:T(8,128)S(1)}, f32[3,2,128,128]{3,2,1,0:T(8,128)S(1)}, u32[]{:S(2)}, u32[]{:S(2)}) collective-permute-start(f32[3,2,128,128]{3,2,1,0:T(8,128)S(1)} %get-tuple-element.28), channel_id=1, source_target_pairs={{16,31},{17,16},{18,17},{19,18},{20,19},{21,20},{22,21},{23,22},{2... | collective-permute-start | bytes 1179656 | tf_op jit(solution)/shard_map/ppermute | solution.py:260
  12.4 1.3 %collective-permute-start.3 = (f32[3,2,128,128]{3,2,1,0:T(8,128)S(1)}, f32[3,2,128,128]{3,2,1,0:T(8,128)S(1)}, u32[]{:S(2)}, u32[]{:S(2)}) collective-permute-start(f32[3,2,128,128]{3,2,1,0:T(8,128)S(1)} %get-tuple-element.28), channel_id=1, source_target_pairs={{0,31},{1,16},{2,17},{3,18},{4,19},{5,20},{6,21},{7,22},{8,23},{9,... | collective-permute-start | bytes 1179656 | tf_op jit(solution)/shard_map/ppermute | solution.py:260
  13.7 0.7 collective-permute-start
  14.4 0.0 collective-permute-done.refs_4_
  14.4 0.0 collective-permute-done.2.refs_7_
  14.4 4.1 %collective-permute-done.4.refs_9_ = f32[3,2,128,128]{3,2,1,0:T(8,128)S(1)} collective-permute-done((f32[3,2,128,128]{3,2,1,0:T(8,128)S(1)}, f32[3,2,128,128]{3,2,1,0:T(8,128)S(1)}, u32[]{:S(2)}, u32[]{:S(2)}) %collective-permute-start.4) | collective-permute-done | bytes 393248 | tf_op jit(solution)/shard_map/ppermute | solution.py:260
  18.5 3.3 %collective-permute-done.3.refs_8_ = f32[3,2,128,128]{3,2,1,0:T(8,128)S(1)} collective-permute-done((f32[3,2,128,128]{3,2,1,0:T(8,128)S(1)}, f32[3,2,128,128]{3,2,1,0:T(8,128)S(1)}, u32[]{:S(2)}, u32[]{:S(2)}) %collective-permute-start.3) | collective-permute-done | bytes 393248 | tf_op jit(solution)/shard_map/ppermute | solution.py:260
  21.8 0.0 copy-done.8
  21.8 6.4 %wave.1 = (f32[3,2,128,128]{3,2,1,0:T(8,128)S(1)}, f32[3,2,128,128]{3,2,1,0:T(8,128)S(1)}, f32[2,64,128]{2,1,0:T(8,128)S(1)}, f32[2,64,128]{2,1,0:T(8,128)S(1)}) custom-call(s32[4]{0:T(128)S(1)} %pad_add_fusion.offsets.refs_0_, bf16[4,2,256,256]{3,2,1,0:T(8,128)(2,1)S(1)} %copy-done.8, f32[2,128,128]{2,1,0:T(8,128)S(1)} %get-tuple-element.21.refs_2_, ...), custom_call_target="tpu_custom_call" | custom-call | flops 5000000000 | bytes 4194304 | tf_op jit(solution)/shard_map/wave/pallas_call | solution.py:229
  28.2 0.0 copy-start.2
  28.2 0.7 %copy-done.2 = f32[3,2,128,128]{3,2,1,0:T(8,128)} copy-done((f32[3,2,128,128]{3,2,1,0:T(8,128)}, f32[3,2,128,128]{3,2,1,0:T(8,128)S(1)}, u32[]{:S(2)}) %copy-start.2) | copy-done | bytes 393240
  28.9 0.0 copy-start.4
  28.9 0.8 %copy-done.4 = f32[3,2,128,128]{3,2,1,0:T(8,128)} copy-done((f32[3,2,128,128]{3,2,1,0:T(8,128)}, f32[3,2,128,128]{3,2,1,0:T(8,128)S(1)}, u32[]{:S(2)}) %copy-start.4) | copy-done | bytes 393240
  29.7 1.7 %collective-permute-start.5 = (f32[2,64,128]{2,1,0:T(8,128)S(1)}, f32[2,64,128]{2,1,0:T(8,128)S(1)}, u32[]{:S(2)}, u32[]{:S(2)}) collective-permute-start(f32[2,64,128]{2,1,0:T(8,128)S(1)} %get-tuple-element.30), channel_id=1, source_target_pairs={{0,16},{16,0},{1,17},{17,1},{2,18},{18,2},{3,19},{19,3},{4,20},{20... | collective-permute-start | bytes 196616 | tf_op jit(solution)/shard_map/ppermute | solution.py:300
  31.4 0.9 %collective-permute-done.5 = f32[2,64,128]{2,1,0:T(8,128)S(1)} collective-permute-done((f32[2,64,128]{2,1,0:T(8,128)S(1)}, f32[2,64,128]{2,1,0:T(8,128)S(1)}, u32[]{:S(2)}, u32[]{:S(2)}) %collective-permute-start.5) | collective-permute-done | bytes 65568 | tf_op jit(solution)/shard_map/ppermute | solution.py:300
  32.3 0.0 copy-start.10
  32.3 4.7 %collective-permute-start.6 = (f32[2,64,128]{2,1,0:T(8,128)S(1)}, f32[2,64,128]{2,1,0:T(8,128)S(1)}, u32[]{:S(2)}, u32[]{:S(2)}) collective-permute-start(f32[2,64,128]{2,1,0:T(8,128)S(1)} %add.6.refs_0_), channel_id=1, source_target_pairs={{0,1},{1,0},{2,3},{3,2},{4,5},{5,4},{6,7},{7,6},{8,9},{9,8},{10,11... | collective-permute-start | bytes 196616 | tf_op jit(solution)/shard_map/ppermute | solution.py:248
  37.0 1.7 %collective-permute-done.6.refs_1_ = f32[2,64,128]{2,1,0:T(8,128)S(1)} collective-permute-done((f32[2,64,128]{2,1,0:T(8,128)S(1)}, f32[2,64,128]{2,1,0:T(8,128)S(1)}, u32[]{:S(2)}, u32[]{:S(2)}) %collective-permute-start.6) | collective-permute-done | bytes 65568 | tf_op jit(solution)/shard_map/ppermute | solution.py:248
  38.6 0.0 copy-start.13
  38.6 0.0 copy-done.10
  38.7 0.6 copy-done.13
  39.3 1.5 %add_then.3 = (f32[2,64,128]{2,1,0:T(8,128)}, f32[3,2,128,128]{3,2,1,0:T(8,128)}, f32[3,2,128,128]{3,2,1,0:T(8,128)}) custom-call(f32[2,64,128]{2,1,0:T(8,128)} %copy-done.10, f32[2,64,128]{2,1,0:T(8,128)} %copy-done.13, f32[3,2,128,128]{3,2,1,0:T(8,128)} %copy-done.2, f32[3,2,128,128]{3,2,1,0:T(8,128)} %copy-done.4), custom_call_target="tpu_custom_call", output_to_operand_aliasing={{1}: (2, {}), {2}: (3, {})} | custom-call | tf_op jit(solution)/shard_map/add_then/pallas_call | solution.py:215
  40.8 0.0 collective-permute-start.9
  40.8 2.4 %collective-permute-start.12 = (f32[3,2,128,128]{3,2,1,0:T(8,128)}, f32[3,2,128,128]{3,2,1,0:T(8,128)S(1)}, u32[]{:S(2)}, u32[]{:S(2)}) collective-permute-start(f32[3,2,128,128]{3,2,1,0:T(8,128)} %get-tuple-element.34.refs_2_), channel_id=1, source_target_pairs={{16,17},{17,18},{18,19},{19,20},{20,21},{21,22},{22,23},{23,24},{2... | collective-permute-start | bytes 1179656 | tf_op jit(solution)/shard_map/ppermute | solution.py:260
  43.2 1.3 %collective-permute-start.11 = (f32[3,2,128,128]{3,2,1,0:T(8,128)}, f32[3,2,128,128]{3,2,1,0:T(8,128)S(1)}, u32[]{:S(2)}, u32[]{:S(2)}) collective-permute-start(f32[3,2,128,128]{3,2,1,0:T(8,128)} %get-tuple-element.35), channel_id=1, source_target_pairs={{16,1},{17,2},{18,3},{19,4},{20,5},{21,6},{22,7},{23,8},{24,9},{25... | collective-permute-start | bytes 1179656 | tf_op jit(solution)/shard_map/ppermute | solution.py:260
  44.5 2.7 %collective-permute-start.7 = (f32[2,64,128]{2,1,0:T(8,128)}, f32[2,64,128]{2,1,0:T(8,128)S(1)}, u32[]{:S(2)}, u32[]{:S(2)}) collective-permute-start(f32[2,64,128]{2,1,0:T(8,128)} %get-tuple-element.33), channel_id=1, source_target_pairs={{0,2},{1,3},{2,0},{3,1},{4,6},{5,7},{6,4},{7,5},{8,10},{9,11},{10,... | collective-permute-start | bytes 196616 | tf_op jit(solution)/shard_map/ppermute | solution.py:248
  47.2 1.9 %collective-permute-done.7 = f32[2,64,128]{2,1,0:T(8,128)S(1)} collective-permute-done((f32[2,64,128]{2,1,0:T(8,128)}, f32[2,64,128]{2,1,0:T(8,128)S(1)}, u32[]{:S(2)}, u32[]{:S(2)}) %collective-permute-start.7) | collective-permute-done | bytes 65568 | tf_op jit(solution)/shard_map/ppermute | solution.py:248
  49.1 0.9 %add.7.refs_0_ = f32[2,64,128]{2,1,0:T(8,128)S(1)} add(f32[2,64,128]{2,1,0:T(8,128)} %get-tuple-element.33, f32[2,64,128]{2,1,0:T(8,128)S(1)} %collective-permute-done.7) | non-fusion elementwise | flops 16384 | bytes 196608 | tf_op jit(solution)/shard_map/add | solution.py:308
  50.0 0.0 copy-start.9
  50.0 0.1 collective-permute-start.8
  50.0 0.0 collective-permute-done.9.refs_3_
  50.1 0.0 copy-start.3
  50.1 1.0 %copy-done.3 = f32[3,2,128,128]{3,2,1,0:T(8,128)S(1)} copy-done((f32[3,2,128,128]{3,2,1,0:T(8,128)S(1)}, f32[3,2,128,128]{3,2,1,0:T(8,128)}, u32[]{:S(2)}) %copy-start.3) | copy-done | bytes 393240
  51.0 1.1 %place.1.refs_2_ = f32[3,2,128,256]{3,2,1,0:T(8,128)S(1)} custom-call(s32[4]{0:T(128)S(1)} %pad_add_fusion.offsets.refs_0_, s32[4]{0:T(128)S(1)} %collective-permute-done.1.offsets_prev.refs_1_.refs_0_, f32[3,2,128,128]{3,2,1,0:T(8,128)S(1)} %copy-done.3, f32[3,2,128,128]{3,2,1,0:T(8,128)S(1)} %collective-permute-done.9.refs_3_), custom_call_target="tpu_custom_call" | custom-call | flops 2000000000 | bytes 1572864 | tf_op jit(solution)/shard_map/place/pallas_call | solution.py:229
  52.2 0.0 copy-done.9
  52.2 0.0 copy-start
  52.2 0.9 %copy-done = f32[3,2,128,256]{3,2,1,0:T(8,128)} copy-done((f32[3,2,128,256]{3,2,1,0:T(8,128)}, f32[3,2,128,256]{3,2,1,0:T(8,128)S(1)}, u32[]{:S(2)}) %copy-start) | copy-done | bytes 786456
  53.1 0.7 %collective-permute-done.8.refs_1_ = f32[2,64,128]{2,1,0:T(8,128)S(1)} collective-permute-done((f32[2,64,128]{2,1,0:T(8,128)S(1)}, f32[2,64,128]{2,1,0:T(8,128)S(1)}, u32[]{:S(2)}, u32[]{:S(2)}) %collective-permute-start.8) | collective-permute-done | bytes 65568 | tf_op jit(solution)/shard_map/ppermute | solution.py:248
  53.8 0.0 copy-start.12
  53.8 0.6 copy-done.12
  54.4 1.5 %add_then.4 = (f32[2,64,128]{2,1,0:T(8,128)}, f32[3,2,128,256]{3,2,1,0:T(8,128)}) custom-call(f32[2,64,128]{2,1,0:T(8,128)} %copy-done.9, f32[2,64,128]{2,1,0:T(8,128)} %copy-done.12, f32[3,2,128,256]{3,2,1,0:T(8,128)} %copy-done), custom_call_target="tpu_custom_call", output_to_operand_aliasing={{1}: (2, {})} | custom-call | tf_op jit(solution)/shard_map/add_then/pallas_call | solution.py:215
  55.9 12.0 %collective-permute-start.10 = (f32[2,64,128]{2,1,0:T(8,128)}, f32[2,64,128]{2,1,0:T(8,128)S(1)}, u32[]{:S(2)}, u32[]{:S(2)}) collective-permute-start(f32[2,64,128]{2,1,0:T(8,128)} %get-tuple-element.36.refs_0_), channel_id=1, source_target_pairs={{0,8},{1,9},{2,10},{3,11},{4,12},{5,13},{6,14},{7,15},{8,0},{9,1},... | collective-permute-start | bytes 196616 | tf_op jit(solution)/shard_map/ppermute | solution.py:248
  67.9 0.0 collective-permute-done.12.refs_3_
  67.9 0.0 collective-permute-done.11.refs_2_
  67.9 0.0 copy-start.1
  67.9 1.1 %copy-done.1 = f32[3,2,128,256]{3,2,1,0:T(8,128)S(1)} copy-done((f32[3,2,128,256]{3,2,1,0:T(8,128)S(1)}, f32[3,2,128,256]{3,2,1,0:T(8,128)}, u32[]{:S(2)}) %copy-start.1) | copy-done | bytes 786456
  69.1 1.7 %spill.1.refs_2_ = f32[3,2,128,256]{3,2,1,0:T(8,128)} custom-call(s32[4]{0:T(128)S(1)} %collective-permute-done.1.offsets_prev.refs_1_.refs_0_, f32[3,2,128,256]{3,2,1,0:T(8,128)S(1)} %copy-done.1, f32[3,2,128,128]{3,2,1,0:T(8,128)S(1)} %collective-permute-done.11.refs_2_, f32[3,2,128,128]{3,2,1,0:T(8,128)S(1)} %collective-permute-done.12.refs_3_), custom_call_target="tpu_custom_call" | custom-call | flops 1000000000 | bytes 2359296 | tf_op jit(solution)/shard_map/spill/pallas_call | solution.py:229
  70.8 0.0 collective-permute-done.10.refs_1_
  70.8 0.0 copy-start.11
  70.8 0.6 copy-done.11
  71.4 1.5 %add_then.5 = (f32[2,64,128]{2,1,0:T(8,128)}, f32[3,2,128,256]{3,2,1,0:T(8,128)}) custom-call(f32[2,64,128]{2,1,0:T(8,128)} %get-tuple-element.36.refs_0_, f32[2,64,128]{2,1,0:T(8,128)} %copy-done.11, f32[3,2,128,256]{3,2,1,0:T(8,128)} %spill.1.refs_2_), custom_call_target="tpu_custom_call", output_to_operand_aliasing={{1}: (2, {})} | custom-call | tf_op jit(solution)/shard_map/add_then/pallas_call | solution.py:215
  (1 shorter events, 0.0 us)
Async XLA Ops:
  1.4 5.0 %collective-permute-start.1 = (s32[4]{0:T(128)S(1)}, s32[4]{0:T(128)S(1)}, u32[]{:S(2)}, u32[]{:S(2)}) collective-permute-start(s32[4]{0:T(128)S(1)} %pad_add_fusion.offsets.refs_0_), channel_id=1, source_target_pairs={{0,1},{1,2},{2,3},{3,4},{4,5},{5,6},{6,7},{7,8},{8,9},{9,10},{10,1... | collective-permute-start | bytes 56 | tf_op jit(solution)/shard_map/ppermute | solution.py:263
  2.6 1.1 %copy-start.5 = (f32[3,2,128,256]{3,2,1,0:T(8,128)S(1)}, f32[3,2,128,256]{3,2,1,0:T(8,128)}, u32[]{:S(2)}) copy-start(f32[3,2,128,256]{3,2,1,0:T(8,128)} %objects.1) | copy-start | bytes 2359300
  3.7 0.9 %copy-start.6 = (f32[2,128,128]{2,1,0:T(8,128)S(1)}, f32[2,128,128]{2,1,0:T(8,128)}, u32[]{:S(2)}) copy-start(f32[2,128,128]{2,1,0:T(8,128)} %intensity.1) | copy-start | bytes 393220
  4.6 0.9 %copy-start.7 = (f32[2,128,128]{2,1,0:T(8,128)S(1)}, f32[2,128,128]{2,1,0:T(8,128)}, u32[]{:S(2)}) copy-start(f32[2,128,128]{2,1,0:T(8,128)} %probe.1) | copy-start | bytes 393220
  6.4 15.4 %copy-start.8 = (bf16[4,2,256,256]{3,2,1,0:T(8,128)(2,1)S(1)}, bf16[4,2,256,256]{3,2,1,0:T(8,128)(2,1)}, u32[]{:S(2)}) copy-start(bf16[4,2,256,256]{3,2,1,0:T(8,128)(2,1)} %constant.2.clone.refs_1_) | copy-start | bytes 3145732
  7.4 7.0 %collective-permute-start.2 = (f32[3,2,128,128]{3,2,1,0:T(8,128)S(1)}, f32[3,2,128,128]{3,2,1,0:T(8,128)S(1)}, u32[]{:S(2)}, u32[]{:S(2)}) collective-permute-start(f32[3,2,128,128]{3,2,1,0:T(8,128)S(1)} %get-tuple-element.27), channel_id=1, source_target_pairs={{16,0},{0,16},{17,1},{1,17},{18,2},{2,18},{19,3},{3,19},{20,4},{4,... | collective-permute-start | bytes 1179656 | tf_op jit(solution)/shard_map/ppermute | solution.py:283
  8.5 10.0 %collective-permute-start.4 = (f32[3,2,128,128]{3,2,1,0:T(8,128)S(1)}, f32[3,2,128,128]{3,2,1,0:T(8,128)S(1)}, u32[]{:S(2)}, u32[]{:S(2)}) collective-permute-start(f32[3,2,128,128]{3,2,1,0:T(8,128)S(1)} %get-tuple-element.28), channel_id=1, source_target_pairs={{16,31},{17,16},{18,17},{19,18},{20,19},{21,20},{22,21},{23,22},{2... | collective-permute-start | bytes 1179656 | tf_op jit(solution)/shard_map/ppermute | solution.py:260
  12.4 9.4 %collective-permute-start.3 = (f32[3,2,128,128]{3,2,1,0:T(8,128)S(1)}, f32[3,2,128,128]{3,2,1,0:T(8,128)S(1)}, u32[]{:S(2)}, u32[]{:S(2)}) collective-permute-start(f32[3,2,128,128]{3,2,1,0:T(8,128)S(1)} %get-tuple-element.28), channel_id=1, source_target_pairs={{0,31},{1,16},{2,17},{3,18},{4,19},{5,20},{6,21},{7,22},{8,23},{9,... | collective-permute-start | bytes 1179656 | tf_op jit(solution)/shard_map/ppermute | solution.py:260
  13.7 0.7 collective-permute-start
  28.2 0.8 %copy-start.2 = (f32[3,2,128,128]{3,2,1,0:T(8,128)}, f32[3,2,128,128]{3,2,1,0:T(8,128)S(1)}, u32[]{:S(2)}) copy-start(f32[3,2,128,128]{3,2,1,0:T(8,128)S(1)} %get-tuple-element.31.refs_2_) | copy-start | bytes 1179652
  28.9 0.8 %copy-start.4 = (f32[3,2,128,128]{3,2,1,0:T(8,128)}, f32[3,2,128,128]{3,2,1,0:T(8,128)S(1)}, u32[]{:S(2)}) copy-start(f32[3,2,128,128]{3,2,1,0:T(8,128)S(1)} %get-tuple-element.32.refs_3_) | copy-start | bytes 1179652
  29.7 2.6 %collective-permute-start.5 = (f32[2,64,128]{2,1,0:T(8,128)S(1)}, f32[2,64,128]{2,1,0:T(8,128)S(1)}, u32[]{:S(2)}, u32[]{:S(2)}) collective-permute-start(f32[2,64,128]{2,1,0:T(8,128)S(1)} %get-tuple-element.30), channel_id=1, source_target_pairs={{0,16},{16,0},{1,17},{17,1},{2,18},{18,2},{3,19},{19,3},{4,20},{20... | collective-permute-start | bytes 196616 | tf_op jit(solution)/shard_map/ppermute | solution.py:300
  32.3 6.3 %copy-start.10 = (f32[2,64,128]{2,1,0:T(8,128)}, f32[2,64,128]{2,1,0:T(8,128)S(1)}, u32[]{:S(2)}) copy-start(f32[2,64,128]{2,1,0:T(8,128)S(1)} %add.6.refs_0_) | copy-start | bytes 196612
  32.3 6.3 %collective-permute-start.6 = (f32[2,64,128]{2,1,0:T(8,128)S(1)}, f32[2,64,128]{2,1,0:T(8,128)S(1)}, u32[]{:S(2)}, u32[]{:S(2)}) collective-permute-start(f32[2,64,128]{2,1,0:T(8,128)S(1)} %add.6.refs_0_), channel_id=1, source_target_pairs={{0,1},{1,0},{2,3},{3,2},{4,5},{5,4},{6,7},{7,6},{8,9},{9,8},{10,11... | collective-permute-start | bytes 196616 | tf_op jit(solution)/shard_map/ppermute | solution.py:248
  38.6 0.6 copy-start.13
  40.8 9.3 %collective-permute-start.9 = (f32[3,2,128,128]{3,2,1,0:T(8,128)}, f32[3,2,128,128]{3,2,1,0:T(8,128)S(1)}, u32[]{:S(2)}, u32[]{:S(2)}) collective-permute-start(f32[3,2,128,128]{3,2,1,0:T(8,128)} %get-tuple-element.35), channel_id=1, source_target_pairs={{0,16},{16,0},{1,17},{17,1},{2,18},{18,2},{3,19},{19,3},{4,20},{20... | collective-permute-start | bytes 1179656 | tf_op jit(solution)/shard_map/ppermute | solution.py:315
  40.8 27.1 %collective-permute-start.12 = (f32[3,2,128,128]{3,2,1,0:T(8,128)}, f32[3,2,128,128]{3,2,1,0:T(8,128)S(1)}, u32[]{:S(2)}, u32[]{:S(2)}) collective-permute-start(f32[3,2,128,128]{3,2,1,0:T(8,128)} %get-tuple-element.34.refs_2_), channel_id=1, source_target_pairs={{16,17},{17,18},{18,19},{19,20},{20,21},{21,22},{22,23},{23,24},{2... | collective-permute-start | bytes 1179656 | tf_op jit(solution)/shard_map/ppermute | solution.py:260
  43.2 24.7 %collective-permute-start.11 = (f32[3,2,128,128]{3,2,1,0:T(8,128)}, f32[3,2,128,128]{3,2,1,0:T(8,128)S(1)}, u32[]{:S(2)}, u32[]{:S(2)}) collective-permute-start(f32[3,2,128,128]{3,2,1,0:T(8,128)} %get-tuple-element.35), channel_id=1, source_target_pairs={{16,1},{17,2},{18,3},{19,4},{20,5},{21,6},{22,7},{23,8},{24,9},{25... | collective-permute-start | bytes 1179656 | tf_op jit(solution)/shard_map/ppermute | solution.py:260
  44.5 4.6 %collective-permute-start.7 = (f32[2,64,128]{2,1,0:T(8,128)}, f32[2,64,128]{2,1,0:T(8,128)S(1)}, u32[]{:S(2)}, u32[]{:S(2)}) collective-permute-start(f32[2,64,128]{2,1,0:T(8,128)} %get-tuple-element.33), channel_id=1, source_target_pairs={{0,2},{1,3},{2,0},{3,1},{4,6},{5,7},{6,4},{7,5},{8,10},{9,11},{10,... | collective-permute-start | bytes 196616 | tf_op jit(solution)/shard_map/ppermute | solution.py:248
  50.0 2.2 %copy-start.9 = (f32[2,64,128]{2,1,0:T(8,128)}, f32[2,64,128]{2,1,0:T(8,128)S(1)}, u32[]{:S(2)}) copy-start(f32[2,64,128]{2,1,0:T(8,128)S(1)} %add.7.refs_0_) | copy-start | bytes 196612
  50.0 3.8 %collective-permute-start.8 = (f32[2,64,128]{2,1,0:T(8,128)S(1)}, f32[2,64,128]{2,1,0:T(8,128)S(1)}, u32[]{:S(2)}, u32[]{:S(2)}) collective-permute-start(f32[2,64,128]{2,1,0:T(8,128)S(1)} %add.7.refs_0_), channel_id=1, source_target_pairs={{0,4},{1,5},{2,6},{3,7},{4,0},{5,1},{6,2},{7,3},{8,12},{9,13},{10,... | collective-permute-start | bytes 196616 | tf_op jit(solution)/shard_map/ppermute | solution.py:248
  50.1 1.0 %copy-start.3 = (f32[3,2,128,128]{3,2,1,0:T(8,128)S(1)}, f32[3,2,128,128]{3,2,1,0:T(8,128)}, u32[]{:S(2)}) copy-start(f32[3,2,128,128]{3,2,1,0:T(8,128)} %get-tuple-element.34.refs_2_) | copy-start | bytes 1179652
  52.2 0.9 %copy-start = (f32[3,2,128,256]{3,2,1,0:T(8,128)}, f32[3,2,128,256]{3,2,1,0:T(8,128)S(1)}, u32[]{:S(2)}) copy-start(f32[3,2,128,256]{3,2,1,0:T(8,128)S(1)} %place.1.refs_2_) | copy-start | bytes 2359300
  53.8 0.6 copy-start.12
  55.9 14.9 %collective-permute-start.10 = (f32[2,64,128]{2,1,0:T(8,128)}, f32[2,64,128]{2,1,0:T(8,128)S(1)}, u32[]{:S(2)}, u32[]{:S(2)}) collective-permute-start(f32[2,64,128]{2,1,0:T(8,128)} %get-tuple-element.36.refs_0_), channel_id=1, source_target_pairs={{0,8},{1,9},{2,10},{3,11},{4,12},{5,13},{6,14},{7,15},{8,0},{9,1},... | collective-permute-start | bytes 196616 | tf_op jit(solution)/shard_map/ppermute | solution.py:248
  67.9 1.1 %copy-start.1 = (f32[3,2,128,256]{3,2,1,0:T(8,128)S(1)}, f32[3,2,128,256]{3,2,1,0:T(8,128)}, u32[]{:S(2)}) copy-start(f32[3,2,128,256]{3,2,1,0:T(8,128)} %get-tuple-element.37.refs_1_) | copy-start | bytes 2359300
  70.8 0.6 copy-start.11

commit v5 on v4

--- a/solution.py
+++ b/solution.py
@@ -71,12 +71,9 @@
     return pltpu.roll(part, lax.rem(rows - row, rows), 0)
 
 
-def own_kernel(offsets, objects, intensity, probe, tiles, window_b, measured_b, measured_a, start):
+def own_kernel(offsets, objects, tiles, window_b):
     slab, _, rows, _ = objects.shape
-    a, _, row_b, col_b = share(offsets, rows, 0)
-    measured_a[...] = intensity[a]
-    measured_b[...] = intensity[1 - a]
-    start[...] = probe[...]
+    _, _, row_b, col_b = share(offsets, rows, 0)
     for s in range(slab):
         for p in range(2):
             tile = objects[s, p]
@@ -84,7 +81,7 @@
             window_b[s, p] = cut(tile, row_b, col_b, window_b.shape[-1])
 
 
-def prev_kernel(offsets_prev, tiles, window_b, window_a, halo, other):
+def prev_kernel(offsets_prev, after, tiles, window_b, window_a, halo, other):
     slab, _, rows, _ = tiles.shape
     width = halo.shape[-1]
     _, col_a, row_p, col_p = share(offsets_prev, rows, 1)
@@ -97,7 +94,15 @@
             other[s, p] = jnp.where(on_a, window_b[s, p], window)
 
 
-def wave_kernel(depth_count, offsets, tables, probe, near, far, window_a, window_b, *rest):
+def load_kernel(offsets, offsets_prev, intensity, far, probe, measured, start):
+    rows = probe.shape[-1]
+    near_a, _, _, _ = share(offsets, rows, 0)
+    far_a, _, _, _ = share(offsets_prev, rows, 1)
+    measured[...] = jnp.where(lax.axis_index("depth") == 0, far[far_a], intensity[1 - near_a])
+    start[...] = probe[...]
+
+
+def wave_kernel(depth_count, offsets, tables, probe, measured, window_a, window_b, *rest):
     others, rest = rest[: depth_count - 1], rest[depth_count - 1 :]
     halos, rest = rest[:depth_count], rest[depth_count:]
     grads, probe_parts = rest[:depth_count], rest[depth_count : 2 * depth_count]
@@ -133,8 +138,7 @@
 
     wave = lax.fori_loop(0, count - 1, forward, (probe[0], probe[1]), unroll=True if count <= 8 else 1)
     far_re, far_im = both_sides(*enter(count - 1, *wave), tables, 2)
-    measured = jnp.where(on_a, far[...], near[...])
-    misfit = 2.0 * (far_re * far_re + far_im * far_im - measured)
+    misfit = 2.0 * (far_re * far_re + far_im * far_im - measured[...])
     chi = both_sides(misfit * far_re, misfit * far_im, tables, 3)
 
     def leave(s, chi_re, chi_im):
@@ -162,14 +166,25 @@
             probe_parts[j][p] = waves[0, p, pl.ds(start, rows), :]
 
 
-def placed(x, row, col, mask, cols):
-    x = jnp.where(mask, pltpu.roll(x, lax.rem(row, x.shape[0]), 0), 0.0)
+def turn_kernel(offsets, after, *refs):
+    on_a = lax.axis_index("depth") == 0
+    count = len(refs) // 2
+    for x, out in zip(refs[:count], refs[count:]):
+        slab, _, rows, _ = x.shape
+        _, _, row_b, _ = share(offsets, rows, 0)
+        shift = lax.rem(jnp.where(on_a, 0, row_b), rows)
+        for s in range(slab):
+            for p in range(2):
+                out[s, p] = pltpu.roll(x[s, p], shift, 0)
+
+
+def placed(x, col, mask, cols):
     blank = jnp.zeros((x.shape[0], cols - x.shape[1]), x.dtype)
-    return pltpu.roll(jnp.concatenate([x, blank], axis=1), col, 1)
+    return pltpu.roll(jnp.concatenate([jnp.where(mask, x, 0.0), blank], axis=1), col, 1)
 
 
 def place_kernel(depth_count, offsets, offsets_prev, *refs):
-    *parts, out = refs
+    *parts, out, token = refs
     slab, _, rows, cols = out.shape
     depth = lax.axis_index("depth")
     _, _, row_b, col_b = share(offsets, rows, 0)
@@ -179,20 +194,21 @@
     for j in range(depth_count):
         is_a = depth == j
         is_b = lax.rem(depth + depth_count - 1, depth_count) == j
-        row = jnp.where(is_a, 0, row_b)
+        first = jnp.where(is_a, 0, row_b)
         last = jnp.where(is_a | is_b, rows, 0)
-        corners.append((row, jnp.where(is_a, col_a, col_b), (row_index >= row) & (row_index < last)))
+        corners.append((jnp.where(is_a, col_a, col_b), (row_index >= first) & (row_index < last)))
     for s in range(slab):
         for p in range(2):
             total = None
-            for (row, col, mask), part in zip(corners, parts):
-                x = placed(part[s, p], row, col, mask, cols)
+            for (col, mask), part in zip(corners, parts):
+                x = placed(part[s, p], col, mask, cols)
                 total = x if total is None else total + x
             out[s, p] = total
+    token[...] = jnp.zeros_like(token)
 
 
 def spill_kernel(depth_count, offsets_prev, *refs):
-    before, *spills, out = refs
+    before, *spills, out, token = refs
     slab, _, rows, cols = out.shape
     depth = lax.axis_index("depth")
     _, _, row_p, col_p = share(offsets_prev, rows, 1)
@@ -202,40 +218,25 @@
             x = spills[0][s, p]
             for q in range(1, depth_count):
                 x = jnp.where(depth == q, spills[q][s, p], x)
-            out[s, p] = before[s, p] + placed(x, row_p, col_p, mask, cols)
-
-
-def add_kernel(count, *refs):
-    a, b = refs[:2]
-    refs[2 + count][...] = a[...] + b[...]
-
-
-def add_then(a, b, later):
-    vmem, anywhere = pl.BlockSpec(memory_space=pltpu.VMEM), pl.BlockSpec(memory_space=pl.ANY)
-    out = pl.pallas_call(
-        lambda *refs: add_kernel(len(later), *refs),
-        name="add_then",
-        out_shape=[jax.ShapeDtypeStruct(x.shape, x.dtype) for x in (a, *later)],
-        in_specs=[vmem] * 2 + [anywhere] * len(later),
-        out_specs=[vmem] + [anywhere] * len(later),
-        input_output_aliases={2 + i: 1 + i for i in range(len(later))},
-    )(a, b, *later)
-    return out[0], out[1:]
-
-
-def call(kernel, name, scalars, arrays, outs, scratch=(), work=10**9):
+            out[s, p] = before[s, p] + placed(x, col_p, mask, cols)
+    token[...] = jnp.zeros_like(token)
+
+
+def call(kernel, name, scalars, arrays, outs, scratch=(), work=10**9, after=()):
     vmem = pl.BlockSpec(memory_space=pltpu.VMEM)
     moved = sum(math.prod(x.shape) * x.dtype.itemsize for x in (*arrays, *outs))
     return pl.pallas_call(
         kernel,
         name=name,
         out_shape=outs,
-        in_specs=[pl.BlockSpec(memory_space=pltpu.SMEM)] * len(scalars) + [vmem] * len(arrays),
+        in_specs=[pl.BlockSpec(memory_space=pltpu.SMEM)] * len(scalars)
+        + [pl.BlockSpec(memory_space=pl.ANY)] * len(after)
+        + [vmem] * len(arrays),
         out_specs=[vmem] * len(outs),
         scratch_shapes=scratch,
         compiler_params=pltpu.CompilerParams(vmem_limit_bytes=VMEM_LIMIT),
         cost_estimate=pl.CostEstimate(flops=work, bytes_accessed=moved, transcendentals=0),
-    )(*scalars, *arrays)
+    )(*scalars, *after, *arrays)
 
 
 def sum_round(x, level):
@@ -261,19 +262,20 @@
 
     offsets = jnp.concatenate([row_offsets, col_offsets])
     offsets_prev = lax.ppermute(offsets, "scan", [(i, (i + 1) % scan_count) for i in range(scan_count)])
+    far = across(intensity, 0, 0, 1)
     window = jax.ShapeDtypeStruct((slab, 2, n, n), f32)
-    plane = jax.ShapeDtypeStruct((n, n), f32)
     whole = jax.ShapeDtypeStruct(objects.shape, f32)
-    tiles, window_b, near, passed, start = call(
-        own_kernel,
-        "own",
-        [offsets],
-        [objects, intensity, probe],
-        [whole, window, plane, plane, jax.ShapeDtypeStruct(probe.shape, f32)],
+    token = jax.ShapeDtypeStruct((8, n), f32)
+    tiles, window_b = call(own_kernel, "own", [offsets], [objects], [whole, window])
+    window_a, halo, other = call(prev_kernel, "prev", [offsets_prev], [tiles, window_b], [window] * 3, after=[far])
+    halos = [across(halo, q, 1, -1) for q in range(depth_count)]
+    measured, start = call(
+        load_kernel,
+        "load",
+        [offsets, offsets_prev],
+        [intensity, far, probe],
+        [jax.ShapeDtypeStruct((n, n), f32), jax.ShapeDtypeStruct(probe.shape, f32)],
     )
-    far = across(passed, 0, 0, 1)
-    window_a, halo, other = call(prev_kernel, "prev", [offsets_prev], [tiles, window_b], [window] * 3)
-    halos = [across(halo, q, 1, -1) for q in range(depth_count)]
 
     others = []
     for j in range(1, depth_count):
@@ -288,7 +290,7 @@
         lambda *refs: wave_kernel(depth_count, *refs),
         "wave",
         [offsets],
-        [tables, start, near, far, window_a, window_b, *others, *halos],
+        [tables, start, measured, window_a, window_b, *others, *halos],
         [window] * depth_count + [jax.ShapeDtypeStruct((2, n // depth_count, n), f32)] * depth_count,
         [pltpu.VMEM((count, 2, n, n), f32)] * 2,
         work=5 * 10**9,
@@ -302,9 +304,9 @@
         )
     rounds = scan_count.bit_length() - 1
     paired = scan_count == 1 << rounds and rounds > 2
+    grads = call(turn_kernel, "turn", [offsets], grads, [window] * depth_count, after=[probe_grad])
     if paired:
-        probe_grad, grads = add_then(probe_grad, sum_round(probe_grad, 0), grads)
-        for level in range(1, rounds - 2):
+        for level in range(rounds - 2):
             probe_grad = probe_grad + sum_round(probe_grad, level)
     else:
         probe_grad = lax.psum(probe_grad, "scan")
@@ -313,17 +315,26 @@
     back = [grads[0]]
     for j in range(1, depth_count):
         back.append(lax.ppermute(grads[j], "depth", [(t, (t + j) % depth_count) for t in (0, 1)]))
-    (object_grad,) = call(
-        lambda *refs: place_kernel(depth_count, *refs), "place", [offsets, offsets_prev], back, [whole], work=2 * 10**9
+    object_grad, zero = call(
+        lambda *refs: place_kernel(depth_count, *refs),
+        "place",
+        [offsets, offsets_prev],
+        back,
+        [whole, token],
+        work=2 * 10**9,
     )
     if paired:
-        probe_grad, (object_grad,) = add_then(probe_grad, sum_round(probe_grad, rounds - 2), [object_grad])
+        probe_grad = probe_grad + sum_round(probe_grad, rounds - 2) + zero[0, 0]
         last = sum_round(probe_grad, rounds - 1)
-    (object_grad,) = call(
-        lambda *refs: spill_kernel(depth_count, *refs), "spill", [offsets_prev], [object_grad, *spill], [whole]
+    object_grad, zero = call(
+        lambda *refs: spill_kernel(depth_count, *refs),
+        "spill",
+        [offsets_prev],
+        [object_grad, *spill],
+        [whole, token],
     )
     if paired:
-        probe_grad, (object_grad,) = add_then(probe_grad, last, [object_grad])
+        probe_grad = probe_grad + last + zero[0, 0]
     return object_grad, probe_grad
 
 

time: 73.5 us -> 62.2 us (0.85)
  the two profiles are of different devices: /device:TPU:9 before, /device:TPU:1 now
where the time goes in v5:
time: 62.2 us; the launch traced here: 62 us
  starting transfers between devices  22.5 us (36%)
  waiting for transfers between devices  21.8 us (35%)
  Pallas kernels  12 us (19%)
  other arithmetic  2.69 us (4%)
  local copies, waits for them, and re-layouts  2.23 us (4%)
  between operations  0.79 us (1%)
    ppermute x5, starting transfers between devices, across(): return lax.ppermute(x, ('depth', 'scan'), route)  12.7 us
    pallas_call x7, Pallas kernels, call(): pl.pallas_call(kernel, name=name, out_shape=outs, in_specs=[pl.BlockSpec(...  12 us
    ppermute x4, waiting for transfers between devices, sum_round(): return lax.ppermute(x, ('depth', 'scan'), route)  9.1 us
    ppermute x5, waiting for transfers between devices, across(): return lax.ppermute(x, ('depth', 'scan'), route)  8.47 us
    ppermute x1, starting transfers between devices, body(): others.append(lax.ppermute(payload, 'depth', route))  4.48 us
    ppermute x4, starting transfers between devices, sum_round(): return lax.ppermute(x, ('depth', 'scan'), route)  2.99 us
    ppermute x1, waiting for transfers between devices, body(): lax.ppermute(offsets, 'scan', [(i, (i + 1) % scan_count) for i in range(s...  2.94 us
    ppermute x1, starting transfers between devices, body(): lax.ppermute(offsets, 'scan', [(i, (i + 1) % scan_count) for i in range(s...  2.04 us
  transfers between devices with their start and end apart: 13, of which 7 were waited for; matrix products, arithmetic and copies ran while one was open for 4% of the time, Pallas kernels for 6%

profile of v5, /device:TPU:1, one launch (start us, length us, event | category | flops | bytes accessed | tf_op | source)
XLA Modules:
  0.0 62.0 jit_solution(14974473789752208543)
XLA Ops:
  0.6 0.7 %collective-permute-start.1 = (f32[2,128,128]{2,1,0:T(8,128)}, f32[2,128,128]{2,1,0:T(8,128)S(1)}, u32[]{:S(2)}, u32[]{:S(2)}) collective-permute-start(f32[2,128,128]{2,1,0:T(8,128)} %intensity.1), channel_id=1, source_target_pairs={{0,1},{1,2},{2,3},{3,4},{4,5},{5,6},{6,7},{7,8},{8,9},{9,10},{10,1... | collective-permute-start | bytes 393224 | tf_op jit(solution)/shard_map/ppermute | solution.py:261
  1.3 0.7 %pad_add_fusion.offsets.refs_0_ = s32[4]{0:T(128)S(1)} fusion(s32[2]{0:T(128)} %param.9, s32[2]{0:T(128)} %param.8), kind=kLoop, calls=%fused_computation.2 | loop fusion | flops 4 | bytes 32 | tf_op jit(solution)/shard_map/concatenate | solution.py:263
  2.1 2.0 %collective-permute-start = (s32[4]{0:T(128)S(1)}, s32[4]{0:T(128)S(1)}, u32[]{:S(2)}, u32[]{:S(2)}) collective-permute-start(s32[4]{0:T(128)S(1)} %pad_add_fusion.offsets.refs_0_), channel_id=1, source_target_pairs={{0,1},{1,2},{2,3},{3,4},{4,5},{5,6},{6,7},{7,8},{8,9},{9,10},{10,1... | collective-permute-start | bytes 56 | tf_op jit(solution)/shard_map/ppermute | solution.py:264
  4.1 0.0 copy-start
  4.1 1.1 %copy-done = f32[3,2,128,256]{3,2,1,0:T(8,128)S(1)} copy-done((f32[3,2,128,256]{3,2,1,0:T(8,128)S(1)}, f32[3,2,128,256]{3,2,1,0:T(8,128)}, u32[]{:S(2)}) %copy-start) | copy-done | bytes 786456
  5.2 0.8 %own.1 = (f32[3,2,128,256]{3,2,1,0:T(8,128)S(1)}, f32[3,2,128,128]{3,2,1,0:T(8,128)S(1)}) custom-call(s32[4]{0:T(128)S(1)} %pad_add_fusion.offsets.refs_0_, f32[3,2,128,256]{3,2,1,0:T(8,128)S(1)} %copy-done), custom_call_target="tpu_custom_call" | custom-call | flops 1000000000 | bytes 1966080 | tf_op jit(solution)/shard_map/own/pallas_call | solution.py:228
  6.1 2.9 %collective-permute-done.offsets_prev.refs_1_.refs_0_ = s32[4]{0:T(128)S(1)} collective-permute-done((s32[4]{0:T(128)S(1)}, s32[4]{0:T(128)S(1)}, u32[]{:S(2)}, u32[]{:S(2)}) %collective-permute-start) | collective-permute-done | bytes 48 | tf_op jit(solution)/shard_map/ppermute | solution.py:264
  9.0 0.0 collective-permute-done.1.far.after
  9.0 0.0 copy-start.1
  9.0 0.0 copy-start.2
  9.0 1.0 %prev.1 = (f32[3,2,128,128]{3,2,1,0:T(8,128)S(1)}, f32[3,2,128,128]{3,2,1,0:T(8,128)S(1)}, f32[3,2,128,128]{3,2,1,0:T(8,128)S(1)}) custom-call(s32[4]{0:T(128)S(1)} %collective-permute-done.offsets_prev.refs_1_.refs_0_, f32[2,128,128]{2,1,0:T(8,128)S(1)} %collective-permute-done.1.far.after, f32[3,2,128,256]{3,2,1,0:T(8,128)S(1)} %get-tuple-element.21.tiles, ...), custom_call_target="tpu_custom_call" | custom-call | flops 1000000000 | bytes 2359296 | tf_op jit(solution)/shard_map/prev/pallas_call | solution.py:228
  10.1 4.5 %collective-permute-start.2 = (f32[3,2,128,128]{3,2,1,0:T(8,128)S(1)}, f32[3,2,128,128]{3,2,1,0:T(8,128)S(1)}, u32[]{:S(2)}, u32[]{:S(2)}) collective-permute-start(f32[3,2,128,128]{3,2,1,0:T(8,128)S(1)} %get-tuple-element.24), channel_id=1, source_target_pairs={{16,0},{0,16},{17,1},{1,17},{18,2},{2,18},{19,3},{3,19},{20,4},{4,... | collective-permute-start | bytes 1179656 | tf_op jit(solution)/shard_map/ppermute | solution.py:285
  14.5 0.0 copy-start.3
  14.5 3.1 %collective-permute-start.4 = (f32[3,2,128,128]{3,2,1,0:T(8,128)S(1)}, f32[3,2,128,128]{3,2,1,0:T(8,128)S(1)}, u32[]{:S(2)}, u32[]{:S(2)}) collective-permute-start(f32[3,2,128,128]{3,2,1,0:T(8,128)S(1)} %get-tuple-element.25), channel_id=1, source_target_pairs={{16,31},{17,16},{18,17},{19,18},{20,19},{21,20},{22,21},{23,22},{2... | collective-permute-start | bytes 1179656 | tf_op jit(solution)/shard_map/ppermute | solution.py:261
  17.6 1.3 %collective-permute-start.3 = (f32[3,2,128,128]{3,2,1,0:T(8,128)S(1)}, f32[3,2,128,128]{3,2,1,0:T(8,128)S(1)}, u32[]{:S(2)}, u32[]{:S(2)}) collective-permute-start(f32[3,2,128,128]{3,2,1,0:T(8,128)S(1)} %get-tuple-element.25), channel_id=1, source_target_pairs={{0,31},{1,16},{2,17},{3,18},{4,19},{5,20},{6,21},{7,22},{8,23},{9,... | collective-permute-start | bytes 1179656 | tf_op jit(solution)/shard_map/ppermute | solution.py:261
  18.9 0.0 copy-done.1
  18.9 0.0 copy-done.2
  18.9 0.6 load.1
  19.5 0.0 collective-permute-done.2.refs_6_
  19.5 4.3 %collective-permute-done.4.refs_8_ = f32[3,2,128,128]{3,2,1,0:T(8,128)S(1)} collective-permute-done((f32[3,2,128,128]{3,2,1,0:T(8,128)S(1)}, f32[3,2,128,128]{3,2,1,0:T(8,128)S(1)}, u32[]{:S(2)}, u32[]{:S(2)}) %collective-permute-start.4) | collective-permute-done | bytes 393248 | tf_op jit(solution)/shard_map/ppermute | solution.py:261
  23.8 3.6 %collective-permute-done.3.refs_7_ = f32[3,2,128,128]{3,2,1,0:T(8,128)S(1)} collective-permute-done((f32[3,2,128,128]{3,2,1,0:T(8,128)S(1)}, f32[3,2,128,128]{3,2,1,0:T(8,128)S(1)}, u32[]{:S(2)}, u32[]{:S(2)}) %collective-permute-start.3) | collective-permute-done | bytes 393248 | tf_op jit(solution)/shard_map/ppermute | solution.py:261
  27.4 0.0 copy-done.3
  27.4 6.4 %wave.1 = (f32[3,2,128,128]{3,2,1,0:T(8,128)S(1)}, f32[3,2,128,128]{3,2,1,0:T(8,128)S(1)}, f32[2,64,128]{2,1,0:T(8,128)S(1)}, f32[2,64,128]{2,1,0:T(8,128)S(1)}) custom-call(s32[4]{0:T(128)S(1)} %pad_add_fusion.offsets.refs_0_, bf16[4,2,256,256]{3,2,1,0:T(8,128)(2,1)S(1)} %copy-done.3, f32[2,128,128]{2,1,0:T(8,128)S(1)} %get-tuple-element.19.refs_2_, ...), custom_call_target="tpu_custom_call" | custom-call | flops 5000000000 | bytes 4128768 | tf_op jit(solution)/shard_map/wave/pallas_call | solution.py:228
  33.8 0.1 collective-permute-start.5
  33.9 1.2 %collective-permute-done.5 = f32[2,64,128]{2,1,0:T(8,128)S(1)} collective-permute-done((f32[2,64,128]{2,1,0:T(8,128)S(1)}, f32[2,64,128]{2,1,0:T(8,128)S(1)}, u32[]{:S(2)}, u32[]{:S(2)}) %collective-permute-start.5) | collective-permute-done | bytes 65568 | tf_op jit(solution)/shard_map/ppermute | solution.py:302
  35.1 0.7 %turn.1 = (f32[3,2,128,128]{3,2,1,0:T(8,128)S(1)}, f32[3,2,128,128]{3,2,1,0:T(8,128)S(1)}) custom-call(s32[4]{0:T(128)S(1)} %pad_add_fusion.offsets.refs_0_, f32[2,64,128]{2,1,0:T(8,128)S(1)} %add.27.after, f32[3,2,128,128]{3,2,1,0:T(8,128)S(1)} %get-tuple-element.28.refs_0_, f32[3,2,128,128]{3,2,1,0:T(8,128)S(1)} %get-tuple-element.29.refs_1_), custom_call_target="tpu_custom_call" | custom-call | flops 1000000000 | bytes 1572864 | tf_op jit(solution)/shard_map/turn/pallas_call | solution.py:228
  35.8 0.2 collective-permute-start.6
  36.1 0.0 collective-permute-start.9
  36.1 3.1 %collective-permute-done.9 = f32[2,64,128]{2,1,0:T(8,128)S(1)} collective-permute-done((f32[2,64,128]{2,1,0:T(8,128)S(1)}, f32[2,64,128]{2,1,0:T(8,128)S(1)}, u32[]{:S(2)}, u32[]{:S(2)}) %collective-permute-start.9) | collective-permute-done | bytes 65568 | tf_op jit(solution)/shard_map/ppermute | solution.py:249
  39.2 0.6 collective-permute-start.10
  39.8 3.7 %collective-permute-start.7 = (f32[3,2,128,128]{3,2,1,0:T(8,128)S(1)}, f32[3,2,128,128]{3,2,1,0:T(8,128)S(1)}, u32[]{:S(2)}, u32[]{:S(2)}) collective-permute-start(f32[3,2,128,128]{3,2,1,0:T(8,128)S(1)} %get-tuple-element.31), channel_id=1, source_target_pairs={{16,1},{17,2},{18,3},{19,4},{20,5},{21,6},{22,7},{23,8},{24,9},{25... | collective-permute-start | bytes 1179656 | tf_op jit(solution)/shard_map/ppermute | solution.py:261
  43.5 3.9 %collective-permute-start.8 = (f32[3,2,128,128]{3,2,1,0:T(8,128)S(1)}, f32[3,2,128,128]{3,2,1,0:T(8,128)S(1)}, u32[]{:S(2)}, u32[]{:S(2)}) collective-permute-start(f32[3,2,128,128]{3,2,1,0:T(8,128)S(1)} %get-tuple-element.30.refs_2_), channel_id=1, source_target_pairs={{16,17},{17,18},{18,19},{19,20},{20,21},{21,22},{22,23},{23,24},{2... | collective-permute-start | bytes 1179656 | tf_op jit(solution)/shard_map/ppermute | solution.py:261
  47.4 0.0 collective-permute-done.10
  47.5 0.7 %collective-permute-start.11 = (f32[2,64,128]{2,1,0:T(8,128)S(1)}, f32[2,64,128]{2,1,0:T(8,128)S(1)}, u32[]{:S(2)}, u32[]{:S(2)}) collective-permute-start(f32[2,64,128]{2,1,0:T(8,128)S(1)} %add.29), channel_id=1, source_target_pairs={{0,4},{1,5},{2,6},{3,7},{4,0},{5,1},{6,2},{7,3},{8,12},{9,13},{10,... | collective-permute-start | bytes 196616 | tf_op jit(solution)/shard_map/ppermute | solution.py:249
  48.2 0.0 collective-permute-done.6.refs_3_
  48.2 0.9 %place.1 = (f32[3,2,128,256]{3,2,1,0:T(8,128)S(1)}, f32[8,128]{1,0:T(8,128)S(1)}) custom-call(s32[4]{0:T(128)S(1)} %pad_add_fusion.offsets.refs_0_, s32[4]{0:T(128)S(1)} %collective-permute-done.offsets_prev.refs_1_.refs_0_, f32[3,2,128,128]{3,2,1,0:T(8,128)S(1)} %get-tuple-element.30.refs_2_, f32[3,2,128,128]{3,2,1,0:T(8,128)S(1)} %collective-permute-done.6.refs_3_), custom_call_target="tpu_custom_call" | custom-call | flops 2000000000 | bytes 1576960 | tf_op jit(solution)/shard_map/place/pallas_call | solution.py:228
  49.0 0.5 slice.6
  49.6 6.0 %collective-permute-done.11 = f32[2,64,128]{2,1,0:T(8,128)S(1)} collective-permute-done((f32[2,64,128]{2,1,0:T(8,128)S(1)}, f32[2,64,128]{2,1,0:T(8,128)S(1)}, u32[]{:S(2)}, u32[]{:S(2)}) %collective-permute-start.11) | collective-permute-done | bytes 65568 | tf_op jit(solution)/shard_map/ppermute | solution.py:249
  55.5 0.7 %add_add_fusion.1 = f32[2,64,128]{2,1,0:T(8,128)S(1)} fusion(f32[2,64,128]{2,1,0:T(8,128)S(1)} %add.29, f32[2,64,128]{2,1,0:T(8,128)S(1)} %collective-permute-done.11, f32[]{:T(128)} %bitcast), kind=kLoop, calls=%fused_computation.1 | loop fusion | flops 32768 | bytes 196612 | tf_op jit(solution)/shard_map/add | solution.py:327
  56.2 1.7 %collective-permute-start.12 = (f32[2,64,128]{2,1,0:T(8,128)S(1)}, f32[2,64,128]{2,1,0:T(8,128)S(1)}, u32[]{:S(2)}, u32[]{:S(2)}) collective-permute-start(f32[2,64,128]{2,1,0:T(8,128)S(1)} %add_add_fusion.1), channel_id=1, source_target_pairs={{0,8},{1,9},{2,10},{3,11},{4,12},{5,13},{6,14},{7,15},{8,0},{9,1},... | collective-permute-start | bytes 196616 | tf_op jit(solution)/shard_map/ppermute | solution.py:249
  57.9 0.6 collective-permute-done.8.refs_3_
  58.5 0.0 collective-permute-done.7.refs_2_
  58.5 1.6 %spill.1 = (f32[3,2,128,256]{3,2,1,0:T(8,128)}, f32[8,128]{1,0:T(8,128)S(1)}) custom-call(s32[4]{0:T(128)S(1)} %collective-permute-done.offsets_prev.refs_1_.refs_0_, f32[3,2,128,256]{3,2,1,0:T(8,128)S(1)} %get-tuple-element.32.refs_1_, f32[3,2,128,128]{3,2,1,0:T(8,128)S(1)} %collective-permute-done.7.refs_2_, ...), custom_call_target="tpu_custom_call" | custom-call | flops 1000000000 | bytes 2363392 | tf_op jit(solution)/shard_map/spill/pallas_call | solution.py:228
  60.1 0.6 slice.7
  60.7 0.0 collective-permute-done.12
  60.7 1.3 %add_add_fusion = f32[2,64,128]{2,1,0:T(8,128)} fusion(f32[2,64,128]{2,1,0:T(8,128)S(1)} %add_add_fusion.1, f32[2,64,128]{2,1,0:T(8,128)S(1)} %collective-permute-done.12, f32[]{:T(128)} %bitcast.1), kind=kLoop, calls=%fused_computation | loop fusion | flops 32768 | bytes 196612 | tf_op jit(solution)/shard_map/add | solution.py:337
  (3 shorter events, 0.0 us)
Async XLA Ops:
  0.6 8.4 %collective-permute-start.1 = (f32[2,128,128]{2,1,0:T(8,128)}, f32[2,128,128]{2,1,0:T(8,128)S(1)}, u32[]{:S(2)}, u32[]{:S(2)}) collective-permute-start(f32[2,128,128]{2,1,0:T(8,128)} %intensity.1), channel_id=1, source_target_pairs={{0,1},{1,2},{2,3},{3,4},{4,5},{5,6},{6,7},{7,8},{8,9},{9,10},{10,1... | collective-permute-start | bytes 393224 | tf_op jit(solution)/shard_map/ppermute | solution.py:261
  2.1 7.0 %collective-permute-start = (s32[4]{0:T(128)S(1)}, s32[4]{0:T(128)S(1)}, u32[]{:S(2)}, u32[]{:S(2)}) collective-permute-start(s32[4]{0:T(128)S(1)} %pad_add_fusion.offsets.refs_0_), channel_id=1, source_target_pairs={{0,1},{1,2},{2,3},{3,4},{4,5},{5,6},{6,7},{7,8},{8,9},{9,10},{10,1... | collective-permute-start | bytes 56 | tf_op jit(solution)/shard_map/ppermute | solution.py:264
  4.1 1.1 %copy-start = (f32[3,2,128,256]{3,2,1,0:T(8,128)S(1)}, f32[3,2,128,256]{3,2,1,0:T(8,128)}, u32[]{:S(2)}) copy-start(f32[3,2,128,256]{3,2,1,0:T(8,128)} %objects.1) | copy-start | bytes 2359300
  9.0 9.9 %copy-start.1 = (f32[2,128,128]{2,1,0:T(8,128)S(1)}, f32[2,128,128]{2,1,0:T(8,128)}, u32[]{:S(2)}) copy-start(f32[2,128,128]{2,1,0:T(8,128)} %intensity.1) | copy-start | bytes 393220
  9.0 9.9 %copy-start.2 = (f32[2,128,128]{2,1,0:T(8,128)S(1)}, f32[2,128,128]{2,1,0:T(8,128)}, u32[]{:S(2)}) copy-start(f32[2,128,128]{2,1,0:T(8,128)} %probe.1) | copy-start | bytes 393220
  10.1 9.5 %collective-permute-start.2 = (f32[3,2,128,128]{3,2,1,0:T(8,128)S(1)}, f32[3,2,128,128]{3,2,1,0:T(8,128)S(1)}, u32[]{:S(2)}, u32[]{:S(2)}) collective-permute-start(f32[3,2,128,128]{3,2,1,0:T(8,128)S(1)} %get-tuple-element.24), channel_id=1, source_target_pairs={{16,0},{0,16},{17,1},{1,17},{18,2},{2,18},{19,3},{3,19},{20,4},{4,... | collective-permute-start | bytes 1179656 | tf_op jit(solution)/shard_map/ppermute | solution.py:285
  14.5 12.9 %copy-start.3 = (bf16[4,2,256,256]{3,2,1,0:T(8,128)(2,1)S(1)}, bf16[4,2,256,256]{3,2,1,0:T(8,128)(2,1)}, u32[]{:S(2)}) copy-start(bf16[4,2,256,256]{3,2,1,0:T(8,128)(2,1)} %constant.2.clone.refs_1_) | copy-start | bytes 3145732
  14.5 9.2 %collective-permute-start.4 = (f32[3,2,128,128]{3,2,1,0:T(8,128)S(1)}, f32[3,2,128,128]{3,2,1,0:T(8,128)S(1)}, u32[]{:S(2)}, u32[]{:S(2)}) collective-permute-start(f32[3,2,128,128]{3,2,1,0:T(8,128)S(1)} %get-tuple-element.25), channel_id=1, source_target_pairs={{16,31},{17,16},{18,17},{19,18},{20,19},{21,20},{22,21},{23,22},{2... | collective-permute-start | bytes 1179656 | tf_op jit(solution)/shard_map/ppermute | solution.py:261
  17.6 9.8 %collective-permute-start.3 = (f32[3,2,128,128]{3,2,1,0:T(8,128)S(1)}, f32[3,2,128,128]{3,2,1,0:T(8,128)S(1)}, u32[]{:S(2)}, u32[]{:S(2)}) collective-permute-start(f32[3,2,128,128]{3,2,1,0:T(8,128)S(1)} %get-tuple-element.25), channel_id=1, source_target_pairs={{0,31},{1,16},{2,17},{3,18},{4,19},{5,20},{6,21},{7,22},{8,23},{9,... | collective-permute-start | bytes 1179656 | tf_op jit(solution)/shard_map/ppermute | solution.py:261
  33.8 1.3 %collective-permute-start.5 = (f32[2,64,128]{2,1,0:T(8,128)S(1)}, f32[2,64,128]{2,1,0:T(8,128)S(1)}, u32[]{:S(2)}, u32[]{:S(2)}) collective-permute-start(f32[2,64,128]{2,1,0:T(8,128)S(1)} %get-tuple-element.27), channel_id=1, source_target_pairs={{0,16},{16,0},{1,17},{17,1},{2,18},{18,2},{3,19},{19,3},{4,20},{20... | collective-permute-start | bytes 196616 | tf_op jit(solution)/shard_map/ppermute | solution.py:302
  35.8 12.3 %collective-permute-start.6 = (f32[3,2,128,128]{3,2,1,0:T(8,128)S(1)}, f32[3,2,128,128]{3,2,1,0:T(8,128)S(1)}, u32[]{:S(2)}, u32[]{:S(2)}) collective-permute-start(f32[3,2,128,128]{3,2,1,0:T(8,128)S(1)} %get-tuple-element.31), channel_id=1, source_target_pairs={{0,16},{16,0},{1,17},{17,1},{2,18},{18,2},{3,19},{19,3},{4,20},{20... | collective-permute-start | bytes 1179656 | tf_op jit(solution)/shard_map/ppermute | solution.py:317
  36.1 3.1 %collective-permute-start.9 = (f32[2,64,128]{2,1,0:T(8,128)S(1)}, f32[2,64,128]{2,1,0:T(8,128)S(1)}, u32[]{:S(2)}, u32[]{:S(2)}) collective-permute-start(f32[2,64,128]{2,1,0:T(8,128)S(1)} %add.27.after), channel_id=1, source_target_pairs={{0,1},{1,0},{2,3},{3,2},{4,5},{5,4},{6,7},{7,6},{8,9},{9,8},{10,11... | collective-permute-start | bytes 196616 | tf_op jit(solution)/shard_map/ppermute | solution.py:249
  39.2 8.2 %collective-permute-start.10 = (f32[2,64,128]{2,1,0:T(8,128)S(1)}, f32[2,64,128]{2,1,0:T(8,128)S(1)}, u32[]{:S(2)}, u32[]{:S(2)}) collective-permute-start(f32[2,64,128]{2,1,0:T(8,128)S(1)} %add.28), channel_id=1, source_target_pairs={{0,2},{1,3},{2,0},{3,1},{4,6},{5,7},{6,4},{7,5},{8,10},{9,11},{10,... | collective-permute-start | bytes 196616 | tf_op jit(solution)/shard_map/ppermute | solution.py:249
  39.8 18.7 %collective-permute-start.7 = (f32[3,2,128,128]{3,2,1,0:T(8,128)S(1)}, f32[3,2,128,128]{3,2,1,0:T(8,128)S(1)}, u32[]{:S(2)}, u32[]{:S(2)}) collective-permute-start(f32[3,2,128,128]{3,2,1,0:T(8,128)S(1)} %get-tuple-element.31), channel_id=1, source_target_pairs={{16,1},{17,2},{18,3},{19,4},{20,5},{21,6},{22,7},{23,8},{24,9},{25... | collective-permute-start | bytes 1179656 | tf_op jit(solution)/shard_map/ppermute | solution.py:261
  43.5 15.0 %collective-permute-start.8 = (f32[3,2,128,128]{3,2,1,0:T(8,128)S(1)}, f32[3,2,128,128]{3,2,1,0:T(8,128)S(1)}, u32[]{:S(2)}, u32[]{:S(2)}) collective-permute-start(f32[3,2,128,128]{3,2,1,0:T(8,128)S(1)} %get-tuple-element.30.refs_2_), channel_id=1, source_target_pairs={{16,17},{17,18},{18,19},{19,20},{20,21},{21,22},{22,23},{23,24},{2... | collective-permute-start | bytes 1179656 | tf_op jit(solution)/shard_map/ppermute | solution.py:261
  47.5 8.1 %collective-permute-start.11 = (f32[2,64,128]{2,1,0:T(8,128)S(1)}, f32[2,64,128]{2,1,0:T(8,128)S(1)}, u32[]{:S(2)}, u32[]{:S(2)}) collective-permute-start(f32[2,64,128]{2,1,0:T(8,128)S(1)} %add.29), channel_id=1, source_target_pairs={{0,4},{1,5},{2,6},{3,7},{4,0},{5,1},{6,2},{7,3},{8,12},{9,13},{10,... | collective-permute-start | bytes 196616 | tf_op jit(solution)/shard_map/ppermute | solution.py:249
  56.2 4.5 %collective-permute-start.12 = (f32[2,64,128]{2,1,0:T(8,128)S(1)}, f32[2,64,128]{2,1,0:T(8,128)S(1)}, u32[]{:S(2)}, u32[]{:S(2)}) collective-permute-start(f32[2,64,128]{2,1,0:T(8,128)S(1)} %add_add_fusion.1), channel_id=1, source_target_pairs={{0,8},{1,9},{2,10},{3,11},{4,12},{5,13},{6,14},{7,15},{8,0},{9,1},... | collective-permute-start | bytes 196616 | tf_op jit(solution)/shard_map/ppermute | solution.py:249

commit v6 on v5

--- a/solution.py
+++ b/solution.py
@@ -81,17 +81,23 @@
             window_b[s, p] = cut(tile, row_b, col_b, window_b.shape[-1])
 
 
-def prev_kernel(offsets_prev, after, tiles, window_b, window_a, halo, other):
+def prev_kernel(offsets_prev, after, tiles, window_a, halo):
     slab, _, rows, _ = tiles.shape
     width = halo.shape[-1]
     _, col_a, row_p, col_p = share(offsets_prev, rows, 1)
-    on_a = lax.axis_index("depth") == 0
     for s in range(slab):
         for p in range(2):
             halo[s, p] = cut(tiles[s, p], row_p, col_p, width)
-            window = cut(tiles[s, p], 0, col_a, width)
-            window_a[s, p] = window
-            other[s, p] = jnp.where(on_a, window_b[s, p], window)
+            window_a[s, p] = cut(tiles[s, p], 0, col_a, width)
+
+
+def join_kernel(offsets, after, window_b, halo, joined):
+    slab, _, rows, cols = joined.shape
+    _, _, row_b, _ = share(offsets, rows, 0)
+    inside = lax.broadcasted_iota(jnp.int32, (rows, cols), 0) < rows - row_b
+    for s in range(slab):
+        for p in range(2):
+            joined[s, p] = jnp.where(inside, window_b[s, p], halo[s, p])
 
 
 def load_kernel(offsets, offsets_prev, intensity, far, probe, measured, start):
@@ -102,30 +108,21 @@
     start[...] = probe[...]
 
 
-def wave_kernel(depth_count, offsets, tables, probe, measured, window_a, window_b, *rest):
-    others, rest = rest[: depth_count - 1], rest[depth_count - 1 :]
-    halos, rest = rest[:depth_count], rest[depth_count:]
-    grads, probe_parts = rest[:depth_count], rest[depth_count : 2 * depth_count]
-    layers, waves = rest[2 * depth_count :]
+def wave_kernel(depth_count, tables, probe, measured, window_a, window_b, *rest):
+    others_a, others_b = rest[: depth_count - 1], rest[depth_count - 1 : 2 * depth_count - 2]
+    rest = rest[2 * depth_count - 2 :]
+    grads, (probe_grad, layers, waves) = rest[:depth_count], rest[depth_count:]
     slab = window_a.shape[0]
     n = probe.shape[-1]
     count = slab * depth_count
     depth = lax.axis_index("depth")
     on_a = depth == 0
-    _, _, row_b, _ = share(offsets, n, 0)
-    split = jnp.where(on_a, 0, row_b)
-    inside = lax.broadcasted_iota(jnp.int32, (n, n), 0) < n - split
-    for s in range(slab):
-        for p in range(2):
-            layers[depth * slab + s, p] = jnp.where(on_a, window_a[s, p], window_b[s, p])
-    for j in range(1, depth_count):
+    for j in range(depth_count):
         base = lax.rem(depth - j + depth_count, depth_count) * slab
-        for s in range(slab):
-            layers[base + s] = others[j - 1][s]
-    for q in range(depth_count):
+        of_a, of_b = ((window_a, *others_a)[j], (window_b, *others_b)[j])
         for s in range(slab):
             for p in range(2):
-                layers[q * slab + s, p] = jnp.where(inside, layers[q * slab + s, p], halos[q][s, p])
+                layers[base + s, p] = jnp.where(on_a, of_a[s, p], of_b[s, p])
 
     def enter(s, re, im):
         waves[s, 0] = re
@@ -158,12 +155,9 @@
         for s in range(slab):
             grads[j][s] = waves[base + s]
     rows = n // depth_count
-    waves[0, 0] = jnp.where(depth < 2, grad[0], 0.0)
-    waves[0, 1] = jnp.where(depth < 2, grad[1], 0.0)
-    for j in range(depth_count):
-        start = pl.multiple_of(lax.rem(depth + j, depth_count) * rows, rows)
-        for p in range(2):
-            probe_parts[j][p] = waves[0, p, pl.ds(start, rows), :]
+    for k in range(depth_count):
+        for p in range(2):
+            probe_grad[k, p] = grad[p][k * rows : (k + 1) * rows]
 
 
 def turn_kernel(offsets, after, *refs):
@@ -184,7 +178,7 @@
 
 
 def place_kernel(depth_count, offsets, offsets_prev, *refs):
-    *parts, out, token = refs
+    *parts, out = refs
     slab, _, rows, cols = out.shape
     depth = lax.axis_index("depth")
     _, _, row_b, col_b = share(offsets, rows, 0)
@@ -204,11 +198,19 @@
                 x = placed(part[s, p], col, mask, cols)
                 total = x if total is None else total + x
             out[s, p] = total
-    token[...] = jnp.zeros_like(token)
-
-
-def spill_kernel(depth_count, offsets_prev, *refs):
-    before, *spills, out, token = refs
+
+
+def keep_kernel(after, blocks, *refs):
+    *sent, out = refs
+    depth = lax.axis_index("depth")
+    x = blocks[0]
+    for k, block in enumerate(sent):
+        x = jnp.where(depth == k + 1, block[...], x)
+    out[...] = x
+
+
+def spill_kernel(depth_count, offsets_prev, before, *refs):
+    *spills, out, token = refs
     slab, _, rows, cols = out.shape
     depth = lax.axis_index("depth")
     _, _, row_p, col_p = share(offsets_prev, rows, 1)
@@ -220,6 +222,10 @@
                 x = jnp.where(depth == q, spills[q][s, p], x)
             out[s, p] = before[s, p] + placed(x, col_p, mask, cols)
     token[...] = jnp.zeros_like(token)
+
+
+def add_kernel(after, a, b, out):
+    out[...] = a[...] + b[...]
 
 
 def call(kernel, name, scalars, arrays, outs, scratch=(), work=10**9, after=()):
@@ -239,21 +245,10 @@
     )(*scalars, *after, *arrays)
 
 
-def sum_round(x, level):
-    depth_count, scan_count = lax.axis_size("depth"), lax.axis_size("scan")
-    levels = scan_count.bit_length() - 1
-    route = []
-    for d in range(depth_count):
-        step = 1 << ((level + (d % 2) * (levels // 2)) % levels)
-        route += [(d * scan_count + i, d * scan_count + (i ^ step)) for i in range(scan_count)]
-    return lax.ppermute(x, ("depth", "scan"), route)
-
-
 def body(objects, probe, row_offsets, col_offsets, intensity):
     slab = objects.shape[0]
     n = probe.shape[-1]
     depth_count, scan_count = lax.axis_size("depth"), lax.axis_size("scan")
-    depth = lax.axis_index("depth")
     f32 = jnp.float32
 
     def across(x, source, target, shift):
@@ -265,10 +260,14 @@
     far = across(intensity, 0, 0, 1)
     window = jax.ShapeDtypeStruct((slab, 2, n, n), f32)
     whole = jax.ShapeDtypeStruct(objects.shape, f32)
-    token = jax.ShapeDtypeStruct((8, n), f32)
     tiles, window_b = call(own_kernel, "own", [offsets], [objects], [whole, window])
-    window_a, halo, other = call(prev_kernel, "prev", [offsets_prev], [tiles, window_b], [window] * 3, after=[far])
-    halos = [across(halo, q, 1, -1) for q in range(depth_count)]
+    window_a, halo = call(prev_kernel, "prev", [offsets_prev], [tiles], [window] * 2, after=[far])
+    halo = lax.ppermute(halo, "scan", [((i + 1) % scan_count, i) for i in range(scan_count)])
+
+    def gathered(x, target):
+        return [lax.ppermute(x, "depth", [((target - j) % depth_count, target)]) for j in range(1, depth_count)]
+
+    others_a = gathered(window_a, 0)
     measured, start = call(
         load_kernel,
         "load",
@@ -277,64 +276,59 @@
         [jax.ShapeDtypeStruct((n, n), f32), jax.ShapeDtypeStruct(probe.shape, f32)],
     )
 
-    others = []
-    for j in range(1, depth_count):
-        target = lax.rem(depth + j, depth_count)
-        payload = other if depth_count == 2 else jnp.where(target == 0, window_a, window_b)
-        route = [((t - j) % depth_count, t) for t in (0, 1)]
-        others.append(lax.ppermute(payload, "depth", route))
+    (window_b,) = call(join_kernel, "join", [offsets], [window_b, halo], [window], after=[measured])
+    others_b = gathered(window_b, 1)
 
     tables = jnp.asarray(constant_tables(n))
     count = slab * depth_count
-    parts = call(
+    blocks = jax.ShapeDtypeStruct((depth_count, 2, n // depth_count, n), f32)
+    *grads, probe_grad = call(
         lambda *refs: wave_kernel(depth_count, *refs),
         "wave",
-        [offsets],
-        [tables, start, measured, window_a, window_b, *others, *halos],
-        [window] * depth_count + [jax.ShapeDtypeStruct((2, n // depth_count, n), f32)] * depth_count,
+        [],
+        [tables, start, measured, window_a, window_b, *others_a, *others_b],
+        [window] * depth_count + [blocks],
         [pltpu.VMEM((count, 2, n, n), f32)] * 2,
         work=5 * 10**9,
     )
-    grads, probe_parts = parts[:depth_count], parts[depth_count:]
-
-    probe_grad = probe_parts[0]
-    for j in range(1, depth_count):
-        probe_grad = probe_grad + lax.ppermute(
-            probe_parts[j], "depth", [(t, (t + j) % depth_count) for t in range(depth_count)]
-        )
-    rounds = scan_count.bit_length() - 1
-    paired = scan_count == 1 << rounds and rounds > 2
+
+    probe_grad = probe_grad + lax.ppermute(probe_grad, "depth", [(1, 0)])
     grads = call(turn_kernel, "turn", [offsets], grads, [window] * depth_count, after=[probe_grad])
-    if paired:
-        for level in range(rounds - 2):
-            probe_grad = probe_grad + sum_round(probe_grad, level)
-    else:
-        probe_grad = lax.psum(probe_grad, "scan")
 
     spill = [across(grads[(q - 1) % depth_count], 1, q, 1) for q in range(depth_count)]
     back = [grads[0]]
     for j in range(1, depth_count):
         back.append(lax.ppermute(grads[j], "depth", [(t, (t + j) % depth_count) for t in (0, 1)]))
-    object_grad, zero = call(
+    (object_grad,) = call(
         lambda *refs: place_kernel(depth_count, *refs),
         "place",
         [offsets, offsets_prev],
         back,
-        [whole, token],
+        [whole],
         work=2 * 10**9,
     )
-    if paired:
-        probe_grad = probe_grad + sum_round(probe_grad, rounds - 2) + zero[0, 0]
-        last = sum_round(probe_grad, rounds - 1)
-    object_grad, zero = call(
+    rounds = scan_count.bit_length() - 1
+    if scan_count == 1 << rounds:
+        order = [*range(rounds // 2, rounds), *reversed(range(rounds // 2))]
+        for place, level in enumerate(order):
+            last = lax.ppermute(probe_grad, ("depth", "scan"), [(i, i ^ (1 << level)) for i in range(scan_count)])
+            if place == rounds - 2:
+                (probe_grad,) = call(add_kernel, "add", [], [probe_grad, last], [blocks], after=[object_grad])
+            else:
+                probe_grad = probe_grad + last
+    else:
+        probe_grad = lax.psum(probe_grad, "scan")
+    object_grad, token = call(
         lambda *refs: spill_kernel(depth_count, *refs),
         "spill",
         [offsets_prev],
         [object_grad, *spill],
-        [whole, token],
-    )
-    if paired:
-        probe_grad = probe_grad + last + zero[0, 0]
+        [whole, jax.ShapeDtypeStruct((8, n), f32)],
+    )
+    sent = [lax.ppermute(probe_grad[k], "depth", [(0, k)]) for k in range(1, depth_count)]
+    (probe_grad,) = call(
+        keep_kernel, "keep", [], [probe_grad, *sent], [jax.ShapeDtypeStruct(blocks.shape[1:], f32)], after=[token]
+    )
     return object_grad, probe_grad
 
 

time: 62.2 us -> 74.3 us (1.19)
  the two profiles are of different devices: /device:TPU:1 before, /device:TPU:0 now
where the time goes in v6:
time: 74.3 us; the launch traced here: 73.9 us
  waiting for transfers between devices  34.8 us (47%)
  starting transfers between devices  23.5 us (32%)
  Pallas kernels  12.7 us (17%)
  local copies, waits for them, and re-layouts  1.15 us (2%)
  between operations  0.85 us (1%)
  other arithmetic  0.82 us (1%)
    ppermute x4, waiting for transfers between devices, body(): lax.ppermute(probe_grad, ('depth', 'scan'), [(i, i ^ 1 << level) for i in...  23.3 us
    pallas_call x10, Pallas kernels, call(): pl.pallas_call(kernel, name=name, out_shape=outs, in_specs=[pl.BlockSpec(...  12.7 us
    ppermute x4, starting transfers between devices, body(): lax.ppermute(probe_grad, ('depth', 'scan'), [(i, i ^ 1 << level) for i in...  8.44 us
    ppermute x3, starting transfers between devices, across(): return lax.ppermute(x, ('depth', 'scan'), route)  6.83 us
    ppermute x1, waiting for transfers between devices, body(): lax.ppermute(halo, 'scan', [((i + 1) % scan_count, i) for i in range(scan...  4.57 us
    ppermute x1, waiting for transfers between devices, body(): lax.ppermute(offsets, 'scan', [(i, (i + 1) % scan_count) for i in range(s...  3.67 us
    ppermute x2, starting transfers between devices, gathered(): lax.ppermute(x, 'depth', [((target - j) % depth_count, target)])  2.59 us
    ppermute x1, waiting for transfers between devices, body(): probe_grad = probe_grad + lax.ppermute(probe_grad, 'depth', [(1, 0)])  1.94 us
  transfers between devices with their start and end apart: 14, of which 8 were waited for; matrix products, arithmetic and copies ran while one was open for 1% of the time, Pallas kernels for 6%

profile of v6, /device:TPU:0, one launch (start us, length us, event | category | flops | bytes accessed | tf_op | source)
XLA Modules:
  0.0 73.9 jit_solution(8976787891704194387)
XLA Ops:
  0.6 4.8 %collective-permute-start.1 = (f32[2,128,128]{2,1,0:T(8,128)}, f32[2,128,128]{2,1,0:T(8,128)S(1)}, u32[]{:S(2)}, u32[]{:S(2)}) collective-permute-start(f32[2,128,128]{2,1,0:T(8,128)} %intensity.1), channel_id=1, source_target_pairs={{0,1},{1,2},{2,3},{3,4},{4,5},{5,6},{6,7},{7,8},{8,9},{9,10},{10,1... | collective-permute-start | bytes 393224 | tf_op jit(solution)/shard_map/ppermute | solution.py:256
  5.5 0.7 %pad_add_fusion.offsets.refs_0_ = s32[4]{0:T(128)S(1)} fusion(s32[2]{0:T(128)} %param.9, s32[2]{0:T(128)} %param.8), kind=kLoop, calls=%fused_computation.1 | loop fusion | flops 4 | bytes 32 | tf_op jit(solution)/shard_map/concatenate | solution.py:258
  6.2 1.5 %collective-permute-start = (s32[4]{0:T(128)S(1)}, s32[4]{0:T(128)S(1)}, u32[]{:S(2)}, u32[]{:S(2)}) collective-permute-start(s32[4]{0:T(128)S(1)} %pad_add_fusion.offsets.refs_0_), channel_id=1, source_target_pairs={{0,1},{1,2},{2,3},{3,4},{4,5},{5,6},{6,7},{7,8},{8,9},{9,10},{10,1... | collective-permute-start | bytes 56 | tf_op jit(solution)/shard_map/ppermute | solution.py:259
  7.7 0.0 copy-start
  7.7 1.1 %copy-done = f32[3,2,128,256]{3,2,1,0:T(8,128)S(1)} copy-done((f32[3,2,128,256]{3,2,1,0:T(8,128)S(1)}, f32[3,2,128,256]{3,2,1,0:T(8,128)}, u32[]{:S(2)}) %copy-start) | copy-done | bytes 786456
  8.9 0.8 %own.1 = (f32[3,2,128,256]{3,2,1,0:T(8,128)S(1)}, f32[3,2,128,128]{3,2,1,0:T(8,128)S(1)}) custom-call(s32[4]{0:T(128)S(1)} %pad_add_fusion.offsets.refs_0_, f32[3,2,128,256]{3,2,1,0:T(8,128)S(1)} %copy-done), custom_call_target="tpu_custom_call" | custom-call | flops 1000000000 | bytes 1966080 | tf_op jit(solution)/shard_map/own/pallas_call | solution.py:234
  9.7 3.7 %collective-permute-done.offsets_prev.refs_1_.refs_0_ = s32[4]{0:T(128)S(1)} collective-permute-done((s32[4]{0:T(128)S(1)}, s32[4]{0:T(128)S(1)}, u32[]{:S(2)}, u32[]{:S(2)}) %collective-permute-start) | collective-permute-done | bytes 48 | tf_op jit(solution)/shard_map/ppermute | solution.py:259
  13.4 0.0 collective-permute-done.1.far.after
  13.4 0.0 copy-start.1
  13.4 0.0 copy-start.2
  13.4 1.0 %prev.1 = (f32[3,2,128,128]{3,2,1,0:T(8,128)S(1)}, f32[3,2,128,128]{3,2,1,0:T(8,128)S(1)}) custom-call(s32[4]{0:T(128)S(1)} %collective-permute-done.offsets_prev.refs_1_.refs_0_, f32[2,128,128]{2,1,0:T(8,128)S(1)} %collective-permute-done.1.far.after, f32[3,2,128,256]{3,2,1,0:T(8,128)S(1)} %get-tuple-element.17.tiles), custom_call_target="tpu_custom_call" | custom-call | flops 1000000000 | bytes 1572864 | tf_op jit(solution)/shard_map/prev/pallas_call | solution.py:234
  14.4 1.4 %collective-permute-start.2 = (f32[3,2,128,128]{3,2,1,0:T(8,128)S(1)}, f32[3,2,128,128]{3,2,1,0:T(8,128)S(1)}, u32[]{:S(2)}, u32[]{:S(2)}) collective-permute-start(f32[3,2,128,128]{3,2,1,0:T(8,128)S(1)} %get-tuple-element.20), channel_id=1, source_target_pairs={{1,0},{2,1},{3,2},{4,3},{5,4},{6,5},{7,6},{8,7},{9,8},{10,9},{11,1... | collective-permute-start | bytes 1179656 | tf_op jit(solution)/shard_map/ppermute | solution.py:265
  15.8 1.3 %collective-permute-start.3 = (f32[3,2,128,128]{3,2,1,0:T(8,128)S(1)}, f32[3,2,128,128]{3,2,1,0:T(8,128)S(1)}, u32[]{:S(2)}, u32[]{:S(2)}) collective-permute-start(f32[3,2,128,128]{3,2,1,0:T(8,128)S(1)} %get-tuple-element.18.refs_3_), channel_id=1, source_target_pairs={{16,0},{17,1},{18,2},{19,3},{20,4},{21,5},{22,6},{23,7},{24,8},{25... | collective-permute-start | bytes 1179656 | tf_op jit(solution)/shard_map/ppermute | solution.py:268
  17.1 0.0 copy-done.1
  17.1 0.0 copy-done.2
  17.1 0.6 load.1
  17.7 4.6 %collective-permute-done.2.halo = f32[3,2,128,128]{3,2,1,0:T(8,128)S(1)} collective-permute-done((f32[3,2,128,128]{3,2,1,0:T(8,128)S(1)}, f32[3,2,128,128]{3,2,1,0:T(8,128)S(1)}, u32[]{:S(2)}, u32[]{:S(2)}) %collective-permute-start.2) | collective-permute-done | bytes 393248 | tf_op jit(solution)/shard_map/ppermute | solution.py:265
  22.2 0.0 copy-start.3
  22.2 0.6 join.1.refs_4_
  22.9 1.3 %collective-permute-start.4 = (f32[3,2,128,128]{3,2,1,0:T(8,128)S(1)}, f32[3,2,128,128]{3,2,1,0:T(8,128)S(1)}, u32[]{:S(2)}, u32[]{:S(2)}) collective-permute-start(f32[3,2,128,128]{3,2,1,0:T(8,128)S(1)} %join.1.refs_4_), channel_id=1, source_target_pairs={{0,16},{1,17},{2,18},{3,19},{4,20},{5,21},{6,22},{7,23},{8,24},{9,... | collective-permute-start | bytes 1179656 | tf_op jit(solution)/shard_map/ppermute | solution.py:268
  24.2 0.0 collective-permute-done.3.refs_5_
  24.2 1.3 %collective-permute-done.4.refs_6_ = f32[3,2,128,128]{3,2,1,0:T(8,128)S(1)} collective-permute-done((f32[3,2,128,128]{3,2,1,0:T(8,128)S(1)}, f32[3,2,128,128]{3,2,1,0:T(8,128)S(1)}, u32[]{:S(2)}, u32[]{:S(2)}) %collective-permute-start.4) | collective-permute-done | bytes 393248 | tf_op jit(solution)/shard_map/ppermute | solution.py:268
  25.5 0.0 copy-done.3
  25.5 5.8 %wave.1 = (f32[3,2,128,128]{3,2,1,0:T(8,128)S(1)}, f32[3,2,128,128]{3,2,1,0:T(8,128)S(1)}, f32[2,2,64,128]{3,2,1,0:T(8,128)S(1)}) custom-call(bf16[4,2,256,256]{3,2,1,0:T(8,128)(2,1)S(1)} %copy-done.3, f32[2,128,128]{2,1,0:T(8,128)S(1)} %get-tuple-element.15.refs_1_, f32[128,128]{1,0:T(8,128)S(1)} %get-tuple-element.16.after.refs_2_, ...), custom_call_target="tpu_custom_call" | custom-call | flops 5000000000 | bytes 3735552 | tf_op jit(solution)/shard_map/wave/pallas_call | solution.py:234
  31.3 1.3 %collective-permute-start.5 = (f32[2,2,64,128]{3,2,1,0:T(8,128)S(1)}, f32[2,2,64,128]{3,2,1,0:T(8,128)S(1)}, u32[]{:S(2)}, u32[]{:S(2)}) collective-permute-start(f32[2,2,64,128]{3,2,1,0:T(8,128)S(1)} %get-tuple-element.21), channel_id=1, source_target_pairs={{16,0},{17,1},{18,2},{19,3},{20,4},{21,5},{22,6},{23,7},{24,8},{25... | collective-permute-start | bytes 393224 | tf_op jit(solution)/shard_map/ppermute | solution.py:295
  32.6 1.9 %collective-permute-done.5 = f32[2,2,64,128]{3,2,1,0:T(8,128)S(1)} collective-permute-done((f32[2,2,64,128]{3,2,1,0:T(8,128)S(1)}, f32[2,2,64,128]{3,2,1,0:T(8,128)S(1)}, u32[]{:S(2)}, u32[]{:S(2)}) %collective-permute-start.5) | collective-permute-done | bytes 131104 | tf_op jit(solution)/shard_map/ppermute | solution.py:295
  34.6 0.7 turn.1
  35.3 0.2 collective-permute-start.6
  35.5 1.9 %collective-permute-start.9 = (f32[2,2,64,128]{3,2,1,0:T(8,128)S(1)}, f32[2,2,64,128]{3,2,1,0:T(8,128)S(1)}, u32[]{:S(2)}, u32[]{:S(2)}) collective-permute-start(f32[2,2,64,128]{3,2,1,0:T(8,128)S(1)} %add.13.after), channel_id=1, source_target_pairs={{0,4},{1,5},{2,6},{3,7},{4,0},{5,1},{6,2},{7,3},{8,12},{9,13},{10,... | collective-permute-start | bytes 393224 | tf_op jit(solution)/shard_map/ppermute | solution.py:314
  37.4 4.9 %collective-permute-done.9 = f32[2,2,64,128]{3,2,1,0:T(8,128)S(1)} collective-permute-done((f32[2,2,64,128]{3,2,1,0:T(8,128)S(1)}, f32[2,2,64,128]{3,2,1,0:T(8,128)S(1)}, u32[]{:S(2)}, u32[]{:S(2)}) %collective-permute-start.9) | collective-permute-done | bytes 131104 | tf_op jit(solution)/shard_map/ppermute | solution.py:314
  42.4 2.7 %collective-permute-start.10 = (f32[2,2,64,128]{3,2,1,0:T(8,128)S(1)}, f32[2,2,64,128]{3,2,1,0:T(8,128)S(1)}, u32[]{:S(2)}, u32[]{:S(2)}) collective-permute-start(f32[2,2,64,128]{3,2,1,0:T(8,128)S(1)} %add.14), channel_id=1, source_target_pairs={{0,8},{1,9},{2,10},{3,11},{4,12},{5,13},{6,14},{7,15},{8,0},{9,1},... | collective-permute-start | bytes 393224 | tf_op jit(solution)/shard_map/ppermute | solution.py:314
  45.1 1.3 %collective-permute-start.7 = (f32[3,2,128,128]{3,2,1,0:T(8,128)S(1)}, f32[3,2,128,128]{3,2,1,0:T(8,128)S(1)}, u32[]{:S(2)}, u32[]{:S(2)}) collective-permute-start(f32[3,2,128,128]{3,2,1,0:T(8,128)S(1)} %get-tuple-element.25), channel_id=1, source_target_pairs={{16,1},{17,2},{18,3},{19,4},{20,5},{21,6},{22,7},{23,8},{24,9},{25... | collective-permute-start | bytes 1179656 | tf_op jit(solution)/shard_map/ppermute | solution.py:256
  46.4 0.7 collective-permute-start.8
  47.1 3.9 %collective-permute-done.10 = f32[2,2,64,128]{3,2,1,0:T(8,128)S(1)} collective-permute-done((f32[2,2,64,128]{3,2,1,0:T(8,128)S(1)}, f32[2,2,64,128]{3,2,1,0:T(8,128)S(1)}, u32[]{:S(2)}, u32[]{:S(2)}) %collective-permute-start.10) | collective-permute-done | bytes 131104 | tf_op jit(solution)/shard_map/ppermute | solution.py:314
  51.0 1.9 %collective-permute-start.11 = (f32[2,2,64,128]{3,2,1,0:T(8,128)S(1)}, f32[2,2,64,128]{3,2,1,0:T(8,128)S(1)}, u32[]{:S(2)}, u32[]{:S(2)}) collective-permute-start(f32[2,2,64,128]{3,2,1,0:T(8,128)S(1)} %add.15.a), channel_id=1, source_target_pairs={{0,2},{1,3},{2,0},{3,1},{4,6},{5,7},{6,4},{7,5},{8,10},{9,11},{10,... | collective-permute-start | bytes 393224 | tf_op jit(solution)/shard_map/ppermute | solution.py:314
  52.9 0.0 collective-permute-done.6.refs_3_
  53.0 0.9 %place.1.refs_1_.after = f32[3,2,128,256]{3,2,1,0:T(8,128)S(1)} custom-call(s32[4]{0:T(128)S(1)} %pad_add_fusion.offsets.refs_0_, s32[4]{0:T(128)S(1)} %collective-permute-done.offsets_prev.refs_1_.refs_0_, f32[3,2,128,128]{3,2,1,0:T(8,128)S(1)} %get-tuple-element.24.refs_2_, f32[3,2,128,128]{3,2,1,0:T(8,128)S(1)} %collective-permute-done.6.refs_3_), custom_call_target="tpu_custom_call" | custom-call | flops 2000000000 | bytes 1572864 | tf_op jit(solution)/shard_map/place/pallas_call | solution.py:234
  53.8 9.6 %collective-permute-done.11.b = f32[2,2,64,128]{3,2,1,0:T(8,128)S(1)} collective-permute-done((f32[2,2,64,128]{3,2,1,0:T(8,128)S(1)}, f32[2,2,64,128]{3,2,1,0:T(8,128)S(1)}, u32[]{:S(2)}, u32[]{:S(2)}) %collective-permute-start.11) | collective-permute-done | bytes 131104 | tf_op jit(solution)/shard_map/ppermute | solution.py:314
  63.4 1.9 %collective-permute-start.12 = (f32[2,2,64,128]{3,2,1,0:T(8,128)S(1)}, f32[2,2,64,128]{3,2,1,0:T(8,128)S(1)}, u32[]{:S(2)}, u32[]{:S(2)}) collective-permute-start(f32[2,2,64,128]{3,2,1,0:T(8,128)S(1)} %add.19), channel_id=1, source_target_pairs={{0,1},{1,0},{2,3},{3,2},{4,5},{5,4},{6,7},{7,6},{8,9},{9,8},{10,11... | collective-permute-start | bytes 393224 | tf_op jit(solution)/shard_map/ppermute | solution.py:314
  65.3 4.9 %collective-permute-done.12 = f32[2,2,64,128]{3,2,1,0:T(8,128)S(1)} collective-permute-done((f32[2,2,64,128]{3,2,1,0:T(8,128)S(1)}, f32[2,2,64,128]{3,2,1,0:T(8,128)S(1)}, u32[]{:S(2)}, u32[]{:S(2)}) %collective-permute-start.12) | collective-permute-done | bytes 131104 | tf_op jit(solution)/shard_map/ppermute | solution.py:314
  70.3 1.3 %collective-permute-start.13 = (f32[2,64,128]{2,1,0:T(8,128)S(1)}, f32[2,64,128]{2,1,0:T(8,128)S(1)}, u32[]{:S(2)}, u32[]{:S(2)}) collective-permute-start(f32[2,64,128]{2,1,0:T(8,128)S(1)} %slice_bitcast_fusion), channel_id=1, source_target_pairs={{0,16},{1,17},{2,18},{3,19},{4,20},{5,21},{6,22},{7,23},{8,24},{9,... | collective-permute-start | bytes 196616 | tf_op jit(solution)/shard_map/ppermute | solution.py:328
  71.6 0.0 collective-permute-done.8.refs_3_
  71.6 0.0 collective-permute-done.7.refs_2_
  71.6 1.6 %spill.1 = (f32[3,2,128,256]{3,2,1,0:T(8,128)}, f32[8,128]{1,0:T(8,128)S(1)}) custom-call(s32[4]{0:T(128)S(1)} %collective-permute-done.offsets_prev.refs_1_.refs_0_, f32[3,2,128,256]{3,2,1,0:T(8,128)S(1)} %place.1.refs_1_.after, f32[3,2,128,128]{3,2,1,0:T(8,128)S(1)} %collective-permute-done.7.refs_2_, f32[3,2,128,128]{3,2,1,0:T(8,128)S(1)} %collective-permute-done.8.refs_3_), custom_call_target="tpu_custom_call" | custom-call | flops 1000000000 | bytes 2363392 | tf_op jit(solution)/shard_map/spill/pallas_call | solution.py:234
  73.2 0.0 collective-permute-done.13.refs_0_
  73.2 0.6 keep.1
  (6 shorter events, 0.1 us)
Async XLA Ops:
  0.6 12.7 %collective-permute-start.1 = (f32[2,128,128]{2,1,0:T(8,128)}, f32[2,128,128]{2,1,0:T(8,128)S(1)}, u32[]{:S(2)}, u32[]{:S(2)}) collective-permute-start(f32[2,128,128]{2,1,0:T(8,128)} %intensity.1), channel_id=1, source_target_pairs={{0,1},{1,2},{2,3},{3,4},{4,5},{5,6},{6,7},{7,8},{8,9},{9,10},{10,1... | collective-permute-start | bytes 393224 | tf_op jit(solution)/shard_map/ppermute | solution.py:256
  6.2 7.1 %collective-permute-start = (s32[4]{0:T(128)S(1)}, s32[4]{0:T(128)S(1)}, u32[]{:S(2)}, u32[]{:S(2)}) collective-permute-start(s32[4]{0:T(128)S(1)} %pad_add_fusion.offsets.refs_0_), channel_id=1, source_target_pairs={{0,1},{1,2},{2,3},{3,4},{4,5},{5,6},{6,7},{7,8},{8,9},{9,10},{10,1... | collective-permute-start | bytes 56 | tf_op jit(solution)/shard_map/ppermute | solution.py:259
  7.7 1.1 %copy-start = (f32[3,2,128,256]{3,2,1,0:T(8,128)S(1)}, f32[3,2,128,256]{3,2,1,0:T(8,128)}, u32[]{:S(2)}) copy-start(f32[3,2,128,256]{3,2,1,0:T(8,128)} %objects.1) | copy-start | bytes 2359300
  13.4 3.7 %copy-start.1 = (f32[2,128,128]{2,1,0:T(8,128)S(1)}, f32[2,128,128]{2,1,0:T(8,128)}, u32[]{:S(2)}) copy-start(f32[2,128,128]{2,1,0:T(8,128)} %intensity.1) | copy-start | bytes 393220
  13.4 3.7 %copy-start.2 = (f32[2,128,128]{2,1,0:T(8,128)S(1)}, f32[2,128,128]{2,1,0:T(8,128)}, u32[]{:S(2)}) copy-start(f32[2,128,128]{2,1,0:T(8,128)} %probe.1) | copy-start | bytes 393220
  14.4 7.8 %collective-permute-start.2 = (f32[3,2,128,128]{3,2,1,0:T(8,128)S(1)}, f32[3,2,128,128]{3,2,1,0:T(8,128)S(1)}, u32[]{:S(2)}, u32[]{:S(2)}) collective-permute-start(f32[3,2,128,128]{3,2,1,0:T(8,128)S(1)} %get-tuple-element.20), channel_id=1, source_target_pairs={{1,0},{2,1},{3,2},{4,3},{5,4},{6,5},{7,6},{8,7},{9,8},{10,9},{11,1... | collective-permute-start | bytes 1179656 | tf_op jit(solution)/shard_map/ppermute | solution.py:265
  15.8 8.4 %collective-permute-start.3 = (f32[3,2,128,128]{3,2,1,0:T(8,128)S(1)}, f32[3,2,128,128]{3,2,1,0:T(8,128)S(1)}, u32[]{:S(2)}, u32[]{:S(2)}) collective-permute-start(f32[3,2,128,128]{3,2,1,0:T(8,128)S(1)} %get-tuple-element.18.refs_3_), channel_id=1, source_target_pairs={{16,0},{17,1},{18,2},{19,3},{20,4},{21,5},{22,6},{23,7},{24,8},{25... | collective-permute-start | bytes 1179656 | tf_op jit(solution)/shard_map/ppermute | solution.py:268
  22.2 3.2 %copy-start.3 = (bf16[4,2,256,256]{3,2,1,0:T(8,128)(2,1)S(1)}, bf16[4,2,256,256]{3,2,1,0:T(8,128)(2,1)}, u32[]{:S(2)}) copy-start(bf16[4,2,256,256]{3,2,1,0:T(8,128)(2,1)} %constant.2.clone.refs_0_) | copy-start | bytes 3145732
  22.9 2.6 %collective-permute-start.4 = (f32[3,2,128,128]{3,2,1,0:T(8,128)S(1)}, f32[3,2,128,128]{3,2,1,0:T(8,128)S(1)}, u32[]{:S(2)}, u32[]{:S(2)}) collective-permute-start(f32[3,2,128,128]{3,2,1,0:T(8,128)S(1)} %join.1.refs_4_), channel_id=1, source_target_pairs={{0,16},{1,17},{2,18},{3,19},{4,20},{5,21},{6,22},{7,23},{8,24},{9,... | collective-permute-start | bytes 1179656 | tf_op jit(solution)/shard_map/ppermute | solution.py:268
  31.3 3.2 %collective-permute-start.5 = (f32[2,2,64,128]{3,2,1,0:T(8,128)S(1)}, f32[2,2,64,128]{3,2,1,0:T(8,128)S(1)}, u32[]{:S(2)}, u32[]{:S(2)}) collective-permute-start(f32[2,2,64,128]{3,2,1,0:T(8,128)S(1)} %get-tuple-element.21), channel_id=1, source_target_pairs={{16,0},{17,1},{18,2},{19,3},{20,4},{21,5},{22,6},{23,7},{24,8},{25... | collective-permute-start | bytes 393224 | tf_op jit(solution)/shard_map/ppermute | solution.py:295
  35.3 17.6 %collective-permute-start.6 = (f32[3,2,128,128]{3,2,1,0:T(8,128)S(1)}, f32[3,2,128,128]{3,2,1,0:T(8,128)S(1)}, u32[]{:S(2)}, u32[]{:S(2)}) collective-permute-start(f32[3,2,128,128]{3,2,1,0:T(8,128)S(1)} %get-tuple-element.25), channel_id=1, source_target_pairs={{0,16},{16,0},{1,17},{17,1},{2,18},{18,2},{3,19},{19,3},{4,20},{20... | collective-permute-start | bytes 1179656 | tf_op jit(solution)/shard_map/ppermute | solution.py:301
  35.5 6.8 %collective-permute-start.9 = (f32[2,2,64,128]{3,2,1,0:T(8,128)S(1)}, f32[2,2,64,128]{3,2,1,0:T(8,128)S(1)}, u32[]{:S(2)}, u32[]{:S(2)}) collective-permute-start(f32[2,2,64,128]{3,2,1,0:T(8,128)S(1)} %add.13.after), channel_id=1, source_target_pairs={{0,4},{1,5},{2,6},{3,7},{4,0},{5,1},{6,2},{7,3},{8,12},{9,13},{10,... | collective-permute-start | bytes 393224 | tf_op jit(solution)/shard_map/ppermute | solution.py:314
  42.4 8.6 %collective-permute-start.10 = (f32[2,2,64,128]{3,2,1,0:T(8,128)S(1)}, f32[2,2,64,128]{3,2,1,0:T(8,128)S(1)}, u32[]{:S(2)}, u32[]{:S(2)}) collective-permute-start(f32[2,2,64,128]{3,2,1,0:T(8,128)S(1)} %add.14), channel_id=1, source_target_pairs={{0,8},{1,9},{2,10},{3,11},{4,12},{5,13},{6,14},{7,15},{8,0},{9,1},... | collective-permute-start | bytes 393224 | tf_op jit(solution)/shard_map/ppermute | solution.py:314
  45.1 26.5 %collective-permute-start.7 = (f32[3,2,128,128]{3,2,1,0:T(8,128)S(1)}, f32[3,2,128,128]{3,2,1,0:T(8,128)S(1)}, u32[]{:S(2)}, u32[]{:S(2)}) collective-permute-start(f32[3,2,128,128]{3,2,1,0:T(8,128)S(1)} %get-tuple-element.25), channel_id=1, source_target_pairs={{16,1},{17,2},{18,3},{19,4},{20,5},{21,6},{22,7},{23,8},{24,9},{25... | collective-permute-start | bytes 1179656 | tf_op jit(solution)/shard_map/ppermute | solution.py:256
  46.4 25.2 %collective-permute-start.8 = (f32[3,2,128,128]{3,2,1,0:T(8,128)S(1)}, f32[3,2,128,128]{3,2,1,0:T(8,128)S(1)}, u32[]{:S(2)}, u32[]{:S(2)}) collective-permute-start(f32[3,2,128,128]{3,2,1,0:T(8,128)S(1)} %get-tuple-element.24.refs_2_), channel_id=1, source_target_pairs={{16,17},{17,18},{18,19},{19,20},{20,21},{21,22},{22,23},{23,24},{2... | collective-permute-start | bytes 1179656 | tf_op jit(solution)/shard_map/ppermute | solution.py:256
  51.0 12.4 %collective-permute-start.11 = (f32[2,2,64,128]{3,2,1,0:T(8,128)S(1)}, f32[2,2,64,128]{3,2,1,0:T(8,128)S(1)}, u32[]{:S(2)}, u32[]{:S(2)}) collective-permute-start(f32[2,2,64,128]{3,2,1,0:T(8,128)S(1)} %add.15.a), channel_id=1, source_target_pairs={{0,2},{1,3},{2,0},{3,1},{4,6},{5,7},{6,4},{7,5},{8,10},{9,11},{10,... | collective-permute-start | bytes 393224 | tf_op jit(solution)/shard_map/ppermute | solution.py:314
  63.4 6.9 %collective-permute-start.12 = (f32[2,2,64,128]{3,2,1,0:T(8,128)S(1)}, f32[2,2,64,128]{3,2,1,0:T(8,128)S(1)}, u32[]{:S(2)}, u32[]{:S(2)}) collective-permute-start(f32[2,2,64,128]{3,2,1,0:T(8,128)S(1)} %add.19), channel_id=1, source_target_pairs={{0,1},{1,0},{2,3},{3,2},{4,5},{5,4},{6,7},{7,6},{8,9},{9,8},{10,11... | collective-permute-start | bytes 393224 | tf_op jit(solution)/shard_map/ppermute | solution.py:314
  70.3 2.9 %collective-permute-start.13 = (f32[2,64,128]{2,1,0:T(8,128)S(1)}, f32[2,64,128]{2,1,0:T(8,128)S(1)}, u32[]{:S(2)}, u32[]{:S(2)}) collective-permute-start(f32[2,64,128]{2,1,0:T(8,128)S(1)} %slice_bitcast_fusion), channel_id=1, source_target_pairs={{0,16},{1,17},{2,18},{3,19},{4,20},{5,21},{6,22},{7,23},{8,24},{9,... | collective-permute-start | bytes 196616 | tf_op jit(solution)/shard_map/ppermute | solution.py:328

commit v7 on v6

--- a/solution.py
+++ b/solution.py
@@ -108,10 +108,11 @@
     start[...] = probe[...]
 
 
-def wave_kernel(depth_count, tables, probe, measured, window_a, window_b, *rest):
+def wave_kernel(depth_count, offsets, tables, probe, measured, window_a, window_b, *rest):
     others_a, others_b = rest[: depth_count - 1], rest[depth_count - 1 : 2 * depth_count - 2]
     rest = rest[2 * depth_count - 2 :]
-    grads, (probe_grad, layers, waves) = rest[:depth_count], rest[depth_count:]
+    grads, probe_parts = rest[:depth_count], rest[depth_count : 2 * depth_count]
+    layers, waves = rest[2 * depth_count :]
     slab = window_a.shape[0]
     n = probe.shape[-1]
     count = slab * depth_count
@@ -150,26 +151,20 @@
 
     chi = lax.fori_loop(0, count - 1, backward, chi, unroll=True if count <= 8 else 1)
     grad = leave(0, *chi)
+    _, _, row_b, _ = share(offsets, n, 0)
+    turn = lax.rem(jnp.where(on_a, 0, row_b), n)
     for j in range(depth_count):
         base = lax.rem(depth + j, depth_count) * slab
         for s in range(slab):
-            grads[j][s] = waves[base + s]
+            for p in range(2):
+                grads[j][s, p] = pltpu.roll(waves[base + s, p], turn, 0)
     rows = n // depth_count
-    for k in range(depth_count):
-        for p in range(2):
-            probe_grad[k, p] = grad[p][k * rows : (k + 1) * rows]
-
-
-def turn_kernel(offsets, after, *refs):
-    on_a = lax.axis_index("depth") == 0
-    count = len(refs) // 2
-    for x, out in zip(refs[:count], refs[count:]):
-        slab, _, rows, _ = x.shape
-        _, _, row_b, _ = share(offsets, rows, 0)
-        shift = lax.rem(jnp.where(on_a, 0, row_b), rows)
-        for s in range(slab):
-            for p in range(2):
-                out[s, p] = pltpu.roll(x[s, p], shift, 0)
+    waves[0, 0] = jnp.where(depth < 2, grad[0], 0.0)
+    waves[0, 1] = jnp.where(depth < 2, grad[1], 0.0)
+    for j in range(depth_count):
+        start = pl.multiple_of(lax.rem(depth + j, depth_count) * rows, rows)
+        for p in range(2):
+            probe_parts[j][p] = waves[0, p, pl.ds(start, rows), :]
 
 
 def placed(x, col, mask, cols):
@@ -200,32 +195,29 @@
             out[s, p] = total
 
 
-def keep_kernel(after, blocks, *refs):
-    *sent, out = refs
-    depth = lax.axis_index("depth")
-    x = blocks[0]
-    for k, block in enumerate(sent):
-        x = jnp.where(depth == k + 1, block[...], x)
-    out[...] = x
-
-
-def spill_kernel(depth_count, offsets_prev, before, *refs):
+def step_kernel(depth_count, later, slices, *refs):
+    a, b, *parts = refs[later:-2] if slices else refs[later:-1]
+    total = refs[-2] if slices else refs[-1]
+    total[...] = a[...] + b[...]
+    place = lax.rem(lax.axis_index("depth") + depth_count - 1, depth_count)
+    for j, part in enumerate(parts):
+
+        @pl.when(place == j)
+        def _():
+            for i, s in enumerate(slices):
+                refs[-1][i] = part[s]
+
+
+def spill_kernel(offsets_prev, before, *refs):
     *spills, out, token = refs
     slab, _, rows, cols = out.shape
-    depth = lax.axis_index("depth")
     _, _, row_p, col_p = share(offsets_prev, rows, 1)
     mask = lax.broadcasted_iota(jnp.int32, (rows, spills[0].shape[-1]), 0) < row_p
-    for s in range(slab):
-        for p in range(2):
-            x = spills[0][s, p]
-            for q in range(1, depth_count):
-                x = jnp.where(depth == q, spills[q][s, p], x)
-            out[s, p] = before[s, p] + placed(x, col_p, mask, cols)
+    came = [(spill, i) for spill in spills for i in range(spill.shape[0])]
+    for s in range(slab):
+        for p in range(2):
+            out[s, p] = before[s, p] + placed(came[s][0][came[s][1], p], col_p, mask, cols)
     token[...] = jnp.zeros_like(token)
-
-
-def add_kernel(after, a, b, out):
-    out[...] = a[...] + b[...]
 
 
 def call(kernel, name, scalars, arrays, outs, scratch=(), work=10**9, after=()):
@@ -245,6 +237,16 @@
     )(*scalars, *after, *arrays)
 
 
+def sum_round(x, level):
+    depth_count, scan_count = lax.axis_size("depth"), lax.axis_size("scan")
+    levels = scan_count.bit_length() - 1
+    route = []
+    for d in range(depth_count):
+        step = 1 << ((level + (d % 2) * (levels // 2)) % levels)
+        route += [(d * scan_count + i, d * scan_count + (i ^ step)) for i in range(scan_count)]
+    return lax.ppermute(x, ("depth", "scan"), route)
+
+
 def body(objects, probe, row_offsets, col_offsets, intensity):
     slab = objects.shape[0]
     n = probe.shape[-1]
@@ -281,24 +283,39 @@
 
     tables = jnp.asarray(constant_tables(n))
     count = slab * depth_count
-    blocks = jax.ShapeDtypeStruct((depth_count, 2, n // depth_count, n), f32)
-    *grads, probe_grad = call(
+    parts = call(
         lambda *refs: wave_kernel(depth_count, *refs),
         "wave",
-        [],
+        [offsets],
         [tables, start, measured, window_a, window_b, *others_a, *others_b],
-        [window] * depth_count + [blocks],
+        [window] * depth_count + [jax.ShapeDtypeStruct((2, n // depth_count, n), f32)] * depth_count,
         [pltpu.VMEM((count, 2, n, n), f32)] * 2,
         work=5 * 10**9,
     )
-
-    probe_grad = probe_grad + lax.ppermute(probe_grad, "depth", [(1, 0)])
-    grads = call(turn_kernel, "turn", [offsets], grads, [window] * depth_count, after=[probe_grad])
-
-    spill = [across(grads[(q - 1) % depth_count], 1, q, 1) for q in range(depth_count)]
-    back = [grads[0]]
+    grads, probe_parts = parts[:depth_count], parts[depth_count:]
+
+    back, sums = [grads[0]], [probe_parts[0]]
     for j in range(1, depth_count):
+        sums.append(lax.ppermute(probe_parts[j], "depth", [(t, (t + j) % depth_count) for t in range(depth_count)]))
         back.append(lax.ppermute(grads[j], "depth", [(t, (t + j) % depth_count) for t in (0, 1)]))
+
+    half = jax.ShapeDtypeStruct(sums[0].shape, f32)
+    ahead = [(i, (i + 1) % scan_count) for i in range(scan_count)]
+    rounds = scan_count.bit_length() - 1
+    paired = scan_count == 1 << rounds and rounds > 2
+    spill = []
+
+    def step(a, b, slices, after):
+        outs = [half, jax.ShapeDtypeStruct((len(slices), 2, n, n), f32)] if slices else [half]
+        return call(
+            lambda *refs: step_kernel(depth_count, len(after), slices, *refs),
+            "step",
+            [],
+            [a, b, *(back if slices else [])],
+            outs,
+            after=after,
+        )
+
     (object_grad,) = call(
         lambda *refs: place_kernel(depth_count, *refs),
         "place",
@@ -307,29 +324,27 @@
         [whole],
         work=2 * 10**9,
     )
-    rounds = scan_count.bit_length() - 1
-    if scan_count == 1 << rounds:
-        order = [*range(rounds // 2, rounds), *reversed(range(rounds // 2))]
-        for place, level in enumerate(order):
-            last = lax.ppermute(probe_grad, ("depth", "scan"), [(i, i ^ (1 << level)) for i in range(scan_count)])
-            if place == rounds - 2:
-                (probe_grad,) = call(add_kernel, "add", [], [probe_grad, last], [blocks], after=[object_grad])
-            else:
-                probe_grad = probe_grad + last
+    turns = rounds - 1 if paired else 1
+    share_of = [tuple(range(slab * k // turns, slab * (k + 1) // turns)) for k in range(turns)]
+    total = sums[0]
+    for x in sums[1:-1]:
+        total = total + x
+    other = sums[-1] if depth_count > 1 else jnp.zeros_like(total)
+    for k, slices in enumerate(share_of):
+        total, *payload = step(total, other, slices, spill[k - 2 : k - 1] if k >= 2 else [])
+        other = sum_round(total, k) if paired else jnp.zeros_like(total)
+        spill += [lax.ppermute(x, "scan", ahead) for x in payload]
+    if paired:
+        (total,) = step(total, other, (), [*spill[:-1][-1:], object_grad])
+        other = sum_round(total, rounds - 1)
+    object_grad, token = call(
+        spill_kernel, "spill", [offsets_prev], [object_grad, *spill], [whole, jax.ShapeDtypeStruct((8, n), f32)]
+    )
+    if paired:
+        (total,) = step(total, other, (), [token])
     else:
-        probe_grad = lax.psum(probe_grad, "scan")
-    object_grad, token = call(
-        lambda *refs: spill_kernel(depth_count, *refs),
-        "spill",
-        [offsets_prev],
-        [object_grad, *spill],
-        [whole, jax.ShapeDtypeStruct((8, n), f32)],
-    )
-    sent = [lax.ppermute(probe_grad[k], "depth", [(0, k)]) for k in range(1, depth_count)]
-    (probe_grad,) = call(
-        keep_kernel, "keep", [], [probe_grad, *sent], [jax.ShapeDtypeStruct(blocks.shape[1:], f32)], after=[token]
-    )
-    return object_grad, probe_grad
+        total = lax.psum(total, "scan")
+    return object_grad, total
 
 
 def solution(mesh):

time: 74.3 us -> 55.8 us (0.75)
  waiting for transfers between devices: 34.8 us -> 24.4 us
  starting transfers between devices: 23.5 us -> 15.8 us
    ppermute x6 -> x8, waiting for transfers between devices: 25.3 us -> 14.8 us  [the longest x3 9.69 us: body(): spill += [lax.ppermute(x, 'scan', ahead) for x in payload]]
    ppermute x6 -> x8, starting transfers between devices: 11 us -> 5.02 us  [the longest x3 2.99 us: body(): spill += [lax.ppermute(x, 'scan', ahead) for x in payload]]
    ppermute x3 -> x1, starting transfers between devices: 6.83 us -> 4.85 us  [across(): return lax.ppermute(x, ('depth', 'scan'), route)]
    pallas_call x10 -> x12, Pallas kernels: 12.7 us -> 12.7 us  [call(): pl.pallas_call(kernel, name=name, out_shape=outs, in_specs=[pl.BlockSpec(...]
  transfers between devices with their start and end apart: 14 -> 14, of which waited for: 8 -> 10; matrix products, arithmetic and copies ran while one was open for 1% -> 1% of each run, Pallas kernels for 6% -> 8%
where the time goes in v7:
time: 55.8 us; the launch traced here: 55.5 us
  waiting for transfers between devices  24.4 us (44%)
  starting transfers between devices  15.8 us (28%)
  Pallas kernels  12.7 us (23%)
  local copies, waits for them, and re-layouts  1.14 us (2%)
  between operations  0.8 us (1%)
  other arithmetic  0.75 us (1%)
    pallas_call x12, Pallas kernels, call(): pl.pallas_call(kernel, name=name, out_shape=outs, in_specs=[pl.BlockSpec(...  12.7 us
    ppermute x3, waiting for transfers between devices, body(): spill += [lax.ppermute(x, 'scan', ahead) for x in payload]  9.69 us
    ppermute x1, starting transfers between devices, across(): return lax.ppermute(x, ('depth', 'scan'), route)  4.85 us
    ppermute x1, waiting for transfers between devices, body(): lax.ppermute(halo, 'scan', [((i + 1) % scan_count, i) for i in range(scan...  4.57 us
    ppermute x4, waiting for transfers between devices, sum_round(): return lax.ppermute(x, ('depth', 'scan'), route)  3.85 us
    ppermute x1, waiting for transfers between devices, body(): lax.ppermute(offsets, 'scan', [(i, (i + 1) % scan_count) for i in range(s...  3.67 us
    ppermute x3, starting transfers between devices, body(): spill += [lax.ppermute(x, 'scan', ahead) for x in payload]  2.99 us
    ppermute x2, starting transfers between devices, gathered(): lax.ppermute(x, 'depth', [((target - j) % depth_count, target)])  2.59 us
  transfers between devices with their start and end apart: 14, of which 10 were waited for; matrix products, arithmetic and copies ran while one was open for 1% of the time, Pallas kernels for 8%

profile of v7, /device:TPU:0, one launch (start us, length us, event | category | flops | bytes accessed | tf_op | source)
XLA Modules:
  0.0 55.5 jit_solution(11150716380550497137)
XLA Ops:
  0.6 4.8 %collective-permute-start.1 = (f32[2,128,128]{2,1,0:T(8,128)}, f32[2,128,128]{2,1,0:T(8,128)S(1)}, u32[]{:S(2)}, u32[]{:S(2)}) collective-permute-start(f32[2,128,128]{2,1,0:T(8,128)} %intensity.1), channel_id=1, source_target_pairs={{0,1},{1,2},{2,3},{3,4},{4,5},{5,6},{6,7},{7,8},{8,9},{9,10},{10,1... | collective-permute-start | bytes 393224 | tf_op jit(solution)/shard_map/ppermute | solution.py:258
  5.5 0.7 %pad_add_fusion.offsets.refs_0_ = s32[4]{0:T(128)S(1)} fusion(s32[2]{0:T(128)} %param.9, s32[2]{0:T(128)} %param.8), kind=kLoop, calls=%fused_computation | loop fusion | flops 4 | bytes 32 | tf_op jit(solution)/shard_map/concatenate | solution.py:260
  6.2 1.5 %collective-permute-start = (s32[4]{0:T(128)S(1)}, s32[4]{0:T(128)S(1)}, u32[]{:S(2)}, u32[]{:S(2)}) collective-permute-start(s32[4]{0:T(128)S(1)} %pad_add_fusion.offsets.refs_0_), channel_id=1, source_target_pairs={{0,1},{1,2},{2,3},{3,4},{4,5},{5,6},{6,7},{7,8},{8,9},{9,10},{10,1... | collective-permute-start | bytes 56 | tf_op jit(solution)/shard_map/ppermute | solution.py:261
  7.7 0.0 copy-start
  7.7 1.1 %copy-done = f32[3,2,128,256]{3,2,1,0:T(8,128)S(1)} copy-done((f32[3,2,128,256]{3,2,1,0:T(8,128)S(1)}, f32[3,2,128,256]{3,2,1,0:T(8,128)}, u32[]{:S(2)}) %copy-start) | copy-done | bytes 786456
  8.9 0.8 %own.1 = (f32[3,2,128,256]{3,2,1,0:T(8,128)S(1)}, f32[3,2,128,128]{3,2,1,0:T(8,128)S(1)}) custom-call(s32[4]{0:T(128)S(1)} %pad_add_fusion.offsets.refs_0_, f32[3,2,128,256]{3,2,1,0:T(8,128)S(1)} %copy-done), custom_call_target="tpu_custom_call" | custom-call | flops 1000000000 | bytes 1966080 | tf_op jit(solution)/shard_map/own/pallas_call | solution.py:226
  9.7 3.7 %collective-permute-done.offsets_prev.refs_1_ = s32[4]{0:T(128)S(1)} collective-permute-done((s32[4]{0:T(128)S(1)}, s32[4]{0:T(128)S(1)}, u32[]{:S(2)}, u32[]{:S(2)}) %collective-permute-start) | collective-permute-done | bytes 48 | tf_op jit(solution)/shard_map/ppermute | solution.py:261
  13.4 0.0 collective-permute-done.1.far.after
  13.4 0.0 copy-start.1
  13.4 0.0 copy-start.2
  13.4 1.0 %prev.1 = (f32[3,2,128,128]{3,2,1,0:T(8,128)S(1)}, f32[3,2,128,128]{3,2,1,0:T(8,128)S(1)}) custom-call(s32[4]{0:T(128)S(1)} %collective-permute-done.offsets_prev.refs_1_, f32[2,128,128]{2,1,0:T(8,128)S(1)} %collective-permute-done.1.far.after, f32[3,2,128,256]{3,2,1,0:T(8,128)S(1)} %get-tuple-element.22.tiles), custom_call_target="tpu_custom_call" | custom-call | flops 1000000000 | bytes 1572864 | tf_op jit(solution)/shard_map/prev/pallas_call | solution.py:226
  14.4 1.4 %collective-permute-start.2 = (f32[3,2,128,128]{3,2,1,0:T(8,128)S(1)}, f32[3,2,128,128]{3,2,1,0:T(8,128)S(1)}, u32[]{:S(2)}, u32[]{:S(2)}) collective-permute-start(f32[3,2,128,128]{3,2,1,0:T(8,128)S(1)} %get-tuple-element.25), channel_id=1, source_target_pairs={{1,0},{2,1},{3,2},{4,3},{5,4},{6,5},{7,6},{8,7},{9,8},{10,9},{11,1... | collective-permute-start | bytes 1179656 | tf_op jit(solution)/shard_map/ppermute | solution.py:267
  15.8 1.3 %collective-permute-start.3 = (f32[3,2,128,128]{3,2,1,0:T(8,128)S(1)}, f32[3,2,128,128]{3,2,1,0:T(8,128)S(1)}, u32[]{:S(2)}, u32[]{:S(2)}) collective-permute-start(f32[3,2,128,128]{3,2,1,0:T(8,128)S(1)} %get-tuple-element.23.refs_4_), channel_id=1, source_target_pairs={{16,0},{17,1},{18,2},{19,3},{20,4},{21,5},{22,6},{23,7},{24,8},{25... | collective-permute-start | bytes 1179656 | tf_op jit(solution)/shard_map/ppermute | solution.py:270
  17.1 0.0 copy-done.1
  17.1 0.0 copy-done.2
  17.1 0.6 %load.1 = (f32[128,128]{1,0:T(8,128)S(1)}, f32[2,128,128]{2,1,0:T(8,128)S(1)}) custom-call(s32[4]{0:T(128)S(1)} %pad_add_fusion.offsets.refs_0_, s32[4]{0:T(128)S(1)} %collective-permute-done.offsets_prev.refs_1_, f32[2,128,128]{2,1,0:T(8,128)S(1)} %copy-done.1, f32[2,128,128]{2,1,0:T(8,128)S(1)} %collective-permute-done.1.far.after, ...), custom_call_target="tpu_custom_call" | custom-call | flops 1000000000 | bytes 589824 | tf_op jit(solution)/shard_map/load/pallas_call | solution.py:226
  17.7 4.6 %collective-permute-done.2.halo = f32[3,2,128,128]{3,2,1,0:T(8,128)S(1)} collective-permute-done((f32[3,2,128,128]{3,2,1,0:T(8,128)S(1)}, f32[3,2,128,128]{3,2,1,0:T(8,128)S(1)}, u32[]{:S(2)}, u32[]{:S(2)}) %collective-permute-start.2) | collective-permute-done | bytes 393248 | tf_op jit(solution)/shard_map/ppermute | solution.py:267
  22.2 0.0 copy-start.3
  22.2 0.6 %join.1.refs_5_ = f32[3,2,128,128]{3,2,1,0:T(8,128)S(1)} custom-call(s32[4]{0:T(128)S(1)} %pad_add_fusion.offsets.refs_0_, f32[128,128]{1,0:T(8,128)S(1)} %get-tuple-element.21.after.refs_3_, f32[3,2,128,128]{3,2,1,0:T(8,128)S(1)} %get-tuple-element.24.window_b, f32[3,2,128,128]{3,2,1,0:T(8,128)S(1)} %collective-permute-done.2.halo), custom_call_target="tpu_custom_call" | custom-call | flops 1000000000 | bytes 1179648 | tf_op jit(solution)/shard_map/join/pallas_call | solution.py:226
  22.8 1.3 %collective-permute-start.4 = (f32[3,2,128,128]{3,2,1,0:T(8,128)S(1)}, f32[3,2,128,128]{3,2,1,0:T(8,128)S(1)}, u32[]{:S(2)}, u32[]{:S(2)}) collective-permute-start(f32[3,2,128,128]{3,2,1,0:T(8,128)S(1)} %join.1.refs_5_), channel_id=1, source_target_pairs={{0,16},{1,17},{2,18},{3,19},{4,20},{5,21},{6,22},{7,23},{8,24},{9,... | collective-permute-start | bytes 1179656 | tf_op jit(solution)/shard_map/ppermute | solution.py:270
  24.2 0.0 collective-permute-done.3.refs_6_
  24.2 1.3 %collective-permute-done.4.refs_7_ = f32[3,2,128,128]{3,2,1,0:T(8,128)S(1)} collective-permute-done((f32[3,2,128,128]{3,2,1,0:T(8,128)S(1)}, f32[3,2,128,128]{3,2,1,0:T(8,128)S(1)}, u32[]{:S(2)}, u32[]{:S(2)}) %collective-permute-start.4) | collective-permute-done | bytes 393248 | tf_op jit(solution)/shard_map/ppermute | solution.py:270
  25.5 0.0 copy-done.3
  25.5 6.5 %wave.1 = (f32[3,2,128,128]{3,2,1,0:T(8,128)S(1)}, f32[3,2,128,128]{3,2,1,0:T(8,128)S(1)}, f32[2,64,128]{2,1,0:T(8,128)S(1)}, f32[2,64,128]{2,1,0:T(8,128)S(1)}) custom-call(s32[4]{0:T(128)S(1)} %pad_add_fusion.offsets.refs_0_, bf16[4,2,256,256]{3,2,1,0:T(8,128)(2,1)S(1)} %copy-done.3, f32[2,128,128]{2,1,0:T(8,128)S(1)} %get-tuple-element.20.refs_2_, ...), custom_call_target="tpu_custom_call" | custom-call | flops 5000000000 | bytes 3735552 | tf_op jit(solution)/shard_map/wave/pallas_call | solution.py:226
  32.0 0.4 collective-permute-start.5
  32.4 0.1 collective-permute-start.6
  32.5 1.3 %collective-permute-done.6.refs_1_ = f32[2,64,128]{2,1,0:T(8,128)S(1)} collective-permute-done((f32[2,64,128]{2,1,0:T(8,128)S(1)}, f32[2,64,128]{2,1,0:T(8,128)S(1)}, u32[]{:S(2)}, u32[]{:S(2)}) %collective-permute-start.6) | collective-permute-done | bytes 65568 | tf_op jit(solution)/shard_map/ppermute | solution.py:299
  33.8 0.0 collective-permute-done.5.refs_3_.refs_4_
  33.9 0.1 collective-permute-start.8
  34.0 2.0 %collective-permute-start.7 = (f32[1,2,128,128]{3,2,1,0:T(8,128)S(1)}, f32[1,2,128,128]{3,2,1,0:T(8,128)S(1)}, u32[]{:S(2)}, u32[]{:S(2)}) collective-permute-start(f32[1,2,128,128]{3,2,1,0:T(8,128)S(1)} %get-tuple-element.30), channel_id=1, source_target_pairs={{0,1},{1,2},{2,3},{3,4},{4,5},{5,6},{6,7},{7,8},{8,9},{9,10},{10,1... | collective-permute-start | bytes 393224 | tf_op jit(solution)/shard_map/ppermute | solution.py:336
  36.0 2.6 %collective-permute-done.8.refs_1_ = f32[2,64,128]{2,1,0:T(8,128)S(1)} collective-permute-done((f32[2,64,128]{2,1,0:T(8,128)S(1)}, f32[2,64,128]{2,1,0:T(8,128)S(1)}, u32[]{:S(2)}, u32[]{:S(2)}) %collective-permute-start.8) | collective-permute-done | bytes 65568 | tf_op jit(solution)/shard_map/ppermute | solution.py:247
  38.6 0.1 collective-permute-start.10
  38.7 0.9 %collective-permute-start.9 = (f32[1,2,128,128]{3,2,1,0:T(8,128)S(1)}, f32[1,2,128,128]{3,2,1,0:T(8,128)S(1)}, u32[]{:S(2)}, u32[]{:S(2)}) collective-permute-start(f32[1,2,128,128]{3,2,1,0:T(8,128)S(1)} %get-tuple-element.32), channel_id=1, source_target_pairs={{0,1},{1,2},{2,3},{3,4},{4,5},{5,6},{6,7},{7,8},{8,9},{9,10},{10,1... | collective-permute-start | bytes 393224 | tf_op jit(solution)/shard_map/ppermute | solution.py:336
  39.6 4.1 %collective-permute-done.7.refs_0_ = f32[1,2,128,128]{3,2,1,0:T(8,128)S(1)} collective-permute-done((f32[1,2,128,128]{3,2,1,0:T(8,128)S(1)}, f32[1,2,128,128]{3,2,1,0:T(8,128)S(1)}, u32[]{:S(2)}, u32[]{:S(2)}) %collective-permute-start.7) | collective-permute-done | bytes 131104 | tf_op jit(solution)/shard_map/ppermute | solution.py:336
  43.7 0.6 collective-permute-done.10.refs_2_
  44.3 0.1 collective-permute-start.12
  44.4 0.1 collective-permute-start.11
  44.5 0.9 %place.1.before.refs_1_ = f32[3,2,128,256]{3,2,1,0:T(8,128)S(1)} custom-call(s32[4]{0:T(128)S(1)} %pad_add_fusion.offsets.refs_0_, s32[4]{0:T(128)S(1)} %collective-permute-done.offsets_prev.refs_1_, f32[3,2,128,128]{3,2,1,0:T(8,128)S(1)} %get-tuple-element.26.refs_2_.refs_3_, f32[3,2,128,128]{3,2,1,0:T(8,128)S(1)} %collective-permute-done.5.refs_3_.refs_4_), custom_call_target="tpu_custom_call" | custom-call | flops 2000000000 | bytes 1572864 | tf_op jit(solution)/shard_map/place/pallas_call | solution.py:226
  45.4 2.6 %collective-permute-done.9.refs_1_.refs_0_ = f32[1,2,128,128]{3,2,1,0:T(8,128)S(1)} collective-permute-done((f32[1,2,128,128]{3,2,1,0:T(8,128)S(1)}, f32[1,2,128,128]{3,2,1,0:T(8,128)S(1)}, u32[]{:S(2)}, u32[]{:S(2)}) %collective-permute-start.9) | collective-permute-done | bytes 131104 | tf_op jit(solution)/shard_map/ppermute | solution.py:336
  48.0 0.7 %collective-permute-done.12.refs_3_ = f32[2,64,128]{2,1,0:T(8,128)S(1)} collective-permute-done((f32[2,64,128]{2,1,0:T(8,128)S(1)}, f32[2,64,128]{2,1,0:T(8,128)S(1)}, u32[]{:S(2)}, u32[]{:S(2)}) %collective-permute-start.12) | collective-permute-done | bytes 65568 | tf_op jit(solution)/shard_map/ppermute | solution.py:247
  48.7 1.7 %collective-permute-start.13 = (f32[2,64,128]{2,1,0:T(8,128)S(1)}, f32[2,64,128]{2,1,0:T(8,128)S(1)}, u32[]{:S(2)}, u32[]{:S(2)}) collective-permute-start(f32[2,64,128]{2,1,0:T(8,128)S(1)} %step.8.refs_1_), channel_id=1, source_target_pairs={{0,8},{1,9},{2,10},{3,11},{4,12},{5,13},{6,14},{7,15},{8,0},{9,1},... | collective-permute-start | bytes 196616 | tf_op jit(solution)/shard_map/ppermute | solution.py:247
  50.3 2.9 %collective-permute-done.11.refs_2_ = f32[1,2,128,128]{3,2,1,0:T(8,128)S(1)} collective-permute-done((f32[1,2,128,128]{3,2,1,0:T(8,128)S(1)}, f32[1,2,128,128]{3,2,1,0:T(8,128)S(1)}, u32[]{:S(2)}, u32[]{:S(2)}) %collective-permute-start.11) | collective-permute-done | bytes 131104 | tf_op jit(solution)/shard_map/ppermute | solution.py:336
  53.3 1.6 %spill.1 = (f32[3,2,128,256]{3,2,1,0:T(8,128)}, f32[8,128]{1,0:T(8,128)S(1)}) custom-call(s32[4]{0:T(128)S(1)} %collective-permute-done.offsets_prev.refs_1_, f32[3,2,128,256]{3,2,1,0:T(8,128)S(1)} %place.1.before.refs_1_, f32[1,2,128,128]{3,2,1,0:T(8,128)S(1)} %collective-permute-done.7.refs_0_, ...), custom_call_target="tpu_custom_call" | custom-call | flops 1000000000 | bytes 1970176 | tf_op jit(solution)/shard_map/spill/pallas_call | solution.py:226
  54.9 0.0 collective-permute-done.13.refs_2_
  54.9 0.6 %step.9 = f32[2,64,128]{2,1,0:T(8,128)} custom-call(f32[8,128]{1,0:T(8,128)S(1)} %get-tuple-element.36.refs_0_, f32[2,64,128]{2,1,0:T(8,128)S(1)} %step.8.refs_1_, f32[2,64,128]{2,1,0:T(8,128)S(1)} %collective-permute-done.13.refs_2_), custom_call_target="tpu_custom_call" | custom-call | flops 1000000000 | bytes 196608 | tf_op jit(solution)/shard_map/step/pallas_call | solution.py:226
  (4 shorter events, 0.1 us)
Async XLA Ops:
  0.6 12.7 %collective-permute-start.1 = (f32[2,128,128]{2,1,0:T(8,128)}, f32[2,128,128]{2,1,0:T(8,128)S(1)}, u32[]{:S(2)}, u32[]{:S(2)}) collective-permute-start(f32[2,128,128]{2,1,0:T(8,128)} %intensity.1), channel_id=1, source_target_pairs={{0,1},{1,2},{2,3},{3,4},{4,5},{5,6},{6,7},{7,8},{8,9},{9,10},{10,1... | collective-permute-start | bytes 393224 | tf_op jit(solution)/shard_map/ppermute | solution.py:258
  6.2 7.1 %collective-permute-start = (s32[4]{0:T(128)S(1)}, s32[4]{0:T(128)S(1)}, u32[]{:S(2)}, u32[]{:S(2)}) collective-permute-start(s32[4]{0:T(128)S(1)} %pad_add_fusion.offsets.refs_0_), channel_id=1, source_target_pairs={{0,1},{1,2},{2,3},{3,4},{4,5},{5,6},{6,7},{7,8},{8,9},{9,10},{10,1... | collective-permute-start | bytes 56 | tf_op jit(solution)/shard_map/ppermute | solution.py:261
  7.7 1.1 %copy-start = (f32[3,2,128,256]{3,2,1,0:T(8,128)S(1)}, f32[3,2,128,256]{3,2,1,0:T(8,128)}, u32[]{:S(2)}) copy-start(f32[3,2,128,256]{3,2,1,0:T(8,128)} %objects.1) | copy-start | bytes 2359300
  13.4 3.7 %copy-start.1 = (f32[2,128,128]{2,1,0:T(8,128)S(1)}, f32[2,128,128]{2,1,0:T(8,128)}, u32[]{:S(2)}) copy-start(f32[2,128,128]{2,1,0:T(8,128)} %intensity.1) | copy-start | bytes 393220
  13.4 3.7 %copy-start.2 = (f32[2,128,128]{2,1,0:T(8,128)S(1)}, f32[2,128,128]{2,1,0:T(8,128)}, u32[]{:S(2)}) copy-start(f32[2,128,128]{2,1,0:T(8,128)} %probe.1) | copy-start | bytes 393220
  14.4 7.8 %collective-permute-start.2 = (f32[3,2,128,128]{3,2,1,0:T(8,128)S(1)}, f32[3,2,128,128]{3,2,1,0:T(8,128)S(1)}, u32[]{:S(2)}, u32[]{:S(2)}) collective-permute-start(f32[3,2,128,128]{3,2,1,0:T(8,128)S(1)} %get-tuple-element.25), channel_id=1, source_target_pairs={{1,0},{2,1},{3,2},{4,3},{5,4},{6,5},{7,6},{8,7},{9,8},{10,9},{11,1... | collective-permute-start | bytes 1179656 | tf_op jit(solution)/shard_map/ppermute | solution.py:267
  15.8 8.4 %collective-permute-start.3 = (f32[3,2,128,128]{3,2,1,0:T(8,128)S(1)}, f32[3,2,128,128]{3,2,1,0:T(8,128)S(1)}, u32[]{:S(2)}, u32[]{:S(2)}) collective-permute-start(f32[3,2,128,128]{3,2,1,0:T(8,128)S(1)} %get-tuple-element.23.refs_4_), channel_id=1, source_target_pairs={{16,0},{17,1},{18,2},{19,3},{20,4},{21,5},{22,6},{23,7},{24,8},{25... | collective-permute-start | bytes 1179656 | tf_op jit(solution)/shard_map/ppermute | solution.py:270
  22.2 3.2 %copy-start.3 = (bf16[4,2,256,256]{3,2,1,0:T(8,128)(2,1)S(1)}, bf16[4,2,256,256]{3,2,1,0:T(8,128)(2,1)}, u32[]{:S(2)}) copy-start(bf16[4,2,256,256]{3,2,1,0:T(8,128)(2,1)} %constant.2.clone.refs_1_) | copy-start | bytes 3145732
  22.8 2.6 %collective-permute-start.4 = (f32[3,2,128,128]{3,2,1,0:T(8,128)S(1)}, f32[3,2,128,128]{3,2,1,0:T(8,128)S(1)}, u32[]{:S(2)}, u32[]{:S(2)}) collective-permute-start(f32[3,2,128,128]{3,2,1,0:T(8,128)S(1)} %join.1.refs_5_), channel_id=1, source_target_pairs={{0,16},{1,17},{2,18},{3,19},{4,20},{5,21},{6,22},{7,23},{8,24},{9,... | collective-permute-start | bytes 1179656 | tf_op jit(solution)/shard_map/ppermute | solution.py:270
  32.0 1.9 %collective-permute-start.5 = (f32[3,2,128,128]{3,2,1,0:T(8,128)S(1)}, f32[3,2,128,128]{3,2,1,0:T(8,128)S(1)}, u32[]{:S(2)}, u32[]{:S(2)}) collective-permute-start(f32[3,2,128,128]{3,2,1,0:T(8,128)S(1)} %get-tuple-element.27), channel_id=1, source_target_pairs={{0,16},{16,0},{1,17},{17,1},{2,18},{18,2},{3,19},{19,3},{4,20},{20... | collective-permute-start | bytes 1179656 | tf_op jit(solution)/shard_map/ppermute | solution.py:300
  32.4 1.4 %collective-permute-start.6 = (f32[2,64,128]{2,1,0:T(8,128)S(1)}, f32[2,64,128]{2,1,0:T(8,128)S(1)}, u32[]{:S(2)}, u32[]{:S(2)}) collective-permute-start(f32[2,64,128]{2,1,0:T(8,128)S(1)} %get-tuple-element.29), channel_id=1, source_target_pairs={{0,16},{16,0},{1,17},{17,1},{2,18},{18,2},{3,19},{19,3},{4,20},{20... | collective-permute-start | bytes 196616 | tf_op jit(solution)/shard_map/ppermute | solution.py:299
  33.9 4.7 %collective-permute-start.8 = (f32[2,64,128]{2,1,0:T(8,128)S(1)}, f32[2,64,128]{2,1,0:T(8,128)S(1)}, u32[]{:S(2)}, u32[]{:S(2)}) collective-permute-start(f32[2,64,128]{2,1,0:T(8,128)S(1)} %get-tuple-element.31.refs_0_), channel_id=1, source_target_pairs={{0,1},{1,0},{2,3},{3,2},{4,5},{5,4},{6,7},{7,6},{8,9},{9,8},{10,11... | collective-permute-start | bytes 196616 | tf_op jit(solution)/shard_map/ppermute | solution.py:247
  34.0 9.8 %collective-permute-start.7 = (f32[1,2,128,128]{3,2,1,0:T(8,128)S(1)}, f32[1,2,128,128]{3,2,1,0:T(8,128)S(1)}, u32[]{:S(2)}, u32[]{:S(2)}) collective-permute-start(f32[1,2,128,128]{3,2,1,0:T(8,128)S(1)} %get-tuple-element.30), channel_id=1, source_target_pairs={{0,1},{1,2},{2,3},{3,4},{4,5},{5,6},{6,7},{7,8},{8,9},{9,10},{10,1... | collective-permute-start | bytes 393224 | tf_op jit(solution)/shard_map/ppermute | solution.py:336
  38.6 5.7 %collective-permute-start.10 = (f32[2,64,128]{2,1,0:T(8,128)S(1)}, f32[2,64,128]{2,1,0:T(8,128)S(1)}, u32[]{:S(2)}, u32[]{:S(2)}) collective-permute-start(f32[2,64,128]{2,1,0:T(8,128)S(1)} %get-tuple-element.33.refs_1_), channel_id=1, source_target_pairs={{0,2},{1,3},{2,0},{3,1},{4,6},{5,7},{6,4},{7,5},{8,10},{9,11},{10,... | collective-permute-start | bytes 196616 | tf_op jit(solution)/shard_map/ppermute | solution.py:247
  38.7 9.3 %collective-permute-start.9 = (f32[1,2,128,128]{3,2,1,0:T(8,128)S(1)}, f32[1,2,128,128]{3,2,1,0:T(8,128)S(1)}, u32[]{:S(2)}, u32[]{:S(2)}) collective-permute-start(f32[1,2,128,128]{3,2,1,0:T(8,128)S(1)} %get-tuple-element.32), channel_id=1, source_target_pairs={{0,1},{1,2},{2,3},{3,4},{4,5},{5,6},{6,7},{7,8},{8,9},{9,10},{10,1... | collective-permute-start | bytes 393224 | tf_op jit(solution)/shard_map/ppermute | solution.py:336
  44.3 4.3 %collective-permute-start.12 = (f32[2,64,128]{2,1,0:T(8,128)S(1)}, f32[2,64,128]{2,1,0:T(8,128)S(1)}, u32[]{:S(2)}, u32[]{:S(2)}) collective-permute-start(f32[2,64,128]{2,1,0:T(8,128)S(1)} %get-tuple-element.37.refs_2_), channel_id=1, source_target_pairs={{0,4},{1,5},{2,6},{3,7},{4,0},{5,1},{6,2},{7,3},{8,12},{9,13},{10,... | collective-permute-start | bytes 196616 | tf_op jit(solution)/shard_map/ppermute | solution.py:247
  44.4 8.9 %collective-permute-start.11 = (f32[1,2,128,128]{3,2,1,0:T(8,128)S(1)}, f32[1,2,128,128]{3,2,1,0:T(8,128)S(1)}, u32[]{:S(2)}, u32[]{:S(2)}) collective-permute-start(f32[1,2,128,128]{3,2,1,0:T(8,128)S(1)} %get-tuple-element.34), channel_id=1, source_target_pairs={{0,1},{1,2},{2,3},{3,4},{4,5},{5,6},{6,7},{7,8},{8,9},{9,10},{10,1... | collective-permute-start | bytes 393224 | tf_op jit(solution)/shard_map/ppermute | solution.py:336
  48.7 6.2 %collective-permute-start.13 = (f32[2,64,128]{2,1,0:T(8,128)S(1)}, f32[2,64,128]{2,1,0:T(8,128)S(1)}, u32[]{:S(2)}, u32[]{:S(2)}) collective-permute-start(f32[2,64,128]{2,1,0:T(8,128)S(1)} %step.8.refs_1_), channel_id=1, source_target_pairs={{0,8},{1,9},{2,10},{3,11},{4,12},{5,13},{6,14},{7,15},{8,0},{9,1},... | collective-permute-start | bytes 196616 | tf_op jit(solution)/shard_map/ppermute | solution.py:247

commit v8 on v7

--- a/solution.py
+++ b/solution.py
@@ -81,7 +81,7 @@
             window_b[s, p] = cut(tile, row_b, col_b, window_b.shape[-1])
 
 
-def prev_kernel(offsets_prev, after, tiles, window_a, halo):
+def prev_kernel(offsets_prev, tiles, window_a, halo):
     slab, _, rows, _ = tiles.shape
     width = halo.shape[-1]
     _, col_a, row_p, col_p = share(offsets_prev, rows, 1)
@@ -100,15 +100,14 @@
             joined[s, p] = jnp.where(inside, window_b[s, p], halo[s, p])
 
 
-def load_kernel(offsets, offsets_prev, intensity, far, probe, measured, start):
-    rows = probe.shape[-1]
-    near_a, _, _, _ = share(offsets, rows, 0)
-    far_a, _, _, _ = share(offsets_prev, rows, 1)
-    measured[...] = jnp.where(lax.axis_index("depth") == 0, far[far_a], intensity[1 - near_a])
+def load_kernel(offsets, after, intensity, probe, passed, near, start):
+    a, _, _, _ = share(offsets, probe.shape[-1], 0)
+    passed[...] = intensity[a]
+    near[...] = intensity[1 - a]
     start[...] = probe[...]
 
 
-def wave_kernel(depth_count, offsets, tables, probe, measured, window_a, window_b, *rest):
+def wave_kernel(depth_count, offsets, tables, probe, near, far, window_a, window_b, *rest):
     others_a, others_b = rest[: depth_count - 1], rest[depth_count - 1 : 2 * depth_count - 2]
     rest = rest[2 * depth_count - 2 :]
     grads, probe_parts = rest[:depth_count], rest[depth_count : 2 * depth_count]
@@ -136,7 +135,8 @@
 
     wave = lax.fori_loop(0, count - 1, forward, (probe[0], probe[1]), unroll=True if count <= 8 else 1)
     far_re, far_im = both_sides(*enter(count - 1, *wave), tables, 2)
-    misfit = 2.0 * (far_re * far_re + far_im * far_im - measured[...])
+    measured = jnp.where(on_a, far[...], near[...])
+    misfit = 2.0 * (far_re * far_re + far_im * far_im - measured)
     chi = both_sides(misfit * far_re, misfit * far_im, tables, 3)
 
     def leave(s, chi_re, chi_im):
@@ -259,26 +259,27 @@
 
     offsets = jnp.concatenate([row_offsets, col_offsets])
     offsets_prev = lax.ppermute(offsets, "scan", [(i, (i + 1) % scan_count) for i in range(scan_count)])
-    far = across(intensity, 0, 0, 1)
     window = jax.ShapeDtypeStruct((slab, 2, n, n), f32)
     whole = jax.ShapeDtypeStruct(objects.shape, f32)
     tiles, window_b = call(own_kernel, "own", [offsets], [objects], [whole, window])
-    window_a, halo = call(prev_kernel, "prev", [offsets_prev], [tiles], [window] * 2, after=[far])
+    window_a, halo = call(prev_kernel, "prev", [offsets_prev], [tiles], [window] * 2)
     halo = lax.ppermute(halo, "scan", [((i + 1) % scan_count, i) for i in range(scan_count)])
 
     def gathered(x, target):
         return [lax.ppermute(x, "depth", [((target - j) % depth_count, target)]) for j in range(1, depth_count)]
 
     others_a = gathered(window_a, 0)
-    measured, start = call(
+    plane = jax.ShapeDtypeStruct((n, n), f32)
+    passed, near, start = call(
         load_kernel,
         "load",
-        [offsets, offsets_prev],
-        [intensity, far, probe],
-        [jax.ShapeDtypeStruct((n, n), f32), jax.ShapeDtypeStruct(probe.shape, f32)],
+        [offsets],
+        [intensity, probe],
+        [plane, plane, jax.ShapeDtypeStruct(probe.shape, f32)],
+        after=[window_a],
     )
-
-    (window_b,) = call(join_kernel, "join", [offsets], [window_b, halo], [window], after=[measured])
+    far = across(passed, 0, 0, 1)
+    (window_b,) = call(join_kernel, "join", [offsets], [window_b, halo], [window], after=[far])
     others_b = gathered(window_b, 1)
 
     tables = jnp.asarray(constant_tables(n))
@@ -287,7 +288,7 @@
         lambda *refs: wave_kernel(depth_count, *refs),
         "wave",
         [offsets],
-        [tables, start, measured, window_a, window_b, *others_a, *others_b],
+        [tables, start, near, far, window_a, window_b, *others_a, *others_b],
         [window] * depth_count + [jax.ShapeDtypeStruct((2, n // depth_count, n), f32)] * depth_count,
         [pltpu.VMEM((count, 2, n, n), f32)] * 2,
         work=5 * 10**9,

time: 55.8 us -> 56.4 us (1.011)
  waiting for transfers between devices: 24.4 us -> 27.5 us
  starting transfers between devices: 15.8 us -> 13.4 us
    ppermute x1, waiting for transfers between devices: 0.01 us -> 6.53 us  [across(): return lax.ppermute(x, ('depth', 'scan'), route)]
    ppermute x1, waiting for transfers between devices: 4.57 us -> 0.01 us  [body(): lax.ppermute(halo, 'scan', [((i + 1) % scan_count, i) for i in range(scan...]
    ppermute x1, starting transfers between devices: 4.85 us -> 1.92 us  [across(): return lax.ppermute(x, ('depth', 'scan'), route)]
    ppermute x1, starting transfers between devices: 1.49 us -> 2.94 us  [body(): lax.ppermute(offsets, 'scan', [(i, (i + 1) % scan_count) for i in range(s...]
    ppermute x4, starting transfers between devices: 1.88 us -> 0.53 us  [sum_round(): return lax.ppermute(x, ('depth', 'scan'), route)]
    ppermute x3, waiting for transfers between devices: 9.69 us -> 11 us  [body(): spill += [lax.ppermute(x, 'scan', ahead) for x in payload]]
    ppermute x1, starting transfers between devices: 1.38 us -> 2.08 us  [body(): lax.ppermute(halo, 'scan', [((i + 1) % scan_count, i) for i in range(scan...]
  transfers between devices with their start and end apart: 14 -> 14, of which waited for: 10 -> 10; matrix products, arithmetic and copies ran while one was open for 1% -> 0% of each run, Pallas kernels for 8% -> 8%
where the time goes in v8:
time: 56.4 us; the launch traced here: 56.2 us
  waiting for transfers between devices  27.5 us (49%)
  starting transfers between devices  13.4 us (24%)
  Pallas kernels  12.7 us (23%)
  local copies, waits for them, and re-layouts  1.14 us (2%)
  between operations  0.78 us (1%)
  other arithmetic  0.75 us (1%)
    pallas_call x12, Pallas kernels, call(): pl.pallas_call(kernel, name=name, out_shape=outs, in_specs=[pl.BlockSpec(...  12.7 us
    ppermute x3, waiting for transfers between devices, body(): spill += [lax.ppermute(x, 'scan', ahead) for x in payload]  11 us
    ppermute x1, waiting for transfers between devices, across(): return lax.ppermute(x, ('depth', 'scan'), route)  6.53 us
    ppermute x4, waiting for transfers between devices, sum_round(): return lax.ppermute(x, ('depth', 'scan'), route)  3.85 us
    ppermute x1, waiting for transfers between devices, body(): lax.ppermute(offsets, 'scan', [(i, (i + 1) % scan_count) for i in range(s...  3.53 us
    ppermute x1, starting transfers between devices, body(): lax.ppermute(offsets, 'scan', [(i, (i + 1) % scan_count) for i in range(s...  2.94 us
    ppermute x3, starting transfers between devices, body(): spill += [lax.ppermute(x, 'scan', ahead) for x in payload]  2.71 us
    ppermute x2, starting transfers between devices, gathered(): lax.ppermute(x, 'depth', [((target - j) % depth_count, target)])  2.61 us
  transfers between devices with their start and end apart: 14, of which 10 were waited for; matrix products, arithmetic and copies ran while one was open for 0% of the time, Pallas kernels for 8%

profile of v8, /device:TPU:0, one launch (start us, length us, event | category | flops | bytes accessed | tf_op | source)
XLA Modules:
  0.0 56.2 jit_solution(6003535819240835093)
XLA Ops:
  0.6 0.7 %pad_add_fusion.offsets.refs_0_ = s32[4]{0:T(128)S(1)} fusion(s32[2]{0:T(128)} %param.9, s32[2]{0:T(128)} %param.8), kind=kLoop, calls=%fused_computation | loop fusion | flops 4 | bytes 32 | tf_op jit(solution)/shard_map/concatenate | solution.py:260
  1.4 2.9 %collective-permute-start = (s32[4]{0:T(128)S(1)}, s32[4]{0:T(128)S(1)}, u32[]{:S(2)}, u32[]{:S(2)}) collective-permute-start(s32[4]{0:T(128)S(1)} %pad_add_fusion.offsets.refs_0_), channel_id=1, source_target_pairs={{0,1},{1,2},{2,3},{3,4},{4,5},{5,6},{6,7},{7,8},{8,9},{9,10},{10,1... | collective-permute-start | bytes 56 | tf_op jit(solution)/shard_map/ppermute | solution.py:261
  4.3 0.0 copy-start
  4.3 1.1 %copy-done = f32[3,2,128,256]{3,2,1,0:T(8,128)S(1)} copy-done((f32[3,2,128,256]{3,2,1,0:T(8,128)S(1)}, f32[3,2,128,256]{3,2,1,0:T(8,128)}, u32[]{:S(2)}) %copy-start) | copy-done | bytes 786456
  5.5 0.8 %own.1 = (f32[3,2,128,256]{3,2,1,0:T(8,128)S(1)}, f32[3,2,128,128]{3,2,1,0:T(8,128)S(1)}) custom-call(s32[4]{0:T(128)S(1)} %pad_add_fusion.offsets.refs_0_, f32[3,2,128,256]{3,2,1,0:T(8,128)S(1)} %copy-done), custom_call_target="tpu_custom_call" | custom-call | flops 1000000000 | bytes 1966080 | tf_op jit(solution)/shard_map/own/pallas_call | solution.py:226
  6.3 3.5 %collective-permute-done.offsets_prev.refs_1_ = s32[4]{0:T(128)S(1)} collective-permute-done((s32[4]{0:T(128)S(1)}, s32[4]{0:T(128)S(1)}, u32[]{:S(2)}, u32[]{:S(2)}) %collective-permute-start) | collective-permute-done | bytes 48 | tf_op jit(solution)/shard_map/ppermute | solution.py:261
  9.8 0.0 copy-start.1
  9.8 0.0 copy-start.2
  9.8 1.0 %prev.1 = (f32[3,2,128,128]{3,2,1,0:T(8,128)S(1)}, f32[3,2,128,128]{3,2,1,0:T(8,128)S(1)}) custom-call(s32[4]{0:T(128)S(1)} %collective-permute-done.offsets_prev.refs_1_, f32[3,2,128,256]{3,2,1,0:T(8,128)S(1)} %get-tuple-element.21.tiles), custom_call_target="tpu_custom_call" | custom-call | flops 1000000000 | bytes 1572864 | tf_op jit(solution)/shard_map/prev/pallas_call | solution.py:226
  10.9 2.1 %collective-permute-start.2 = (f32[3,2,128,128]{3,2,1,0:T(8,128)S(1)}, f32[3,2,128,128]{3,2,1,0:T(8,128)S(1)}, u32[]{:S(2)}, u32[]{:S(2)}) collective-permute-start(f32[3,2,128,128]{3,2,1,0:T(8,128)S(1)} %get-tuple-element.27), channel_id=1, source_target_pairs={{1,0},{2,1},{3,2},{4,3},{5,4},{6,5},{7,6},{8,7},{9,8},{10,9},{11,1... | collective-permute-start | bytes 1179656 | tf_op jit(solution)/shard_map/ppermute | solution.py:266
  12.9 0.0 copy-done.1
  12.9 0.0 copy-done.2
  12.9 0.6 %load.1 = (f32[128,128]{1,0:T(8,128)S(1)}, f32[128,128]{1,0:T(8,128)S(1)}, f32[2,128,128]{2,1,0:T(8,128)S(1)}) custom-call(s32[4]{0:T(128)S(1)} %pad_add_fusion.offsets.refs_0_, f32[3,2,128,128]{3,2,1,0:T(8,128)S(1)} %get-tuple-element.22.after.refs_5_, f32[2,128,128]{2,1,0:T(8,128)S(1)} %copy-done.1, f32[2,128,128]{2,1,0:T(8,128)S(1)} %copy-done.2), custom_call_target="tpu_custom_call" | custom-call | flops 1000000000 | bytes 524288 | tf_op jit(solution)/shard_map/load/pallas_call | solution.py:226
  13.5 1.9 %collective-permute-start.1 = (f32[128,128]{1,0:T(8,128)S(1)}, f32[128,128]{1,0:T(8,128)S(1)}, u32[]{:S(2)}, u32[]{:S(2)}) collective-permute-start(f32[128,128]{1,0:T(8,128)S(1)} %get-tuple-element.25), channel_id=1, source_target_pairs={{0,1},{1,2},{2,3},{3,4},{4,5},{5,6},{6,7},{7,8},{8,9},{9,10},{10,1... | collective-permute-start | bytes 196616 | tf_op jit(solution)/shard_map/ppermute | solution.py:258
  15.4 1.3 %collective-permute-start.3 = (f32[3,2,128,128]{3,2,1,0:T(8,128)S(1)}, f32[3,2,128,128]{3,2,1,0:T(8,128)S(1)}, u32[]{:S(2)}, u32[]{:S(2)}) collective-permute-start(f32[3,2,128,128]{3,2,1,0:T(8,128)S(1)} %get-tuple-element.22.after.refs_5_), channel_id=1, source_target_pairs={{16,0},{17,1},{18,2},{19,3},{20,4},{21,5},{22,6},{23,7},{24,8},{25... | collective-permute-start | bytes 1179656 | tf_op jit(solution)/shard_map/ppermute | solution.py:269
  16.7 6.5 %collective-permute-done.1.after.refs_4_ = f32[128,128]{1,0:T(8,128)S(1)} collective-permute-done((f32[128,128]{1,0:T(8,128)S(1)}, f32[128,128]{1,0:T(8,128)S(1)}, u32[]{:S(2)}, u32[]{:S(2)}) %collective-permute-start.1) | collective-permute-done | bytes 65568 | tf_op jit(solution)/shard_map/ppermute | solution.py:258
  23.3 0.0 collective-permute-done.2.halo
  23.3 0.0 copy-start.3
  23.3 0.6 %join.1.refs_6_ = f32[3,2,128,128]{3,2,1,0:T(8,128)S(1)} custom-call(s32[4]{0:T(128)S(1)} %pad_add_fusion.offsets.refs_0_, f32[128,128]{1,0:T(8,128)S(1)} %collective-permute-done.1.after.refs_4_, f32[3,2,128,128]{3,2,1,0:T(8,128)S(1)} %get-tuple-element.26.window_b, f32[3,2,128,128]{3,2,1,0:T(8,128)S(1)} %collective-permute-done.2.halo), custom_call_target="tpu_custom_call" | custom-call | flops 1000000000 | bytes 1179648 | tf_op jit(solution)/shard_map/join/pallas_call | solution.py:226
  23.9 1.3 %collective-permute-start.4 = (f32[3,2,128,128]{3,2,1,0:T(8,128)S(1)}, f32[3,2,128,128]{3,2,1,0:T(8,128)S(1)}, u32[]{:S(2)}, u32[]{:S(2)}) collective-permute-start(f32[3,2,128,128]{3,2,1,0:T(8,128)S(1)} %join.1.refs_6_), channel_id=1, source_target_pairs={{0,16},{1,17},{2,18},{3,19},{4,20},{5,21},{6,22},{7,23},{8,24},{9,... | collective-permute-start | bytes 1179656 | tf_op jit(solution)/shard_map/ppermute | solution.py:269
  25.2 0.0 collective-permute-done.3.refs_7_
  25.2 1.3 %collective-permute-done.4.refs_8_ = f32[3,2,128,128]{3,2,1,0:T(8,128)S(1)} collective-permute-done((f32[3,2,128,128]{3,2,1,0:T(8,128)S(1)}, f32[3,2,128,128]{3,2,1,0:T(8,128)S(1)}, u32[]{:S(2)}, u32[]{:S(2)}) %collective-permute-start.4) | collective-permute-done | bytes 393248 | tf_op jit(solution)/shard_map/ppermute | solution.py:269
  26.5 0.0 copy-done.3
  26.5 6.5 %wave.1 = (f32[3,2,128,128]{3,2,1,0:T(8,128)S(1)}, f32[3,2,128,128]{3,2,1,0:T(8,128)S(1)}, f32[2,64,128]{2,1,0:T(8,128)S(1)}, f32[2,64,128]{2,1,0:T(8,128)S(1)}) custom-call(s32[4]{0:T(128)S(1)} %pad_add_fusion.offsets.refs_0_, bf16[4,2,256,256]{3,2,1,0:T(8,128)(2,1)S(1)} %copy-done.3, f32[2,128,128]{2,1,0:T(8,128)S(1)} %get-tuple-element.23.refs_2_, ...), custom_call_target="tpu_custom_call" | custom-call | flops 5000000000 | bytes 3801088 | tf_op jit(solution)/shard_map/wave/pallas_call | solution.py:226
  33.0 0.4 collective-permute-start.5
  33.4 0.1 collective-permute-start.6
  33.6 1.3 %collective-permute-done.6.refs_1_ = f32[2,64,128]{2,1,0:T(8,128)S(1)} collective-permute-done((f32[2,64,128]{2,1,0:T(8,128)S(1)}, f32[2,64,128]{2,1,0:T(8,128)S(1)}, u32[]{:S(2)}, u32[]{:S(2)}) %collective-permute-start.6) | collective-permute-done | bytes 65568 | tf_op jit(solution)/shard_map/ppermute | solution.py:300
  34.9 0.0 collective-permute-done.5.refs_3_.refs_4_
  34.9 0.1 collective-permute-start.8
  35.0 2.0 %collective-permute-start.7 = (f32[1,2,128,128]{3,2,1,0:T(8,128)S(1)}, f32[1,2,128,128]{3,2,1,0:T(8,128)S(1)}, u32[]{:S(2)}, u32[]{:S(2)}) collective-permute-start(f32[1,2,128,128]{3,2,1,0:T(8,128)S(1)} %get-tuple-element.32), channel_id=1, source_target_pairs={{0,1},{1,2},{2,3},{3,4},{4,5},{5,6},{6,7},{7,8},{8,9},{9,10},{10,1... | collective-permute-start | bytes 393224 | tf_op jit(solution)/shard_map/ppermute | solution.py:337
  37.0 2.4 %collective-permute-done.8.refs_1_ = f32[2,64,128]{2,1,0:T(8,128)S(1)} collective-permute-done((f32[2,64,128]{2,1,0:T(8,128)S(1)}, f32[2,64,128]{2,1,0:T(8,128)S(1)}, u32[]{:S(2)}, u32[]{:S(2)}) %collective-permute-start.8) | collective-permute-done | bytes 65568 | tf_op jit(solution)/shard_map/ppermute | solution.py:247
  39.4 0.1 collective-permute-start.10
  39.5 0.6 %collective-permute-start.9 = (f32[1,2,128,128]{3,2,1,0:T(8,128)S(1)}, f32[1,2,128,128]{3,2,1,0:T(8,128)S(1)}, u32[]{:S(2)}, u32[]{:S(2)}) collective-permute-start(f32[1,2,128,128]{3,2,1,0:T(8,128)S(1)} %get-tuple-element.34), channel_id=1, source_target_pairs={{0,1},{1,2},{2,3},{3,4},{4,5},{5,6},{6,7},{7,8},{8,9},{9,10},{10,1... | collective-permute-start | bytes 393224 | tf_op jit(solution)/shard_map/ppermute | solution.py:337
  40.1 5.0 %collective-permute-done.7.refs_0_ = f32[1,2,128,128]{3,2,1,0:T(8,128)S(1)} collective-permute-done((f32[1,2,128,128]{3,2,1,0:T(8,128)S(1)}, f32[1,2,128,128]{3,2,1,0:T(8,128)S(1)}, u32[]{:S(2)}, u32[]{:S(2)}) %collective-permute-start.7) | collective-permute-done | bytes 131104 | tf_op jit(solution)/shard_map/ppermute | solution.py:337
  45.1 0.1 collective-permute-done.10.refs_2_
  45.2 0.1 collective-permute-start.12
  45.3 0.1 collective-permute-start.11
  45.4 0.9 %place.1.before.refs_1_ = f32[3,2,128,256]{3,2,1,0:T(8,128)S(1)} custom-call(s32[4]{0:T(128)S(1)} %pad_add_fusion.offsets.refs_0_, s32[4]{0:T(128)S(1)} %collective-permute-done.offsets_prev.refs_1_, f32[3,2,128,128]{3,2,1,0:T(8,128)S(1)} %get-tuple-element.28.refs_2_.refs_3_, f32[3,2,128,128]{3,2,1,0:T(8,128)S(1)} %collective-permute-done.5.refs_3_.refs_4_), custom_call_target="tpu_custom_call" | custom-call | flops 2000000000 | bytes 1572864 | tf_op jit(solution)/shard_map/place/pallas_call | solution.py:226
  46.2 1.9 %collective-permute-done.9.refs_1_.refs_0_ = f32[1,2,128,128]{3,2,1,0:T(8,128)S(1)} collective-permute-done((f32[1,2,128,128]{3,2,1,0:T(8,128)S(1)}, f32[1,2,128,128]{3,2,1,0:T(8,128)S(1)}, u32[]{:S(2)}, u32[]{:S(2)}) %collective-permute-start.9) | collective-permute-done | bytes 131104 | tf_op jit(solution)/shard_map/ppermute | solution.py:337
  48.2 1.4 %collective-permute-done.12.refs_3_ = f32[2,64,128]{2,1,0:T(8,128)S(1)} collective-permute-done((f32[2,64,128]{2,1,0:T(8,128)S(1)}, f32[2,64,128]{2,1,0:T(8,128)S(1)}, u32[]{:S(2)}, u32[]{:S(2)}) %collective-permute-start.12) | collective-permute-done | bytes 65568 | tf_op jit(solution)/shard_map/ppermute | solution.py:247
  49.6 0.3 collective-permute-start.13
  49.9 4.1 %collective-permute-done.11.refs_2_ = f32[1,2,128,128]{3,2,1,0:T(8,128)S(1)} collective-permute-done((f32[1,2,128,128]{3,2,1,0:T(8,128)S(1)}, f32[1,2,128,128]{3,2,1,0:T(8,128)S(1)}, u32[]{:S(2)}, u32[]{:S(2)}) %collective-permute-start.11) | collective-permute-done | bytes 131104 | tf_op jit(solution)/shard_map/ppermute | solution.py:337
  53.9 1.6 %spill.1 = (f32[3,2,128,256]{3,2,1,0:T(8,128)}, f32[8,128]{1,0:T(8,128)S(1)}) custom-call(s32[4]{0:T(128)S(1)} %collective-permute-done.offsets_prev.refs_1_, f32[3,2,128,256]{3,2,1,0:T(8,128)S(1)} %place.1.before.refs_1_, f32[1,2,128,128]{3,2,1,0:T(8,128)S(1)} %collective-permute-done.7.refs_0_, ...), custom_call_target="tpu_custom_call" | custom-call | flops 1000000000 | bytes 1970176 | tf_op jit(solution)/shard_map/spill/pallas_call | solution.py:226
  55.6 0.0 collective-permute-done.13.refs_2_
  55.6 0.6 %step.9 = f32[2,64,128]{2,1,0:T(8,128)} custom-call(f32[8,128]{1,0:T(8,128)S(1)} %get-tuple-element.38.refs_0_, f32[2,64,128]{2,1,0:T(8,128)S(1)} %step.8.refs_1_, f32[2,64,128]{2,1,0:T(8,128)S(1)} %collective-permute-done.13.refs_2_), custom_call_target="tpu_custom_call" | custom-call | flops 1000000000 | bytes 196608 | tf_op jit(solution)/shard_map/step/pallas_call | solution.py:226
  (4 shorter events, 0.1 us)
Async XLA Ops:
  1.4 8.4 %collective-permute-start = (s32[4]{0:T(128)S(1)}, s32[4]{0:T(128)S(1)}, u32[]{:S(2)}, u32[]{:S(2)}) collective-permute-start(s32[4]{0:T(128)S(1)} %pad_add_fusion.offsets.refs_0_), channel_id=1, source_target_pairs={{0,1},{1,2},{2,3},{3,4},{4,5},{5,6},{6,7},{7,8},{8,9},{9,10},{10,1... | collective-permute-start | bytes 56 | tf_op jit(solution)/shard_map/ppermute | solution.py:261
  4.3 1.1 %copy-start = (f32[3,2,128,256]{3,2,1,0:T(8,128)S(1)}, f32[3,2,128,256]{3,2,1,0:T(8,128)}, u32[]{:S(2)}) copy-start(f32[3,2,128,256]{3,2,1,0:T(8,128)} %objects.1) | copy-start | bytes 2359300
  9.8 3.1 %copy-start.1 = (f32[2,128,128]{2,1,0:T(8,128)S(1)}, f32[2,128,128]{2,1,0:T(8,128)}, u32[]{:S(2)}) copy-start(f32[2,128,128]{2,1,0:T(8,128)} %intensity.1) | copy-start | bytes 393220
  9.8 3.1 %copy-start.2 = (f32[2,128,128]{2,1,0:T(8,128)S(1)}, f32[2,128,128]{2,1,0:T(8,128)}, u32[]{:S(2)}) copy-start(f32[2,128,128]{2,1,0:T(8,128)} %probe.1) | copy-start | bytes 393220
  10.9 12.4 %collective-permute-start.2 = (f32[3,2,128,128]{3,2,1,0:T(8,128)S(1)}, f32[3,2,128,128]{3,2,1,0:T(8,128)S(1)}, u32[]{:S(2)}, u32[]{:S(2)}) collective-permute-start(f32[3,2,128,128]{3,2,1,0:T(8,128)S(1)} %get-tuple-element.27), channel_id=1, source_target_pairs={{1,0},{2,1},{3,2},{4,3},{5,4},{6,5},{7,6},{8,7},{9,8},{10,9},{11,1... | collective-permute-start | bytes 1179656 | tf_op jit(solution)/shard_map/ppermute | solution.py:266
  13.5 9.8 %collective-permute-start.1 = (f32[128,128]{1,0:T(8,128)S(1)}, f32[128,128]{1,0:T(8,128)S(1)}, u32[]{:S(2)}, u32[]{:S(2)}) collective-permute-start(f32[128,128]{1,0:T(8,128)S(1)} %get-tuple-element.25), channel_id=1, source_target_pairs={{0,1},{1,2},{2,3},{3,4},{4,5},{5,6},{6,7},{7,8},{8,9},{9,10},{10,1... | collective-permute-start | bytes 196616 | tf_op jit(solution)/shard_map/ppermute | solution.py:258
  15.4 9.8 %collective-permute-start.3 = (f32[3,2,128,128]{3,2,1,0:T(8,128)S(1)}, f32[3,2,128,128]{3,2,1,0:T(8,128)S(1)}, u32[]{:S(2)}, u32[]{:S(2)}) collective-permute-start(f32[3,2,128,128]{3,2,1,0:T(8,128)S(1)} %get-tuple-element.22.after.refs_5_), channel_id=1, source_target_pairs={{16,0},{17,1},{18,2},{19,3},{20,4},{21,5},{22,6},{23,7},{24,8},{25... | collective-permute-start | bytes 1179656 | tf_op jit(solution)/shard_map/ppermute | solution.py:269
  23.3 3.2 %copy-start.3 = (bf16[4,2,256,256]{3,2,1,0:T(8,128)(2,1)S(1)}, bf16[4,2,256,256]{3,2,1,0:T(8,128)(2,1)}, u32[]{:S(2)}) copy-start(bf16[4,2,256,256]{3,2,1,0:T(8,128)(2,1)} %constant.2.clone.refs_1_) | copy-start | bytes 3145732
  23.9 2.6 %collective-permute-start.4 = (f32[3,2,128,128]{3,2,1,0:T(8,128)S(1)}, f32[3,2,128,128]{3,2,1,0:T(8,128)S(1)}, u32[]{:S(2)}, u32[]{:S(2)}) collective-permute-start(f32[3,2,128,128]{3,2,1,0:T(8,128)S(1)} %join.1.refs_6_), channel_id=1, source_target_pairs={{0,16},{1,17},{2,18},{3,19},{4,20},{5,21},{6,22},{7,23},{8,24},{9,... | collective-permute-start | bytes 1179656 | tf_op jit(solution)/shard_map/ppermute | solution.py:269
  33.0 1.9 %collective-permute-start.5 = (f32[3,2,128,128]{3,2,1,0:T(8,128)S(1)}, f32[3,2,128,128]{3,2,1,0:T(8,128)S(1)}, u32[]{:S(2)}, u32[]{:S(2)}) collective-permute-start(f32[3,2,128,128]{3,2,1,0:T(8,128)S(1)} %get-tuple-element.29), channel_id=1, source_target_pairs={{0,16},{16,0},{1,17},{17,1},{2,18},{18,2},{3,19},{19,3},{4,20},{20... | collective-permute-start | bytes 1179656 | tf_op jit(solution)/shard_map/ppermute | solution.py:301
  33.4 1.4 %collective-permute-start.6 = (f32[2,64,128]{2,1,0:T(8,128)S(1)}, f32[2,64,128]{2,1,0:T(8,128)S(1)}, u32[]{:S(2)}, u32[]{:S(2)}) collective-permute-start(f32[2,64,128]{2,1,0:T(8,128)S(1)} %get-tuple-element.31), channel_id=1, source_target_pairs={{0,16},{16,0},{1,17},{17,1},{2,18},{18,2},{3,19},{19,3},{4,20},{20... | collective-permute-start | bytes 196616 | tf_op jit(solution)/shard_map/ppermute | solution.py:300
  34.9 4.5 %collective-permute-start.8 = (f32[2,64,128]{2,1,0:T(8,128)S(1)}, f32[2,64,128]{2,1,0:T(8,128)S(1)}, u32[]{:S(2)}, u32[]{:S(2)}) collective-permute-start(f32[2,64,128]{2,1,0:T(8,128)S(1)} %get-tuple-element.33.refs_0_), channel_id=1, source_target_pairs={{0,1},{1,0},{2,3},{3,2},{4,5},{5,4},{6,7},{7,6},{8,9},{9,8},{10,11... | collective-permute-start | bytes 196616 | tf_op jit(solution)/shard_map/ppermute | solution.py:247
  35.0 10.1 %collective-permute-start.7 = (f32[1,2,128,128]{3,2,1,0:T(8,128)S(1)}, f32[1,2,128,128]{3,2,1,0:T(8,128)S(1)}, u32[]{:S(2)}, u32[]{:S(2)}) collective-permute-start(f32[1,2,128,128]{3,2,1,0:T(8,128)S(1)} %get-tuple-element.32), channel_id=1, source_target_pairs={{0,1},{1,2},{2,3},{3,4},{4,5},{5,6},{6,7},{7,8},{8,9},{9,10},{10,1... | collective-permute-start | bytes 393224 | tf_op jit(solution)/shard_map/ppermute | solution.py:337
  39.4 5.8 %collective-permute-start.10 = (f32[2,64,128]{2,1,0:T(8,128)S(1)}, f32[2,64,128]{2,1,0:T(8,128)S(1)}, u32[]{:S(2)}, u32[]{:S(2)}) collective-permute-start(f32[2,64,128]{2,1,0:T(8,128)S(1)} %get-tuple-element.35.refs_1_), channel_id=1, source_target_pairs={{0,2},{1,3},{2,0},{3,1},{4,6},{5,7},{6,4},{7,5},{8,10},{9,11},{10,... | collective-permute-start | bytes 196616 | tf_op jit(solution)/shard_map/ppermute | solution.py:247
  39.5 8.7 %collective-permute-start.9 = (f32[1,2,128,128]{3,2,1,0:T(8,128)S(1)}, f32[1,2,128,128]{3,2,1,0:T(8,128)S(1)}, u32[]{:S(2)}, u32[]{:S(2)}) collective-permute-start(f32[1,2,128,128]{3,2,1,0:T(8,128)S(1)} %get-tuple-element.34), channel_id=1, source_target_pairs={{0,1},{1,2},{2,3},{3,4},{4,5},{5,6},{6,7},{7,8},{8,9},{9,10},{10,1... | collective-permute-start | bytes 393224 | tf_op jit(solution)/shard_map/ppermute | solution.py:337
  45.2 4.3 %collective-permute-start.12 = (f32[2,64,128]{2,1,0:T(8,128)S(1)}, f32[2,64,128]{2,1,0:T(8,128)S(1)}, u32[]{:S(2)}, u32[]{:S(2)}) collective-permute-start(f32[2,64,128]{2,1,0:T(8,128)S(1)} %get-tuple-element.39.refs_2_), channel_id=1, source_target_pairs={{0,4},{1,5},{2,6},{3,7},{4,0},{5,1},{6,2},{7,3},{8,12},{9,13},{10,... | collective-permute-start | bytes 196616 | tf_op jit(solution)/shard_map/ppermute | solution.py:247
  45.3 8.7 %collective-permute-start.11 = (f32[1,2,128,128]{3,2,1,0:T(8,128)S(1)}, f32[1,2,128,128]{3,2,1,0:T(8,128)S(1)}, u32[]{:S(2)}, u32[]{:S(2)}) collective-permute-start(f32[1,2,128,128]{3,2,1,0:T(8,128)S(1)} %get-tuple-element.36), channel_id=1, source_target_pairs={{0,1},{1,2},{2,3},{3,4},{4,5},{5,6},{6,7},{7,8},{8,9},{9,10},{10,1... | collective-permute-start | bytes 393224 | tf_op jit(solution)/shard_map/ppermute | solution.py:337
  49.6 6.0 %collective-permute-start.13 = (f32[2,64,128]{2,1,0:T(8,128)S(1)}, f32[2,64,128]{2,1,0:T(8,128)S(1)}, u32[]{:S(2)}, u32[]{:S(2)}) collective-permute-start(f32[2,64,128]{2,1,0:T(8,128)S(1)} %step.8.refs_1_), channel_id=1, source_target_pairs={{0,8},{1,9},{2,10},{3,11},{4,12},{5,13},{6,14},{7,15},{8,0},{9,1},... | collective-permute-start | bytes 196616 | tf_op jit(solution)/shard_map/ppermute | solution.py:247

commit v9 on v7

--- a/solution.py
+++ b/solution.py
@@ -41,12 +41,12 @@
 
 def times_right(x, high, low):
     x_high, x_low = halves(x)
-    return dot(x_high, high) + (dot(x_low, high) + dot(x_high, low))
+    return dot(jnp.concatenate([x_high, x_low, x_high], axis=1), jnp.concatenate([high, high, low], axis=0))
 
 
 def times_left(high, low, x):
     x_high, x_low = halves(x)
-    return dot(high, x_high) + (dot(high, x_low) + dot(low, x_high))
+    return dot(jnp.concatenate([high, high, low], axis=1), jnp.concatenate([x_high, x_low, x_high], axis=0))
 
 
 def both_sides(re, im, tables, which):
@@ -57,12 +57,9 @@
     return z[:n], z[n:]
 
 
-def share(offsets, tile_rows, chips_back):
-    count = lax.axis_size("scan")
-    base = lax.rem(lax.axis_index("scan") + count - chips_back, count) * tile_rows
-    second = offsets[1] - base == tile_rows
-    a = jnp.where(second, 1, 0)
-    return a, offsets[2 + a], offsets[1 - a] - base, offsets[3 - a]
+def share(offsets, tile_rows):
+    a = jnp.where(offsets[1] >= offsets[0], 1, 0)
+    return a, offsets[2 + a], offsets[1 - a] - offsets[a] + tile_rows, offsets[3 - a]
 
 
 def cut(tile, row, col, width):
@@ -73,7 +70,7 @@
 
 def own_kernel(offsets, objects, tiles, window_b):
     slab, _, rows, _ = objects.shape
-    _, _, row_b, col_b = share(offsets, rows, 0)
+    _, _, row_b, col_b = share(offsets, rows)
     for s in range(slab):
         for p in range(2):
             tile = objects[s, p]
@@ -84,7 +81,7 @@
 def prev_kernel(offsets_prev, after, tiles, window_a, halo):
     slab, _, rows, _ = tiles.shape
     width = halo.shape[-1]
-    _, col_a, row_p, col_p = share(offsets_prev, rows, 1)
+    _, col_a, row_p, col_p = share(offsets_prev, rows)
     for s in range(slab):
         for p in range(2):
             halo[s, p] = cut(tiles[s, p], row_p, col_p, width)
@@ -93,7 +90,7 @@
 
 def join_kernel(offsets, after, window_b, halo, joined):
     slab, _, rows, cols = joined.shape
-    _, _, row_b, _ = share(offsets, rows, 0)
+    _, _, row_b, _ = share(offsets, rows)
     inside = lax.broadcasted_iota(jnp.int32, (rows, cols), 0) < rows - row_b
     for s in range(slab):
         for p in range(2):
@@ -102,8 +99,8 @@
 
 def load_kernel(offsets, offsets_prev, intensity, far, probe, measured, start):
     rows = probe.shape[-1]
-    near_a, _, _, _ = share(offsets, rows, 0)
-    far_a, _, _, _ = share(offsets_prev, rows, 1)
+    near_a, _, _, _ = share(offsets, rows)
+    far_a, _, _, _ = share(offsets_prev, rows)
     measured[...] = jnp.where(lax.axis_index("depth") == 0, far[far_a], intensity[1 - near_a])
     start[...] = probe[...]
 
@@ -151,7 +148,7 @@
 
     chi = lax.fori_loop(0, count - 1, backward, chi, unroll=True if count <= 8 else 1)
     grad = leave(0, *chi)
-    _, _, row_b, _ = share(offsets, n, 0)
+    _, _, row_b, _ = share(offsets, n)
     turn = lax.rem(jnp.where(on_a, 0, row_b), n)
     for j in range(depth_count):
         base = lax.rem(depth + j, depth_count) * slab
@@ -176,8 +173,8 @@
     *parts, out = refs
     slab, _, rows, cols = out.shape
     depth = lax.axis_index("depth")
-    _, _, row_b, col_b = share(offsets, rows, 0)
-    _, col_a, _, _ = share(offsets_prev, rows, 1)
+    _, _, row_b, col_b = share(offsets, rows)
+    _, col_a, _, _ = share(offsets_prev, rows)
     row_index = lax.broadcasted_iota(jnp.int32, (rows, parts[0].shape[-1]), 0)
     corners = []
     for j in range(depth_count):
@@ -211,7 +208,7 @@
 def spill_kernel(offsets_prev, before, *refs):
     *spills, out, token = refs
     slab, _, rows, cols = out.shape
-    _, _, row_p, col_p = share(offsets_prev, rows, 1)
+    _, _, row_p, col_p = share(offsets_prev, rows)
     mask = lax.broadcasted_iota(jnp.int32, (rows, spills[0].shape[-1]), 0) < row_p
     came = [(spill, i) for spill in spills for i in range(spill.shape[0])]
     for s in range(slab):
@@ -325,17 +322,18 @@
         work=2 * 10**9,
     )
     turns = rounds - 1 if paired else 1
-    share_of = [tuple(range(slab * k // turns, slab * (k + 1) // turns)) for k in range(turns)]
+    cuts = [0, slab // 3] + [slab] * (turns - 1) if turns > 1 else [0, slab]
+    share_of = [tuple(range(cuts[k], cuts[k + 1])) for k in range(turns)]
     total = sums[0]
     for x in sums[1:-1]:
         total = total + x
     other = sums[-1] if depth_count > 1 else jnp.zeros_like(total)
     for k, slices in enumerate(share_of):
-        total, *payload = step(total, other, slices, spill[k - 2 : k - 1] if k >= 2 else [])
+        total, *payload = step(total, other, slices, spill[:1] if k == 2 else [])
         other = sum_round(total, k) if paired else jnp.zeros_like(total)
         spill += [lax.ppermute(x, "scan", ahead) for x in payload]
     if paired:
-        (total,) = step(total, other, (), [*spill[:-1][-1:], object_grad])
+        (total,) = step(total, other, (), [object_grad])
         other = sum_round(total, rounds - 1)
     object_grad, token = call(
         spill_kernel, "spill", [offsets_prev], [object_grad, *spill], [whole, jax.ShapeDtypeStruct((8, n), f32)]

time: 55.8 us -> 54.7 us (0.980)
  waiting for transfers between devices: 24.4 us -> 22.5 us
  starting transfers between devices: 15.8 us -> 16.7 us
    ppermute x3 -> x2, waiting for transfers between devices: 9.69 us -> 4.13 us  [body(): spill += [lax.ppermute(x, 'scan', ahead) for x in payload]]
    ppermute x4, waiting for transfers between devices: 3.85 us -> 7.47 us  [sum_round(): return lax.ppermute(x, ('depth', 'scan'), route)]
    ppermute x4, starting transfers between devices: 1.88 us -> 2.88 us  [sum_round(): return lax.ppermute(x, ('depth', 'scan'), route)]
    ppermute x3 -> x2, starting transfers between devices: 2.99 us -> 2.94 us  [body(): spill += [lax.ppermute(x, 'scan', ahead) for x in payload]]
  transfers between devices with their start and end apart: 14 -> 13, of which waited for: 10 -> 9; matrix products, arithmetic and copies ran while one was open for 1% -> 1% of each run, Pallas kernels for 8% -> 8%
where the time goes in v9:
time: 54.7 us; the launch traced here: 54.5 us
  waiting for transfers between devices  22.5 us (41%)
  starting transfers between devices  16.7 us (31%)
  Pallas kernels  12.7 us (23%)
  local copies, waits for them, and re-layouts  1.14 us (2%)
  between operations  0.79 us (1%)
  other arithmetic  0.75 us (1%)
    pallas_call x12, Pallas kernels, call(): pl.pallas_call(kernel, name=name, out_shape=outs, in_specs=[pl.BlockSpec(...  12.7 us
    ppermute x4, waiting for transfers between devices, sum_round(): return lax.ppermute(x, ('depth', 'scan'), route)  7.47 us
    ppermute x1, starting transfers between devices, across(): return lax.ppermute(x, ('depth', 'scan'), route)  4.85 us
    ppermute x1, waiting for transfers between devices, body(): lax.ppermute(halo, 'scan', [((i + 1) % scan_count, i) for i in range(scan...  4.57 us
    ppermute x2, waiting for transfers between devices, body(): spill += [lax.ppermute(x, 'scan', ahead) for x in payload]  4.13 us
    ppermute x1, waiting for transfers between devices, body(): lax.ppermute(offsets, 'scan', [(i, (i + 1) % scan_count) for i in range(s...  3.67 us
    ppermute x2, starting transfers between devices, body(): spill += [lax.ppermute(x, 'scan', ahead) for x in payload]  2.94 us
    ppermute x4, starting transfers between devices, sum_round(): return lax.ppermute(x, ('depth', 'scan'), route)  2.88 us
  transfers between devices with their start and end apart: 13, of which 9 were waited for; matrix products, arithmetic and copies ran while one was open for 1% of the time, Pallas kernels for 8%

profile of v9, /device:TPU:0, one launch (start us, length us, event | category | flops | bytes accessed | tf_op | source)
XLA Modules:
  0.0 54.5 jit_solution(14961891970183269950)
XLA Ops:
  0.6 4.8 %collective-permute-start.1 = (f32[2,128,128]{2,1,0:T(8,128)}, f32[2,128,128]{2,1,0:T(8,128)S(1)}, u32[]{:S(2)}, u32[]{:S(2)}) collective-permute-start(f32[2,128,128]{2,1,0:T(8,128)} %intensity.1), channel_id=1, source_target_pairs={{0,1},{1,2},{2,3},{3,4},{4,5},{5,6},{6,7},{7,8},{8,9},{9,10},{10,1... | collective-permute-start | bytes 393224 | tf_op jit(solution)/shard_map/ppermute | solution.py:255
  5.5 0.7 %pad_add_fusion.offsets.refs_0_ = s32[4]{0:T(128)S(1)} fusion(s32[2]{0:T(128)} %param.9, s32[2]{0:T(128)} %param.8), kind=kLoop, calls=%fused_computation | loop fusion | flops 4 | bytes 32 | tf_op jit(solution)/shard_map/concatenate | solution.py:257
  6.2 1.5 %collective-permute-start = (s32[4]{0:T(128)S(1)}, s32[4]{0:T(128)S(1)}, u32[]{:S(2)}, u32[]{:S(2)}) collective-permute-start(s32[4]{0:T(128)S(1)} %pad_add_fusion.offsets.refs_0_), channel_id=1, source_target_pairs={{0,1},{1,2},{2,3},{3,4},{4,5},{5,6},{6,7},{7,8},{8,9},{9,10},{10,1... | collective-permute-start | bytes 56 | tf_op jit(solution)/shard_map/ppermute | solution.py:258
  7.7 0.0 copy-start
  7.7 1.1 %copy-done = f32[3,2,128,256]{3,2,1,0:T(8,128)S(1)} copy-done((f32[3,2,128,256]{3,2,1,0:T(8,128)S(1)}, f32[3,2,128,256]{3,2,1,0:T(8,128)}, u32[]{:S(2)}) %copy-start) | copy-done | bytes 786456
  8.9 0.8 %own.1 = (f32[3,2,128,256]{3,2,1,0:T(8,128)S(1)}, f32[3,2,128,128]{3,2,1,0:T(8,128)S(1)}) custom-call(s32[4]{0:T(128)S(1)} %pad_add_fusion.offsets.refs_0_, f32[3,2,128,256]{3,2,1,0:T(8,128)S(1)} %copy-done), custom_call_target="tpu_custom_call" | custom-call | flops 1000000000 | bytes 1966080 | tf_op jit(solution)/shard_map/own/pallas_call | solution.py:223
  9.7 3.7 %collective-permute-done.offsets_prev.refs_1_ = s32[4]{0:T(128)S(1)} collective-permute-done((s32[4]{0:T(128)S(1)}, s32[4]{0:T(128)S(1)}, u32[]{:S(2)}, u32[]{:S(2)}) %collective-permute-start) | collective-permute-done | bytes 48 | tf_op jit(solution)/shard_map/ppermute | solution.py:258
  13.4 0.0 collective-permute-done.1.far.after
  13.4 0.0 copy-start.1
  13.4 0.0 copy-start.2
  13.4 1.0 %prev.1 = (f32[3,2,128,128]{3,2,1,0:T(8,128)S(1)}, f32[3,2,128,128]{3,2,1,0:T(8,128)S(1)}) custom-call(s32[4]{0:T(128)S(1)} %collective-permute-done.offsets_prev.refs_1_, f32[2,128,128]{2,1,0:T(8,128)S(1)} %collective-permute-done.1.far.after, f32[3,2,128,256]{3,2,1,0:T(8,128)S(1)} %get-tuple-element.20.tiles), custom_call_target="tpu_custom_call" | custom-call | flops 1000000000 | bytes 1572864 | tf_op jit(solution)/shard_map/prev/pallas_call | solution.py:223
  14.4 1.4 %collective-permute-start.2 = (f32[3,2,128,128]{3,2,1,0:T(8,128)S(1)}, f32[3,2,128,128]{3,2,1,0:T(8,128)S(1)}, u32[]{:S(2)}, u32[]{:S(2)}) collective-permute-start(f32[3,2,128,128]{3,2,1,0:T(8,128)S(1)} %get-tuple-element.23), channel_id=1, source_target_pairs={{1,0},{2,1},{3,2},{4,3},{5,4},{6,5},{7,6},{8,7},{9,8},{10,9},{11,1... | collective-permute-start | bytes 1179656 | tf_op jit(solution)/shard_map/ppermute | solution.py:264
  15.8 1.3 %collective-permute-start.3 = (f32[3,2,128,128]{3,2,1,0:T(8,128)S(1)}, f32[3,2,128,128]{3,2,1,0:T(8,128)S(1)}, u32[]{:S(2)}, u32[]{:S(2)}) collective-permute-start(f32[3,2,128,128]{3,2,1,0:T(8,128)S(1)} %get-tuple-element.21.refs_4_), channel_id=1, source_target_pairs={{16,0},{17,1},{18,2},{19,3},{20,4},{21,5},{22,6},{23,7},{24,8},{25... | collective-permute-start | bytes 1179656 | tf_op jit(solution)/shard_map/ppermute | solution.py:267
  17.1 0.0 copy-done.1
  17.1 0.0 copy-done.2
  17.1 0.6 %load.1 = (f32[128,128]{1,0:T(8,128)S(1)}, f32[2,128,128]{2,1,0:T(8,128)S(1)}) custom-call(s32[4]{0:T(128)S(1)} %pad_add_fusion.offsets.refs_0_, s32[4]{0:T(128)S(1)} %collective-permute-done.offsets_prev.refs_1_, f32[2,128,128]{2,1,0:T(8,128)S(1)} %copy-done.1, f32[2,128,128]{2,1,0:T(8,128)S(1)} %collective-permute-done.1.far.after, ...), custom_call_target="tpu_custom_call" | custom-call | flops 1000000000 | bytes 589824 | tf_op jit(solution)/shard_map/load/pallas_call | solution.py:223
  17.7 4.6 %collective-permute-done.2.halo = f32[3,2,128,128]{3,2,1,0:T(8,128)S(1)} collective-permute-done((f32[3,2,128,128]{3,2,1,0:T(8,128)S(1)}, f32[3,2,128,128]{3,2,1,0:T(8,128)S(1)}, u32[]{:S(2)}, u32[]{:S(2)}) %collective-permute-start.2) | collective-permute-done | bytes 393248 | tf_op jit(solution)/shard_map/ppermute | solution.py:264
  22.2 0.0 copy-start.3
  22.2 0.6 %join.1.refs_5_ = f32[3,2,128,128]{3,2,1,0:T(8,128)S(1)} custom-call(s32[4]{0:T(128)S(1)} %pad_add_fusion.offsets.refs_0_, f32[128,128]{1,0:T(8,128)S(1)} %get-tuple-element.19.after.refs_3_, f32[3,2,128,128]{3,2,1,0:T(8,128)S(1)} %get-tuple-element.22.window_b, f32[3,2,128,128]{3,2,1,0:T(8,128)S(1)} %collective-permute-done.2.halo), custom_call_target="tpu_custom_call" | custom-call | flops 1000000000 | bytes 1179648 | tf_op jit(solution)/shard_map/join/pallas_call | solution.py:223
  22.8 1.3 %collective-permute-start.4 = (f32[3,2,128,128]{3,2,1,0:T(8,128)S(1)}, f32[3,2,128,128]{3,2,1,0:T(8,128)S(1)}, u32[]{:S(2)}, u32[]{:S(2)}) collective-permute-start(f32[3,2,128,128]{3,2,1,0:T(8,128)S(1)} %join.1.refs_5_), channel_id=1, source_target_pairs={{0,16},{1,17},{2,18},{3,19},{4,20},{5,21},{6,22},{7,23},{8,24},{9,... | collective-permute-start | bytes 1179656 | tf_op jit(solution)/shard_map/ppermute | solution.py:267
  24.2 0.0 collective-permute-done.3.refs_6_
  24.2 1.3 %collective-permute-done.4.refs_7_ = f32[3,2,128,128]{3,2,1,0:T(8,128)S(1)} collective-permute-done((f32[3,2,128,128]{3,2,1,0:T(8,128)S(1)}, f32[3,2,128,128]{3,2,1,0:T(8,128)S(1)}, u32[]{:S(2)}, u32[]{:S(2)}) %collective-permute-start.4) | collective-permute-done | bytes 393248 | tf_op jit(solution)/shard_map/ppermute | solution.py:267
  25.5 0.0 copy-done.3
  25.5 6.5 %wave.1 = (f32[3,2,128,128]{3,2,1,0:T(8,128)S(1)}, f32[3,2,128,128]{3,2,1,0:T(8,128)S(1)}, f32[2,64,128]{2,1,0:T(8,128)S(1)}, f32[2,64,128]{2,1,0:T(8,128)S(1)}) custom-call(s32[4]{0:T(128)S(1)} %pad_add_fusion.offsets.refs_0_, bf16[4,2,256,256]{3,2,1,0:T(8,128)(2,1)S(1)} %copy-done.3, f32[2,128,128]{2,1,0:T(8,128)S(1)} %get-tuple-element.18.refs_2_, ...), custom_call_target="tpu_custom_call" | custom-call | flops 5000000000 | bytes 3735552 | tf_op jit(solution)/shard_map/wave/pallas_call | solution.py:223
  31.9 0.4 collective-permute-start.5
  32.4 0.1 collective-permute-start.6
  32.5 1.3 %collective-permute-done.6.refs_1_ = f32[2,64,128]{2,1,0:T(8,128)S(1)} collective-permute-done((f32[2,64,128]{2,1,0:T(8,128)S(1)}, f32[2,64,128]{2,1,0:T(8,128)S(1)}, u32[]{:S(2)}, u32[]{:S(2)}) %collective-permute-start.6) | collective-permute-done | bytes 65568 | tf_op jit(solution)/shard_map/ppermute | solution.py:296
  33.8 0.0 collective-permute-done.5.refs_3_
  33.9 0.1 collective-permute-start.8
  33.9 2.0 %collective-permute-start.7 = (f32[1,2,128,128]{3,2,1,0:T(8,128)S(1)}, f32[1,2,128,128]{3,2,1,0:T(8,128)S(1)}, u32[]{:S(2)}, u32[]{:S(2)}) collective-permute-start(f32[1,2,128,128]{3,2,1,0:T(8,128)S(1)} %get-tuple-element.28), channel_id=1, source_target_pairs={{0,1},{1,2},{2,3},{3,4},{4,5},{5,6},{6,7},{7,8},{8,9},{9,10},{10,1... | collective-permute-start | bytes 393224 | tf_op jit(solution)/shard_map/ppermute | solution.py:334
  35.9 2.6 %collective-permute-done.8.refs_1_ = f32[2,64,128]{2,1,0:T(8,128)S(1)} collective-permute-done((f32[2,64,128]{2,1,0:T(8,128)S(1)}, f32[2,64,128]{2,1,0:T(8,128)S(1)}, u32[]{:S(2)}, u32[]{:S(2)}) %collective-permute-start.8) | collective-permute-done | bytes 65568 | tf_op jit(solution)/shard_map/ppermute | solution.py:244
  38.6 0.1 collective-permute-start.10
  38.7 0.9 %collective-permute-start.9 = (f32[2,2,128,128]{3,2,1,0:T(8,128)S(1)}, f32[2,2,128,128]{3,2,1,0:T(8,128)S(1)}, u32[]{:S(2)}, u32[]{:S(2)}) collective-permute-start(f32[2,2,128,128]{3,2,1,0:T(8,128)S(1)} %get-tuple-element.30), channel_id=1, source_target_pairs={{0,1},{1,2},{2,3},{3,4},{4,5},{5,6},{6,7},{7,8},{8,9},{9,10},{10,1... | collective-permute-start | bytes 786440 | tf_op jit(solution)/shard_map/ppermute | solution.py:334
  39.6 4.1 %collective-permute-done.7.refs_0_ = f32[1,2,128,128]{3,2,1,0:T(8,128)S(1)} collective-permute-done((f32[1,2,128,128]{3,2,1,0:T(8,128)S(1)}, f32[1,2,128,128]{3,2,1,0:T(8,128)S(1)}, u32[]{:S(2)}, u32[]{:S(2)}) %collective-permute-start.7) | collective-permute-done | bytes 131104 | tf_op jit(solution)/shard_map/ppermute | solution.py:334
  43.7 0.6 %collective-permute-done.10.refs_2_ = f32[2,64,128]{2,1,0:T(8,128)S(1)} collective-permute-done((f32[2,64,128]{2,1,0:T(8,128)S(1)}, f32[2,64,128]{2,1,0:T(8,128)S(1)}, u32[]{:S(2)}, u32[]{:S(2)}) %collective-permute-start.10) | collective-permute-done | bytes 65568 | tf_op jit(solution)/shard_map/ppermute | solution.py:244
  44.3 0.1 collective-permute-start.11
  44.4 0.9 %place.1.before.refs_0_ = f32[3,2,128,256]{3,2,1,0:T(8,128)S(1)} custom-call(s32[4]{0:T(128)S(1)} %pad_add_fusion.offsets.refs_0_, s32[4]{0:T(128)S(1)} %collective-permute-done.offsets_prev.refs_1_, f32[3,2,128,128]{3,2,1,0:T(8,128)S(1)} %get-tuple-element.24.refs_2_, f32[3,2,128,128]{3,2,1,0:T(8,128)S(1)} %collective-permute-done.5.refs_3_), custom_call_target="tpu_custom_call" | custom-call | flops 2000000000 | bytes 1572864 | tf_op jit(solution)/shard_map/place/pallas_call | solution.py:223
  45.2 3.4 %collective-permute-done.11.refs_2_ = f32[2,64,128]{2,1,0:T(8,128)S(1)} collective-permute-done((f32[2,64,128]{2,1,0:T(8,128)S(1)}, f32[2,64,128]{2,1,0:T(8,128)S(1)}, u32[]{:S(2)}, u32[]{:S(2)}) %collective-permute-start.11) | collective-permute-done | bytes 65568 | tf_op jit(solution)/shard_map/ppermute | solution.py:244
  48.6 2.7 %collective-permute-start.12 = (f32[2,64,128]{2,1,0:T(8,128)S(1)}, f32[2,64,128]{2,1,0:T(8,128)S(1)}, u32[]{:S(2)}, u32[]{:S(2)}) collective-permute-start(f32[2,64,128]{2,1,0:T(8,128)S(1)} %step.8.refs_1_), channel_id=1, source_target_pairs={{0,8},{1,9},{2,10},{3,11},{4,12},{5,13},{6,14},{7,15},{8,0},{9,1},... | collective-permute-start | bytes 196616 | tf_op jit(solution)/shard_map/ppermute | solution.py:244
  51.3 0.0 collective-permute-done.9.refs_1_
  51.3 1.6 %spill.1 = (f32[3,2,128,256]{3,2,1,0:T(8,128)}, f32[8,128]{1,0:T(8,128)S(1)}) custom-call(s32[4]{0:T(128)S(1)} %collective-permute-done.offsets_prev.refs_1_, f32[3,2,128,256]{3,2,1,0:T(8,128)S(1)} %place.1.before.refs_0_, f32[1,2,128,128]{3,2,1,0:T(8,128)S(1)} %collective-permute-done.7.refs_0_, f32[2,2,128,128]{3,2,1,0:T(8,128)S(1)} %collective-permute-done.9.refs_1_), custom_call_target="tpu_custom_call" | custom-call | flops 1000000000 | bytes 1970176 | tf_op jit(solution)/shard_map/spill/pallas_call | solution.py:223
  52.9 1.0 %collective-permute-done.12.refs_2_ = f32[2,64,128]{2,1,0:T(8,128)S(1)} collective-permute-done((f32[2,64,128]{2,1,0:T(8,128)S(1)}, f32[2,64,128]{2,1,0:T(8,128)S(1)}, u32[]{:S(2)}, u32[]{:S(2)}) %collective-permute-start.12) | collective-permute-done | bytes 65568 | tf_op jit(solution)/shard_map/ppermute | solution.py:244
  53.9 0.6 %step.9 = f32[2,64,128]{2,1,0:T(8,128)} custom-call(f32[8,128]{1,0:T(8,128)S(1)} %get-tuple-element.32.refs_0_, f32[2,64,128]{2,1,0:T(8,128)S(1)} %step.8.refs_1_, f32[2,64,128]{2,1,0:T(8,128)S(1)} %collective-permute-done.12.refs_2_), custom_call_target="tpu_custom_call" | custom-call | flops 1000000000 | bytes 196608 | tf_op jit(solution)/shard_map/step/pallas_call | solution.py:223
  (4 shorter events, 0.1 us)
Async XLA Ops:
  0.6 12.7 %collective-permute-start.1 = (f32[2,128,128]{2,1,0:T(8,128)}, f32[2,128,128]{2,1,0:T(8,128)S(1)}, u32[]{:S(2)}, u32[]{:S(2)}) collective-permute-start(f32[2,128,128]{2,1,0:T(8,128)} %intensity.1), channel_id=1, source_target_pairs={{0,1},{1,2},{2,3},{3,4},{4,5},{5,6},{6,7},{7,8},{8,9},{9,10},{10,1... | collective-permute-start | bytes 393224 | tf_op jit(solution)/shard_map/ppermute | solution.py:255
  6.2 7.1 %collective-permute-start = (s32[4]{0:T(128)S(1)}, s32[4]{0:T(128)S(1)}, u32[]{:S(2)}, u32[]{:S(2)}) collective-permute-start(s32[4]{0:T(128)S(1)} %pad_add_fusion.offsets.refs_0_), channel_id=1, source_target_pairs={{0,1},{1,2},{2,3},{3,4},{4,5},{5,6},{6,7},{7,8},{8,9},{9,10},{10,1... | collective-permute-start | bytes 56 | tf_op jit(solution)/shard_map/ppermute | solution.py:258
  7.7 1.1 %copy-start = (f32[3,2,128,256]{3,2,1,0:T(8,128)S(1)}, f32[3,2,128,256]{3,2,1,0:T(8,128)}, u32[]{:S(2)}) copy-start(f32[3,2,128,256]{3,2,1,0:T(8,128)} %objects.1) | copy-start | bytes 2359300
  13.4 3.7 %copy-start.1 = (f32[2,128,128]{2,1,0:T(8,128)S(1)}, f32[2,128,128]{2,1,0:T(8,128)}, u32[]{:S(2)}) copy-start(f32[2,128,128]{2,1,0:T(8,128)} %intensity.1) | copy-start | bytes 393220
  13.4 3.7 %copy-start.2 = (f32[2,128,128]{2,1,0:T(8,128)S(1)}, f32[2,128,128]{2,1,0:T(8,128)}, u32[]{:S(2)}) copy-start(f32[2,128,128]{2,1,0:T(8,128)} %probe.1) | copy-start | bytes 393220
  14.4 7.8 %collective-permute-start.2 = (f32[3,2,128,128]{3,2,1,0:T(8,128)S(1)}, f32[3,2,128,128]{3,2,1,0:T(8,128)S(1)}, u32[]{:S(2)}, u32[]{:S(2)}) collective-permute-start(f32[3,2,128,128]{3,2,1,0:T(8,128)S(1)} %get-tuple-element.23), channel_id=1, source_target_pairs={{1,0},{2,1},{3,2},{4,3},{5,4},{6,5},{7,6},{8,7},{9,8},{10,9},{11,1... | collective-permute-start | bytes 1179656 | tf_op jit(solution)/shard_map/ppermute | solution.py:264
  15.8 8.4 %collective-permute-start.3 = (f32[3,2,128,128]{3,2,1,0:T(8,128)S(1)}, f32[3,2,128,128]{3,2,1,0:T(8,128)S(1)}, u32[]{:S(2)}, u32[]{:S(2)}) collective-permute-start(f32[3,2,128,128]{3,2,1,0:T(8,128)S(1)} %get-tuple-element.21.refs_4_), channel_id=1, source_target_pairs={{16,0},{17,1},{18,2},{19,3},{20,4},{21,5},{22,6},{23,7},{24,8},{25... | collective-permute-start | bytes 1179656 | tf_op jit(solution)/shard_map/ppermute | solution.py:267
  22.2 3.2 %copy-start.3 = (bf16[4,2,256,256]{3,2,1,0:T(8,128)(2,1)S(1)}, bf16[4,2,256,256]{3,2,1,0:T(8,128)(2,1)}, u32[]{:S(2)}) copy-start(bf16[4,2,256,256]{3,2,1,0:T(8,128)(2,1)} %constant.2.clone.refs_1_) | copy-start | bytes 3145732
  22.8 2.6 %collective-permute-start.4 = (f32[3,2,128,128]{3,2,1,0:T(8,128)S(1)}, f32[3,2,128,128]{3,2,1,0:T(8,128)S(1)}, u32[]{:S(2)}, u32[]{:S(2)}) collective-permute-start(f32[3,2,128,128]{3,2,1,0:T(8,128)S(1)} %join.1.refs_5_), channel_id=1, source_target_pairs={{0,16},{1,17},{2,18},{3,19},{4,20},{5,21},{6,22},{7,23},{8,24},{9,... | collective-permute-start | bytes 1179656 | tf_op jit(solution)/shard_map/ppermute | solution.py:267
  31.9 1.9 %collective-permute-start.5 = (f32[3,2,128,128]{3,2,1,0:T(8,128)S(1)}, f32[3,2,128,128]{3,2,1,0:T(8,128)S(1)}, u32[]{:S(2)}, u32[]{:S(2)}) collective-permute-start(f32[3,2,128,128]{3,2,1,0:T(8,128)S(1)} %get-tuple-element.25), channel_id=1, source_target_pairs={{0,16},{16,0},{1,17},{17,1},{2,18},{18,2},{3,19},{19,3},{4,20},{20... | collective-permute-start | bytes 1179656 | tf_op jit(solution)/shard_map/ppermute | solution.py:297
  32.4 1.4 %collective-permute-start.6 = (f32[2,64,128]{2,1,0:T(8,128)S(1)}, f32[2,64,128]{2,1,0:T(8,128)S(1)}, u32[]{:S(2)}, u32[]{:S(2)}) collective-permute-start(f32[2,64,128]{2,1,0:T(8,128)S(1)} %get-tuple-element.27), channel_id=1, source_target_pairs={{0,16},{16,0},{1,17},{17,1},{2,18},{18,2},{3,19},{19,3},{4,20},{20... | collective-permute-start | bytes 196616 | tf_op jit(solution)/shard_map/ppermute | solution.py:296
  33.9 4.7 %collective-permute-start.8 = (f32[2,64,128]{2,1,0:T(8,128)S(1)}, f32[2,64,128]{2,1,0:T(8,128)S(1)}, u32[]{:S(2)}, u32[]{:S(2)}) collective-permute-start(f32[2,64,128]{2,1,0:T(8,128)S(1)} %get-tuple-element.29.refs_0_), channel_id=1, source_target_pairs={{0,1},{1,0},{2,3},{3,2},{4,5},{5,4},{6,7},{7,6},{8,9},{9,8},{10,11... | collective-permute-start | bytes 196616 | tf_op jit(solution)/shard_map/ppermute | solution.py:244
  33.9 9.8 %collective-permute-start.7 = (f32[1,2,128,128]{3,2,1,0:T(8,128)S(1)}, f32[1,2,128,128]{3,2,1,0:T(8,128)S(1)}, u32[]{:S(2)}, u32[]{:S(2)}) collective-permute-start(f32[1,2,128,128]{3,2,1,0:T(8,128)S(1)} %get-tuple-element.28), channel_id=1, source_target_pairs={{0,1},{1,2},{2,3},{3,4},{4,5},{5,6},{6,7},{7,8},{8,9},{9,10},{10,1... | collective-permute-start | bytes 393224 | tf_op jit(solution)/shard_map/ppermute | solution.py:334
  38.6 5.7 %collective-permute-start.10 = (f32[2,64,128]{2,1,0:T(8,128)S(1)}, f32[2,64,128]{2,1,0:T(8,128)S(1)}, u32[]{:S(2)}, u32[]{:S(2)}) collective-permute-start(f32[2,64,128]{2,1,0:T(8,128)S(1)} %get-tuple-element.33.refs_1_), channel_id=1, source_target_pairs={{0,2},{1,3},{2,0},{3,1},{4,6},{5,7},{6,4},{7,5},{8,10},{9,11},{10,... | collective-permute-start | bytes 196616 | tf_op jit(solution)/shard_map/ppermute | solution.py:244
  38.7 12.6 %collective-permute-start.9 = (f32[2,2,128,128]{3,2,1,0:T(8,128)S(1)}, f32[2,2,128,128]{3,2,1,0:T(8,128)S(1)}, u32[]{:S(2)}, u32[]{:S(2)}) collective-permute-start(f32[2,2,128,128]{3,2,1,0:T(8,128)S(1)} %get-tuple-element.30), channel_id=1, source_target_pairs={{0,1},{1,2},{2,3},{3,4},{4,5},{5,6},{6,7},{7,8},{8,9},{9,10},{10,1... | collective-permute-start | bytes 786440 | tf_op jit(solution)/shard_map/ppermute | solution.py:334
  44.3 4.3 %collective-permute-start.11 = (f32[2,64,128]{2,1,0:T(8,128)S(1)}, f32[2,64,128]{2,1,0:T(8,128)S(1)}, u32[]{:S(2)}, u32[]{:S(2)}) collective-permute-start(f32[2,64,128]{2,1,0:T(8,128)S(1)} %step.7.refs_1_), channel_id=1, source_target_pairs={{0,4},{1,5},{2,6},{3,7},{4,0},{5,1},{6,2},{7,3},{8,12},{9,13},{10,... | collective-permute-start | bytes 196616 | tf_op jit(solution)/shard_map/ppermute | solution.py:244
  48.6 5.2 %collective-permute-start.12 = (f32[2,64,128]{2,1,0:T(8,128)S(1)}, f32[2,64,128]{2,1,0:T(8,128)S(1)}, u32[]{:S(2)}, u32[]{:S(2)}) collective-permute-start(f32[2,64,128]{2,1,0:T(8,128)S(1)} %step.8.refs_1_), channel_id=1, source_target_pairs={{0,8},{1,9},{2,10},{3,11},{4,12},{5,13},{6,14},{7,15},{8,0},{9,1},... | collective-permute-start | bytes 196616 | tf_op jit(solution)/shard_map/ppermute | solution.py:244

commit v10 on v9

--- a/solution.py
+++ b/solution.py
@@ -46,15 +46,15 @@
 
 def times_left(high, low, x):
     x_high, x_low = halves(x)
-    return dot(jnp.concatenate([high, high, low], axis=1), jnp.concatenate([x_high, x_low, x_high], axis=0))
+    y = dot(jnp.concatenate([high, high, low], axis=1), jnp.concatenate([x_high, x_low, x_high], axis=0))
+    n = x.shape[0]
+    return y[:n, :n] - y[n:, n:], y[:n, n:] + y[n:, :n]
 
 
 def both_sides(re, im, tables, which):
     n = re.shape[0]
     y = times_right(jnp.concatenate([re, im], axis=1), tables[which ^ 1, 0], tables[which ^ 1, 1])
-    y = jnp.concatenate([y[:, :n], y[:, n:]], axis=0)
-    z = times_left(tables[which, 0], tables[which, 1], y)
-    return z[:n], z[n:]
+    return times_left(tables[which, 0, :, :n], tables[which, 1, :, :n], y)
 
 
 def share(offsets, tile_rows):
@@ -256,7 +256,7 @@
 
     offsets = jnp.concatenate([row_offsets, col_offsets])
     offsets_prev = lax.ppermute(offsets, "scan", [(i, (i + 1) % scan_count) for i in range(scan_count)])
-    far = across(intensity, 0, 0, 1)
+    far = across(intensity, 1, 0, 1)
     window = jax.ShapeDtypeStruct((slab, 2, n, n), f32)
     whole = jax.ShapeDtypeStruct(objects.shape, f32)
     tiles, window_b = call(own_kernel, "own", [offsets], [objects], [whole, window])

time: 54.7 us -> 57.6 us (1.053)
  starting transfers between devices: 16.7 us -> 19.8 us
    ppermute x1, starting transfers between devices: 4.85 us -> 1.29 us  [across(): return lax.ppermute(x, ('depth', 'scan'), route)]
    ppermute x1, waiting for transfers between devices: 4.57 us -> 6.95 us  [body(): lax.ppermute(halo, 'scan', [((i + 1) % scan_count, i) for i in range(scan...]
    ppermute x4, starting transfers between devices: 2.88 us -> 4.67 us  [sum_round(): return lax.ppermute(x, ('depth', 'scan'), route)]
    ppermute x4, waiting for transfers between devices: 7.47 us -> 5.77 us  [sum_round(): return lax.ppermute(x, ('depth', 'scan'), route)]
    ppermute x1, starting transfers between devices: 1.38 us -> 2.98 us  [body(): lax.ppermute(halo, 'scan', [((i + 1) % scan_count, i) for i in range(scan...]
    ppermute x1, starting transfers between devices: 1.49 us -> 2.94 us  [body(): lax.ppermute(offsets, 'scan', [(i, (i + 1) % scan_count) for i in range(s...]
    ppermute x2, starting transfers between devices: 2.94 us -> 4.01 us  [body(): spill += [lax.ppermute(x, 'scan', ahead) for x in payload]]
    ppermute x2, waiting for transfers between devices: 4.13 us -> 3.23 us  [body(): spill += [lax.ppermute(x, 'scan', ahead) for x in payload]]
where the time goes in v10:
time: 57.6 us; the launch traced here: 57.2 us
  waiting for transfers between devices  22.1 us (38%)
  starting transfers between devices  19.8 us (34%)
  Pallas kernels  12.6 us (22%)
  local copies, waits for them, and re-layouts  1.14 us (2%)
  between operations  0.76 us (1%)
  other arithmetic  0.75 us (1%)
    pallas_call x12, Pallas kernels, call(): pl.pallas_call(kernel, name=name, out_shape=outs, in_specs=[pl.BlockSpec(...  12.6 us
    ppermute x1, waiting for transfers between devices, body(): lax.ppermute(halo, 'scan', [((i + 1) % scan_count, i) for i in range(scan...  6.95 us
    ppermute x4, waiting for transfers between devices, sum_round(): return lax.ppermute(x, ('depth', 'scan'), route)  5.77 us
    ppermute x4, starting transfers between devices, sum_round(): return lax.ppermute(x, ('depth', 'scan'), route)  4.67 us
    ppermute x2, starting transfers between devices, body(): spill += [lax.ppermute(x, 'scan', ahead) for x in payload]  4.01 us
    ppermute x1, waiting for transfers between devices, body(): lax.ppermute(offsets, 'scan', [(i, (i + 1) % scan_count) for i in range(s...  3.54 us
    ppermute x2, starting transfers between devices, gathered(): lax.ppermute(x, 'depth', [((target - j) % depth_count, target)])  3.32 us
    ppermute x2, waiting for transfers between devices, body(): spill += [lax.ppermute(x, 'scan', ahead) for x in payload]  3.23 us
  transfers between devices with their start and end apart: 13, of which 9 were waited for; matrix products, arithmetic and copies ran while one was open for 1% of the time, Pallas kernels for 8%

profile of v10, /device:TPU:0, one launch (start us, length us, event | category | flops | bytes accessed | tf_op | source)
XLA Modules:
  0.0 57.2 jit_solution(9933039285698247858)
XLA Ops:
  0.6 1.3 %collective-permute-start.1 = (f32[2,128,128]{2,1,0:T(8,128)}, f32[2,128,128]{2,1,0:T(8,128)S(1)}, u32[]{:S(2)}, u32[]{:S(2)}) collective-permute-start(f32[2,128,128]{2,1,0:T(8,128)} %intensity.1), channel_id=1, source_target_pairs={{16,1},{17,2},{18,3},{19,4},{20,5},{21,6},{22,7},{23,8},{24,9},{25... | collective-permute-start | bytes 393224 | tf_op jit(solution)/shard_map/ppermute | solution.py:255
  1.9 0.7 %pad_add_fusion.offsets.refs_0_ = s32[4]{0:T(128)S(1)} fusion(s32[2]{0:T(128)} %param.9, s32[2]{0:T(128)} %param.8), kind=kLoop, calls=%fused_computation | loop fusion | flops 4 | bytes 32 | tf_op jit(solution)/shard_map/concatenate | solution.py:257
  2.7 2.9 %collective-permute-start = (s32[4]{0:T(128)S(1)}, s32[4]{0:T(128)S(1)}, u32[]{:S(2)}, u32[]{:S(2)}) collective-permute-start(s32[4]{0:T(128)S(1)} %pad_add_fusion.offsets.refs_0_), channel_id=1, source_target_pairs={{0,1},{1,2},{2,3},{3,4},{4,5},{5,6},{6,7},{7,8},{8,9},{9,10},{10,1... | collective-permute-start | bytes 56 | tf_op jit(solution)/shard_map/ppermute | solution.py:258
  5.6 0.0 copy-start
  5.6 1.1 %copy-done = f32[3,2,128,256]{3,2,1,0:T(8,128)S(1)} copy-done((f32[3,2,128,256]{3,2,1,0:T(8,128)S(1)}, f32[3,2,128,256]{3,2,1,0:T(8,128)}, u32[]{:S(2)}) %copy-start) | copy-done | bytes 786456
  6.8 0.8 %own.1 = (f32[3,2,128,256]{3,2,1,0:T(8,128)S(1)}, f32[3,2,128,128]{3,2,1,0:T(8,128)S(1)}) custom-call(s32[4]{0:T(128)S(1)} %pad_add_fusion.offsets.refs_0_, f32[3,2,128,256]{3,2,1,0:T(8,128)S(1)} %copy-done), custom_call_target="tpu_custom_call" | custom-call | flops 1000000000 | bytes 1966080 | tf_op jit(solution)/shard_map/own/pallas_call | solution.py:223
  7.6 3.5 %collective-permute-done.offsets_prev.refs_1_ = s32[4]{0:T(128)S(1)} collective-permute-done((s32[4]{0:T(128)S(1)}, s32[4]{0:T(128)S(1)}, u32[]{:S(2)}, u32[]{:S(2)}) %collective-permute-start) | collective-permute-done | bytes 48 | tf_op jit(solution)/shard_map/ppermute | solution.py:258
  11.1 0.0 collective-permute-done.1.far.after
  11.1 0.0 copy-start.1
  11.1 0.0 copy-start.2
  11.1 1.0 %prev.1 = (f32[3,2,128,128]{3,2,1,0:T(8,128)S(1)}, f32[3,2,128,128]{3,2,1,0:T(8,128)S(1)}) custom-call(s32[4]{0:T(128)S(1)} %collective-permute-done.offsets_prev.refs_1_, f32[2,128,128]{2,1,0:T(8,128)S(1)} %collective-permute-done.1.far.after, f32[3,2,128,256]{3,2,1,0:T(8,128)S(1)} %get-tuple-element.20.tiles), custom_call_target="tpu_custom_call" | custom-call | flops 1000000000 | bytes 1572864 | tf_op jit(solution)/shard_map/prev/pallas_call | solution.py:223
  12.2 3.0 %collective-permute-start.2 = (f32[3,2,128,128]{3,2,1,0:T(8,128)S(1)}, f32[3,2,128,128]{3,2,1,0:T(8,128)S(1)}, u32[]{:S(2)}, u32[]{:S(2)}) collective-permute-start(f32[3,2,128,128]{3,2,1,0:T(8,128)S(1)} %get-tuple-element.23), channel_id=1, source_target_pairs={{1,0},{2,1},{3,2},{4,3},{5,4},{6,5},{7,6},{8,7},{9,8},{10,9},{11,1... | collective-permute-start | bytes 1179656 | tf_op jit(solution)/shard_map/ppermute | solution.py:264
  15.2 1.3 %collective-permute-start.3 = (f32[3,2,128,128]{3,2,1,0:T(8,128)S(1)}, f32[3,2,128,128]{3,2,1,0:T(8,128)S(1)}, u32[]{:S(2)}, u32[]{:S(2)}) collective-permute-start(f32[3,2,128,128]{3,2,1,0:T(8,128)S(1)} %get-tuple-element.21.refs_4_), channel_id=1, source_target_pairs={{16,0},{17,1},{18,2},{19,3},{20,4},{21,5},{22,6},{23,7},{24,8},{25... | collective-permute-start | bytes 1179656 | tf_op jit(solution)/shard_map/ppermute | solution.py:267
  16.4 0.0 copy-done.1
  16.5 0.0 copy-done.2
  16.5 0.6 load.1
  17.0 6.9 %collective-permute-done.2.halo = f32[3,2,128,128]{3,2,1,0:T(8,128)S(1)} collective-permute-done((f32[3,2,128,128]{3,2,1,0:T(8,128)S(1)}, f32[3,2,128,128]{3,2,1,0:T(8,128)S(1)}, u32[]{:S(2)}, u32[]{:S(2)}) %collective-permute-start.2) | collective-permute-done | bytes 393248 | tf_op jit(solution)/shard_map/ppermute | solution.py:264
  24.0 0.0 copy-start.3
  24.0 0.6 %join.1.refs_5_ = f32[3,2,128,128]{3,2,1,0:T(8,128)S(1)} custom-call(s32[4]{0:T(128)S(1)} %pad_add_fusion.offsets.refs_0_, f32[128,128]{1,0:T(8,128)S(1)} %get-tuple-element.19.after.refs_3_, f32[3,2,128,128]{3,2,1,0:T(8,128)S(1)} %get-tuple-element.22.window_b, f32[3,2,128,128]{3,2,1,0:T(8,128)S(1)} %collective-permute-done.2.halo), custom_call_target="tpu_custom_call" | custom-call | flops 1000000000 | bytes 1179648 | tf_op jit(solution)/shard_map/join/pallas_call | solution.py:223
  24.6 2.0 %collective-permute-start.4 = (f32[3,2,128,128]{3,2,1,0:T(8,128)S(1)}, f32[3,2,128,128]{3,2,1,0:T(8,128)S(1)}, u32[]{:S(2)}, u32[]{:S(2)}) collective-permute-start(f32[3,2,128,128]{3,2,1,0:T(8,128)S(1)} %join.1.refs_5_), channel_id=1, source_target_pairs={{0,16},{1,17},{2,18},{3,19},{4,20},{5,21},{6,22},{7,23},{8,24},{9,... | collective-permute-start | bytes 1179656 | tf_op jit(solution)/shard_map/ppermute | solution.py:267
  26.6 0.0 collective-permute-done.3.refs_6_
  26.6 1.3 %collective-permute-done.4.refs_7_ = f32[3,2,128,128]{3,2,1,0:T(8,128)S(1)} collective-permute-done((f32[3,2,128,128]{3,2,1,0:T(8,128)S(1)}, f32[3,2,128,128]{3,2,1,0:T(8,128)S(1)}, u32[]{:S(2)}, u32[]{:S(2)}) %collective-permute-start.4) | collective-permute-done | bytes 393248 | tf_op jit(solution)/shard_map/ppermute | solution.py:267
  27.9 0.0 copy-done.3
  27.9 6.4 %wave.1 = (f32[3,2,128,128]{3,2,1,0:T(8,128)S(1)}, f32[3,2,128,128]{3,2,1,0:T(8,128)S(1)}, f32[2,64,128]{2,1,0:T(8,128)S(1)}, f32[2,64,128]{2,1,0:T(8,128)S(1)}) custom-call(s32[4]{0:T(128)S(1)} %pad_add_fusion.offsets.refs_0_, bf16[4,2,256,256]{3,2,1,0:T(8,128)(2,1)S(1)} %copy-done.3, f32[2,128,128]{2,1,0:T(8,128)S(1)} %get-tuple-element.18.refs_2_, ...), custom_call_target="tpu_custom_call" | custom-call | flops 5000000000 | bytes 3735552 | tf_op jit(solution)/shard_map/wave/pallas_call | solution.py:223
  34.4 0.4 collective-permute-start.5
  34.8 0.1 collective-permute-start.6
  34.9 1.3 %collective-permute-done.6.refs_1_ = f32[2,64,128]{2,1,0:T(8,128)S(1)} collective-permute-done((f32[2,64,128]{2,1,0:T(8,128)S(1)}, f32[2,64,128]{2,1,0:T(8,128)S(1)}, u32[]{:S(2)}, u32[]{:S(2)}) %collective-permute-start.6) | collective-permute-done | bytes 65568 | tf_op jit(solution)/shard_map/ppermute | solution.py:296
  36.2 0.0 collective-permute-done.5.refs_3_
  36.3 0.1 collective-permute-start.8
  36.4 2.0 %collective-permute-start.7 = (f32[1,2,128,128]{3,2,1,0:T(8,128)S(1)}, f32[1,2,128,128]{3,2,1,0:T(8,128)S(1)}, u32[]{:S(2)}, u32[]{:S(2)}) collective-permute-start(f32[1,2,128,128]{3,2,1,0:T(8,128)S(1)} %get-tuple-element.28), channel_id=1, source_target_pairs={{0,1},{1,2},{2,3},{3,4},{4,5},{5,6},{6,7},{7,8},{8,9},{9,10},{10,1... | collective-permute-start | bytes 393224 | tf_op jit(solution)/shard_map/ppermute | solution.py:334
  38.4 2.6 %collective-permute-done.8.refs_1_ = f32[2,64,128]{2,1,0:T(8,128)S(1)} collective-permute-done((f32[2,64,128]{2,1,0:T(8,128)S(1)}, f32[2,64,128]{2,1,0:T(8,128)S(1)}, u32[]{:S(2)}, u32[]{:S(2)}) %collective-permute-start.8) | collective-permute-done | bytes 65568 | tf_op jit(solution)/shard_map/ppermute | solution.py:244
  41.0 0.1 collective-permute-start.10
  41.1 2.0 %collective-permute-start.9 = (f32[2,2,128,128]{3,2,1,0:T(8,128)S(1)}, f32[2,2,128,128]{3,2,1,0:T(8,128)S(1)}, u32[]{:S(2)}, u32[]{:S(2)}) collective-permute-start(f32[2,2,128,128]{3,2,1,0:T(8,128)S(1)} %get-tuple-element.30), channel_id=1, source_target_pairs={{0,1},{1,2},{2,3},{3,4},{4,5},{5,6},{6,7},{7,8},{8,9},{9,10},{10,1... | collective-permute-start | bytes 786440 | tf_op jit(solution)/shard_map/ppermute | solution.py:334
  43.2 3.2 %collective-permute-done.7.refs_0_ = f32[1,2,128,128]{3,2,1,0:T(8,128)S(1)} collective-permute-done((f32[1,2,128,128]{3,2,1,0:T(8,128)S(1)}, f32[1,2,128,128]{3,2,1,0:T(8,128)S(1)}, u32[]{:S(2)}, u32[]{:S(2)}) %collective-permute-start.7) | collective-permute-done | bytes 131104 | tf_op jit(solution)/shard_map/ppermute | solution.py:334
  46.4 0.5 collective-permute-done.10.refs_2_
  47.0 2.0 %collective-permute-start.11 = (f32[2,64,128]{2,1,0:T(8,128)S(1)}, f32[2,64,128]{2,1,0:T(8,128)S(1)}, u32[]{:S(2)}, u32[]{:S(2)}) collective-permute-start(f32[2,64,128]{2,1,0:T(8,128)S(1)} %step.7.refs_1_), channel_id=1, source_target_pairs={{0,4},{1,5},{2,6},{3,7},{4,0},{5,1},{6,2},{7,3},{8,12},{9,13},{10,... | collective-permute-start | bytes 196616 | tf_op jit(solution)/shard_map/ppermute | solution.py:244
  48.9 0.9 %place.1.before.refs_0_ = f32[3,2,128,256]{3,2,1,0:T(8,128)S(1)} custom-call(s32[4]{0:T(128)S(1)} %pad_add_fusion.offsets.refs_0_, s32[4]{0:T(128)S(1)} %collective-permute-done.offsets_prev.refs_1_, f32[3,2,128,128]{3,2,1,0:T(8,128)S(1)} %get-tuple-element.24.refs_2_, f32[3,2,128,128]{3,2,1,0:T(8,128)S(1)} %collective-permute-done.5.refs_3_), custom_call_target="tpu_custom_call" | custom-call | flops 2000000000 | bytes 1572864 | tf_op jit(solution)/shard_map/place/pallas_call | solution.py:223
  49.8 1.5 %collective-permute-done.11.refs_2_ = f32[2,64,128]{2,1,0:T(8,128)S(1)} collective-permute-done((f32[2,64,128]{2,1,0:T(8,128)S(1)}, f32[2,64,128]{2,1,0:T(8,128)S(1)}, u32[]{:S(2)}, u32[]{:S(2)}) %collective-permute-start.11) | collective-permute-done | bytes 65568 | tf_op jit(solution)/shard_map/ppermute | solution.py:244
  51.3 2.5 %collective-permute-start.12 = (f32[2,64,128]{2,1,0:T(8,128)S(1)}, f32[2,64,128]{2,1,0:T(8,128)S(1)}, u32[]{:S(2)}, u32[]{:S(2)}) collective-permute-start(f32[2,64,128]{2,1,0:T(8,128)S(1)} %step.8.refs_1_), channel_id=1, source_target_pairs={{0,8},{1,9},{2,10},{3,11},{4,12},{5,13},{6,14},{7,15},{8,0},{9,1},... | collective-permute-start | bytes 196616 | tf_op jit(solution)/shard_map/ppermute | solution.py:244
  53.8 0.0 collective-permute-done.9.refs_1_
  53.8 1.6 %spill.1 = (f32[3,2,128,256]{3,2,1,0:T(8,128)}, f32[8,128]{1,0:T(8,128)S(1)}) custom-call(s32[4]{0:T(128)S(1)} %collective-permute-done.offsets_prev.refs_1_, f32[3,2,128,256]{3,2,1,0:T(8,128)S(1)} %place.1.before.refs_0_, f32[1,2,128,128]{3,2,1,0:T(8,128)S(1)} %collective-permute-done.7.refs_0_, f32[2,2,128,128]{3,2,1,0:T(8,128)S(1)} %collective-permute-done.9.refs_1_), custom_call_target="tpu_custom_call" | custom-call | flops 1000000000 | bytes 1970176 | tf_op jit(solution)/shard_map/spill/pallas_call | solution.py:223
  55.4 1.1 %collective-permute-done.12.refs_2_ = f32[2,64,128]{2,1,0:T(8,128)S(1)} collective-permute-done((f32[2,64,128]{2,1,0:T(8,128)S(1)}, f32[2,64,128]{2,1,0:T(8,128)S(1)}, u32[]{:S(2)}, u32[]{:S(2)}) %collective-permute-start.12) | collective-permute-done | bytes 65568 | tf_op jit(solution)/shard_map/ppermute | solution.py:244
  56.5 0.6 %step.9 = f32[2,64,128]{2,1,0:T(8,128)} custom-call(f32[8,128]{1,0:T(8,128)S(1)} %get-tuple-element.32.refs_0_, f32[2,64,128]{2,1,0:T(8,128)S(1)} %step.8.refs_1_, f32[2,64,128]{2,1,0:T(8,128)S(1)} %collective-permute-done.12.refs_2_), custom_call_target="tpu_custom_call" | custom-call | flops 1000000000 | bytes 196608 | tf_op jit(solution)/shard_map/step/pallas_call | solution.py:223
  (4 shorter events, 0.1 us)
Async XLA Ops:
  0.6 10.5 %collective-permute-start.1 = (f32[2,128,128]{2,1,0:T(8,128)}, f32[2,128,128]{2,1,0:T(8,128)S(1)}, u32[]{:S(2)}, u32[]{:S(2)}) collective-permute-start(f32[2,128,128]{2,1,0:T(8,128)} %intensity.1), channel_id=1, source_target_pairs={{16,1},{17,2},{18,3},{19,4},{20,5},{21,6},{22,7},{23,8},{24,9},{25... | collective-permute-start | bytes 393224 | tf_op jit(solution)/shard_map/ppermute | solution.py:255
  2.7 8.4 %collective-permute-start = (s32[4]{0:T(128)S(1)}, s32[4]{0:T(128)S(1)}, u32[]{:S(2)}, u32[]{:S(2)}) collective-permute-start(s32[4]{0:T(128)S(1)} %pad_add_fusion.offsets.refs_0_), channel_id=1, source_target_pairs={{0,1},{1,2},{2,3},{3,4},{4,5},{5,6},{6,7},{7,8},{8,9},{9,10},{10,1... | collective-permute-start | bytes 56 | tf_op jit(solution)/shard_map/ppermute | solution.py:258
  5.6 1.1 %copy-start = (f32[3,2,128,256]{3,2,1,0:T(8,128)S(1)}, f32[3,2,128,256]{3,2,1,0:T(8,128)}, u32[]{:S(2)}) copy-start(f32[3,2,128,256]{3,2,1,0:T(8,128)} %objects.1) | copy-start | bytes 2359300
  11.1 5.3 %copy-start.1 = (f32[2,128,128]{2,1,0:T(8,128)S(1)}, f32[2,128,128]{2,1,0:T(8,128)}, u32[]{:S(2)}) copy-start(f32[2,128,128]{2,1,0:T(8,128)} %intensity.1) | copy-start | bytes 393220
  11.1 5.3 %copy-start.2 = (f32[2,128,128]{2,1,0:T(8,128)S(1)}, f32[2,128,128]{2,1,0:T(8,128)}, u32[]{:S(2)}) copy-start(f32[2,128,128]{2,1,0:T(8,128)} %probe.1) | copy-start | bytes 393220
  12.2 11.8 %collective-permute-start.2 = (f32[3,2,128,128]{3,2,1,0:T(8,128)S(1)}, f32[3,2,128,128]{3,2,1,0:T(8,128)S(1)}, u32[]{:S(2)}, u32[]{:S(2)}) collective-permute-start(f32[3,2,128,128]{3,2,1,0:T(8,128)S(1)} %get-tuple-element.23), channel_id=1, source_target_pairs={{1,0},{2,1},{3,2},{4,3},{5,4},{6,5},{7,6},{8,7},{9,8},{10,9},{11,1... | collective-permute-start | bytes 1179656 | tf_op jit(solution)/shard_map/ppermute | solution.py:264
  15.2 11.5 %collective-permute-start.3 = (f32[3,2,128,128]{3,2,1,0:T(8,128)S(1)}, f32[3,2,128,128]{3,2,1,0:T(8,128)S(1)}, u32[]{:S(2)}, u32[]{:S(2)}) collective-permute-start(f32[3,2,128,128]{3,2,1,0:T(8,128)S(1)} %get-tuple-element.21.refs_4_), channel_id=1, source_target_pairs={{16,0},{17,1},{18,2},{19,3},{20,4},{21,5},{22,6},{23,7},{24,8},{25... | collective-permute-start | bytes 1179656 | tf_op jit(solution)/shard_map/ppermute | solution.py:267
  24.0 4.0 %copy-start.3 = (bf16[4,2,256,256]{3,2,1,0:T(8,128)(2,1)S(1)}, bf16[4,2,256,256]{3,2,1,0:T(8,128)(2,1)}, u32[]{:S(2)}) copy-start(bf16[4,2,256,256]{3,2,1,0:T(8,128)(2,1)} %constant.2.clone.refs_1_) | copy-start | bytes 3145732
  24.6 3.4 %collective-permute-start.4 = (f32[3,2,128,128]{3,2,1,0:T(8,128)S(1)}, f32[3,2,128,128]{3,2,1,0:T(8,128)S(1)}, u32[]{:S(2)}, u32[]{:S(2)}) collective-permute-start(f32[3,2,128,128]{3,2,1,0:T(8,128)S(1)} %join.1.refs_5_), channel_id=1, source_target_pairs={{0,16},{1,17},{2,18},{3,19},{4,20},{5,21},{6,22},{7,23},{8,24},{9,... | collective-permute-start | bytes 1179656 | tf_op jit(solution)/shard_map/ppermute | solution.py:267
  34.4 1.9 %collective-permute-start.5 = (f32[3,2,128,128]{3,2,1,0:T(8,128)S(1)}, f32[3,2,128,128]{3,2,1,0:T(8,128)S(1)}, u32[]{:S(2)}, u32[]{:S(2)}) collective-permute-start(f32[3,2,128,128]{3,2,1,0:T(8,128)S(1)} %get-tuple-element.25), channel_id=1, source_target_pairs={{0,16},{16,0},{1,17},{17,1},{2,18},{18,2},{3,19},{19,3},{4,20},{20... | collective-permute-start | bytes 1179656 | tf_op jit(solution)/shard_map/ppermute | solution.py:297
  34.8 1.4 %collective-permute-start.6 = (f32[2,64,128]{2,1,0:T(8,128)S(1)}, f32[2,64,128]{2,1,0:T(8,128)S(1)}, u32[]{:S(2)}, u32[]{:S(2)}) collective-permute-start(f32[2,64,128]{2,1,0:T(8,128)S(1)} %get-tuple-element.27), channel_id=1, source_target_pairs={{0,16},{16,0},{1,17},{17,1},{2,18},{18,2},{3,19},{19,3},{4,20},{20... | collective-permute-start | bytes 196616 | tf_op jit(solution)/shard_map/ppermute | solution.py:296
  36.3 4.7 %collective-permute-start.8 = (f32[2,64,128]{2,1,0:T(8,128)S(1)}, f32[2,64,128]{2,1,0:T(8,128)S(1)}, u32[]{:S(2)}, u32[]{:S(2)}) collective-permute-start(f32[2,64,128]{2,1,0:T(8,128)S(1)} %get-tuple-element.29.refs_0_), channel_id=1, source_target_pairs={{0,1},{1,0},{2,3},{3,2},{4,5},{5,4},{6,7},{7,6},{8,9},{9,8},{10,11... | collective-permute-start | bytes 196616 | tf_op jit(solution)/shard_map/ppermute | solution.py:244
  36.4 10.0 %collective-permute-start.7 = (f32[1,2,128,128]{3,2,1,0:T(8,128)S(1)}, f32[1,2,128,128]{3,2,1,0:T(8,128)S(1)}, u32[]{:S(2)}, u32[]{:S(2)}) collective-permute-start(f32[1,2,128,128]{3,2,1,0:T(8,128)S(1)} %get-tuple-element.28), channel_id=1, source_target_pairs={{0,1},{1,2},{2,3},{3,4},{4,5},{5,6},{6,7},{7,8},{8,9},{9,10},{10,1... | collective-permute-start | bytes 393224 | tf_op jit(solution)/shard_map/ppermute | solution.py:334
  41.0 5.9 %collective-permute-start.10 = (f32[2,64,128]{2,1,0:T(8,128)S(1)}, f32[2,64,128]{2,1,0:T(8,128)S(1)}, u32[]{:S(2)}, u32[]{:S(2)}) collective-permute-start(f32[2,64,128]{2,1,0:T(8,128)S(1)} %get-tuple-element.33.refs_1_), channel_id=1, source_target_pairs={{0,2},{1,3},{2,0},{3,1},{4,6},{5,7},{6,4},{7,5},{8,10},{9,11},{10,... | collective-permute-start | bytes 196616 | tf_op jit(solution)/shard_map/ppermute | solution.py:244
  41.1 12.7 %collective-permute-start.9 = (f32[2,2,128,128]{3,2,1,0:T(8,128)S(1)}, f32[2,2,128,128]{3,2,1,0:T(8,128)S(1)}, u32[]{:S(2)}, u32[]{:S(2)}) collective-permute-start(f32[2,2,128,128]{3,2,1,0:T(8,128)S(1)} %get-tuple-element.30), channel_id=1, source_target_pairs={{0,1},{1,2},{2,3},{3,4},{4,5},{5,6},{6,7},{7,8},{8,9},{9,10},{10,1... | collective-permute-start | bytes 786440 | tf_op jit(solution)/shard_map/ppermute | solution.py:334
  47.0 4.3 %collective-permute-start.11 = (f32[2,64,128]{2,1,0:T(8,128)S(1)}, f32[2,64,128]{2,1,0:T(8,128)S(1)}, u32[]{:S(2)}, u32[]{:S(2)}) collective-permute-start(f32[2,64,128]{2,1,0:T(8,128)S(1)} %step.7.refs_1_), channel_id=1, source_target_pairs={{0,4},{1,5},{2,6},{3,7},{4,0},{5,1},{6,2},{7,3},{8,12},{9,13},{10,... | collective-permute-start | bytes 196616 | tf_op jit(solution)/shard_map/ppermute | solution.py:244
  51.3 5.2 %collective-permute-start.12 = (f32[2,64,128]{2,1,0:T(8,128)S(1)}, f32[2,64,128]{2,1,0:T(8,128)S(1)}, u32[]{:S(2)}, u32[]{:S(2)}) collective-permute-start(f32[2,64,128]{2,1,0:T(8,128)S(1)} %step.8.refs_1_), channel_id=1, source_target_pairs={{0,8},{1,9},{2,10},{3,11},{4,12},{5,13},{6,14},{7,15},{8,0},{9,1},... | collective-permute-start | bytes 196616 | tf_op jit(solution)/shard_map/ppermute | solution.py:244

commit v11 on v10

--- a/solution.py
+++ b/solution.py
@@ -78,23 +78,41 @@
             window_b[s, p] = cut(tile, row_b, col_b, window_b.shape[-1])
 
 
-def prev_kernel(offsets_prev, after, tiles, window_a, halo):
+def halo_kernel(offsets_prev, tiles, halo):
     slab, _, rows, _ = tiles.shape
-    width = halo.shape[-1]
-    _, col_a, row_p, col_p = share(offsets_prev, rows)
-    for s in range(slab):
-        for p in range(2):
-            halo[s, p] = cut(tiles[s, p], row_p, col_p, width)
-            window_a[s, p] = cut(tiles[s, p], 0, col_a, width)
-
-
-def join_kernel(offsets, after, window_b, halo, joined):
-    slab, _, rows, cols = joined.shape
+    _, _, row_p, col_p = share(offsets_prev, rows)
+    for s in range(slab):
+        for p in range(2):
+            halo[s, p] = cut(tiles[s, p], row_p, col_p, halo.shape[-1])
+
+
+def ahead_kernel(offsets_prev, after, tiles, window_a):
+    slab, _, rows, _ = tiles.shape
+    _, col_a, _, _ = share(offsets_prev, rows)
+    for s in range(slab):
+        for p in range(2):
+            window_a[s, p] = cut(tiles[s, p], 0, col_a, window_a.shape[-1])
+
+
+def hold_kernel(count, *refs):
+    refs[count + 1][...] = refs[count][...]
+
+
+def joined(inside, window_b, halo, s, p):
+    return jnp.where(inside, window_b[s, p], halo[s, p])
+
+
+def rows_here(offsets, rows, cols):
     _, _, row_b, _ = share(offsets, rows)
-    inside = lax.broadcasted_iota(jnp.int32, (rows, cols), 0) < rows - row_b
-    for s in range(slab):
-        for p in range(2):
-            joined[s, p] = jnp.where(inside, window_b[s, p], halo[s, p])
+    return lax.broadcasted_iota(jnp.int32, (rows, cols), 0) < rows - row_b
+
+
+def join_kernel(offsets, window_b, halo, out):
+    slab, _, rows, cols = out.shape
+    inside = rows_here(offsets, rows, cols)
+    for s in range(slab):
+        for p in range(2):
+            out[s, p] = joined(inside, window_b, halo, s, p)
 
 
 def load_kernel(offsets, offsets_prev, intensity, far, probe, measured, start):
@@ -105,49 +123,69 @@
     start[...] = probe[...]
 
 
-def wave_kernel(depth_count, offsets, tables, probe, measured, window_a, window_b, *rest):
-    others_a, others_b = rest[: depth_count - 1], rest[depth_count - 1 : 2 * depth_count - 2]
-    rest = rest[2 * depth_count - 2 :]
+def enter(s, re, im, layers, waves):
+    waves[s, 0] = re
+    waves[s, 1] = im
+    o_re, o_im = layers[s, 0], layers[s, 1]
+    return re * o_re - im * o_im, re * o_im + im * o_re
+
+
+def leave(s, chi_re, chi_im, layers, waves):
+    w_re, w_im = waves[s, 0], waves[s, 1]
+    o_re, o_im = layers[s, 0], layers[s, 1]
+    waves[s, 0] = w_re * chi_re + w_im * chi_im
+    waves[s, 1] = w_re * chi_im - w_im * chi_re
+    return o_re * chi_re + o_im * chi_im, o_re * chi_im - o_im * chi_re
+
+
+def steps(count, body, start):
+    return lax.fori_loop(0, count, body, start, unroll=True if count <= 8 else 1)
+
+
+def first_kernel(after, tables, probe, window_a, window_b, layers, waves, state):
+    on_a = lax.axis_index("depth") == 0
+    slab = layers.shape[0]
+    for s in range(slab):
+        for p in range(2):
+            layers[s, p] = jnp.where(on_a, window_a[s, p], window_b[s, p])
+
+    def forward(s, wave):
+        return both_sides(*enter(s, *wave, layers, waves), tables, 0)
+
+    state[0], state[1] = steps(slab, forward, (probe[0], probe[1]))
+
+
+def wave_kernel(depth_count, offsets, tables, state, measured, layers_0, waves_0, window_b, halo, *rest):
+    others_a, others_b = rest[: depth_count - 1], rest[depth_count - 1 : 2 * depth_count - 3]
+    rest = rest[2 * depth_count - 3 :]
     grads, probe_parts = rest[:depth_count], rest[depth_count : 2 * depth_count]
     layers, waves = rest[2 * depth_count :]
-    slab = window_a.shape[0]
-    n = probe.shape[-1]
+    slab, n = window_b.shape[0], state.shape[-1]
     count = slab * depth_count
     depth = lax.axis_index("depth")
     on_a = depth == 0
-    for j in range(depth_count):
-        base = lax.rem(depth - j + depth_count, depth_count) * slab
-        of_a, of_b = ((window_a, *others_a)[j], (window_b, *others_b)[j])
+    inside = rows_here(offsets, n, n)
+    for s in range(slab):
+        layers[s] = layers_0[s]
+        waves[s] = waves_0[s]
+    for q in range(1, depth_count):
         for s in range(slab):
             for p in range(2):
-                layers[base + s, p] = jnp.where(on_a, of_a[s, p], of_b[s, p])
-
-    def enter(s, re, im):
-        waves[s, 0] = re
-        waves[s, 1] = im
-        o_re, o_im = layers[s, 0], layers[s, 1]
-        return re * o_re - im * o_im, re * o_im + im * o_re
-
-    def forward(s, wave):
-        return both_sides(*enter(s, *wave), tables, 0)
-
-    wave = lax.fori_loop(0, count - 1, forward, (probe[0], probe[1]), unroll=True if count <= 8 else 1)
-    far_re, far_im = both_sides(*enter(count - 1, *wave), tables, 2)
+                of_b = joined(inside, window_b, halo, s, p) if q == 1 else others_b[depth_count - 1 - q][s, p]
+                layers[q * slab + s, p] = jnp.where(on_a, others_a[depth_count - 1 - q][s, p], of_b)
+
+    def forward(t, wave):
+        return both_sides(*enter(slab + t, *wave, layers, waves), tables, 0)
+
+    wave = steps(count - 1 - slab, forward, (state[0], state[1]))
+    far_re, far_im = both_sides(*enter(count - 1, *wave, layers, waves), tables, 2)
     misfit = 2.0 * (far_re * far_re + far_im * far_im - measured[...])
     chi = both_sides(misfit * far_re, misfit * far_im, tables, 3)
 
-    def leave(s, chi_re, chi_im):
-        w_re, w_im = waves[s, 0], waves[s, 1]
-        o_re, o_im = layers[s, 0], layers[s, 1]
-        waves[s, 0] = w_re * chi_re + w_im * chi_im
-        waves[s, 1] = w_re * chi_im - w_im * chi_re
-        return o_re * chi_re + o_im * chi_im, o_re * chi_im - o_im * chi_re
-
     def backward(t, chi):
-        return both_sides(*leave(count - 1 - t, *chi), tables, 1)
-
-    chi = lax.fori_loop(0, count - 1, backward, chi, unroll=True if count <= 8 else 1)
-    grad = leave(0, *chi)
+        return both_sides(*leave(count - 1 - t, *chi, layers, waves), tables, 1)
+
+    grad = leave(0, *steps(count - 1, backward, chi), layers, waves)
     _, _, row_b, _ = share(offsets, n)
     turn = lax.rem(jnp.where(on_a, 0, row_b), n)
     for j in range(depth_count):
@@ -256,17 +294,21 @@
 
     offsets = jnp.concatenate([row_offsets, col_offsets])
     offsets_prev = lax.ppermute(offsets, "scan", [(i, (i + 1) % scan_count) for i in range(scan_count)])
-    far = across(intensity, 1, 0, 1)
+    far = across(intensity, 0, 0, 1)
     window = jax.ShapeDtypeStruct((slab, 2, n, n), f32)
     whole = jax.ShapeDtypeStruct(objects.shape, f32)
     tiles, window_b = call(own_kernel, "own", [offsets], [objects], [whole, window])
-    window_a, halo = call(prev_kernel, "prev", [offsets_prev], [tiles], [window] * 2, after=[far])
-    halo = lax.ppermute(halo, "scan", [((i + 1) % scan_count, i) for i in range(scan_count)])
-
-    def gathered(x, target):
-        return [lax.ppermute(x, "depth", [((target - j) % depth_count, target)]) for j in range(1, depth_count)]
-
-    others_a = gathered(window_a, 0)
+    (halo,) = call(halo_kernel, "halo", [offsets_prev], [tiles], [window])
+    (window_a,) = call(ahead_kernel, "ahead", [offsets_prev], [tiles], [window], after=[halo])
+
+    others_a = [lax.ppermute(window_a, "depth", [(-j % depth_count, 0)]) for j in range(1, depth_count)]
+    halo_0 = across(halo, 0, 0, -1)
+    waits = [*others_a, far]
+    (halo,) = call(lambda *refs: hold_kernel(len(waits), *refs), "hold", [], [halo], [window], after=waits)
+    route = [
+        (d * scan_count + (i + 1) % scan_count, d * scan_count + i) for d in range(1, depth_count) for i in range(scan_count)
+    ]
+    halo = lax.ppermute(halo, ("depth", "scan"), route)
     measured, start = call(
         load_kernel,
         "load",
@@ -274,17 +316,28 @@
         [intensity, far, probe],
         [jax.ShapeDtypeStruct((n, n), f32), jax.ShapeDtypeStruct(probe.shape, f32)],
     )
-
-    (window_b,) = call(join_kernel, "join", [offsets], [window_b, halo], [window], after=[measured])
-    others_b = gathered(window_b, 1)
-
+    (first_b,) = call(join_kernel, "join", [offsets], [window_b, halo_0], [window])
+    first_b = lax.ppermute(first_b, "depth", [(0, 1)])
     tables = jnp.asarray(constant_tables(n))
+    layers, waves, state = call(
+        first_kernel,
+        "first",
+        [],
+        [tables, start, window_a, first_b],
+        [window, window, jax.ShapeDtypeStruct((2, n, n), f32)],
+        work=2 * 10**9,
+        after=[measured],
+    )
+    others_b = []
+    if depth_count > 2:
+        (third_b,) = call(join_kernel, "join", [offsets], [window_b, halo], [window])
+        others_b = [lax.ppermute(third_b, "depth", [((1 - j) % depth_count, 1)]) for j in range(2, depth_count)]
     count = slab * depth_count
     parts = call(
         lambda *refs: wave_kernel(depth_count, *refs),
         "wave",
         [offsets],
-        [tables, start, measured, window_a, window_b, *others_a, *others_b],
+        [tables, state, measured, layers, waves, window_b, halo, *others_a, *others_b],
         [window] * depth_count + [jax.ShapeDtypeStruct((2, n // depth_count, n), f32)] * depth_count,
         [pltpu.VMEM((count, 2, n, n), f32)] * 2,
         work=5 * 10**9,

time: 57.6 us -> 58.6 us (1.017)
  waiting for transfers between devices: 22.1 us -> 24.3 us
  starting transfers between devices: 19.8 us -> 17.8 us
  Pallas kernels: 12.6 us -> 13.4 us
    ppermute x3, waiting for transfers between devices: 8.25 us -> 0.01 us  [the longest x1 0.01 us: body(): lax.ppermute(window_a, 'depth', [(-j % depth_count, 0)])]
    ppermute x1 -> x2, waiting for transfers between devices: 0.01 us -> 6.56 us  [across(): return lax.ppermute(x, ('depth', 'scan'), route)]
    ppermute x1 -> x2, starting transfers between devices: 1.29 us -> 5.98 us  [across(): return lax.ppermute(x, ('depth', 'scan'), route)]
    ppermute x4, waiting for transfers between devices: 5.77 us -> 8.56 us  [sum_round(): return lax.ppermute(x, ('depth', 'scan'), route)]
    ppermute x3, starting transfers between devices: 6.3 us -> 3.56 us  [the longest x1 1.45 us: body(): first_b = lax.ppermute(first_b, 'depth', [(0, 1)])]
    ppermute x4, starting transfers between devices: 4.67 us -> 2.11 us  [sum_round(): return lax.ppermute(x, ('depth', 'scan'), route)]
    ppermute x2, starting transfers between devices: 4.01 us -> 2.69 us  [body(): spill += [lax.ppermute(x, 'scan', ahead) for x in payload]]
    ppermute x2, waiting for transfers between devices: 3.23 us -> 4.36 us  [body(): spill += [lax.ppermute(x, 'scan', ahead) for x in payload]]
  transfers between devices with their start and end apart: 13 -> 14, of which waited for: 9 -> 9; matrix products, arithmetic and copies ran while one was open for 1% -> 0% of each run, Pallas kernels for 8% -> 12%
where the time goes in v11:
time: 58.6 us; the launch traced here: 58.3 us
  waiting for transfers between devices  24.3 us (41%)
  starting transfers between devices  17.8 us (30%)
  Pallas kernels  13.4 us (23%)
  local copies, waits for them, and re-layouts  1.15 us (2%)
  between operations  0.86 us (1%)
  other arithmetic  0.75 us (1%)
    pallas_call x15, Pallas kernels, call(): pl.pallas_call(kernel, name=name, out_shape=outs, in_specs=[pl.BlockSpec(...  13.4 us
    ppermute x4, waiting for transfers between devices, sum_round(): return lax.ppermute(x, ('depth', 'scan'), route)  8.56 us
    ppermute x2, waiting for transfers between devices, across(): return lax.ppermute(x, ('depth', 'scan'), route)  6.56 us
    ppermute x2, starting transfers between devices, across(): return lax.ppermute(x, ('depth', 'scan'), route)  5.98 us
    ppermute x2, waiting for transfers between devices, body(): spill += [lax.ppermute(x, 'scan', ahead) for x in payload]  4.36 us
    ppermute x1, waiting for transfers between devices, body(): lax.ppermute(offsets, 'scan', [(i, (i + 1) % scan_count) for i in range(s...  3.54 us
    ppermute x1, starting transfers between devices, body(): lax.ppermute(offsets, 'scan', [(i, (i + 1) % scan_count) for i in range(s...  2.94 us
    ppermute x2, starting transfers between devices, body(): spill += [lax.ppermute(x, 'scan', ahead) for x in payload]  2.69 us
  transfers between devices with their start and end apart: 14, of which 9 were waited for; matrix products, arithmetic and copies ran while one was open for 0% of the time, Pallas kernels for 12%

profile of v11, /device:TPU:0, one launch (start us, length us, event | category | flops | bytes accessed | tf_op | source)
XLA Modules:
  0.0 58.3 jit_solution(15367542608098549869)
XLA Ops:
  0.6 0.7 %pad_add_fusion.offsets.refs_0_ = s32[4]{0:T(128)S(1)} fusion(s32[2]{0:T(128)} %param.9, s32[2]{0:T(128)} %param.8), kind=kLoop, calls=%fused_computation | loop fusion | flops 4 | bytes 32 | tf_op jit(solution)/shard_map/concatenate | solution.py:295
  1.4 2.9 %collective-permute-start = (s32[4]{0:T(128)S(1)}, s32[4]{0:T(128)S(1)}, u32[]{:S(2)}, u32[]{:S(2)}) collective-permute-start(s32[4]{0:T(128)S(1)} %pad_add_fusion.offsets.refs_0_), channel_id=1, source_target_pairs={{0,1},{1,2},{2,3},{3,4},{4,5},{5,6},{6,7},{7,8},{8,9},{9,10},{10,1... | collective-permute-start | bytes 56 | tf_op jit(solution)/shard_map/ppermute | solution.py:296
  4.3 0.0 copy-start
  4.3 1.1 %copy-done = f32[3,2,128,256]{3,2,1,0:T(8,128)S(1)} copy-done((f32[3,2,128,256]{3,2,1,0:T(8,128)S(1)}, f32[3,2,128,256]{3,2,1,0:T(8,128)}, u32[]{:S(2)}) %copy-start) | copy-done | bytes 786456
  5.5 0.8 %own.1 = (f32[3,2,128,256]{3,2,1,0:T(8,128)S(1)}, f32[3,2,128,128]{3,2,1,0:T(8,128)S(1)}) custom-call(s32[4]{0:T(128)S(1)} %pad_add_fusion.offsets.refs_0_, f32[3,2,128,256]{3,2,1,0:T(8,128)S(1)} %copy-done), custom_call_target="tpu_custom_call" | custom-call | flops 1000000000 | bytes 1966080 | tf_op jit(solution)/shard_map/own/pallas_call | solution.py:261
  6.3 3.5 %collective-permute-done.offsets_prev.refs_1_ = s32[4]{0:T(128)S(1)} collective-permute-done((s32[4]{0:T(128)S(1)}, s32[4]{0:T(128)S(1)}, u32[]{:S(2)}, u32[]{:S(2)}) %collective-permute-start) | collective-permute-done | bytes 48 | tf_op jit(solution)/shard_map/ppermute | solution.py:296
  9.8 0.8 %halo.1.after.refs_2_ = f32[3,2,128,128]{3,2,1,0:T(8,128)S(1)} custom-call(s32[4]{0:T(128)S(1)} %collective-permute-done.offsets_prev.refs_1_, f32[3,2,128,256]{3,2,1,0:T(8,128)S(1)} %get-tuple-element.21.tiles), custom_call_target="tpu_custom_call" | custom-call | flops 1000000000 | bytes 1179648 | tf_op jit(solution)/shard_map/halo/pallas_call | solution.py:261
  10.7 0.0 copy-start.1
  10.7 4.1 %collective-permute-start.2 = (f32[3,2,128,128]{3,2,1,0:T(8,128)S(1)}, f32[3,2,128,128]{3,2,1,0:T(8,128)S(1)}, u32[]{:S(2)}, u32[]{:S(2)}) collective-permute-start(f32[3,2,128,128]{3,2,1,0:T(8,128)S(1)} %halo.1.after.refs_2_), channel_id=1, source_target_pairs={{0,15},{1,0},{2,1},{3,2},{4,3},{5,4},{6,5},{7,6},{8,7},{9,8},{10,9... | collective-permute-start | bytes 1179656 | tf_op jit(solution)/shard_map/ppermute | solution.py:293
  14.7 0.8 %ahead.1.window_a = f32[3,2,128,128]{3,2,1,0:T(8,128)S(1)} custom-call(s32[4]{0:T(128)S(1)} %collective-permute-done.offsets_prev.refs_1_, f32[3,2,128,128]{3,2,1,0:T(8,128)S(1)} %halo.1.after.refs_2_, f32[3,2,128,256]{3,2,1,0:T(8,128)S(1)} %get-tuple-element.21.tiles), custom_call_target="tpu_custom_call" | custom-call | flops 1000000000 | bytes 1179648 | tf_op jit(solution)/shard_map/ahead/pallas_call | solution.py:261
  15.6 1.3 %collective-permute-start.4 = (f32[3,2,128,128]{3,2,1,0:T(8,128)S(1)}, f32[3,2,128,128]{3,2,1,0:T(8,128)S(1)}, u32[]{:S(2)}, u32[]{:S(2)}) collective-permute-start(f32[3,2,128,128]{3,2,1,0:T(8,128)S(1)} %ahead.1.window_a), channel_id=1, source_target_pairs={{16,0},{17,1},{18,2},{19,3},{20,4},{21,5},{22,6},{23,7},{24,8},{25... | collective-permute-start | bytes 1179656 | tf_op jit(solution)/shard_map/ppermute | solution.py:304
  16.9 0.0 copy-done.1
  16.9 1.9 %collective-permute-start.1 = (f32[2,128,128]{2,1,0:T(8,128)S(1)}, f32[2,128,128]{2,1,0:T(8,128)S(1)}, u32[]{:S(2)}, u32[]{:S(2)}) collective-permute-start(f32[2,128,128]{2,1,0:T(8,128)S(1)} %copy-done.1), channel_id=1, source_target_pairs={{0,1},{1,2},{2,3},{3,4},{4,5},{5,6},{6,7},{7,8},{8,9},{9,10},{10,1... | collective-permute-start | bytes 393224 | tf_op jit(solution)/shard_map/ppermute | solution.py:293
  18.8 1.7 %collective-permute-done.2.halo = f32[3,2,128,128]{3,2,1,0:T(8,128)S(1)} collective-permute-done((f32[3,2,128,128]{3,2,1,0:T(8,128)S(1)}, f32[3,2,128,128]{3,2,1,0:T(8,128)S(1)}, u32[]{:S(2)}, u32[]{:S(2)}) %collective-permute-start.2) | collective-permute-done | bytes 393248 | tf_op jit(solution)/shard_map/ppermute | solution.py:293
  20.5 0.6 %join.1 = f32[3,2,128,128]{3,2,1,0:T(8,128)S(1)} custom-call(s32[4]{0:T(128)S(1)} %pad_add_fusion.offsets.refs_0_, f32[3,2,128,128]{3,2,1,0:T(8,128)S(1)} %get-tuple-element.22.window_b.refs_6_, f32[3,2,128,128]{3,2,1,0:T(8,128)S(1)} %collective-permute-done.2.halo), custom_call_target="tpu_custom_call" | custom-call | flops 1000000000 | bytes 1179648 | tf_op jit(solution)/shard_map/join/pallas_call | solution.py:261
  21.1 0.0 copy-start.2
  21.1 1.4 %collective-permute-start.3 = (f32[3,2,128,128]{3,2,1,0:T(8,128)S(1)}, f32[3,2,128,128]{3,2,1,0:T(8,128)S(1)}, u32[]{:S(2)}, u32[]{:S(2)}) collective-permute-start(f32[3,2,128,128]{3,2,1,0:T(8,128)S(1)} %join.1), channel_id=1, source_target_pairs={{0,16},{1,17},{2,18},{3,19},{4,20},{5,21},{6,22},{7,23},{8,24},{9,... | collective-permute-start | bytes 1179656 | tf_op jit(solution)/shard_map/ppermute | solution.py:320
  22.6 4.9 %collective-permute-done.1.far.refs_1_ = f32[2,128,128]{2,1,0:T(8,128)S(1)} collective-permute-done((f32[2,128,128]{2,1,0:T(8,128)S(1)}, f32[2,128,128]{2,1,0:T(8,128)S(1)}, u32[]{:S(2)}, u32[]{:S(2)}) %collective-permute-start.1) | collective-permute-done | bytes 131104 | tf_op jit(solution)/shard_map/ppermute | solution.py:293
  27.4 0.0 collective-permute-done.4.refs_0_.refs_8_
  27.5 0.0 copy-start.3
  27.5 0.8 %collective-permute-start.5 = (f32[3,2,128,128]{3,2,1,0:T(8,128)S(1)}, f32[3,2,128,128]{3,2,1,0:T(8,128)S(1)}, u32[]{:S(2)}, u32[]{:S(2)}) collective-permute-start(f32[3,2,128,128]{3,2,1,0:T(8,128)S(1)} %hold.1), channel_id=1, source_target_pairs={{17,16},{18,17},{19,18},{20,19},{21,20},{22,21},{23,22},{24,23},{2... | collective-permute-start | bytes 1179656 | tf_op jit(solution)/shard_map/ppermute | solution.py:311
  28.3 0.0 copy-done.2
  28.3 0.6 load.1
  28.9 0.0 collective-permute-done.3.window_b
  28.9 0.0 copy-done.3
  28.9 1.4 %first.1 = (f32[3,2,128,128]{3,2,1,0:T(8,128)S(1)}, f32[3,2,128,128]{3,2,1,0:T(8,128)S(1)}, f32[2,128,128]{2,1,0:T(8,128)S(1)}) custom-call(f32[128,128]{1,0:T(8,128)S(1)} %get-tuple-element.19.after.refs_3_, bf16[4,2,256,256]{3,2,1,0:T(8,128)(2,1)S(1)} %copy-done.3, f32[2,128,128]{2,1,0:T(8,128)S(1)} %get-tuple-element.20.probe, ...), custom_call_target="tpu_custom_call" | custom-call | flops 2000000000 | bytes 2883584 | tf_op jit(solution)/shard_map/first/pallas_call | solution.py:261
  30.3 0.0 collective-permute-done.5.refs_7_
  30.4 5.1 %wave.1 = (f32[3,2,128,128]{3,2,1,0:T(8,128)S(1)}, f32[3,2,128,128]{3,2,1,0:T(8,128)S(1)}, f32[2,64,128]{2,1,0:T(8,128)S(1)}, f32[2,64,128]{2,1,0:T(8,128)S(1)}) custom-call(s32[4]{0:T(128)S(1)} %pad_add_fusion.offsets.refs_0_, bf16[4,2,256,256]{3,2,1,0:T(8,128)(2,1)S(1)} %copy-done.3, f32[2,128,128]{2,1,0:T(8,128)S(1)} %get-tuple-element.23.refs_2_, ...), custom_call_target="tpu_custom_call" | custom-call | flops 5000000000 | bytes 4128768 | tf_op jit(solution)/shard_map/wave/pallas_call | solution.py:261
  35.4 0.1 collective-permute-start.6
  35.5 0.5 collective-permute-start.7
  36.0 1.3 %collective-permute-done.7.refs_1_ = f32[2,64,128]{2,1,0:T(8,128)S(1)} collective-permute-done((f32[2,64,128]{2,1,0:T(8,128)S(1)}, f32[2,64,128]{2,1,0:T(8,128)S(1)}, u32[]{:S(2)}, u32[]{:S(2)}) %collective-permute-start.7) | collective-permute-done | bytes 65568 | tf_op jit(solution)/shard_map/ppermute | solution.py:349
  37.3 0.0 collective-permute-done.6.refs_3_
  37.3 0.1 collective-permute-start.9
  37.4 2.0 %collective-permute-start.8 = (f32[1,2,128,128]{3,2,1,0:T(8,128)S(1)}, f32[1,2,128,128]{3,2,1,0:T(8,128)S(1)}, u32[]{:S(2)}, u32[]{:S(2)}) collective-permute-start(f32[1,2,128,128]{3,2,1,0:T(8,128)S(1)} %get-tuple-element.30), channel_id=1, source_target_pairs={{0,1},{1,2},{2,3},{3,4},{4,5},{5,6},{6,7},{7,8},{8,9},{9,10},{10,1... | collective-permute-start | bytes 393224 | tf_op jit(solution)/shard_map/ppermute | solution.py:387
  39.4 2.2 %collective-permute-done.9.refs_1_ = f32[2,64,128]{2,1,0:T(8,128)S(1)} collective-permute-done((f32[2,64,128]{2,1,0:T(8,128)S(1)}, f32[2,64,128]{2,1,0:T(8,128)S(1)}, u32[]{:S(2)}, u32[]{:S(2)}) %collective-permute-start.9) | collective-permute-done | bytes 65568 | tf_op jit(solution)/shard_map/ppermute | solution.py:282
  41.7 0.1 collective-permute-start.11
  41.8 0.7 %collective-permute-start.10 = (f32[2,2,128,128]{3,2,1,0:T(8,128)S(1)}, f32[2,2,128,128]{3,2,1,0:T(8,128)S(1)}, u32[]{:S(2)}, u32[]{:S(2)}) collective-permute-start(f32[2,2,128,128]{3,2,1,0:T(8,128)S(1)} %get-tuple-element.32), channel_id=1, source_target_pairs={{0,1},{1,2},{2,3},{3,4},{4,5},{5,6},{6,7},{7,8},{8,9},{9,10},{10,1... | collective-permute-start | bytes 786440 | tf_op jit(solution)/shard_map/ppermute | solution.py:387
  42.5 4.4 %collective-permute-done.8.refs_0_ = f32[1,2,128,128]{3,2,1,0:T(8,128)S(1)} collective-permute-done((f32[1,2,128,128]{3,2,1,0:T(8,128)S(1)}, f32[1,2,128,128]{3,2,1,0:T(8,128)S(1)}, u32[]{:S(2)}, u32[]{:S(2)}) %collective-permute-start.8) | collective-permute-done | bytes 131104 | tf_op jit(solution)/shard_map/ppermute | solution.py:387
  46.8 0.5 collective-permute-done.11.refs_2_
  47.4 0.1 collective-permute-start.12
  47.5 0.9 %place.1.before.refs_0_ = f32[3,2,128,256]{3,2,1,0:T(8,128)S(1)} custom-call(s32[4]{0:T(128)S(1)} %pad_add_fusion.offsets.refs_0_, s32[4]{0:T(128)S(1)} %collective-permute-done.offsets_prev.refs_1_, f32[3,2,128,128]{3,2,1,0:T(8,128)S(1)} %get-tuple-element.26.refs_2_, f32[3,2,128,128]{3,2,1,0:T(8,128)S(1)} %collective-permute-done.6.refs_3_), custom_call_target="tpu_custom_call" | custom-call | flops 2000000000 | bytes 1572864 | tf_op jit(solution)/shard_map/place/pallas_call | solution.py:261
  48.3 3.4 %collective-permute-done.12.refs_2_ = f32[2,64,128]{2,1,0:T(8,128)S(1)} collective-permute-done((f32[2,64,128]{2,1,0:T(8,128)S(1)}, f32[2,64,128]{2,1,0:T(8,128)S(1)}, u32[]{:S(2)}, u32[]{:S(2)}) %collective-permute-start.12) | collective-permute-done | bytes 65568 | tf_op jit(solution)/shard_map/ppermute | solution.py:282
  51.7 1.9 %collective-permute-start.13 = (f32[2,64,128]{2,1,0:T(8,128)S(1)}, f32[2,64,128]{2,1,0:T(8,128)S(1)}, u32[]{:S(2)}, u32[]{:S(2)}) collective-permute-start(f32[2,64,128]{2,1,0:T(8,128)S(1)} %step.8.refs_1_), channel_id=1, source_target_pairs={{0,8},{1,9},{2,10},{3,11},{4,12},{5,13},{6,14},{7,15},{8,0},{9,1},... | collective-permute-start | bytes 196616 | tf_op jit(solution)/shard_map/ppermute | solution.py:282
  53.6 0.0 collective-permute-done.10.refs_1_
  53.6 1.6 %spill.1 = (f32[3,2,128,256]{3,2,1,0:T(8,128)}, f32[8,128]{1,0:T(8,128)S(1)}) custom-call(s32[4]{0:T(128)S(1)} %collective-permute-done.offsets_prev.refs_1_, f32[3,2,128,256]{3,2,1,0:T(8,128)S(1)} %place.1.before.refs_0_, f32[1,2,128,128]{3,2,1,0:T(8,128)S(1)} %collective-permute-done.8.refs_0_, f32[2,2,128,128]{3,2,1,0:T(8,128)S(1)} %collective-permute-done.10.refs_1_), custom_call_target="tpu_custom_call" | custom-call | flops 1000000000 | bytes 1970176 | tf_op jit(solution)/shard_map/spill/pallas_call | solution.py:261
  55.2 2.4 %collective-permute-done.13.refs_2_ = f32[2,64,128]{2,1,0:T(8,128)S(1)} collective-permute-done((f32[2,64,128]{2,1,0:T(8,128)S(1)}, f32[2,64,128]{2,1,0:T(8,128)S(1)}, u32[]{:S(2)}, u32[]{:S(2)}) %collective-permute-start.13) | collective-permute-done | bytes 65568 | tf_op jit(solution)/shard_map/ppermute | solution.py:282
  57.7 0.6 %step.9 = f32[2,64,128]{2,1,0:T(8,128)} custom-call(f32[8,128]{1,0:T(8,128)S(1)} %get-tuple-element.34.refs_0_, f32[2,64,128]{2,1,0:T(8,128)S(1)} %step.8.refs_1_, f32[2,64,128]{2,1,0:T(8,128)S(1)} %collective-permute-done.13.refs_2_), custom_call_target="tpu_custom_call" | custom-call | flops 1000000000 | bytes 196608 | tf_op jit(solution)/shard_map/step/pallas_call | solution.py:261
  (5 shorter events, 0.1 us)
Async XLA Ops:
  1.4 8.4 %collective-permute-start = (s32[4]{0:T(128)S(1)}, s32[4]{0:T(128)S(1)}, u32[]{:S(2)}, u32[]{:S(2)}) collective-permute-start(s32[4]{0:T(128)S(1)} %pad_add_fusion.offsets.refs_0_), channel_id=1, source_target_pairs={{0,1},{1,2},{2,3},{3,4},{4,5},{5,6},{6,7},{7,8},{8,9},{9,10},{10,1... | collective-permute-start | bytes 56 | tf_op jit(solution)/shard_map/ppermute | solution.py:296
  4.3 1.1 %copy-start = (f32[3,2,128,256]{3,2,1,0:T(8,128)S(1)}, f32[3,2,128,256]{3,2,1,0:T(8,128)}, u32[]{:S(2)}) copy-start(f32[3,2,128,256]{3,2,1,0:T(8,128)} %objects.1) | copy-start | bytes 2359300
  10.7 6.2 %copy-start.1 = (f32[2,128,128]{2,1,0:T(8,128)S(1)}, f32[2,128,128]{2,1,0:T(8,128)}, u32[]{:S(2)}) copy-start(f32[2,128,128]{2,1,0:T(8,128)} %intensity.1) | copy-start | bytes 393220
  10.7 9.8 %collective-permute-start.2 = (f32[3,2,128,128]{3,2,1,0:T(8,128)S(1)}, f32[3,2,128,128]{3,2,1,0:T(8,128)S(1)}, u32[]{:S(2)}, u32[]{:S(2)}) collective-permute-start(f32[3,2,128,128]{3,2,1,0:T(8,128)S(1)} %halo.1.after.refs_2_), channel_id=1, source_target_pairs={{0,15},{1,0},{2,1},{3,2},{4,3},{5,4},{6,5},{7,6},{8,7},{9,8},{10,9... | collective-permute-start | bytes 1179656 | tf_op jit(solution)/shard_map/ppermute | solution.py:293
  15.6 11.9 %collective-permute-start.4 = (f32[3,2,128,128]{3,2,1,0:T(8,128)S(1)}, f32[3,2,128,128]{3,2,1,0:T(8,128)S(1)}, u32[]{:S(2)}, u32[]{:S(2)}) collective-permute-start(f32[3,2,128,128]{3,2,1,0:T(8,128)S(1)} %ahead.1.window_a), channel_id=1, source_target_pairs={{16,0},{17,1},{18,2},{19,3},{20,4},{21,5},{22,6},{23,7},{24,8},{25... | collective-permute-start | bytes 1179656 | tf_op jit(solution)/shard_map/ppermute | solution.py:304
  16.9 10.6 %collective-permute-start.1 = (f32[2,128,128]{2,1,0:T(8,128)S(1)}, f32[2,128,128]{2,1,0:T(8,128)S(1)}, u32[]{:S(2)}, u32[]{:S(2)}) collective-permute-start(f32[2,128,128]{2,1,0:T(8,128)S(1)} %copy-done.1), channel_id=1, source_target_pairs={{0,1},{1,2},{2,3},{3,4},{4,5},{5,6},{6,7},{7,8},{8,9},{9,10},{10,1... | collective-permute-start | bytes 393224 | tf_op jit(solution)/shard_map/ppermute | solution.py:293
  21.1 7.2 %copy-start.2 = (f32[2,128,128]{2,1,0:T(8,128)S(1)}, f32[2,128,128]{2,1,0:T(8,128)}, u32[]{:S(2)}) copy-start(f32[2,128,128]{2,1,0:T(8,128)} %probe.1) | copy-start | bytes 393220
  21.1 7.8 %collective-permute-start.3 = (f32[3,2,128,128]{3,2,1,0:T(8,128)S(1)}, f32[3,2,128,128]{3,2,1,0:T(8,128)S(1)}, u32[]{:S(2)}, u32[]{:S(2)}) collective-permute-start(f32[3,2,128,128]{3,2,1,0:T(8,128)S(1)} %join.1), channel_id=1, source_target_pairs={{0,16},{1,17},{2,18},{3,19},{4,20},{5,21},{6,22},{7,23},{8,24},{9,... | collective-permute-start | bytes 1179656 | tf_op jit(solution)/shard_map/ppermute | solution.py:320
  27.5 1.4 %copy-start.3 = (bf16[4,2,256,256]{3,2,1,0:T(8,128)(2,1)S(1)}, bf16[4,2,256,256]{3,2,1,0:T(8,128)(2,1)}, u32[]{:S(2)}) copy-start(bf16[4,2,256,256]{3,2,1,0:T(8,128)(2,1)} %constant.2.clone.tables.refs_1_) | copy-start | bytes 3145732
  27.5 2.9 %collective-permute-start.5 = (f32[3,2,128,128]{3,2,1,0:T(8,128)S(1)}, f32[3,2,128,128]{3,2,1,0:T(8,128)S(1)}, u32[]{:S(2)}, u32[]{:S(2)}) collective-permute-start(f32[3,2,128,128]{3,2,1,0:T(8,128)S(1)} %hold.1), channel_id=1, source_target_pairs={{17,16},{18,17},{19,18},{20,19},{21,20},{22,21},{23,22},{24,23},{2... | collective-permute-start | bytes 1179656 | tf_op jit(solution)/shard_map/ppermute | solution.py:311
  35.4 1.9 %collective-permute-start.6 = (f32[3,2,128,128]{3,2,1,0:T(8,128)S(1)}, f32[3,2,128,128]{3,2,1,0:T(8,128)S(1)}, u32[]{:S(2)}, u32[]{:S(2)}) collective-permute-start(f32[3,2,128,128]{3,2,1,0:T(8,128)S(1)} %get-tuple-element.27), channel_id=1, source_target_pairs={{0,16},{16,0},{1,17},{17,1},{2,18},{18,2},{3,19},{19,3},{4,20},{20... | collective-permute-start | bytes 1179656 | tf_op jit(solution)/shard_map/ppermute | solution.py:350
  35.5 1.8 %collective-permute-start.7 = (f32[2,64,128]{2,1,0:T(8,128)S(1)}, f32[2,64,128]{2,1,0:T(8,128)S(1)}, u32[]{:S(2)}, u32[]{:S(2)}) collective-permute-start(f32[2,64,128]{2,1,0:T(8,128)S(1)} %get-tuple-element.29), channel_id=1, source_target_pairs={{0,16},{16,0},{1,17},{17,1},{2,18},{18,2},{3,19},{19,3},{4,20},{20... | collective-permute-start | bytes 196616 | tf_op jit(solution)/shard_map/ppermute | solution.py:349
  37.3 4.3 %collective-permute-start.9 = (f32[2,64,128]{2,1,0:T(8,128)S(1)}, f32[2,64,128]{2,1,0:T(8,128)S(1)}, u32[]{:S(2)}, u32[]{:S(2)}) collective-permute-start(f32[2,64,128]{2,1,0:T(8,128)S(1)} %get-tuple-element.31.refs_0_), channel_id=1, source_target_pairs={{0,1},{1,0},{2,3},{3,2},{4,5},{5,4},{6,7},{7,6},{8,9},{9,8},{10,11... | collective-permute-start | bytes 196616 | tf_op jit(solution)/shard_map/ppermute | solution.py:282
  37.4 9.4 %collective-permute-start.8 = (f32[1,2,128,128]{3,2,1,0:T(8,128)S(1)}, f32[1,2,128,128]{3,2,1,0:T(8,128)S(1)}, u32[]{:S(2)}, u32[]{:S(2)}) collective-permute-start(f32[1,2,128,128]{3,2,1,0:T(8,128)S(1)} %get-tuple-element.30), channel_id=1, source_target_pairs={{0,1},{1,2},{2,3},{3,4},{4,5},{5,6},{6,7},{7,8},{8,9},{9,10},{10,1... | collective-permute-start | bytes 393224 | tf_op jit(solution)/shard_map/ppermute | solution.py:387
  41.7 5.7 %collective-permute-start.11 = (f32[2,64,128]{2,1,0:T(8,128)S(1)}, f32[2,64,128]{2,1,0:T(8,128)S(1)}, u32[]{:S(2)}, u32[]{:S(2)}) collective-permute-start(f32[2,64,128]{2,1,0:T(8,128)S(1)} %get-tuple-element.35.refs_1_), channel_id=1, source_target_pairs={{0,2},{1,3},{2,0},{3,1},{4,6},{5,7},{6,4},{7,5},{8,10},{9,11},{10,... | collective-permute-start | bytes 196616 | tf_op jit(solution)/shard_map/ppermute | solution.py:282
  41.8 11.8 %collective-permute-start.10 = (f32[2,2,128,128]{3,2,1,0:T(8,128)S(1)}, f32[2,2,128,128]{3,2,1,0:T(8,128)S(1)}, u32[]{:S(2)}, u32[]{:S(2)}) collective-permute-start(f32[2,2,128,128]{3,2,1,0:T(8,128)S(1)} %get-tuple-element.32), channel_id=1, source_target_pairs={{0,1},{1,2},{2,3},{3,4},{4,5},{5,6},{6,7},{7,8},{8,9},{9,10},{10,1... | collective-permute-start | bytes 786440 | tf_op jit(solution)/shard_map/ppermute | solution.py:387
  47.4 4.3 %collective-permute-start.12 = (f32[2,64,128]{2,1,0:T(8,128)S(1)}, f32[2,64,128]{2,1,0:T(8,128)S(1)}, u32[]{:S(2)}, u32[]{:S(2)}) collective-permute-start(f32[2,64,128]{2,1,0:T(8,128)S(1)} %step.7.refs_1_), channel_id=1, source_target_pairs={{0,4},{1,5},{2,6},{3,7},{4,0},{5,1},{6,2},{7,3},{8,12},{9,13},{10,... | collective-permute-start | bytes 196616 | tf_op jit(solution)/shard_map/ppermute | solution.py:282
  51.7 5.9 %collective-permute-start.13 = (f32[2,64,128]{2,1,0:T(8,128)S(1)}, f32[2,64,128]{2,1,0:T(8,128)S(1)}, u32[]{:S(2)}, u32[]{:S(2)}) collective-permute-start(f32[2,64,128]{2,1,0:T(8,128)S(1)} %step.8.refs_1_), channel_id=1, source_target_pairs={{0,8},{1,9},{2,10},{3,11},{4,12},{5,13},{6,14},{7,15},{8,0},{9,1},... | collective-permute-start | bytes 196616 | tf_op jit(solution)/shard_map/ppermute | solution.py:282

commit v12 on v10

--- a/solution.py
+++ b/solution.py
@@ -88,10 +88,14 @@
             window_a[s, p] = cut(tiles[s, p], 0, col_a, width)
 
 
+def rows_here(offsets, rows, cols):
+    _, _, row_b, _ = share(offsets, rows)
+    return lax.broadcasted_iota(jnp.int32, (rows, cols), 0) < rows - row_b
+
+
 def join_kernel(offsets, after, window_b, halo, joined):
     slab, _, rows, cols = joined.shape
-    _, _, row_b, _ = share(offsets, rows)
-    inside = lax.broadcasted_iota(jnp.int32, (rows, cols), 0) < rows - row_b
+    inside = rows_here(offsets, rows, cols)
     for s in range(slab):
         for p in range(2):
             joined[s, p] = jnp.where(inside, window_b[s, p], halo[s, p])
@@ -101,11 +105,11 @@
     rows = probe.shape[-1]
     near_a, _, _, _ = share(offsets, rows)
     far_a, _, _, _ = share(offsets_prev, rows)
-    measured[...] = jnp.where(lax.axis_index("depth") == 0, far[far_a], intensity[1 - near_a])
+    measured[...] = jnp.where(lax.axis_index("depth") == 1, far[far_a], intensity[1 - near_a])
     start[...] = probe[...]
 
 
-def wave_kernel(depth_count, offsets, tables, probe, measured, window_a, window_b, *rest):
+def wave_kernel(depth_count, offsets, tables, probe, measured, window_a, window_b, halo, *rest):
     others_a, others_b = rest[: depth_count - 1], rest[depth_count - 1 : 2 * depth_count - 2]
     rest = rest[2 * depth_count - 2 :]
     grads, probe_parts = rest[:depth_count], rest[depth_count : 2 * depth_count]
@@ -114,13 +118,15 @@
     n = probe.shape[-1]
     count = slab * depth_count
     depth = lax.axis_index("depth")
-    on_a = depth == 0
-    for j in range(depth_count):
-        base = lax.rem(depth - j + depth_count, depth_count) * slab
-        of_a, of_b = ((window_a, *others_a)[j], (window_b, *others_b)[j])
+    on_a = depth == 1
+    inside = rows_here(offsets, n, n)
+    for q in range(depth_count):
+        of_a = (window_a, *others_a)[(1 - q) % depth_count]
+        of_b = others_b[depth_count - 1 - q] if q else None
         for s in range(slab):
             for p in range(2):
-                layers[base + s, p] = jnp.where(on_a, of_a[s, p], of_b[s, p])
+                b_layer = of_b[s, p] if q else jnp.where(inside, window_b[s, p], halo[s, p])
+                layers[q * slab + s, p] = jnp.where(on_a, of_a[s, p], b_layer)
 
     def enter(s, re, im):
         waves[s, 0] = re
@@ -178,8 +184,8 @@
     row_index = lax.broadcasted_iota(jnp.int32, (rows, parts[0].shape[-1]), 0)
     corners = []
     for j in range(depth_count):
-        is_a = depth == j
-        is_b = lax.rem(depth + depth_count - 1, depth_count) == j
+        is_b = depth == j
+        is_a = lax.rem(depth + depth_count - 1, depth_count) == j
         first = jnp.where(is_a, 0, row_b)
         last = jnp.where(is_a | is_b, rows, 0)
         corners.append((jnp.where(is_a, col_a, col_b), (row_index >= first) & (row_index < last)))
@@ -196,7 +202,7 @@
     a, b, *parts = refs[later:-2] if slices else refs[later:-1]
     total = refs[-2] if slices else refs[-1]
     total[...] = a[...] + b[...]
-    place = lax.rem(lax.axis_index("depth") + depth_count - 1, depth_count)
+    place = lax.axis_index("depth")
     for j, part in enumerate(parts):
 
         @pl.when(place == j)
@@ -256,17 +262,21 @@
 
     offsets = jnp.concatenate([row_offsets, col_offsets])
     offsets_prev = lax.ppermute(offsets, "scan", [(i, (i + 1) % scan_count) for i in range(scan_count)])
-    far = across(intensity, 1, 0, 1)
+    far = across(intensity, 0, 1, 1)
     window = jax.ShapeDtypeStruct((slab, 2, n, n), f32)
     whole = jax.ShapeDtypeStruct(objects.shape, f32)
     tiles, window_b = call(own_kernel, "own", [offsets], [objects], [whole, window])
     window_a, halo = call(prev_kernel, "prev", [offsets_prev], [tiles], [window] * 2, after=[far])
-    halo = lax.ppermute(halo, "scan", [((i + 1) % scan_count, i) for i in range(scan_count)])
+    halo_0 = across(halo, 0, 0, -1)
+    route = [
+        (d * scan_count + (i + 1) % scan_count, d * scan_count + i) for d in range(1, depth_count) for i in range(scan_count)
+    ]
+    halo = lax.ppermute(halo, ("depth", "scan"), route)
 
     def gathered(x, target):
         return [lax.ppermute(x, "depth", [((target - j) % depth_count, target)]) for j in range(1, depth_count)]
 
-    others_a = gathered(window_a, 0)
+    others_a = gathered(window_a, 1)
     measured, start = call(
         load_kernel,
         "load",
@@ -275,8 +285,8 @@
         [jax.ShapeDtypeStruct((n, n), f32), jax.ShapeDtypeStruct(probe.shape, f32)],
     )
 
-    (window_b,) = call(join_kernel, "join", [offsets], [window_b, halo], [window], after=[measured])
-    others_b = gathered(window_b, 1)
+    (joined,) = call(join_kernel, "join", [offsets], [window_b, halo], [window], after=[measured])
+    others_b = gathered(joined, 0)
 
     tables = jnp.asarray(constant_tables(n))
     count = slab * depth_count
@@ -284,7 +294,7 @@
         lambda *refs: wave_kernel(depth_count, *refs),
         "wave",
         [offsets],
-        [tables, start, measured, window_a, window_b, *others_a, *others_b],
+        [tables, start, measured, window_a, window_b, halo_0, *others_a, *others_b],
         [window] * depth_count + [jax.ShapeDtypeStruct((2, n // depth_count, n), f32)] * depth_count,
         [pltpu.VMEM((count, 2, n, n), f32)] * 2,
         work=5 * 10**9,

time: 57.6 us -> 57.5 us (level)
  waiting for transfers between devices: 22.1 us -> 23.4 us
  starting transfers between devices: 19.8 us -> 18.6 us
    ppermute x1, waiting for transfers between devices: 6.95 us -> 0.01 us  [body(): halo = lax.ppermute(halo, ('depth', 'scan'), route)]
    ppermute x1 -> x2, starting transfers between devices: 1.29 us -> 7.44 us  [across(): return lax.ppermute(x, ('depth', 'scan'), route)]
    ppermute x1 -> x2, waiting for transfers between devices: 0.01 us -> 4.05 us  [across(): return lax.ppermute(x, ('depth', 'scan'), route)]
    ppermute x4, waiting for transfers between devices: 5.77 us -> 8.65 us  [sum_round(): return lax.ppermute(x, ('depth', 'scan'), route)]
    ppermute x4, starting transfers between devices: 4.67 us -> 2.26 us  [sum_round(): return lax.ppermute(x, ('depth', 'scan'), route)]
    ppermute x1, starting transfers between devices: 2.98 us -> 0.69 us  [body(): halo = lax.ppermute(halo, ('depth', 'scan'), route)]
    ppermute x2, waiting for transfers between devices: 3.23 us -> 4.77 us  [body(): spill += [lax.ppermute(x, 'scan', ahead) for x in payload]]
    ppermute x1, starting transfers between devices: 2.94 us -> 1.49 us  [body(): lax.ppermute(offsets, 'scan', [(i, (i + 1) % scan_count) for i in range(s...]
  transfers between devices with their start and end apart: 13 -> 14, of which waited for: 9 -> 9; matrix products, arithmetic and copies ran while one was open for 1% -> 1% of each run, Pallas kernels for 8% -> 8%
where the time goes in v12:
time: 57.5 us; the launch traced here: 57.3 us
  waiting for transfers between devices  23.4 us (41%)
  starting transfers between devices  18.6 us (32%)
  Pallas kernels  12.6 us (22%)
  local copies, waits for them, and re-layouts  1.15 us (2%)
  between operations  0.82 us (1%)
  other arithmetic  0.75 us (1%)
    pallas_call x12, Pallas kernels, call(): pl.pallas_call(kernel, name=name, out_shape=outs, in_specs=[pl.BlockSpec(...  12.6 us
    ppermute x4, waiting for transfers between devices, sum_round(): return lax.ppermute(x, ('depth', 'scan'), route)  8.65 us
    ppermute x2, starting transfers between devices, across(): return lax.ppermute(x, ('depth', 'scan'), route)  7.44 us
    ppermute x2, waiting for transfers between devices, body(): spill += [lax.ppermute(x, 'scan', ahead) for x in payload]  4.77 us
    ppermute x2, waiting for transfers between devices, across(): return lax.ppermute(x, ('depth', 'scan'), route)  4.05 us
    ppermute x1, waiting for transfers between devices, body(): lax.ppermute(offsets, 'scan', [(i, (i + 1) % scan_count) for i in range(s...  3.67 us
    ppermute x2, starting transfers between devices, body(): spill += [lax.ppermute(x, 'scan', ahead) for x in payload]  3.39 us
    ppermute x2, starting transfers between devices, gathered(): lax.ppermute(x, 'depth', [((target - j) % depth_count, target)])  2.78 us
  transfers between devices with their start and end apart: 14, of which 9 were waited for; matrix products, arithmetic and copies ran while one was open for 1% of the time, Pallas kernels for 8%

profile of v12, /device:TPU:0, one launch (start us, length us, event | category | flops | bytes accessed | tf_op | source)
XLA Modules:
  0.0 57.3 jit_solution(11312197775587881897)
XLA Ops:
  0.6 4.3 %collective-permute-start.1 = (f32[2,128,128]{2,1,0:T(8,128)}, f32[2,128,128]{2,1,0:T(8,128)S(1)}, u32[]{:S(2)}, u32[]{:S(2)}) collective-permute-start(f32[2,128,128]{2,1,0:T(8,128)} %intensity.1), channel_id=1, source_target_pairs={{0,17},{1,18},{2,19},{3,20},{4,21},{5,22},{6,23},{7,24},{8,25},{9,... | collective-permute-start | bytes 393224 | tf_op jit(solution)/shard_map/ppermute | solution.py:261
  4.9 0.7 %pad_add_fusion.offsets.refs_0_ = s32[4]{0:T(128)S(1)} fusion(s32[2]{0:T(128)} %param.9, s32[2]{0:T(128)} %param.8), kind=kLoop, calls=%fused_computation | loop fusion | flops 4 | bytes 32 | tf_op jit(solution)/shard_map/concatenate | solution.py:263
  5.7 1.5 %collective-permute-start = (s32[4]{0:T(128)S(1)}, s32[4]{0:T(128)S(1)}, u32[]{:S(2)}, u32[]{:S(2)}) collective-permute-start(s32[4]{0:T(128)S(1)} %pad_add_fusion.offsets.refs_0_), channel_id=1, source_target_pairs={{0,1},{1,2},{2,3},{3,4},{4,5},{5,6},{6,7},{7,8},{8,9},{9,10},{10,1... | collective-permute-start | bytes 56 | tf_op jit(solution)/shard_map/ppermute | solution.py:264
  7.2 0.0 copy-start
  7.2 1.1 %copy-done = f32[3,2,128,256]{3,2,1,0:T(8,128)S(1)} copy-done((f32[3,2,128,256]{3,2,1,0:T(8,128)S(1)}, f32[3,2,128,256]{3,2,1,0:T(8,128)}, u32[]{:S(2)}) %copy-start) | copy-done | bytes 786456
  8.3 0.8 %own.1 = (f32[3,2,128,256]{3,2,1,0:T(8,128)S(1)}, f32[3,2,128,128]{3,2,1,0:T(8,128)S(1)}) custom-call(s32[4]{0:T(128)S(1)} %pad_add_fusion.offsets.refs_0_, f32[3,2,128,256]{3,2,1,0:T(8,128)S(1)} %copy-done), custom_call_target="tpu_custom_call" | custom-call | flops 1000000000 | bytes 1966080 | tf_op jit(solution)/shard_map/own/pallas_call | solution.py:229
  9.1 3.7 %collective-permute-done.offsets_prev.refs_1_ = s32[4]{0:T(128)S(1)} collective-permute-done((s32[4]{0:T(128)S(1)}, s32[4]{0:T(128)S(1)}, u32[]{:S(2)}, u32[]{:S(2)}) %collective-permute-start) | collective-permute-done | bytes 48 | tf_op jit(solution)/shard_map/ppermute | solution.py:264
  12.8 0.0 collective-permute-done.1.far.after
  12.8 0.0 copy-start.1
  12.8 0.0 copy-start.2
  12.8 1.0 %prev.1 = (f32[3,2,128,128]{3,2,1,0:T(8,128)S(1)}, f32[3,2,128,128]{3,2,1,0:T(8,128)S(1)}) custom-call(s32[4]{0:T(128)S(1)} %collective-permute-done.offsets_prev.refs_1_, f32[2,128,128]{2,1,0:T(8,128)S(1)} %collective-permute-done.1.far.after, f32[3,2,128,256]{3,2,1,0:T(8,128)S(1)} %get-tuple-element.20.tiles), custom_call_target="tpu_custom_call" | custom-call | flops 1000000000 | bytes 1572864 | tf_op jit(solution)/shard_map/prev/pallas_call | solution.py:229
  13.9 0.7 %collective-permute-start.4 = (f32[3,2,128,128]{3,2,1,0:T(8,128)S(1)}, f32[3,2,128,128]{3,2,1,0:T(8,128)S(1)}, u32[]{:S(2)}, u32[]{:S(2)}) collective-permute-start(f32[3,2,128,128]{3,2,1,0:T(8,128)S(1)} %get-tuple-element.23), channel_id=1, source_target_pairs={{17,16},{18,17},{19,18},{20,19},{21,20},{22,21},{23,22},{24,23},{2... | collective-permute-start | bytes 1179656 | tf_op jit(solution)/shard_map/ppermute | solution.py:274
  14.5 3.1 %collective-permute-start.2 = (f32[3,2,128,128]{3,2,1,0:T(8,128)S(1)}, f32[3,2,128,128]{3,2,1,0:T(8,128)S(1)}, u32[]{:S(2)}, u32[]{:S(2)}) collective-permute-start(f32[3,2,128,128]{3,2,1,0:T(8,128)S(1)} %get-tuple-element.23), channel_id=1, source_target_pairs={{0,15},{1,0},{2,1},{3,2},{4,3},{5,4},{6,5},{7,6},{8,7},{9,8},{10,9... | collective-permute-start | bytes 1179656 | tf_op jit(solution)/shard_map/ppermute | solution.py:261
  17.7 1.5 %collective-permute-start.3 = (f32[3,2,128,128]{3,2,1,0:T(8,128)S(1)}, f32[3,2,128,128]{3,2,1,0:T(8,128)S(1)}, u32[]{:S(2)}, u32[]{:S(2)}) collective-permute-start(f32[3,2,128,128]{3,2,1,0:T(8,128)S(1)} %get-tuple-element.21.refs_4_), channel_id=1, source_target_pairs={{0,16},{1,17},{2,18},{3,19},{4,20},{5,21},{6,22},{7,23},{8,24},{9,... | collective-permute-start | bytes 1179656 | tf_op jit(solution)/shard_map/ppermute | solution.py:277
  19.2 0.0 copy-done.1
  19.2 0.0 copy-done.2
  19.2 0.6 load.1
  19.8 0.0 collective-permute-done.4.halo
  19.8 0.0 copy-start.3
  19.8 0.6 %join.1 = f32[3,2,128,128]{3,2,1,0:T(8,128)S(1)} custom-call(s32[4]{0:T(128)S(1)} %pad_add_fusion.offsets.refs_0_, f32[128,128]{1,0:T(8,128)S(1)} %get-tuple-element.19.after.refs_3_, f32[3,2,128,128]{3,2,1,0:T(8,128)S(1)} %get-tuple-element.22.window_b.refs_5_, f32[3,2,128,128]{3,2,1,0:T(8,128)S(1)} %collective-permute-done.4.halo), custom_call_target="tpu_custom_call" | custom-call | flops 1000000000 | bytes 1179648 | tf_op jit(solution)/shard_map/join/pallas_call | solution.py:229
  20.4 1.3 %collective-permute-start.5 = (f32[3,2,128,128]{3,2,1,0:T(8,128)S(1)}, f32[3,2,128,128]{3,2,1,0:T(8,128)S(1)}, u32[]{:S(2)}, u32[]{:S(2)}) collective-permute-start(f32[3,2,128,128]{3,2,1,0:T(8,128)S(1)} %join.1), channel_id=1, source_target_pairs={{16,0},{17,1},{18,2},{19,3},{20,4},{21,5},{22,6},{23,7},{24,8},{25... | collective-permute-start | bytes 1179656 | tf_op jit(solution)/shard_map/ppermute | solution.py:277
  21.7 0.0 collective-permute-done.3.refs_7_
  21.7 4.0 %collective-permute-done.2.refs_6_ = f32[3,2,128,128]{3,2,1,0:T(8,128)S(1)} collective-permute-done((f32[3,2,128,128]{3,2,1,0:T(8,128)S(1)}, f32[3,2,128,128]{3,2,1,0:T(8,128)S(1)}, u32[]{:S(2)}, u32[]{:S(2)}) %collective-permute-start.2) | collective-permute-done | bytes 393248 | tf_op jit(solution)/shard_map/ppermute | solution.py:261
  25.8 0.9 %collective-permute-done.5.refs_8_ = f32[3,2,128,128]{3,2,1,0:T(8,128)S(1)} collective-permute-done((f32[3,2,128,128]{3,2,1,0:T(8,128)S(1)}, f32[3,2,128,128]{3,2,1,0:T(8,128)S(1)}, u32[]{:S(2)}, u32[]{:S(2)}) %collective-permute-start.5) | collective-permute-done | bytes 393248 | tf_op jit(solution)/shard_map/ppermute | solution.py:277
  26.7 0.0 copy-done.3
  26.7 6.4 %wave.1 = (f32[3,2,128,128]{3,2,1,0:T(8,128)S(1)}, f32[3,2,128,128]{3,2,1,0:T(8,128)S(1)}, f32[2,64,128]{2,1,0:T(8,128)S(1)}, f32[2,64,128]{2,1,0:T(8,128)S(1)}) custom-call(s32[4]{0:T(128)S(1)} %pad_add_fusion.offsets.refs_0_, bf16[4,2,256,256]{3,2,1,0:T(8,128)(2,1)S(1)} %copy-done.3, f32[2,128,128]{2,1,0:T(8,128)S(1)} %get-tuple-element.18.refs_2_, ...), custom_call_target="tpu_custom_call" | custom-call | flops 5000000000 | bytes 4128768 | tf_op jit(solution)/shard_map/wave/pallas_call | solution.py:229
  33.1 0.2 collective-permute-start.6
  33.3 0.4 collective-permute-start.7
  33.7 1.3 %collective-permute-done.7.refs_1_ = f32[2,64,128]{2,1,0:T(8,128)S(1)} collective-permute-done((f32[2,64,128]{2,1,0:T(8,128)S(1)}, f32[2,64,128]{2,1,0:T(8,128)S(1)}, u32[]{:S(2)}, u32[]{:S(2)}) %collective-permute-start.7) | collective-permute-done | bytes 65568 | tf_op jit(solution)/shard_map/ppermute | solution.py:306
  35.0 0.0 collective-permute-done.6.refs_3_
  35.0 0.1 collective-permute-start.9
  35.1 2.0 %collective-permute-start.8 = (f32[1,2,128,128]{3,2,1,0:T(8,128)S(1)}, f32[1,2,128,128]{3,2,1,0:T(8,128)S(1)}, u32[]{:S(2)}, u32[]{:S(2)}) collective-permute-start(f32[1,2,128,128]{3,2,1,0:T(8,128)S(1)} %get-tuple-element.28), channel_id=1, source_target_pairs={{0,1},{1,2},{2,3},{3,4},{4,5},{5,6},{6,7},{7,8},{8,9},{9,10},{10,1... | collective-permute-start | bytes 393224 | tf_op jit(solution)/shard_map/ppermute | solution.py:344
  37.1 2.3 %collective-permute-done.9.refs_1_ = f32[2,64,128]{2,1,0:T(8,128)S(1)} collective-permute-done((f32[2,64,128]{2,1,0:T(8,128)S(1)}, f32[2,64,128]{2,1,0:T(8,128)S(1)}, u32[]{:S(2)}, u32[]{:S(2)}) %collective-permute-start.9) | collective-permute-done | bytes 65568 | tf_op jit(solution)/shard_map/ppermute | solution.py:250
  39.4 0.1 collective-permute-start.11
  39.5 1.4 %collective-permute-start.10 = (f32[2,2,128,128]{3,2,1,0:T(8,128)S(1)}, f32[2,2,128,128]{3,2,1,0:T(8,128)S(1)}, u32[]{:S(2)}, u32[]{:S(2)}) collective-permute-start(f32[2,2,128,128]{3,2,1,0:T(8,128)S(1)} %get-tuple-element.30), channel_id=1, source_target_pairs={{0,1},{1,2},{2,3},{3,4},{4,5},{5,6},{6,7},{7,8},{8,9},{9,10},{10,1... | collective-permute-start | bytes 786440 | tf_op jit(solution)/shard_map/ppermute | solution.py:344
  40.9 4.8 %collective-permute-done.8.refs_0_ = f32[1,2,128,128]{3,2,1,0:T(8,128)S(1)} collective-permute-done((f32[1,2,128,128]{3,2,1,0:T(8,128)S(1)}, f32[1,2,128,128]{3,2,1,0:T(8,128)S(1)}, u32[]{:S(2)}, u32[]{:S(2)}) %collective-permute-start.8) | collective-permute-done | bytes 131104 | tf_op jit(solution)/shard_map/ppermute | solution.py:344
  45.7 0.7 %collective-permute-done.11.refs_2_ = f32[2,64,128]{2,1,0:T(8,128)S(1)} collective-permute-done((f32[2,64,128]{2,1,0:T(8,128)S(1)}, f32[2,64,128]{2,1,0:T(8,128)S(1)}, u32[]{:S(2)}, u32[]{:S(2)}) %collective-permute-start.11) | collective-permute-done | bytes 65568 | tf_op jit(solution)/shard_map/ppermute | solution.py:250
  46.4 0.1 collective-permute-start.12
  46.4 0.9 %place.1.before.refs_0_ = f32[3,2,128,256]{3,2,1,0:T(8,128)S(1)} custom-call(s32[4]{0:T(128)S(1)} %pad_add_fusion.offsets.refs_0_, s32[4]{0:T(128)S(1)} %collective-permute-done.offsets_prev.refs_1_, f32[3,2,128,128]{3,2,1,0:T(8,128)S(1)} %get-tuple-element.24.refs_2_, f32[3,2,128,128]{3,2,1,0:T(8,128)S(1)} %collective-permute-done.6.refs_3_), custom_call_target="tpu_custom_call" | custom-call | flops 2000000000 | bytes 1572864 | tf_op jit(solution)/shard_map/place/pallas_call | solution.py:229
  47.3 3.4 %collective-permute-done.12.refs_2_ = f32[2,64,128]{2,1,0:T(8,128)S(1)} collective-permute-done((f32[2,64,128]{2,1,0:T(8,128)S(1)}, f32[2,64,128]{2,1,0:T(8,128)S(1)}, u32[]{:S(2)}, u32[]{:S(2)}) %collective-permute-start.12) | collective-permute-done | bytes 65568 | tf_op jit(solution)/shard_map/ppermute | solution.py:250
  50.7 2.0 %collective-permute-start.13 = (f32[2,64,128]{2,1,0:T(8,128)S(1)}, f32[2,64,128]{2,1,0:T(8,128)S(1)}, u32[]{:S(2)}, u32[]{:S(2)}) collective-permute-start(f32[2,64,128]{2,1,0:T(8,128)S(1)} %step.8.refs_1_), channel_id=1, source_target_pairs={{0,8},{1,9},{2,10},{3,11},{4,12},{5,13},{6,14},{7,15},{8,0},{9,1},... | collective-permute-start | bytes 196616 | tf_op jit(solution)/shard_map/ppermute | solution.py:250
  52.8 0.0 collective-permute-done.10.refs_1_
  52.8 1.6 %spill.1 = (f32[3,2,128,256]{3,2,1,0:T(8,128)}, f32[8,128]{1,0:T(8,128)S(1)}) custom-call(s32[4]{0:T(128)S(1)} %collective-permute-done.offsets_prev.refs_1_, f32[3,2,128,256]{3,2,1,0:T(8,128)S(1)} %place.1.before.refs_0_, f32[1,2,128,128]{3,2,1,0:T(8,128)S(1)} %collective-permute-done.8.refs_0_, f32[2,2,128,128]{3,2,1,0:T(8,128)S(1)} %collective-permute-done.10.refs_1_), custom_call_target="tpu_custom_call" | custom-call | flops 1000000000 | bytes 1970176 | tf_op jit(solution)/shard_map/spill/pallas_call | solution.py:229
  54.4 2.3 %collective-permute-done.13.refs_2_ = f32[2,64,128]{2,1,0:T(8,128)S(1)} collective-permute-done((f32[2,64,128]{2,1,0:T(8,128)S(1)}, f32[2,64,128]{2,1,0:T(8,128)S(1)}, u32[]{:S(2)}, u32[]{:S(2)}) %collective-permute-start.13) | collective-permute-done | bytes 65568 | tf_op jit(solution)/shard_map/ppermute | solution.py:250
  56.6 0.6 %step.9 = f32[2,64,128]{2,1,0:T(8,128)} custom-call(f32[8,128]{1,0:T(8,128)S(1)} %get-tuple-element.32.refs_0_, f32[2,64,128]{2,1,0:T(8,128)S(1)} %step.8.refs_1_, f32[2,64,128]{2,1,0:T(8,128)S(1)} %collective-permute-done.13.refs_2_), custom_call_target="tpu_custom_call" | custom-call | flops 1000000000 | bytes 196608 | tf_op jit(solution)/shard_map/step/pallas_call | solution.py:229
  (4 shorter events, 0.1 us)
Async XLA Ops:
  0.6 12.2 %collective-permute-start.1 = (f32[2,128,128]{2,1,0:T(8,128)}, f32[2,128,128]{2,1,0:T(8,128)S(1)}, u32[]{:S(2)}, u32[]{:S(2)}) collective-permute-start(f32[2,128,128]{2,1,0:T(8,128)} %intensity.1), channel_id=1, source_target_pairs={{0,17},{1,18},{2,19},{3,20},{4,21},{5,22},{6,23},{7,24},{8,25},{9,... | collective-permute-start | bytes 393224 | tf_op jit(solution)/shard_map/ppermute | solution.py:261
  5.7 7.1 %collective-permute-start = (s32[4]{0:T(128)S(1)}, s32[4]{0:T(128)S(1)}, u32[]{:S(2)}, u32[]{:S(2)}) collective-permute-start(s32[4]{0:T(128)S(1)} %pad_add_fusion.offsets.refs_0_), channel_id=1, source_target_pairs={{0,1},{1,2},{2,3},{3,4},{4,5},{5,6},{6,7},{7,8},{8,9},{9,10},{10,1... | collective-permute-start | bytes 56 | tf_op jit(solution)/shard_map/ppermute | solution.py:264
  7.2 1.1 %copy-start = (f32[3,2,128,256]{3,2,1,0:T(8,128)S(1)}, f32[3,2,128,256]{3,2,1,0:T(8,128)}, u32[]{:S(2)}) copy-start(f32[3,2,128,256]{3,2,1,0:T(8,128)} %objects.1) | copy-start | bytes 2359300
  12.8 6.4 %copy-start.1 = (f32[2,128,128]{2,1,0:T(8,128)S(1)}, f32[2,128,128]{2,1,0:T(8,128)}, u32[]{:S(2)}) copy-start(f32[2,128,128]{2,1,0:T(8,128)} %intensity.1) | copy-start | bytes 393220
  12.8 6.4 %copy-start.2 = (f32[2,128,128]{2,1,0:T(8,128)S(1)}, f32[2,128,128]{2,1,0:T(8,128)}, u32[]{:S(2)}) copy-start(f32[2,128,128]{2,1,0:T(8,128)} %probe.1) | copy-start | bytes 393220
  13.9 5.9 %collective-permute-start.4 = (f32[3,2,128,128]{3,2,1,0:T(8,128)S(1)}, f32[3,2,128,128]{3,2,1,0:T(8,128)S(1)}, u32[]{:S(2)}, u32[]{:S(2)}) collective-permute-start(f32[3,2,128,128]{3,2,1,0:T(8,128)S(1)} %get-tuple-element.23), channel_id=1, source_target_pairs={{17,16},{18,17},{19,18},{20,19},{21,20},{22,21},{23,22},{24,23},{2... | collective-permute-start | bytes 1179656 | tf_op jit(solution)/shard_map/ppermute | solution.py:274
  14.5 11.2 %collective-permute-start.2 = (f32[3,2,128,128]{3,2,1,0:T(8,128)S(1)}, f32[3,2,128,128]{3,2,1,0:T(8,128)S(1)}, u32[]{:S(2)}, u32[]{:S(2)}) collective-permute-start(f32[3,2,128,128]{3,2,1,0:T(8,128)S(1)} %get-tuple-element.23), channel_id=1, source_target_pairs={{0,15},{1,0},{2,1},{3,2},{4,3},{5,4},{6,5},{7,6},{8,7},{9,8},{10,9... | collective-permute-start | bytes 1179656 | tf_op jit(solution)/shard_map/ppermute | solution.py:261
  17.7 4.0 %collective-permute-start.3 = (f32[3,2,128,128]{3,2,1,0:T(8,128)S(1)}, f32[3,2,128,128]{3,2,1,0:T(8,128)S(1)}, u32[]{:S(2)}, u32[]{:S(2)}) collective-permute-start(f32[3,2,128,128]{3,2,1,0:T(8,128)S(1)} %get-tuple-element.21.refs_4_), channel_id=1, source_target_pairs={{0,16},{1,17},{2,18},{3,19},{4,20},{5,21},{6,22},{7,23},{8,24},{9,... | collective-permute-start | bytes 1179656 | tf_op jit(solution)/shard_map/ppermute | solution.py:277
  19.8 6.9 %copy-start.3 = (bf16[4,2,256,256]{3,2,1,0:T(8,128)(2,1)S(1)}, bf16[4,2,256,256]{3,2,1,0:T(8,128)(2,1)}, u32[]{:S(2)}) copy-start(bf16[4,2,256,256]{3,2,1,0:T(8,128)(2,1)} %constant.2.clone.refs_1_) | copy-start | bytes 3145732
  20.4 6.3 %collective-permute-start.5 = (f32[3,2,128,128]{3,2,1,0:T(8,128)S(1)}, f32[3,2,128,128]{3,2,1,0:T(8,128)S(1)}, u32[]{:S(2)}, u32[]{:S(2)}) collective-permute-start(f32[3,2,128,128]{3,2,1,0:T(8,128)S(1)} %join.1), channel_id=1, source_target_pairs={{16,0},{17,1},{18,2},{19,3},{20,4},{21,5},{22,6},{23,7},{24,8},{25... | collective-permute-start | bytes 1179656 | tf_op jit(solution)/shard_map/ppermute | solution.py:277
  33.1 1.9 %collective-permute-start.6 = (f32[3,2,128,128]{3,2,1,0:T(8,128)S(1)}, f32[3,2,128,128]{3,2,1,0:T(8,128)S(1)}, u32[]{:S(2)}, u32[]{:S(2)}) collective-permute-start(f32[3,2,128,128]{3,2,1,0:T(8,128)S(1)} %get-tuple-element.25), channel_id=1, source_target_pairs={{0,16},{16,0},{1,17},{17,1},{2,18},{18,2},{3,19},{19,3},{4,20},{20... | collective-permute-start | bytes 1179656 | tf_op jit(solution)/shard_map/ppermute | solution.py:307
  33.3 1.7 %collective-permute-start.7 = (f32[2,64,128]{2,1,0:T(8,128)S(1)}, f32[2,64,128]{2,1,0:T(8,128)S(1)}, u32[]{:S(2)}, u32[]{:S(2)}) collective-permute-start(f32[2,64,128]{2,1,0:T(8,128)S(1)} %get-tuple-element.27), channel_id=1, source_target_pairs={{0,16},{16,0},{1,17},{17,1},{2,18},{18,2},{3,19},{19,3},{4,20},{20... | collective-permute-start | bytes 196616 | tf_op jit(solution)/shard_map/ppermute | solution.py:306
  35.0 4.4 %collective-permute-start.9 = (f32[2,64,128]{2,1,0:T(8,128)S(1)}, f32[2,64,128]{2,1,0:T(8,128)S(1)}, u32[]{:S(2)}, u32[]{:S(2)}) collective-permute-start(f32[2,64,128]{2,1,0:T(8,128)S(1)} %get-tuple-element.29.refs_0_), channel_id=1, source_target_pairs={{0,1},{1,0},{2,3},{3,2},{4,5},{5,4},{6,7},{7,6},{8,9},{9,8},{10,11... | collective-permute-start | bytes 196616 | tf_op jit(solution)/shard_map/ppermute | solution.py:250
  35.1 10.6 %collective-permute-start.8 = (f32[1,2,128,128]{3,2,1,0:T(8,128)S(1)}, f32[1,2,128,128]{3,2,1,0:T(8,128)S(1)}, u32[]{:S(2)}, u32[]{:S(2)}) collective-permute-start(f32[1,2,128,128]{3,2,1,0:T(8,128)S(1)} %get-tuple-element.28), channel_id=1, source_target_pairs={{0,1},{1,2},{2,3},{3,4},{4,5},{5,6},{6,7},{7,8},{8,9},{9,10},{10,1... | collective-permute-start | bytes 393224 | tf_op jit(solution)/shard_map/ppermute | solution.py:344
  39.4 6.9 %collective-permute-start.11 = (f32[2,64,128]{2,1,0:T(8,128)S(1)}, f32[2,64,128]{2,1,0:T(8,128)S(1)}, u32[]{:S(2)}, u32[]{:S(2)}) collective-permute-start(f32[2,64,128]{2,1,0:T(8,128)S(1)} %get-tuple-element.33.refs_1_), channel_id=1, source_target_pairs={{0,2},{1,3},{2,0},{3,1},{4,6},{5,7},{6,4},{7,5},{8,10},{9,11},{10,... | collective-permute-start | bytes 196616 | tf_op jit(solution)/shard_map/ppermute | solution.py:250
  39.5 13.2 %collective-permute-start.10 = (f32[2,2,128,128]{3,2,1,0:T(8,128)S(1)}, f32[2,2,128,128]{3,2,1,0:T(8,128)S(1)}, u32[]{:S(2)}, u32[]{:S(2)}) collective-permute-start(f32[2,2,128,128]{3,2,1,0:T(8,128)S(1)} %get-tuple-element.30), channel_id=1, source_target_pairs={{0,1},{1,2},{2,3},{3,4},{4,5},{5,6},{6,7},{7,8},{8,9},{9,10},{10,1... | collective-permute-start | bytes 786440 | tf_op jit(solution)/shard_map/ppermute | solution.py:344
  46.4 4.3 %collective-permute-start.12 = (f32[2,64,128]{2,1,0:T(8,128)S(1)}, f32[2,64,128]{2,1,0:T(8,128)S(1)}, u32[]{:S(2)}, u32[]{:S(2)}) collective-permute-start(f32[2,64,128]{2,1,0:T(8,128)S(1)} %step.7.refs_1_), channel_id=1, source_target_pairs={{0,4},{1,5},{2,6},{3,7},{4,0},{5,1},{6,2},{7,3},{8,12},{9,13},{10,... | collective-permute-start | bytes 196616 | tf_op jit(solution)/shard_map/ppermute | solution.py:250
  50.7 5.9 %collective-permute-start.13 = (f32[2,64,128]{2,1,0:T(8,128)S(1)}, f32[2,64,128]{2,1,0:T(8,128)S(1)}, u32[]{:S(2)}, u32[]{:S(2)}) collective-permute-start(f32[2,64,128]{2,1,0:T(8,128)S(1)} %step.8.refs_1_), channel_id=1, source_target_pairs={{0,8},{1,9},{2,10},{3,11},{4,12},{5,13},{6,14},{7,15},{8,0},{9,1},... | collective-permute-start | bytes 196616 | tf_op jit(solution)/shard_map/ppermute | solution.py:250

commit v13 on v10

--- a/solution.py
+++ b/solution.py
@@ -88,13 +88,8 @@
             window_a[s, p] = cut(tiles[s, p], 0, col_a, width)
 
 
-def join_kernel(offsets, after, window_b, halo, joined):
-    slab, _, rows, cols = joined.shape
-    _, _, row_b, _ = share(offsets, rows)
-    inside = lax.broadcasted_iota(jnp.int32, (rows, cols), 0) < rows - row_b
-    for s in range(slab):
-        for p in range(2):
-            joined[s, p] = jnp.where(inside, window_b[s, p], halo[s, p])
+def hold_kernel(after, x, out):
+    out[...] = x[...]
 
 
 def load_kernel(offsets, offsets_prev, intensity, far, probe, measured, start):
@@ -105,9 +100,9 @@
     start[...] = probe[...]
 
 
-def wave_kernel(depth_count, offsets, tables, probe, measured, window_a, window_b, *rest):
-    others_a, others_b = rest[: depth_count - 1], rest[depth_count - 1 : 2 * depth_count - 2]
-    rest = rest[2 * depth_count - 2 :]
+def wave_kernel(depth_count, offsets, tables, probe, measured, window_a, window_b, halo, *rest):
+    others_a, others_b, halos = (rest[(depth_count - 1) * k : (depth_count - 1) * (k + 1)] for k in range(3))
+    rest = rest[3 * depth_count - 3 :]
     grads, probe_parts = rest[:depth_count], rest[depth_count : 2 * depth_count]
     layers, waves = rest[2 * depth_count :]
     slab = window_a.shape[0]
@@ -115,12 +110,15 @@
     count = slab * depth_count
     depth = lax.axis_index("depth")
     on_a = depth == 0
-    for j in range(depth_count):
-        base = lax.rem(depth - j + depth_count, depth_count) * slab
-        of_a, of_b = ((window_a, *others_a)[j], (window_b, *others_b)[j])
+    _, _, row_b, _ = share(offsets, n)
+    inside = lax.broadcasted_iota(jnp.int32, (n, n), 0) < n - row_b
+    for q in range(depth_count):
+        of_a = (window_a, *others_a)[-q % depth_count]
+        of_b, below = (window_b, *others_b)[(1 - q) % depth_count], (halo, *halos)[(1 - q) % depth_count]
         for s in range(slab):
             for p in range(2):
-                layers[base + s, p] = jnp.where(on_a, of_a[s, p], of_b[s, p])
+                b_layer = jnp.where(inside, of_b[s, p], below[s, p])
+                layers[q * slab + s, p] = jnp.where(on_a, of_a[s, p], b_layer)
 
     def enter(s, re, im):
         waves[s, 0] = re
@@ -148,7 +146,6 @@
 
     chi = lax.fori_loop(0, count - 1, backward, chi, unroll=True if count <= 8 else 1)
     grad = leave(0, *chi)
-    _, _, row_b, _ = share(offsets, n)
     turn = lax.rem(jnp.where(on_a, 0, row_b), n)
     for j in range(depth_count):
         base = lax.rem(depth + j, depth_count) * slab
@@ -256,7 +253,7 @@
 
     offsets = jnp.concatenate([row_offsets, col_offsets])
     offsets_prev = lax.ppermute(offsets, "scan", [(i, (i + 1) % scan_count) for i in range(scan_count)])
-    far = across(intensity, 1, 0, 1)
+    far = across(intensity, 0, 0, 1)
     window = jax.ShapeDtypeStruct((slab, 2, n, n), f32)
     whole = jax.ShapeDtypeStruct(objects.shape, f32)
     tiles, window_b = call(own_kernel, "own", [offsets], [objects], [whole, window])
@@ -275,8 +272,8 @@
         [jax.ShapeDtypeStruct((n, n), f32), jax.ShapeDtypeStruct(probe.shape, f32)],
     )
 
-    (window_b,) = call(join_kernel, "join", [offsets], [window_b, halo], [window], after=[measured])
-    others_b = gathered(window_b, 1)
+    (halo,) = call(hold_kernel, "hold", [], [halo], [window], after=[measured])
+    others_b, halos = gathered(window_b, 1), gathered(halo, 1)
 
     tables = jnp.asarray(constant_tables(n))
     count = slab * depth_count
@@ -284,7 +281,7 @@
         lambda *refs: wave_kernel(depth_count, *refs),
         "wave",
         [offsets],
-        [tables, start, measured, window_a, window_b, *others_a, *others_b],
+        [tables, start, measured, window_a, window_b, halo, *others_a, *others_b, *halos],
         [window] * depth_count + [jax.ShapeDtypeStruct((2, n // depth_count, n), f32)] * depth_count,
         [pltpu.VMEM((count, 2, n, n), f32)] * 2,
         work=5 * 10**9,

time: 57.6 us -> 54.3 us (0.943)
  starting transfers between devices: 19.8 us -> 18.1 us
  waiting for transfers between devices: 22.1 us -> 21.2 us
  Pallas kernels: 12.6 us -> 12 us
    ppermute x1, waiting for transfers between devices: 6.95 us -> 3.25 us  [body(): lax.ppermute(halo, 'scan', [((i + 1) % scan_count, i) for i in range(scan...]
    ppermute x1, starting transfers between devices: 1.29 us -> 4.85 us  [across(): return lax.ppermute(x, ('depth', 'scan'), route)]
    ppermute x4, starting transfers between devices: 4.67 us -> 2.89 us  [sum_round(): return lax.ppermute(x, ('depth', 'scan'), route)]
    ppermute x4, waiting for transfers between devices: 5.77 us -> 7.46 us  [sum_round(): return lax.ppermute(x, ('depth', 'scan'), route)]
    ppermute x1, starting transfers between devices: 2.98 us -> 1.38 us  [body(): lax.ppermute(halo, 'scan', [((i + 1) % scan_count, i) for i in range(scan...]
    ppermute x1, starting transfers between devices: 2.94 us -> 1.49 us  [body(): lax.ppermute(offsets, 'scan', [(i, (i + 1) % scan_count) for i in range(s...]
    ppermute x2, starting transfers between devices: 4.01 us -> 2.88 us  [body(): spill += [lax.ppermute(x, 'scan', ahead) for x in payload]]
    ppermute x2, waiting for transfers between devices: 3.23 us -> 4.2 us  [body(): spill += [lax.ppermute(x, 'scan', ahead) for x in payload]]
  transfers between devices with their start and end apart: 13 -> 14, of which waited for: 9 -> 9; matrix products, arithmetic and copies ran while one was open for 1% -> 1% of each run, Pallas kernels for 8% -> 7%
where the time goes in v13:
time: 54.3 us; the launch traced here: 54 us
  waiting for transfers between devices  21.2 us (39%)
  starting transfers between devices  18.1 us (33%)
  Pallas kernels  12 us (22%)
  local copies, waits for them, and re-layouts  1.14 us (2%)
  between operations  0.8 us (1%)
  other arithmetic  0.75 us (1%)
    pallas_call x12, Pallas kernels, call(): pl.pallas_call(kernel, name=name, out_shape=outs, in_specs=[pl.BlockSpec(...  12 us
    ppermute x4, waiting for transfers between devices, sum_round(): return lax.ppermute(x, ('depth', 'scan'), route)  7.46 us
    ppermute x1, starting transfers between devices, across(): return lax.ppermute(x, ('depth', 'scan'), route)  4.85 us
    ppermute x2, waiting for transfers between devices, body(): spill += [lax.ppermute(x, 'scan', ahead) for x in payload]  4.2 us
    ppermute x3, starting transfers between devices, gathered(): lax.ppermute(x, 'depth', [((target - j) % depth_count, target)])  4.04 us
    ppermute x1, waiting for transfers between devices, body(): lax.ppermute(offsets, 'scan', [(i, (i + 1) % scan_count) for i in range(s...  3.67 us
    ppermute x1, waiting for transfers between devices, body(): lax.ppermute(halo, 'scan', [((i + 1) % scan_count, i) for i in range(scan...  3.25 us
    ppermute x4, starting transfers between devices, sum_round(): return lax.ppermute(x, ('depth', 'scan'), route)  2.89 us
  transfers between devices with their start and end apart: 14, of which 9 were waited for; matrix products, arithmetic and copies ran while one was open for 1% of the time, Pallas kernels for 7%

profile of v13, /device:TPU:0, one launch (start us, length us, event | category | flops | bytes accessed | tf_op | source)
XLA Modules:
  0.0 54.0 jit_solution(16155093095307877169)
XLA Ops:
  0.6 4.8 %collective-permute-start.1 = (f32[2,128,128]{2,1,0:T(8,128)}, f32[2,128,128]{2,1,0:T(8,128)S(1)}, u32[]{:S(2)}, u32[]{:S(2)}) collective-permute-start(f32[2,128,128]{2,1,0:T(8,128)} %intensity.1), channel_id=1, source_target_pairs={{0,1},{1,2},{2,3},{3,4},{4,5},{5,6},{6,7},{7,8},{8,9},{9,10},{10,1... | collective-permute-start | bytes 393224 | tf_op jit(solution)/shard_map/ppermute | solution.py:252
  5.5 0.7 %pad_add_fusion.offsets.refs_0_ = s32[4]{0:T(128)S(1)} fusion(s32[2]{0:T(128)} %param.9, s32[2]{0:T(128)} %param.8), kind=kLoop, calls=%fused_computation | loop fusion | flops 4 | bytes 32 | tf_op jit(solution)/shard_map/concatenate | solution.py:254
  6.2 1.5 %collective-permute-start = (s32[4]{0:T(128)S(1)}, s32[4]{0:T(128)S(1)}, u32[]{:S(2)}, u32[]{:S(2)}) collective-permute-start(s32[4]{0:T(128)S(1)} %pad_add_fusion.offsets.refs_0_), channel_id=1, source_target_pairs={{0,1},{1,2},{2,3},{3,4},{4,5},{5,6},{6,7},{7,8},{8,9},{9,10},{10,1... | collective-permute-start | bytes 56 | tf_op jit(solution)/shard_map/ppermute | solution.py:255
  7.7 0.0 copy-start
  7.7 1.1 %copy-done = f32[3,2,128,256]{3,2,1,0:T(8,128)S(1)} copy-done((f32[3,2,128,256]{3,2,1,0:T(8,128)S(1)}, f32[3,2,128,256]{3,2,1,0:T(8,128)}, u32[]{:S(2)}) %copy-start) | copy-done | bytes 786456
  8.9 0.8 %own.1 = (f32[3,2,128,256]{3,2,1,0:T(8,128)S(1)}, f32[3,2,128,128]{3,2,1,0:T(8,128)S(1)}) custom-call(s32[4]{0:T(128)S(1)} %pad_add_fusion.offsets.refs_0_, f32[3,2,128,256]{3,2,1,0:T(8,128)S(1)} %copy-done), custom_call_target="tpu_custom_call" | custom-call | flops 1000000000 | bytes 1966080 | tf_op jit(solution)/shard_map/own/pallas_call | solution.py:220
  9.7 3.7 %collective-permute-done.offsets_prev.refs_1_ = s32[4]{0:T(128)S(1)} collective-permute-done((s32[4]{0:T(128)S(1)}, s32[4]{0:T(128)S(1)}, u32[]{:S(2)}, u32[]{:S(2)}) %collective-permute-start) | collective-permute-done | bytes 48 | tf_op jit(solution)/shard_map/ppermute | solution.py:255
  13.4 0.0 collective-permute-done.1.far.after
  13.4 0.0 copy-start.1
  13.4 0.0 copy-start.2
  13.4 1.0 %prev.1 = (f32[3,2,128,128]{3,2,1,0:T(8,128)S(1)}, f32[3,2,128,128]{3,2,1,0:T(8,128)S(1)}) custom-call(s32[4]{0:T(128)S(1)} %collective-permute-done.offsets_prev.refs_1_, f32[2,128,128]{2,1,0:T(8,128)S(1)} %collective-permute-done.1.far.after, f32[3,2,128,256]{3,2,1,0:T(8,128)S(1)} %get-tuple-element.20.tiles), custom_call_target="tpu_custom_call" | custom-call | flops 1000000000 | bytes 1572864 | tf_op jit(solution)/shard_map/prev/pallas_call | solution.py:220
  14.4 1.4 %collective-permute-start.2 = (f32[3,2,128,128]{3,2,1,0:T(8,128)S(1)}, f32[3,2,128,128]{3,2,1,0:T(8,128)S(1)}, u32[]{:S(2)}, u32[]{:S(2)}) collective-permute-start(f32[3,2,128,128]{3,2,1,0:T(8,128)S(1)} %get-tuple-element.23), channel_id=1, source_target_pairs={{1,0},{2,1},{3,2},{4,3},{5,4},{6,5},{7,6},{8,7},{9,8},{10,9},{11,1... | collective-permute-start | bytes 1179656 | tf_op jit(solution)/shard_map/ppermute | solution.py:261
  15.8 1.3 %collective-permute-start.4 = (f32[3,2,128,128]{3,2,1,0:T(8,128)S(1)}, f32[3,2,128,128]{3,2,1,0:T(8,128)S(1)}, u32[]{:S(2)}, u32[]{:S(2)}) collective-permute-start(f32[3,2,128,128]{3,2,1,0:T(8,128)S(1)} %get-tuple-element.22.refs_5_), channel_id=1, source_target_pairs={{0,16},{1,17},{2,18},{3,19},{4,20},{5,21},{6,22},{7,23},{8,24},{9,... | collective-permute-start | bytes 1179656 | tf_op jit(solution)/shard_map/ppermute | solution.py:264
  17.1 1.3 %collective-permute-start.3 = (f32[3,2,128,128]{3,2,1,0:T(8,128)S(1)}, f32[3,2,128,128]{3,2,1,0:T(8,128)S(1)}, u32[]{:S(2)}, u32[]{:S(2)}) collective-permute-start(f32[3,2,128,128]{3,2,1,0:T(8,128)S(1)} %get-tuple-element.21.refs_4_), channel_id=1, source_target_pairs={{16,0},{17,1},{18,2},{19,3},{20,4},{21,5},{22,6},{23,7},{24,8},{25... | collective-permute-start | bytes 1179656 | tf_op jit(solution)/shard_map/ppermute | solution.py:264
  18.4 0.0 copy-done.1
  18.4 0.0 copy-done.2
  18.4 0.6 %load.1 = (f32[128,128]{1,0:T(8,128)S(1)}, f32[2,128,128]{2,1,0:T(8,128)S(1)}) custom-call(s32[4]{0:T(128)S(1)} %pad_add_fusion.offsets.refs_0_, s32[4]{0:T(128)S(1)} %collective-permute-done.offsets_prev.refs_1_, f32[2,128,128]{2,1,0:T(8,128)S(1)} %copy-done.1, f32[2,128,128]{2,1,0:T(8,128)S(1)} %collective-permute-done.1.far.after, ...), custom_call_target="tpu_custom_call" | custom-call | flops 1000000000 | bytes 589824 | tf_op jit(solution)/shard_map/load/pallas_call | solution.py:220
  19.0 3.2 %collective-permute-done.2.x = f32[3,2,128,128]{3,2,1,0:T(8,128)S(1)} collective-permute-done((f32[3,2,128,128]{3,2,1,0:T(8,128)S(1)}, f32[3,2,128,128]{3,2,1,0:T(8,128)S(1)}, u32[]{:S(2)}, u32[]{:S(2)}) %collective-permute-start.2) | collective-permute-done | bytes 393248 | tf_op jit(solution)/shard_map/ppermute | solution.py:261
  22.2 0.0 copy-start.3
  22.3 1.4 %collective-permute-start.5 = (f32[3,2,128,128]{3,2,1,0:T(8,128)S(1)}, f32[3,2,128,128]{3,2,1,0:T(8,128)S(1)}, u32[]{:S(2)}, u32[]{:S(2)}) collective-permute-start(f32[3,2,128,128]{3,2,1,0:T(8,128)S(1)} %hold.1.refs_6_), channel_id=1, source_target_pairs={{0,16},{1,17},{2,18},{3,19},{4,20},{5,21},{6,22},{7,23},{8,24},{9,... | collective-permute-start | bytes 1179656 | tf_op jit(solution)/shard_map/ppermute | solution.py:264
  23.7 0.0 collective-permute-done.4.refs_8_
  23.7 0.0 collective-permute-done.3.refs_7_
  23.7 1.3 %collective-permute-done.5.refs_9_ = f32[3,2,128,128]{3,2,1,0:T(8,128)S(1)} collective-permute-done((f32[3,2,128,128]{3,2,1,0:T(8,128)S(1)}, f32[3,2,128,128]{3,2,1,0:T(8,128)S(1)}, u32[]{:S(2)}, u32[]{:S(2)}) %collective-permute-start.5) | collective-permute-done | bytes 393248 | tf_op jit(solution)/shard_map/ppermute | solution.py:264
  25.0 0.0 copy-done.3
  25.0 6.4 %wave.1 = (f32[3,2,128,128]{3,2,1,0:T(8,128)S(1)}, f32[3,2,128,128]{3,2,1,0:T(8,128)S(1)}, f32[2,64,128]{2,1,0:T(8,128)S(1)}, f32[2,64,128]{2,1,0:T(8,128)S(1)}) custom-call(s32[4]{0:T(128)S(1)} %pad_add_fusion.offsets.refs_0_, bf16[4,2,256,256]{3,2,1,0:T(8,128)(2,1)S(1)} %copy-done.3, f32[2,128,128]{2,1,0:T(8,128)S(1)} %get-tuple-element.18.refs_2_, ...), custom_call_target="tpu_custom_call" | custom-call | flops 5000000000 | bytes 4521984 | tf_op jit(solution)/shard_map/wave/pallas_call | solution.py:220
  31.4 0.4 collective-permute-start.6
  31.9 0.1 collective-permute-start.7
  32.0 1.3 %collective-permute-done.7.refs_1_ = f32[2,64,128]{2,1,0:T(8,128)S(1)} collective-permute-done((f32[2,64,128]{2,1,0:T(8,128)S(1)}, f32[2,64,128]{2,1,0:T(8,128)S(1)}, u32[]{:S(2)}, u32[]{:S(2)}) %collective-permute-start.7) | collective-permute-done | bytes 65568 | tf_op jit(solution)/shard_map/ppermute | solution.py:293
  33.3 0.0 collective-permute-done.6.refs_3_
  33.4 0.1 collective-permute-start.9
  33.4 2.0 %collective-permute-start.8 = (f32[1,2,128,128]{3,2,1,0:T(8,128)S(1)}, f32[1,2,128,128]{3,2,1,0:T(8,128)S(1)}, u32[]{:S(2)}, u32[]{:S(2)}) collective-permute-start(f32[1,2,128,128]{3,2,1,0:T(8,128)S(1)} %get-tuple-element.28), channel_id=1, source_target_pairs={{0,1},{1,2},{2,3},{3,4},{4,5},{5,6},{6,7},{7,8},{8,9},{9,10},{10,1... | collective-permute-start | bytes 393224 | tf_op jit(solution)/shard_map/ppermute | solution.py:331
  35.5 2.6 %collective-permute-done.9.refs_1_ = f32[2,64,128]{2,1,0:T(8,128)S(1)} collective-permute-done((f32[2,64,128]{2,1,0:T(8,128)S(1)}, f32[2,64,128]{2,1,0:T(8,128)S(1)}, u32[]{:S(2)}, u32[]{:S(2)}) %collective-permute-start.9) | collective-permute-done | bytes 65568 | tf_op jit(solution)/shard_map/ppermute | solution.py:241
  38.1 0.1 collective-permute-start.11
  38.2 0.9 %collective-permute-start.10 = (f32[2,2,128,128]{3,2,1,0:T(8,128)S(1)}, f32[2,2,128,128]{3,2,1,0:T(8,128)S(1)}, u32[]{:S(2)}, u32[]{:S(2)}) collective-permute-start(f32[2,2,128,128]{3,2,1,0:T(8,128)S(1)} %get-tuple-element.30), channel_id=1, source_target_pairs={{0,1},{1,2},{2,3},{3,4},{4,5},{5,6},{6,7},{7,8},{8,9},{9,10},{10,1... | collective-permute-start | bytes 786440 | tf_op jit(solution)/shard_map/ppermute | solution.py:331
  39.0 4.2 %collective-permute-done.8.refs_0_ = f32[1,2,128,128]{3,2,1,0:T(8,128)S(1)} collective-permute-done((f32[1,2,128,128]{3,2,1,0:T(8,128)S(1)}, f32[1,2,128,128]{3,2,1,0:T(8,128)S(1)}, u32[]{:S(2)}, u32[]{:S(2)}) %collective-permute-start.8) | collective-permute-done | bytes 131104 | tf_op jit(solution)/shard_map/ppermute | solution.py:331
  43.2 0.6 %collective-permute-done.11.refs_2_ = f32[2,64,128]{2,1,0:T(8,128)S(1)} collective-permute-done((f32[2,64,128]{2,1,0:T(8,128)S(1)}, f32[2,64,128]{2,1,0:T(8,128)S(1)}, u32[]{:S(2)}, u32[]{:S(2)}) %collective-permute-start.11) | collective-permute-done | bytes 65568 | tf_op jit(solution)/shard_map/ppermute | solution.py:241
  43.8 0.1 collective-permute-start.12
  43.9 0.9 %place.1.before.refs_0_ = f32[3,2,128,256]{3,2,1,0:T(8,128)S(1)} custom-call(s32[4]{0:T(128)S(1)} %pad_add_fusion.offsets.refs_0_, s32[4]{0:T(128)S(1)} %collective-permute-done.offsets_prev.refs_1_, f32[3,2,128,128]{3,2,1,0:T(8,128)S(1)} %get-tuple-element.24.refs_2_, f32[3,2,128,128]{3,2,1,0:T(8,128)S(1)} %collective-permute-done.6.refs_3_), custom_call_target="tpu_custom_call" | custom-call | flops 2000000000 | bytes 1572864 | tf_op jit(solution)/shard_map/place/pallas_call | solution.py:220
  44.8 3.4 %collective-permute-done.12.refs_2_ = f32[2,64,128]{2,1,0:T(8,128)S(1)} collective-permute-done((f32[2,64,128]{2,1,0:T(8,128)S(1)}, f32[2,64,128]{2,1,0:T(8,128)S(1)}, u32[]{:S(2)}, u32[]{:S(2)}) %collective-permute-start.12) | collective-permute-done | bytes 65568 | tf_op jit(solution)/shard_map/ppermute | solution.py:241
  48.1 2.7 %collective-permute-start.13 = (f32[2,64,128]{2,1,0:T(8,128)S(1)}, f32[2,64,128]{2,1,0:T(8,128)S(1)}, u32[]{:S(2)}, u32[]{:S(2)}) collective-permute-start(f32[2,64,128]{2,1,0:T(8,128)S(1)} %step.8.refs_1_), channel_id=1, source_target_pairs={{0,8},{1,9},{2,10},{3,11},{4,12},{5,13},{6,14},{7,15},{8,0},{9,1},... | collective-permute-start | bytes 196616 | tf_op jit(solution)/shard_map/ppermute | solution.py:241
  50.8 0.0 collective-permute-done.10.refs_1_
  50.8 1.6 %spill.1 = (f32[3,2,128,256]{3,2,1,0:T(8,128)}, f32[8,128]{1,0:T(8,128)S(1)}) custom-call(s32[4]{0:T(128)S(1)} %collective-permute-done.offsets_prev.refs_1_, f32[3,2,128,256]{3,2,1,0:T(8,128)S(1)} %place.1.before.refs_0_, f32[1,2,128,128]{3,2,1,0:T(8,128)S(1)} %collective-permute-done.8.refs_0_, f32[2,2,128,128]{3,2,1,0:T(8,128)S(1)} %collective-permute-done.10.refs_1_), custom_call_target="tpu_custom_call" | custom-call | flops 1000000000 | bytes 1970176 | tf_op jit(solution)/shard_map/spill/pallas_call | solution.py:220
  52.4 0.9 %collective-permute-done.13.refs_2_ = f32[2,64,128]{2,1,0:T(8,128)S(1)} collective-permute-done((f32[2,64,128]{2,1,0:T(8,128)S(1)}, f32[2,64,128]{2,1,0:T(8,128)S(1)}, u32[]{:S(2)}, u32[]{:S(2)}) %collective-permute-start.13) | collective-permute-done | bytes 65568 | tf_op jit(solution)/shard_map/ppermute | solution.py:241
  53.4 0.6 %step.9 = f32[2,64,128]{2,1,0:T(8,128)} custom-call(f32[8,128]{1,0:T(8,128)S(1)} %get-tuple-element.32.refs_0_, f32[2,64,128]{2,1,0:T(8,128)S(1)} %step.8.refs_1_, f32[2,64,128]{2,1,0:T(8,128)S(1)} %collective-permute-done.13.refs_2_), custom_call_target="tpu_custom_call" | custom-call | flops 1000000000 | bytes 196608 | tf_op jit(solution)/shard_map/step/pallas_call | solution.py:220
  (5 shorter events, 0.1 us)
Async XLA Ops:
  0.6 12.7 %collective-permute-start.1 = (f32[2,128,128]{2,1,0:T(8,128)}, f32[2,128,128]{2,1,0:T(8,128)S(1)}, u32[]{:S(2)}, u32[]{:S(2)}) collective-permute-start(f32[2,128,128]{2,1,0:T(8,128)} %intensity.1), channel_id=1, source_target_pairs={{0,1},{1,2},{2,3},{3,4},{4,5},{5,6},{6,7},{7,8},{8,9},{9,10},{10,1... | collective-permute-start | bytes 393224 | tf_op jit(solution)/shard_map/ppermute | solution.py:252
  6.2 7.1 %collective-permute-start = (s32[4]{0:T(128)S(1)}, s32[4]{0:T(128)S(1)}, u32[]{:S(2)}, u32[]{:S(2)}) collective-permute-start(s32[4]{0:T(128)S(1)} %pad_add_fusion.offsets.refs_0_), channel_id=1, source_target_pairs={{0,1},{1,2},{2,3},{3,4},{4,5},{5,6},{6,7},{7,8},{8,9},{9,10},{10,1... | collective-permute-start | bytes 56 | tf_op jit(solution)/shard_map/ppermute | solution.py:255
  7.7 1.1 %copy-start = (f32[3,2,128,256]{3,2,1,0:T(8,128)S(1)}, f32[3,2,128,256]{3,2,1,0:T(8,128)}, u32[]{:S(2)}) copy-start(f32[3,2,128,256]{3,2,1,0:T(8,128)} %objects.1) | copy-start | bytes 2359300
  13.4 5.0 %copy-start.1 = (f32[2,128,128]{2,1,0:T(8,128)S(1)}, f32[2,128,128]{2,1,0:T(8,128)}, u32[]{:S(2)}) copy-start(f32[2,128,128]{2,1,0:T(8,128)} %intensity.1) | copy-start | bytes 393220
  13.4 5.0 %copy-start.2 = (f32[2,128,128]{2,1,0:T(8,128)S(1)}, f32[2,128,128]{2,1,0:T(8,128)}, u32[]{:S(2)}) copy-start(f32[2,128,128]{2,1,0:T(8,128)} %probe.1) | copy-start | bytes 393220
  14.4 7.8 %collective-permute-start.2 = (f32[3,2,128,128]{3,2,1,0:T(8,128)S(1)}, f32[3,2,128,128]{3,2,1,0:T(8,128)S(1)}, u32[]{:S(2)}, u32[]{:S(2)}) collective-permute-start(f32[3,2,128,128]{3,2,1,0:T(8,128)S(1)} %get-tuple-element.23), channel_id=1, source_target_pairs={{1,0},{2,1},{3,2},{4,3},{5,4},{6,5},{7,6},{8,7},{9,8},{10,9},{11,1... | collective-permute-start | bytes 1179656 | tf_op jit(solution)/shard_map/ppermute | solution.py:261
  15.8 7.9 %collective-permute-start.4 = (f32[3,2,128,128]{3,2,1,0:T(8,128)S(1)}, f32[3,2,128,128]{3,2,1,0:T(8,128)S(1)}, u32[]{:S(2)}, u32[]{:S(2)}) collective-permute-start(f32[3,2,128,128]{3,2,1,0:T(8,128)S(1)} %get-tuple-element.22.refs_5_), channel_id=1, source_target_pairs={{0,16},{1,17},{2,18},{3,19},{4,20},{5,21},{6,22},{7,23},{8,24},{9,... | collective-permute-start | bytes 1179656 | tf_op jit(solution)/shard_map/ppermute | solution.py:264
  17.1 6.6 %collective-permute-start.3 = (f32[3,2,128,128]{3,2,1,0:T(8,128)S(1)}, f32[3,2,128,128]{3,2,1,0:T(8,128)S(1)}, u32[]{:S(2)}, u32[]{:S(2)}) collective-permute-start(f32[3,2,128,128]{3,2,1,0:T(8,128)S(1)} %get-tuple-element.21.refs_4_), channel_id=1, source_target_pairs={{16,0},{17,1},{18,2},{19,3},{20,4},{21,5},{22,6},{23,7},{24,8},{25... | collective-permute-start | bytes 1179656 | tf_op jit(solution)/shard_map/ppermute | solution.py:264
  22.2 2.8 %copy-start.3 = (bf16[4,2,256,256]{3,2,1,0:T(8,128)(2,1)S(1)}, bf16[4,2,256,256]{3,2,1,0:T(8,128)(2,1)}, u32[]{:S(2)}) copy-start(bf16[4,2,256,256]{3,2,1,0:T(8,128)(2,1)} %constant.2.clone.refs_1_) | copy-start | bytes 3145732
  22.3 2.8 %collective-permute-start.5 = (f32[3,2,128,128]{3,2,1,0:T(8,128)S(1)}, f32[3,2,128,128]{3,2,1,0:T(8,128)S(1)}, u32[]{:S(2)}, u32[]{:S(2)}) collective-permute-start(f32[3,2,128,128]{3,2,1,0:T(8,128)S(1)} %hold.1.refs_6_), channel_id=1, source_target_pairs={{0,16},{1,17},{2,18},{3,19},{4,20},{5,21},{6,22},{7,23},{8,24},{9,... | collective-permute-start | bytes 1179656 | tf_op jit(solution)/shard_map/ppermute | solution.py:264
  31.4 1.9 %collective-permute-start.6 = (f32[3,2,128,128]{3,2,1,0:T(8,128)S(1)}, f32[3,2,128,128]{3,2,1,0:T(8,128)S(1)}, u32[]{:S(2)}, u32[]{:S(2)}) collective-permute-start(f32[3,2,128,128]{3,2,1,0:T(8,128)S(1)} %get-tuple-element.25), channel_id=1, source_target_pairs={{0,16},{16,0},{1,17},{17,1},{2,18},{18,2},{3,19},{19,3},{4,20},{20... | collective-permute-start | bytes 1179656 | tf_op jit(solution)/shard_map/ppermute | solution.py:294
  31.9 1.4 %collective-permute-start.7 = (f32[2,64,128]{2,1,0:T(8,128)S(1)}, f32[2,64,128]{2,1,0:T(8,128)S(1)}, u32[]{:S(2)}, u32[]{:S(2)}) collective-permute-start(f32[2,64,128]{2,1,0:T(8,128)S(1)} %get-tuple-element.27), channel_id=1, source_target_pairs={{0,16},{16,0},{1,17},{17,1},{2,18},{18,2},{3,19},{19,3},{4,20},{20... | collective-permute-start | bytes 196616 | tf_op jit(solution)/shard_map/ppermute | solution.py:293
  33.4 4.7 %collective-permute-start.9 = (f32[2,64,128]{2,1,0:T(8,128)S(1)}, f32[2,64,128]{2,1,0:T(8,128)S(1)}, u32[]{:S(2)}, u32[]{:S(2)}) collective-permute-start(f32[2,64,128]{2,1,0:T(8,128)S(1)} %get-tuple-element.29.refs_0_), channel_id=1, source_target_pairs={{0,1},{1,0},{2,3},{3,2},{4,5},{5,4},{6,7},{7,6},{8,9},{9,8},{10,11... | collective-permute-start | bytes 196616 | tf_op jit(solution)/shard_map/ppermute | solution.py:241
  33.4 9.8 %collective-permute-start.8 = (f32[1,2,128,128]{3,2,1,0:T(8,128)S(1)}, f32[1,2,128,128]{3,2,1,0:T(8,128)S(1)}, u32[]{:S(2)}, u32[]{:S(2)}) collective-permute-start(f32[1,2,128,128]{3,2,1,0:T(8,128)S(1)} %get-tuple-element.28), channel_id=1, source_target_pairs={{0,1},{1,2},{2,3},{3,4},{4,5},{5,6},{6,7},{7,8},{8,9},{9,10},{10,1... | collective-permute-start | bytes 393224 | tf_op jit(solution)/shard_map/ppermute | solution.py:331
  38.1 5.7 %collective-permute-start.11 = (f32[2,64,128]{2,1,0:T(8,128)S(1)}, f32[2,64,128]{2,1,0:T(8,128)S(1)}, u32[]{:S(2)}, u32[]{:S(2)}) collective-permute-start(f32[2,64,128]{2,1,0:T(8,128)S(1)} %get-tuple-element.33.refs_1_), channel_id=1, source_target_pairs={{0,2},{1,3},{2,0},{3,1},{4,6},{5,7},{6,4},{7,5},{8,10},{9,11},{10,... | collective-permute-start | bytes 196616 | tf_op jit(solution)/shard_map/ppermute | solution.py:241
  38.2 12.7 %collective-permute-start.10 = (f32[2,2,128,128]{3,2,1,0:T(8,128)S(1)}, f32[2,2,128,128]{3,2,1,0:T(8,128)S(1)}, u32[]{:S(2)}, u32[]{:S(2)}) collective-permute-start(f32[2,2,128,128]{3,2,1,0:T(8,128)S(1)} %get-tuple-element.30), channel_id=1, source_target_pairs={{0,1},{1,2},{2,3},{3,4},{4,5},{5,6},{6,7},{7,8},{8,9},{9,10},{10,1... | collective-permute-start | bytes 786440 | tf_op jit(solution)/shard_map/ppermute | solution.py:331
  43.8 4.3 %collective-permute-start.12 = (f32[2,64,128]{2,1,0:T(8,128)S(1)}, f32[2,64,128]{2,1,0:T(8,128)S(1)}, u32[]{:S(2)}, u32[]{:S(2)}) collective-permute-start(f32[2,64,128]{2,1,0:T(8,128)S(1)} %step.7.refs_1_), channel_id=1, source_target_pairs={{0,4},{1,5},{2,6},{3,7},{4,0},{5,1},{6,2},{7,3},{8,12},{9,13},{10,... | collective-permute-start | bytes 196616 | tf_op jit(solution)/shard_map/ppermute | solution.py:241
  48.1 5.2 %collective-permute-start.13 = (f32[2,64,128]{2,1,0:T(8,128)S(1)}, f32[2,64,128]{2,1,0:T(8,128)S(1)}, u32[]{:S(2)}, u32[]{:S(2)}) collective-permute-start(f32[2,64,128]{2,1,0:T(8,128)S(1)} %step.8.refs_1_), channel_id=1, source_target_pairs={{0,8},{1,9},{2,10},{3,11},{4,12},{5,13},{6,14},{7,15},{8,0},{9,1},... | collective-permute-start | bytes 196616 | tf_op jit(solution)/shard_map/ppermute | solution.py:241

commit v14 on v12

--- a/solution.py
+++ b/solution.py
@@ -78,14 +78,15 @@
             window_b[s, p] = cut(tile, row_b, col_b, window_b.shape[-1])
 
 
-def prev_kernel(offsets_prev, after, tiles, window_a, halo):
+def prev_kernel(offsets_prev, tiles, far, packed, halo):
     slab, _, rows, _ = tiles.shape
     width = halo.shape[-1]
-    _, col_a, row_p, col_p = share(offsets_prev, rows)
+    a, col_a, row_p, col_p = share(offsets_prev, rows)
+    packed[2 * slab] = far[a]
     for s in range(slab):
         for p in range(2):
             halo[s, p] = cut(tiles[s, p], row_p, col_p, width)
-            window_a[s, p] = cut(tiles[s, p], 0, col_a, width)
+            packed[2 * s + p] = cut(tiles[s, p], 0, col_a, width)
 
 
 def rows_here(offsets, rows, cols):
@@ -101,32 +102,31 @@
             joined[s, p] = jnp.where(inside, window_b[s, p], halo[s, p])
 
 
-def load_kernel(offsets, offsets_prev, intensity, far, probe, measured, start):
-    rows = probe.shape[-1]
-    near_a, _, _, _ = share(offsets, rows)
-    far_a, _, _, _ = share(offsets_prev, rows)
-    measured[...] = jnp.where(lax.axis_index("depth") == 1, far[far_a], intensity[1 - near_a])
+def load_kernel(offsets, after, intensity, probe, near, start):
+    a, _, _, _ = share(offsets, probe.shape[-1])
+    near[...] = intensity[1 - a]
     start[...] = probe[...]
 
 
-def wave_kernel(depth_count, offsets, tables, probe, measured, window_a, window_b, halo, *rest):
+def wave_kernel(depth_count, offsets, tables, probe, near, packed, window_b, halo, *rest):
     others_a, others_b = rest[: depth_count - 1], rest[depth_count - 1 : 2 * depth_count - 2]
     rest = rest[2 * depth_count - 2 :]
     grads, probe_parts = rest[:depth_count], rest[depth_count : 2 * depth_count]
     layers, waves = rest[2 * depth_count :]
-    slab = window_a.shape[0]
+    slab = window_b.shape[0]
     n = probe.shape[-1]
     count = slab * depth_count
     depth = lax.axis_index("depth")
     on_a = depth == 1
+    _, _, row_b, _ = share(offsets, n)
     inside = rows_here(offsets, n, n)
     for q in range(depth_count):
-        of_a = (window_a, *others_a)[(1 - q) % depth_count]
-        of_b = others_b[depth_count - 1 - q] if q else None
+        of_a = (packed, *others_a)[(1 - q) % depth_count]
+        of_b = (window_b, *others_b)[-q % depth_count]
         for s in range(slab):
             for p in range(2):
-                b_layer = of_b[s, p] if q else jnp.where(inside, window_b[s, p], halo[s, p])
-                layers[q * slab + s, p] = jnp.where(on_a, of_a[s, p], b_layer)
+                b_layer = of_b[s, p] if q else jnp.where(inside, of_b[s, p], halo[s, p])
+                layers[q * slab + s, p] = jnp.where(on_a, of_a[2 * s + p], b_layer)
 
     def enter(s, re, im):
         waves[s, 0] = re
@@ -139,7 +139,8 @@
 
     wave = lax.fori_loop(0, count - 1, forward, (probe[0], probe[1]), unroll=True if count <= 8 else 1)
     far_re, far_im = both_sides(*enter(count - 1, *wave), tables, 2)
-    misfit = 2.0 * (far_re * far_re + far_im * far_im - measured[...])
+    measured = jnp.where(on_a, others_a[0][2 * slab], near[...])
+    misfit = 2.0 * (far_re * far_re + far_im * far_im - measured)
     chi = both_sides(misfit * far_re, misfit * far_im, tables, 3)
 
     def leave(s, chi_re, chi_im):
@@ -154,7 +155,6 @@
 
     chi = lax.fori_loop(0, count - 1, backward, chi, unroll=True if count <= 8 else 1)
     grad = leave(0, *chi)
-    _, _, row_b, _ = share(offsets, n)
     turn = lax.rem(jnp.where(on_a, 0, row_b), n)
     for j in range(depth_count):
         base = lax.rem(depth + j, depth_count) * slab
@@ -262,11 +262,13 @@
 
     offsets = jnp.concatenate([row_offsets, col_offsets])
     offsets_prev = lax.ppermute(offsets, "scan", [(i, (i + 1) % scan_count) for i in range(scan_count)])
-    far = across(intensity, 0, 1, 1)
+    far = across(intensity, 0, 0, 1)
     window = jax.ShapeDtypeStruct((slab, 2, n, n), f32)
     whole = jax.ShapeDtypeStruct(objects.shape, f32)
     tiles, window_b = call(own_kernel, "own", [offsets], [objects], [whole, window])
-    window_a, halo = call(prev_kernel, "prev", [offsets_prev], [tiles], [window] * 2, after=[far])
+    packed, halo = call(
+        prev_kernel, "prev", [offsets_prev], [tiles, far], [jax.ShapeDtypeStruct((2 * slab + 1, n, n), f32), window]
+    )
     halo_0 = across(halo, 0, 0, -1)
     route = [
         (d * scan_count + (i + 1) % scan_count, d * scan_count + i) for d in range(1, depth_count) for i in range(scan_count)
@@ -276,16 +278,16 @@
     def gathered(x, target):
         return [lax.ppermute(x, "depth", [((target - j) % depth_count, target)]) for j in range(1, depth_count)]
 
-    others_a = gathered(window_a, 1)
-    measured, start = call(
+    others_a = gathered(packed, 1)
+    near, start = call(
         load_kernel,
         "load",
-        [offsets, offsets_prev],
-        [intensity, far, probe],
+        [offsets],
+        [intensity, probe],
         [jax.ShapeDtypeStruct((n, n), f32), jax.ShapeDtypeStruct(probe.shape, f32)],
-    )
-
-    (joined,) = call(join_kernel, "join", [offsets], [window_b, halo], [window], after=[measured])
+        after=others_a[:1],
+    )
+    (joined,) = call(join_kernel, "join", [offsets], [window_b, halo], [window], after=[near])
     others_b = gathered(joined, 0)
 
     tables = jnp.asarray(constant_tables(n))
@@ -294,7 +296,7 @@
         lambda *refs: wave_kernel(depth_count, *refs),
         "wave",
         [offsets],
-        [tables, start, measured, window_a, window_b, halo_0, *others_a, *others_b],
+        [tables, start, near, packed, window_b, halo_0, *others_a, *others_b],
         [window] * depth_count + [jax.ShapeDtypeStruct((2, n // depth_count, n), f32)] * depth_count,
         [pltpu.VMEM((count, 2, n, n), f32)] * 2,
         work=5 * 10**9,

time: 57.5 us -> 55.1 us (0.958)
  waiting for transfers between devices: 23.4 us -> 20 us
  starting transfers between devices: 18.6 us -> 19.6 us
    ppermute x4, waiting for transfers between devices: 8.65 us -> 7.37 us  [sum_round(): return lax.ppermute(x, ('depth', 'scan'), route)]
    ppermute x2, waiting for transfers between devices: 4.77 us -> 3.68 us  [body(): spill += [lax.ppermute(x, 'scan', ahead) for x in payload]]
    ppermute x2, waiting for transfers between devices: 0.91 us -> 0.01 us  [gathered(): lax.ppermute(x, 'depth', [((target - j) % depth_count, target)])]
    ppermute x2, starting transfers between devices: 7.44 us -> 8.08 us  [across(): return lax.ppermute(x, ('depth', 'scan'), route)]
  transfers between devices with their start and end apart: 14 -> 14, of which waited for: 9 -> 8; matrix products, arithmetic and copies ran while one was open for 1% -> 1% of each run, Pallas kernels for 8% -> 8%
where the time goes in v14:
time: 55.1 us; the launch traced here: 54.9 us
  waiting for transfers between devices  20 us (36%)
  starting transfers between devices  19.6 us (36%)
  Pallas kernels  12.6 us (23%)
  local copies, waits for them, and re-layouts  1.15 us (2%)
  between operations  0.82 us (1%)
  other arithmetic  0.75 us (1%)
    pallas_call x12, Pallas kernels, call(): pl.pallas_call(kernel, name=name, out_shape=outs, in_specs=[pl.BlockSpec(...  12.6 us
    ppermute x2, starting transfers between devices, across(): return lax.ppermute(x, ('depth', 'scan'), route)  8.08 us
    ppermute x4, waiting for transfers between devices, sum_round(): return lax.ppermute(x, ('depth', 'scan'), route)  7.37 us
    ppermute x2, waiting for transfers between devices, across(): return lax.ppermute(x, ('depth', 'scan'), route)  3.92 us
    ppermute x2, waiting for transfers between devices, body(): spill += [lax.ppermute(x, 'scan', ahead) for x in payload]  3.68 us
    ppermute x1, waiting for transfers between devices, body(): lax.ppermute(offsets, 'scan', [(i, (i + 1) % scan_count) for i in range(s...  3.67 us
    ppermute x2, starting transfers between devices, body(): spill += [lax.ppermute(x, 'scan', ahead) for x in payload]  3.41 us
    ppermute x4, starting transfers between devices, sum_round(): return lax.ppermute(x, ('depth', 'scan'), route)  2.76 us
  transfers between devices with their start and end apart: 14, of which 8 were waited for; matrix products, arithmetic and copies ran while one was open for 1% of the time, Pallas kernels for 8%

profile of v14, /device:TPU:0, one launch (start us, length us, event | category | flops | bytes accessed | tf_op | source)
XLA Modules:
  0.0 54.9 jit_solution(4943135326586552653)
XLA Ops:
  0.6 4.8 %collective-permute-start.1 = (f32[2,128,128]{2,1,0:T(8,128)}, f32[2,128,128]{2,1,0:T(8,128)S(1)}, u32[]{:S(2)}, u32[]{:S(2)}) collective-permute-start(f32[2,128,128]{2,1,0:T(8,128)} %intensity.1), channel_id=1, source_target_pairs={{0,1},{1,2},{2,3},{3,4},{4,5},{5,6},{6,7},{7,8},{8,9},{9,10},{10,1... | collective-permute-start | bytes 393224 | tf_op jit(solution)/shard_map/ppermute | solution.py:261
  5.5 0.7 %pad_add_fusion.offsets.refs_0_ = s32[4]{0:T(128)S(1)} fusion(s32[2]{0:T(128)} %param.9, s32[2]{0:T(128)} %param.8), kind=kLoop, calls=%fused_computation | loop fusion | flops 4 | bytes 32 | tf_op jit(solution)/shard_map/concatenate | solution.py:263
  6.2 1.5 %collective-permute-start = (s32[4]{0:T(128)S(1)}, s32[4]{0:T(128)S(1)}, u32[]{:S(2)}, u32[]{:S(2)}) collective-permute-start(s32[4]{0:T(128)S(1)} %pad_add_fusion.offsets.refs_0_), channel_id=1, source_target_pairs={{0,1},{1,2},{2,3},{3,4},{4,5},{5,6},{6,7},{7,8},{8,9},{9,10},{10,1... | collective-permute-start | bytes 56 | tf_op jit(solution)/shard_map/ppermute | solution.py:264
  7.7 0.0 copy-start
  7.7 1.1 %copy-done = f32[3,2,128,256]{3,2,1,0:T(8,128)S(1)} copy-done((f32[3,2,128,256]{3,2,1,0:T(8,128)S(1)}, f32[3,2,128,256]{3,2,1,0:T(8,128)}, u32[]{:S(2)}) %copy-start) | copy-done | bytes 786456
  8.9 0.8 %own.1 = (f32[3,2,128,256]{3,2,1,0:T(8,128)S(1)}, f32[3,2,128,128]{3,2,1,0:T(8,128)S(1)}) custom-call(s32[4]{0:T(128)S(1)} %pad_add_fusion.offsets.refs_0_, f32[3,2,128,256]{3,2,1,0:T(8,128)S(1)} %copy-done), custom_call_target="tpu_custom_call" | custom-call | flops 1000000000 | bytes 1966080 | tf_op jit(solution)/shard_map/own/pallas_call | solution.py:229
  9.7 3.7 %collective-permute-done.offsets_prev.refs_1_ = s32[4]{0:T(128)S(1)} collective-permute-done((s32[4]{0:T(128)S(1)}, s32[4]{0:T(128)S(1)}, u32[]{:S(2)}, u32[]{:S(2)}) %collective-permute-start) | collective-permute-done | bytes 48 | tf_op jit(solution)/shard_map/ppermute | solution.py:264
  13.4 0.0 collective-permute-done.1.far
  13.4 0.0 copy-start.1
  13.4 0.0 copy-start.2
  13.4 1.0 %prev.1 = (f32[7,128,128]{2,1,0:T(8,128)S(1)}, f32[3,2,128,128]{3,2,1,0:T(8,128)S(1)}) custom-call(s32[4]{0:T(128)S(1)} %collective-permute-done.offsets_prev.refs_1_, f32[3,2,128,256]{3,2,1,0:T(8,128)S(1)} %get-tuple-element.18.tiles, f32[2,128,128]{2,1,0:T(8,128)S(1)} %collective-permute-done.1.far), custom_call_target="tpu_custom_call" | custom-call | flops 1000000000 | bytes 1769472 | tf_op jit(solution)/shard_map/prev/pallas_call | solution.py:229
  14.4 1.3 %collective-permute-start.2 = (f32[7,128,128]{2,1,0:T(8,128)S(1)}, f32[7,128,128]{2,1,0:T(8,128)S(1)}, u32[]{:S(2)}, u32[]{:S(2)}) collective-permute-start(f32[7,128,128]{2,1,0:T(8,128)S(1)} %get-tuple-element.19.refs_4_), channel_id=1, source_target_pairs={{0,16},{1,17},{2,18},{3,19},{4,20},{5,21},{6,22},{7,23},{8,24},{9,... | collective-permute-start | bytes 1376264 | tf_op jit(solution)/shard_map/ppermute | solution.py:279
  15.7 0.7 %collective-permute-start.4 = (f32[3,2,128,128]{3,2,1,0:T(8,128)S(1)}, f32[3,2,128,128]{3,2,1,0:T(8,128)S(1)}, u32[]{:S(2)}, u32[]{:S(2)}) collective-permute-start(f32[3,2,128,128]{3,2,1,0:T(8,128)S(1)} %get-tuple-element.23), channel_id=1, source_target_pairs={{17,16},{18,17},{19,18},{20,19},{21,20},{22,21},{23,22},{24,23},{2... | collective-permute-start | bytes 1179656 | tf_op jit(solution)/shard_map/ppermute | solution.py:276
  16.4 3.2 %collective-permute-start.3 = (f32[3,2,128,128]{3,2,1,0:T(8,128)S(1)}, f32[3,2,128,128]{3,2,1,0:T(8,128)S(1)}, u32[]{:S(2)}, u32[]{:S(2)}) collective-permute-start(f32[3,2,128,128]{3,2,1,0:T(8,128)S(1)} %get-tuple-element.23), channel_id=1, source_target_pairs={{0,15},{1,0},{2,1},{3,2},{4,3},{5,4},{6,5},{7,6},{8,7},{9,8},{10,9... | collective-permute-start | bytes 1179656 | tf_op jit(solution)/shard_map/ppermute | solution.py:261
  19.7 0.0 collective-permute-done.2.after.refs_7_
  19.7 0.0 copy-done.1
  19.7 0.0 copy-done.2
  19.7 0.6 %load.1 = (f32[128,128]{1,0:T(8,128)S(1)}, f32[2,128,128]{2,1,0:T(8,128)S(1)}) custom-call(s32[4]{0:T(128)S(1)} %pad_add_fusion.offsets.refs_0_, f32[7,128,128]{2,1,0:T(8,128)S(1)} %collective-permute-done.2.after.refs_7_, f32[2,128,128]{2,1,0:T(8,128)S(1)} %copy-done.1, f32[2,128,128]{2,1,0:T(8,128)S(1)} %copy-done.2), custom_call_target="tpu_custom_call" | custom-call | flops 1000000000 | bytes 458752 | tf_op jit(solution)/shard_map/load/pallas_call | solution.py:229
  20.3 0.0 collective-permute-done.4.halo
  20.3 0.0 copy-start.3
  20.3 0.6 %join.1 = f32[3,2,128,128]{3,2,1,0:T(8,128)S(1)} custom-call(s32[4]{0:T(128)S(1)} %pad_add_fusion.offsets.refs_0_, f32[128,128]{1,0:T(8,128)S(1)} %get-tuple-element.21.after.refs_3_, f32[3,2,128,128]{3,2,1,0:T(8,128)S(1)} %get-tuple-element.22.window_b.refs_5_, f32[3,2,128,128]{3,2,1,0:T(8,128)S(1)} %collective-permute-done.4.halo), custom_call_target="tpu_custom_call" | custom-call | flops 1000000000 | bytes 1179648 | tf_op jit(solution)/shard_map/join/pallas_call | solution.py:229
  20.9 1.3 %collective-permute-start.5 = (f32[3,2,128,128]{3,2,1,0:T(8,128)S(1)}, f32[3,2,128,128]{3,2,1,0:T(8,128)S(1)}, u32[]{:S(2)}, u32[]{:S(2)}) collective-permute-start(f32[3,2,128,128]{3,2,1,0:T(8,128)S(1)} %join.1), channel_id=1, source_target_pairs={{16,0},{17,1},{18,2},{19,3},{20,4},{21,5},{22,6},{23,7},{24,8},{25... | collective-permute-start | bytes 1179656 | tf_op jit(solution)/shard_map/ppermute | solution.py:279
  22.2 3.9 %collective-permute-done.3.refs_6_ = f32[3,2,128,128]{3,2,1,0:T(8,128)S(1)} collective-permute-done((f32[3,2,128,128]{3,2,1,0:T(8,128)S(1)}, f32[3,2,128,128]{3,2,1,0:T(8,128)S(1)}, u32[]{:S(2)}, u32[]{:S(2)}) %collective-permute-start.3) | collective-permute-done | bytes 393248 | tf_op jit(solution)/shard_map/ppermute | solution.py:261
  26.1 0.0 collective-permute-done.5.refs_8_
  26.1 0.0 copy-done.3
  26.1 6.4 %wave.1 = (f32[3,2,128,128]{3,2,1,0:T(8,128)S(1)}, f32[3,2,128,128]{3,2,1,0:T(8,128)S(1)}, f32[2,64,128]{2,1,0:T(8,128)S(1)}, f32[2,64,128]{2,1,0:T(8,128)S(1)}) custom-call(s32[4]{0:T(128)S(1)} %pad_add_fusion.offsets.refs_0_, bf16[4,2,256,256]{3,2,1,0:T(8,128)(2,1)S(1)} %copy-done.3, f32[2,128,128]{2,1,0:T(8,128)S(1)} %get-tuple-element.20.refs_2_, ...), custom_call_target="tpu_custom_call" | custom-call | flops 5000000000 | bytes 4259840 | tf_op jit(solution)/shard_map/wave/pallas_call | solution.py:229
  32.5 0.1 collective-permute-start.6
  32.6 0.5 collective-permute-start.7
  33.1 1.3 %collective-permute-done.7.refs_1_ = f32[2,64,128]{2,1,0:T(8,128)S(1)} collective-permute-done((f32[2,64,128]{2,1,0:T(8,128)S(1)}, f32[2,64,128]{2,1,0:T(8,128)S(1)}, u32[]{:S(2)}, u32[]{:S(2)}) %collective-permute-start.7) | collective-permute-done | bytes 65568 | tf_op jit(solution)/shard_map/ppermute | solution.py:308
  34.4 0.0 collective-permute-done.6.refs_3_
  34.4 0.1 collective-permute-start.9
  34.5 2.0 %collective-permute-start.8 = (f32[1,2,128,128]{3,2,1,0:T(8,128)S(1)}, f32[1,2,128,128]{3,2,1,0:T(8,128)S(1)}, u32[]{:S(2)}, u32[]{:S(2)}) collective-permute-start(f32[1,2,128,128]{3,2,1,0:T(8,128)S(1)} %get-tuple-element.28), channel_id=1, source_target_pairs={{0,1},{1,2},{2,3},{3,4},{4,5},{5,6},{6,7},{7,8},{8,9},{9,10},{10,1... | collective-permute-start | bytes 393224 | tf_op jit(solution)/shard_map/ppermute | solution.py:346
  36.5 2.4 %collective-permute-done.9.refs_1_ = f32[2,64,128]{2,1,0:T(8,128)S(1)} collective-permute-done((f32[2,64,128]{2,1,0:T(8,128)S(1)}, f32[2,64,128]{2,1,0:T(8,128)S(1)}, u32[]{:S(2)}, u32[]{:S(2)}) %collective-permute-start.9) | collective-permute-done | bytes 65568 | tf_op jit(solution)/shard_map/ppermute | solution.py:250
  38.9 0.1 collective-permute-start.11
  39.0 1.4 %collective-permute-start.10 = (f32[2,2,128,128]{3,2,1,0:T(8,128)S(1)}, f32[2,2,128,128]{3,2,1,0:T(8,128)S(1)}, u32[]{:S(2)}, u32[]{:S(2)}) collective-permute-start(f32[2,2,128,128]{3,2,1,0:T(8,128)S(1)} %get-tuple-element.30), channel_id=1, source_target_pairs={{0,1},{1,2},{2,3},{3,4},{4,5},{5,6},{6,7},{7,8},{8,9},{9,10},{10,1... | collective-permute-start | bytes 786440 | tf_op jit(solution)/shard_map/ppermute | solution.py:346
  40.4 3.7 %collective-permute-done.8.refs_0_ = f32[1,2,128,128]{3,2,1,0:T(8,128)S(1)} collective-permute-done((f32[1,2,128,128]{3,2,1,0:T(8,128)S(1)}, f32[1,2,128,128]{3,2,1,0:T(8,128)S(1)}, u32[]{:S(2)}, u32[]{:S(2)}) %collective-permute-start.8) | collective-permute-done | bytes 131104 | tf_op jit(solution)/shard_map/ppermute | solution.py:346
  44.1 0.6 %collective-permute-done.11.refs_2_ = f32[2,64,128]{2,1,0:T(8,128)S(1)} collective-permute-done((f32[2,64,128]{2,1,0:T(8,128)S(1)}, f32[2,64,128]{2,1,0:T(8,128)S(1)}, u32[]{:S(2)}, u32[]{:S(2)}) %collective-permute-start.11) | collective-permute-done | bytes 65568 | tf_op jit(solution)/shard_map/ppermute | solution.py:250
  44.6 0.1 collective-permute-start.12
  44.7 0.9 %place.1.before.refs_0_ = f32[3,2,128,256]{3,2,1,0:T(8,128)S(1)} custom-call(s32[4]{0:T(128)S(1)} %pad_add_fusion.offsets.refs_0_, s32[4]{0:T(128)S(1)} %collective-permute-done.offsets_prev.refs_1_, f32[3,2,128,128]{3,2,1,0:T(8,128)S(1)} %get-tuple-element.24.refs_2_, f32[3,2,128,128]{3,2,1,0:T(8,128)S(1)} %collective-permute-done.6.refs_3_), custom_call_target="tpu_custom_call" | custom-call | flops 2000000000 | bytes 1572864 | tf_op jit(solution)/shard_map/place/pallas_call | solution.py:229
  45.6 3.4 %collective-permute-done.12.refs_2_ = f32[2,64,128]{2,1,0:T(8,128)S(1)} collective-permute-done((f32[2,64,128]{2,1,0:T(8,128)S(1)}, f32[2,64,128]{2,1,0:T(8,128)S(1)}, u32[]{:S(2)}, u32[]{:S(2)}) %collective-permute-start.12) | collective-permute-done | bytes 65568 | tf_op jit(solution)/shard_map/ppermute | solution.py:250
  49.0 2.5 %collective-permute-start.13 = (f32[2,64,128]{2,1,0:T(8,128)S(1)}, f32[2,64,128]{2,1,0:T(8,128)S(1)}, u32[]{:S(2)}, u32[]{:S(2)}) collective-permute-start(f32[2,64,128]{2,1,0:T(8,128)S(1)} %step.8.refs_1_), channel_id=1, source_target_pairs={{0,8},{1,9},{2,10},{3,11},{4,12},{5,13},{6,14},{7,15},{8,0},{9,1},... | collective-permute-start | bytes 196616 | tf_op jit(solution)/shard_map/ppermute | solution.py:250
  51.5 0.0 collective-permute-done.10.refs_1_
  51.5 1.6 %spill.1 = (f32[3,2,128,256]{3,2,1,0:T(8,128)}, f32[8,128]{1,0:T(8,128)S(1)}) custom-call(s32[4]{0:T(128)S(1)} %collective-permute-done.offsets_prev.refs_1_, f32[3,2,128,256]{3,2,1,0:T(8,128)S(1)} %place.1.before.refs_0_, f32[1,2,128,128]{3,2,1,0:T(8,128)S(1)} %collective-permute-done.8.refs_0_, f32[2,2,128,128]{3,2,1,0:T(8,128)S(1)} %collective-permute-done.10.refs_1_), custom_call_target="tpu_custom_call" | custom-call | flops 1000000000 | bytes 1970176 | tf_op jit(solution)/shard_map/spill/pallas_call | solution.py:229
  53.1 1.1 %collective-permute-done.13.refs_2_ = f32[2,64,128]{2,1,0:T(8,128)S(1)} collective-permute-done((f32[2,64,128]{2,1,0:T(8,128)S(1)}, f32[2,64,128]{2,1,0:T(8,128)S(1)}, u32[]{:S(2)}, u32[]{:S(2)}) %collective-permute-start.13) | collective-permute-done | bytes 65568 | tf_op jit(solution)/shard_map/ppermute | solution.py:250
  54.2 0.6 %step.9 = f32[2,64,128]{2,1,0:T(8,128)} custom-call(f32[8,128]{1,0:T(8,128)S(1)} %get-tuple-element.32.refs_0_, f32[2,64,128]{2,1,0:T(8,128)S(1)} %step.8.refs_1_, f32[2,64,128]{2,1,0:T(8,128)S(1)} %collective-permute-done.13.refs_2_), custom_call_target="tpu_custom_call" | custom-call | flops 1000000000 | bytes 196608 | tf_op jit(solution)/shard_map/step/pallas_call | solution.py:229
  (4 shorter events, 0.1 us)
Async XLA Ops:
  0.6 12.7 %collective-permute-start.1 = (f32[2,128,128]{2,1,0:T(8,128)}, f32[2,128,128]{2,1,0:T(8,128)S(1)}, u32[]{:S(2)}, u32[]{:S(2)}) collective-permute-start(f32[2,128,128]{2,1,0:T(8,128)} %intensity.1), channel_id=1, source_target_pairs={{0,1},{1,2},{2,3},{3,4},{4,5},{5,6},{6,7},{7,8},{8,9},{9,10},{10,1... | collective-permute-start | bytes 393224 | tf_op jit(solution)/shard_map/ppermute | solution.py:261
  6.2 7.1 %collective-permute-start = (s32[4]{0:T(128)S(1)}, s32[4]{0:T(128)S(1)}, u32[]{:S(2)}, u32[]{:S(2)}) collective-permute-start(s32[4]{0:T(128)S(1)} %pad_add_fusion.offsets.refs_0_), channel_id=1, source_target_pairs={{0,1},{1,2},{2,3},{3,4},{4,5},{5,6},{6,7},{7,8},{8,9},{9,10},{10,1... | collective-permute-start | bytes 56 | tf_op jit(solution)/shard_map/ppermute | solution.py:264
  7.7 1.1 %copy-start = (f32[3,2,128,256]{3,2,1,0:T(8,128)S(1)}, f32[3,2,128,256]{3,2,1,0:T(8,128)}, u32[]{:S(2)}) copy-start(f32[3,2,128,256]{3,2,1,0:T(8,128)} %objects.1) | copy-start | bytes 2359300
  13.4 6.3 %copy-start.1 = (f32[2,128,128]{2,1,0:T(8,128)S(1)}, f32[2,128,128]{2,1,0:T(8,128)}, u32[]{:S(2)}) copy-start(f32[2,128,128]{2,1,0:T(8,128)} %intensity.1) | copy-start | bytes 393220
  13.4 6.3 %copy-start.2 = (f32[2,128,128]{2,1,0:T(8,128)S(1)}, f32[2,128,128]{2,1,0:T(8,128)}, u32[]{:S(2)}) copy-start(f32[2,128,128]{2,1,0:T(8,128)} %probe.1) | copy-start | bytes 393220
  14.4 5.3 %collective-permute-start.2 = (f32[7,128,128]{2,1,0:T(8,128)S(1)}, f32[7,128,128]{2,1,0:T(8,128)S(1)}, u32[]{:S(2)}, u32[]{:S(2)}) collective-permute-start(f32[7,128,128]{2,1,0:T(8,128)S(1)} %get-tuple-element.19.refs_4_), channel_id=1, source_target_pairs={{0,16},{1,17},{2,18},{3,19},{4,20},{5,21},{6,22},{7,23},{8,24},{9,... | collective-permute-start | bytes 1376264 | tf_op jit(solution)/shard_map/ppermute | solution.py:279
  15.7 4.5 %collective-permute-start.4 = (f32[3,2,128,128]{3,2,1,0:T(8,128)S(1)}, f32[3,2,128,128]{3,2,1,0:T(8,128)S(1)}, u32[]{:S(2)}, u32[]{:S(2)}) collective-permute-start(f32[3,2,128,128]{3,2,1,0:T(8,128)S(1)} %get-tuple-element.23), channel_id=1, source_target_pairs={{17,16},{18,17},{19,18},{20,19},{21,20},{22,21},{23,22},{24,23},{2... | collective-permute-start | bytes 1179656 | tf_op jit(solution)/shard_map/ppermute | solution.py:276
  16.4 9.7 %collective-permute-start.3 = (f32[3,2,128,128]{3,2,1,0:T(8,128)S(1)}, f32[3,2,128,128]{3,2,1,0:T(8,128)S(1)}, u32[]{:S(2)}, u32[]{:S(2)}) collective-permute-start(f32[3,2,128,128]{3,2,1,0:T(8,128)S(1)} %get-tuple-element.23), channel_id=1, source_target_pairs={{0,15},{1,0},{2,1},{3,2},{4,3},{5,4},{6,5},{7,6},{8,7},{9,8},{10,9... | collective-permute-start | bytes 1179656 | tf_op jit(solution)/shard_map/ppermute | solution.py:261
  20.3 5.8 %copy-start.3 = (bf16[4,2,256,256]{3,2,1,0:T(8,128)(2,1)S(1)}, bf16[4,2,256,256]{3,2,1,0:T(8,128)(2,1)}, u32[]{:S(2)}) copy-start(bf16[4,2,256,256]{3,2,1,0:T(8,128)(2,1)} %constant.2.clone.refs_1_) | copy-start | bytes 3145732
  20.9 5.2 %collective-permute-start.5 = (f32[3,2,128,128]{3,2,1,0:T(8,128)S(1)}, f32[3,2,128,128]{3,2,1,0:T(8,128)S(1)}, u32[]{:S(2)}, u32[]{:S(2)}) collective-permute-start(f32[3,2,128,128]{3,2,1,0:T(8,128)S(1)} %join.1), channel_id=1, source_target_pairs={{16,0},{17,1},{18,2},{19,3},{20,4},{21,5},{22,6},{23,7},{24,8},{25... | collective-permute-start | bytes 1179656 | tf_op jit(solution)/shard_map/ppermute | solution.py:279
  32.5 1.9 %collective-permute-start.6 = (f32[3,2,128,128]{3,2,1,0:T(8,128)S(1)}, f32[3,2,128,128]{3,2,1,0:T(8,128)S(1)}, u32[]{:S(2)}, u32[]{:S(2)}) collective-permute-start(f32[3,2,128,128]{3,2,1,0:T(8,128)S(1)} %get-tuple-element.25), channel_id=1, source_target_pairs={{0,16},{16,0},{1,17},{17,1},{2,18},{18,2},{3,19},{19,3},{4,20},{20... | collective-permute-start | bytes 1179656 | tf_op jit(solution)/shard_map/ppermute | solution.py:309
  32.6 1.8 %collective-permute-start.7 = (f32[2,64,128]{2,1,0:T(8,128)S(1)}, f32[2,64,128]{2,1,0:T(8,128)S(1)}, u32[]{:S(2)}, u32[]{:S(2)}) collective-permute-start(f32[2,64,128]{2,1,0:T(8,128)S(1)} %get-tuple-element.27), channel_id=1, source_target_pairs={{0,16},{16,0},{1,17},{17,1},{2,18},{18,2},{3,19},{19,3},{4,20},{20... | collective-permute-start | bytes 196616 | tf_op jit(solution)/shard_map/ppermute | solution.py:308
  34.4 4.5 %collective-permute-start.9 = (f32[2,64,128]{2,1,0:T(8,128)S(1)}, f32[2,64,128]{2,1,0:T(8,128)S(1)}, u32[]{:S(2)}, u32[]{:S(2)}) collective-permute-start(f32[2,64,128]{2,1,0:T(8,128)S(1)} %get-tuple-element.29.refs_0_), channel_id=1, source_target_pairs={{0,1},{1,0},{2,3},{3,2},{4,5},{5,4},{6,7},{7,6},{8,9},{9,8},{10,11... | collective-permute-start | bytes 196616 | tf_op jit(solution)/shard_map/ppermute | solution.py:250
  34.5 9.6 %collective-permute-start.8 = (f32[1,2,128,128]{3,2,1,0:T(8,128)S(1)}, f32[1,2,128,128]{3,2,1,0:T(8,128)S(1)}, u32[]{:S(2)}, u32[]{:S(2)}) collective-permute-start(f32[1,2,128,128]{3,2,1,0:T(8,128)S(1)} %get-tuple-element.28), channel_id=1, source_target_pairs={{0,1},{1,2},{2,3},{3,4},{4,5},{5,6},{6,7},{7,8},{8,9},{9,10},{10,1... | collective-permute-start | bytes 393224 | tf_op jit(solution)/shard_map/ppermute | solution.py:346
  38.9 5.7 %collective-permute-start.11 = (f32[2,64,128]{2,1,0:T(8,128)S(1)}, f32[2,64,128]{2,1,0:T(8,128)S(1)}, u32[]{:S(2)}, u32[]{:S(2)}) collective-permute-start(f32[2,64,128]{2,1,0:T(8,128)S(1)} %get-tuple-element.33.refs_1_), channel_id=1, source_target_pairs={{0,2},{1,3},{2,0},{3,1},{4,6},{5,7},{6,4},{7,5},{8,10},{9,11},{10,... | collective-permute-start | bytes 196616 | tf_op jit(solution)/shard_map/ppermute | solution.py:250
  39.0 12.5 %collective-permute-start.10 = (f32[2,2,128,128]{3,2,1,0:T(8,128)S(1)}, f32[2,2,128,128]{3,2,1,0:T(8,128)S(1)}, u32[]{:S(2)}, u32[]{:S(2)}) collective-permute-start(f32[2,2,128,128]{3,2,1,0:T(8,128)S(1)} %get-tuple-element.30), channel_id=1, source_target_pairs={{0,1},{1,2},{2,3},{3,4},{4,5},{5,6},{6,7},{7,8},{8,9},{9,10},{10,1... | collective-permute-start | bytes 786440 | tf_op jit(solution)/shard_map/ppermute | solution.py:346
  44.6 4.3 %collective-permute-start.12 = (f32[2,64,128]{2,1,0:T(8,128)S(1)}, f32[2,64,128]{2,1,0:T(8,128)S(1)}, u32[]{:S(2)}, u32[]{:S(2)}) collective-permute-start(f32[2,64,128]{2,1,0:T(8,128)S(1)} %step.7.refs_1_), channel_id=1, source_target_pairs={{0,4},{1,5},{2,6},{3,7},{4,0},{5,1},{6,2},{7,3},{8,12},{9,13},{10,... | collective-permute-start | bytes 196616 | tf_op jit(solution)/shard_map/ppermute | solution.py:250
  49.0 5.2 %collective-permute-start.13 = (f32[2,64,128]{2,1,0:T(8,128)S(1)}, f32[2,64,128]{2,1,0:T(8,128)S(1)}, u32[]{:S(2)}, u32[]{:S(2)}) collective-permute-start(f32[2,64,128]{2,1,0:T(8,128)S(1)} %step.8.refs_1_), channel_id=1, source_target_pairs={{0,8},{1,9},{2,10},{3,11},{4,12},{5,13},{6,14},{7,15},{8,0},{9,1},... | collective-permute-start | bytes 196616 | tf_op jit(solution)/shard_map/ppermute | solution.py:250

commit v15 on v13

--- a/solution.py
+++ b/solution.py
@@ -236,7 +236,7 @@
     levels = scan_count.bit_length() - 1
     route = []
     for d in range(depth_count):
-        step = 1 << ((level + (d % 2) * (levels // 2)) % levels)
+        step = 1 << (1 + (level - 1 + d % 2) % (levels - 1) if level else 0)
         route += [(d * scan_count + i, d * scan_count + (i ^ step)) for i in range(scan_count)]
     return lax.ppermute(x, ("depth", "scan"), route)
 

time: 54.3 us -> 58.8 us (1.083)
  starting transfers between devices: 18.1 us -> 21.3 us
  waiting for transfers between devices: 21.2 us -> 22.1 us
    ppermute x4, starting transfers between devices: 2.89 us -> 5.71 us  [sum_round(): return lax.ppermute(x, ('depth', 'scan'), route)]
    ppermute x4, waiting for transfers between devices: 7.46 us -> 9.21 us  [sum_round(): return lax.ppermute(x, ('depth', 'scan'), route)]
    ppermute x2, waiting for transfers between devices: 4.2 us -> 3.37 us  [body(): spill += [lax.ppermute(x, 'scan', ahead) for x in payload]]
where the time goes in v15:
time: 58.8 us; the launch traced here: 58.1 us
  waiting for transfers between devices  22.1 us (38%)
  starting transfers between devices  21.3 us (36%)
  Pallas kernels  12 us (20%)
  local copies, waits for them, and re-layouts  1.14 us (2%)
  between operations  0.79 us (1%)
  other arithmetic  0.75 us (1%)
    pallas_call x12, Pallas kernels, call(): pl.pallas_call(kernel, name=name, out_shape=outs, in_specs=[pl.BlockSpec(...  12 us
    ppermute x4, waiting for transfers between devices, sum_round(): return lax.ppermute(x, ('depth', 'scan'), route)  9.21 us
    ppermute x4, starting transfers between devices, sum_round(): return lax.ppermute(x, ('depth', 'scan'), route)  5.71 us
    ppermute x1, starting transfers between devices, across(): return lax.ppermute(x, ('depth', 'scan'), route)  4.85 us
    ppermute x3, starting transfers between devices, gathered(): lax.ppermute(x, 'depth', [((target - j) % depth_count, target)])  4.04 us
    ppermute x1, waiting for transfers between devices, body(): lax.ppermute(offsets, 'scan', [(i, (i + 1) % scan_count) for i in range(s...  3.67 us
    ppermute x2, waiting for transfers between devices, body(): spill += [lax.ppermute(x, 'scan', ahead) for x in payload]  3.37 us
    ppermute x2, starting transfers between devices, body(): spill += [lax.ppermute(x, 'scan', ahead) for x in payload]  3.25 us
  transfers between devices with their start and end apart: 14, of which 9 were waited for; matrix products, arithmetic and copies ran while one was open for 1% of the time, Pallas kernels for 7%

profile of v15, /device:TPU:0, one launch (start us, length us, event | category | flops | bytes accessed | tf_op | source)
XLA Modules:
  0.0 58.1 jit_solution(5582242778959784889)
XLA Ops:
  0.6 4.8 %collective-permute-start.1 = (f32[2,128,128]{2,1,0:T(8,128)}, f32[2,128,128]{2,1,0:T(8,128)S(1)}, u32[]{:S(2)}, u32[]{:S(2)}) collective-permute-start(f32[2,128,128]{2,1,0:T(8,128)} %intensity.1), channel_id=1, source_target_pairs={{0,1},{1,2},{2,3},{3,4},{4,5},{5,6},{6,7},{7,8},{8,9},{9,10},{10,1... | collective-permute-start | bytes 393224 | tf_op jit(solution)/shard_map/ppermute | solution.py:252
  5.5 0.7 %pad_add_fusion.offsets.refs_0_ = s32[4]{0:T(128)S(1)} fusion(s32[2]{0:T(128)} %param.9, s32[2]{0:T(128)} %param.8), kind=kLoop, calls=%fused_computation | loop fusion | flops 4 | bytes 32 | tf_op jit(solution)/shard_map/concatenate | solution.py:254
  6.2 1.5 %collective-permute-start = (s32[4]{0:T(128)S(1)}, s32[4]{0:T(128)S(1)}, u32[]{:S(2)}, u32[]{:S(2)}) collective-permute-start(s32[4]{0:T(128)S(1)} %pad_add_fusion.offsets.refs_0_), channel_id=1, source_target_pairs={{0,1},{1,2},{2,3},{3,4},{4,5},{5,6},{6,7},{7,8},{8,9},{9,10},{10,1... | collective-permute-start | bytes 56 | tf_op jit(solution)/shard_map/ppermute | solution.py:255
  7.7 0.0 copy-start
  7.7 1.1 %copy-done = f32[3,2,128,256]{3,2,1,0:T(8,128)S(1)} copy-done((f32[3,2,128,256]{3,2,1,0:T(8,128)S(1)}, f32[3,2,128,256]{3,2,1,0:T(8,128)}, u32[]{:S(2)}) %copy-start) | copy-done | bytes 786456
  8.9 0.8 %own.1 = (f32[3,2,128,256]{3,2,1,0:T(8,128)S(1)}, f32[3,2,128,128]{3,2,1,0:T(8,128)S(1)}) custom-call(s32[4]{0:T(128)S(1)} %pad_add_fusion.offsets.refs_0_, f32[3,2,128,256]{3,2,1,0:T(8,128)S(1)} %copy-done), custom_call_target="tpu_custom_call" | custom-call | flops 1000000000 | bytes 1966080 | tf_op jit(solution)/shard_map/own/pallas_call | solution.py:220
  9.7 3.7 %collective-permute-done.offsets_prev.refs_1_ = s32[4]{0:T(128)S(1)} collective-permute-done((s32[4]{0:T(128)S(1)}, s32[4]{0:T(128)S(1)}, u32[]{:S(2)}, u32[]{:S(2)}) %collective-permute-start) | collective-permute-done | bytes 48 | tf_op jit(solution)/shard_map/ppermute | solution.py:255
  13.4 0.0 collective-permute-done.1.far.after
  13.4 0.0 copy-start.1
  13.4 0.0 copy-start.2
  13.4 1.0 %prev.1 = (f32[3,2,128,128]{3,2,1,0:T(8,128)S(1)}, f32[3,2,128,128]{3,2,1,0:T(8,128)S(1)}) custom-call(s32[4]{0:T(128)S(1)} %collective-permute-done.offsets_prev.refs_1_, f32[2,128,128]{2,1,0:T(8,128)S(1)} %collective-permute-done.1.far.after, f32[3,2,128,256]{3,2,1,0:T(8,128)S(1)} %get-tuple-element.20.tiles), custom_call_target="tpu_custom_call" | custom-call | flops 1000000000 | bytes 1572864 | tf_op jit(solution)/shard_map/prev/pallas_call | solution.py:220
  14.4 1.4 %collective-permute-start.2 = (f32[3,2,128,128]{3,2,1,0:T(8,128)S(1)}, f32[3,2,128,128]{3,2,1,0:T(8,128)S(1)}, u32[]{:S(2)}, u32[]{:S(2)}) collective-permute-start(f32[3,2,128,128]{3,2,1,0:T(8,128)S(1)} %get-tuple-element.23), channel_id=1, source_target_pairs={{1,0},{2,1},{3,2},{4,3},{5,4},{6,5},{7,6},{8,7},{9,8},{10,9},{11,1... | collective-permute-start | bytes 1179656 | tf_op jit(solution)/shard_map/ppermute | solution.py:261
  15.8 1.3 %collective-permute-start.4 = (f32[3,2,128,128]{3,2,1,0:T(8,128)S(1)}, f32[3,2,128,128]{3,2,1,0:T(8,128)S(1)}, u32[]{:S(2)}, u32[]{:S(2)}) collective-permute-start(f32[3,2,128,128]{3,2,1,0:T(8,128)S(1)} %get-tuple-element.22.refs_5_), channel_id=1, source_target_pairs={{0,16},{1,17},{2,18},{3,19},{4,20},{5,21},{6,22},{7,23},{8,24},{9,... | collective-permute-start | bytes 1179656 | tf_op jit(solution)/shard_map/ppermute | solution.py:264
  17.1 1.3 %collective-permute-start.3 = (f32[3,2,128,128]{3,2,1,0:T(8,128)S(1)}, f32[3,2,128,128]{3,2,1,0:T(8,128)S(1)}, u32[]{:S(2)}, u32[]{:S(2)}) collective-permute-start(f32[3,2,128,128]{3,2,1,0:T(8,128)S(1)} %get-tuple-element.21.refs_4_), channel_id=1, source_target_pairs={{16,0},{17,1},{18,2},{19,3},{20,4},{21,5},{22,6},{23,7},{24,8},{25... | collective-permute-start | bytes 1179656 | tf_op jit(solution)/shard_map/ppermute | solution.py:264
  18.4 0.0 copy-done.1
  18.4 0.0 copy-done.2
  18.4 0.6 load.1
  19.0 3.2 %collective-permute-done.2.x = f32[3,2,128,128]{3,2,1,0:T(8,128)S(1)} collective-permute-done((f32[3,2,128,128]{3,2,1,0:T(8,128)S(1)}, f32[3,2,128,128]{3,2,1,0:T(8,128)S(1)}, u32[]{:S(2)}, u32[]{:S(2)}) %collective-permute-start.2) | collective-permute-done | bytes 393248 | tf_op jit(solution)/shard_map/ppermute | solution.py:261
  22.2 0.0 copy-start.3
  22.3 1.4 %collective-permute-start.5 = (f32[3,2,128,128]{3,2,1,0:T(8,128)S(1)}, f32[3,2,128,128]{3,2,1,0:T(8,128)S(1)}, u32[]{:S(2)}, u32[]{:S(2)}) collective-permute-start(f32[3,2,128,128]{3,2,1,0:T(8,128)S(1)} %hold.1.refs_6_), channel_id=1, source_target_pairs={{0,16},{1,17},{2,18},{3,19},{4,20},{5,21},{6,22},{7,23},{8,24},{9,... | collective-permute-start | bytes 1179656 | tf_op jit(solution)/shard_map/ppermute | solution.py:264
  23.7 0.0 collective-permute-done.4.refs_8_
  23.7 0.0 collective-permute-done.3.refs_7_
  23.7 1.3 %collective-permute-done.5.refs_9_ = f32[3,2,128,128]{3,2,1,0:T(8,128)S(1)} collective-permute-done((f32[3,2,128,128]{3,2,1,0:T(8,128)S(1)}, f32[3,2,128,128]{3,2,1,0:T(8,128)S(1)}, u32[]{:S(2)}, u32[]{:S(2)}) %collective-permute-start.5) | collective-permute-done | bytes 393248 | tf_op jit(solution)/shard_map/ppermute | solution.py:264
  25.0 0.0 copy-done.3
  25.0 6.4 %wave.1 = (f32[3,2,128,128]{3,2,1,0:T(8,128)S(1)}, f32[3,2,128,128]{3,2,1,0:T(8,128)S(1)}, f32[2,64,128]{2,1,0:T(8,128)S(1)}, f32[2,64,128]{2,1,0:T(8,128)S(1)}) custom-call(s32[4]{0:T(128)S(1)} %pad_add_fusion.offsets.refs_0_, bf16[4,2,256,256]{3,2,1,0:T(8,128)(2,1)S(1)} %copy-done.3, f32[2,128,128]{2,1,0:T(8,128)S(1)} %get-tuple-element.18.refs_2_, ...), custom_call_target="tpu_custom_call" | custom-call | flops 5000000000 | bytes 4521984 | tf_op jit(solution)/shard_map/wave/pallas_call | solution.py:220
  31.4 0.4 collective-permute-start.6
  31.9 0.1 collective-permute-start.7
  32.0 1.3 %collective-permute-done.7.refs_1_ = f32[2,64,128]{2,1,0:T(8,128)S(1)} collective-permute-done((f32[2,64,128]{2,1,0:T(8,128)S(1)}, f32[2,64,128]{2,1,0:T(8,128)S(1)}, u32[]{:S(2)}, u32[]{:S(2)}) %collective-permute-start.7) | collective-permute-done | bytes 65568 | tf_op jit(solution)/shard_map/ppermute | solution.py:293
  33.3 0.0 collective-permute-done.6.refs_3_
  33.4 0.1 collective-permute-start.9
  33.4 2.0 %collective-permute-start.8 = (f32[1,2,128,128]{3,2,1,0:T(8,128)S(1)}, f32[1,2,128,128]{3,2,1,0:T(8,128)S(1)}, u32[]{:S(2)}, u32[]{:S(2)}) collective-permute-start(f32[1,2,128,128]{3,2,1,0:T(8,128)S(1)} %get-tuple-element.28), channel_id=1, source_target_pairs={{0,1},{1,2},{2,3},{3,4},{4,5},{5,6},{6,7},{7,8},{8,9},{9,10},{10,1... | collective-permute-start | bytes 393224 | tf_op jit(solution)/shard_map/ppermute | solution.py:331
  35.5 2.9 %collective-permute-done.9.refs_1_ = f32[2,64,128]{2,1,0:T(8,128)S(1)} collective-permute-done((f32[2,64,128]{2,1,0:T(8,128)S(1)}, f32[2,64,128]{2,1,0:T(8,128)S(1)}, u32[]{:S(2)}, u32[]{:S(2)}) %collective-permute-start.9) | collective-permute-done | bytes 65568 | tf_op jit(solution)/shard_map/ppermute | solution.py:241
  38.4 0.1 collective-permute-start.11
  38.5 1.2 %collective-permute-start.10 = (f32[2,2,128,128]{3,2,1,0:T(8,128)S(1)}, f32[2,2,128,128]{3,2,1,0:T(8,128)S(1)}, u32[]{:S(2)}, u32[]{:S(2)}) collective-permute-start(f32[2,2,128,128]{3,2,1,0:T(8,128)S(1)} %get-tuple-element.30), channel_id=1, source_target_pairs={{0,1},{1,2},{2,3},{3,4},{4,5},{5,6},{6,7},{7,8},{8,9},{9,10},{10,1... | collective-permute-start | bytes 786440 | tf_op jit(solution)/shard_map/ppermute | solution.py:331
  39.7 3.4 %collective-permute-done.8.refs_0_ = f32[1,2,128,128]{3,2,1,0:T(8,128)S(1)} collective-permute-done((f32[1,2,128,128]{3,2,1,0:T(8,128)S(1)}, f32[1,2,128,128]{3,2,1,0:T(8,128)S(1)}, u32[]{:S(2)}, u32[]{:S(2)}) %collective-permute-start.8) | collective-permute-done | bytes 131104 | tf_op jit(solution)/shard_map/ppermute | solution.py:331
  43.1 2.9 %collective-permute-done.11.refs_2_ = f32[2,64,128]{2,1,0:T(8,128)S(1)} collective-permute-done((f32[2,64,128]{2,1,0:T(8,128)S(1)}, f32[2,64,128]{2,1,0:T(8,128)S(1)}, u32[]{:S(2)}, u32[]{:S(2)}) %collective-permute-start.11) | collective-permute-done | bytes 65568 | tf_op jit(solution)/shard_map/ppermute | solution.py:241
  46.0 0.6 %collective-permute-start.12 = (f32[2,64,128]{2,1,0:T(8,128)S(1)}, f32[2,64,128]{2,1,0:T(8,128)S(1)}, u32[]{:S(2)}, u32[]{:S(2)}) collective-permute-start(f32[2,64,128]{2,1,0:T(8,128)S(1)} %step.7.refs_1_), channel_id=1, source_target_pairs={{0,4},{1,5},{2,6},{3,7},{4,0},{5,1},{6,2},{7,3},{8,12},{9,13},{10,... | collective-permute-start | bytes 196616 | tf_op jit(solution)/shard_map/ppermute | solution.py:241
  46.6 0.9 %place.1.before.refs_0_ = f32[3,2,128,256]{3,2,1,0:T(8,128)S(1)} custom-call(s32[4]{0:T(128)S(1)} %pad_add_fusion.offsets.refs_0_, s32[4]{0:T(128)S(1)} %collective-permute-done.offsets_prev.refs_1_, f32[3,2,128,128]{3,2,1,0:T(8,128)S(1)} %get-tuple-element.24.refs_2_, f32[3,2,128,128]{3,2,1,0:T(8,128)S(1)} %collective-permute-done.6.refs_3_), custom_call_target="tpu_custom_call" | custom-call | flops 2000000000 | bytes 1572864 | tf_op jit(solution)/shard_map/place/pallas_call | solution.py:220
  47.5 2.8 %collective-permute-done.12.refs_2_ = f32[2,64,128]{2,1,0:T(8,128)S(1)} collective-permute-done((f32[2,64,128]{2,1,0:T(8,128)S(1)}, f32[2,64,128]{2,1,0:T(8,128)S(1)}, u32[]{:S(2)}, u32[]{:S(2)}) %collective-permute-start.12) | collective-permute-done | bytes 65568 | tf_op jit(solution)/shard_map/ppermute | solution.py:241
  50.3 4.9 %collective-permute-start.13 = (f32[2,64,128]{2,1,0:T(8,128)S(1)}, f32[2,64,128]{2,1,0:T(8,128)S(1)}, u32[]{:S(2)}, u32[]{:S(2)}) collective-permute-start(f32[2,64,128]{2,1,0:T(8,128)S(1)} %step.8.refs_1_), channel_id=1, source_target_pairs={{0,8},{1,9},{2,10},{3,11},{4,12},{5,13},{6,14},{7,15},{8,0},{9,1},... | collective-permute-start | bytes 196616 | tf_op jit(solution)/shard_map/ppermute | solution.py:241
  55.2 0.0 collective-permute-done.10.refs_1_
  55.2 1.6 %spill.1 = (f32[3,2,128,256]{3,2,1,0:T(8,128)}, f32[8,128]{1,0:T(8,128)S(1)}) custom-call(s32[4]{0:T(128)S(1)} %collective-permute-done.offsets_prev.refs_1_, f32[3,2,128,256]{3,2,1,0:T(8,128)S(1)} %place.1.before.refs_0_, f32[1,2,128,128]{3,2,1,0:T(8,128)S(1)} %collective-permute-done.8.refs_0_, f32[2,2,128,128]{3,2,1,0:T(8,128)S(1)} %collective-permute-done.10.refs_1_), custom_call_target="tpu_custom_call" | custom-call | flops 1000000000 | bytes 1970176 | tf_op jit(solution)/shard_map/spill/pallas_call | solution.py:220
  56.8 0.6 %collective-permute-done.13.refs_2_ = f32[2,64,128]{2,1,0:T(8,128)S(1)} collective-permute-done((f32[2,64,128]{2,1,0:T(8,128)S(1)}, f32[2,64,128]{2,1,0:T(8,128)S(1)}, u32[]{:S(2)}, u32[]{:S(2)}) %collective-permute-start.13) | collective-permute-done | bytes 65568 | tf_op jit(solution)/shard_map/ppermute | solution.py:241
  57.5 0.6 %step.9 = f32[2,64,128]{2,1,0:T(8,128)} custom-call(f32[8,128]{1,0:T(8,128)S(1)} %get-tuple-element.32.refs_0_, f32[2,64,128]{2,1,0:T(8,128)S(1)} %step.8.refs_1_, f32[2,64,128]{2,1,0:T(8,128)S(1)} %collective-permute-done.13.refs_2_), custom_call_target="tpu_custom_call" | custom-call | flops 1000000000 | bytes 196608 | tf_op jit(solution)/shard_map/step/pallas_call | solution.py:220
  (5 shorter events, 0.1 us)
Async XLA Ops:
  0.6 12.7 %collective-permute-start.1 = (f32[2,128,128]{2,1,0:T(8,128)}, f32[2,128,128]{2,1,0:T(8,128)S(1)}, u32[]{:S(2)}, u32[]{:S(2)}) collective-permute-start(f32[2,128,128]{2,1,0:T(8,128)} %intensity.1), channel_id=1, source_target_pairs={{0,1},{1,2},{2,3},{3,4},{4,5},{5,6},{6,7},{7,8},{8,9},{9,10},{10,1... | collective-permute-start | bytes 393224 | tf_op jit(solution)/shard_map/ppermute | solution.py:252
  6.2 7.1 %collective-permute-start = (s32[4]{0:T(128)S(1)}, s32[4]{0:T(128)S(1)}, u32[]{:S(2)}, u32[]{:S(2)}) collective-permute-start(s32[4]{0:T(128)S(1)} %pad_add_fusion.offsets.refs_0_), channel_id=1, source_target_pairs={{0,1},{1,2},{2,3},{3,4},{4,5},{5,6},{6,7},{7,8},{8,9},{9,10},{10,1... | collective-permute-start | bytes 56 | tf_op jit(solution)/shard_map/ppermute | solution.py:255
  7.7 1.1 %copy-start = (f32[3,2,128,256]{3,2,1,0:T(8,128)S(1)}, f32[3,2,128,256]{3,2,1,0:T(8,128)}, u32[]{:S(2)}) copy-start(f32[3,2,128,256]{3,2,1,0:T(8,128)} %objects.1) | copy-start | bytes 2359300
  13.4 5.0 %copy-start.1 = (f32[2,128,128]{2,1,0:T(8,128)S(1)}, f32[2,128,128]{2,1,0:T(8,128)}, u32[]{:S(2)}) copy-start(f32[2,128,128]{2,1,0:T(8,128)} %intensity.1) | copy-start | bytes 393220
  13.4 5.0 %copy-start.2 = (f32[2,128,128]{2,1,0:T(8,128)S(1)}, f32[2,128,128]{2,1,0:T(8,128)}, u32[]{:S(2)}) copy-start(f32[2,128,128]{2,1,0:T(8,128)} %probe.1) | copy-start | bytes 393220
  14.4 7.8 %collective-permute-start.2 = (f32[3,2,128,128]{3,2,1,0:T(8,128)S(1)}, f32[3,2,128,128]{3,2,1,0:T(8,128)S(1)}, u32[]{:S(2)}, u32[]{:S(2)}) collective-permute-start(f32[3,2,128,128]{3,2,1,0:T(8,128)S(1)} %get-tuple-element.23), channel_id=1, source_target_pairs={{1,0},{2,1},{3,2},{4,3},{5,4},{6,5},{7,6},{8,7},{9,8},{10,9},{11,1... | collective-permute-start | bytes 1179656 | tf_op jit(solution)/shard_map/ppermute | solution.py:261
  15.8 7.9 %collective-permute-start.4 = (f32[3,2,128,128]{3,2,1,0:T(8,128)S(1)}, f32[3,2,128,128]{3,2,1,0:T(8,128)S(1)}, u32[]{:S(2)}, u32[]{:S(2)}) collective-permute-start(f32[3,2,128,128]{3,2,1,0:T(8,128)S(1)} %get-tuple-element.22.refs_5_), channel_id=1, source_target_pairs={{0,16},{1,17},{2,18},{3,19},{4,20},{5,21},{6,22},{7,23},{8,24},{9,... | collective-permute-start | bytes 1179656 | tf_op jit(solution)/shard_map/ppermute | solution.py:264
  17.1 6.6 %collective-permute-start.3 = (f32[3,2,128,128]{3,2,1,0:T(8,128)S(1)}, f32[3,2,128,128]{3,2,1,0:T(8,128)S(1)}, u32[]{:S(2)}, u32[]{:S(2)}) collective-permute-start(f32[3,2,128,128]{3,2,1,0:T(8,128)S(1)} %get-tuple-element.21.refs_4_), channel_id=1, source_target_pairs={{16,0},{17,1},{18,2},{19,3},{20,4},{21,5},{22,6},{23,7},{24,8},{25... | collective-permute-start | bytes 1179656 | tf_op jit(solution)/shard_map/ppermute | solution.py:264
  22.2 2.8 %copy-start.3 = (bf16[4,2,256,256]{3,2,1,0:T(8,128)(2,1)S(1)}, bf16[4,2,256,256]{3,2,1,0:T(8,128)(2,1)}, u32[]{:S(2)}) copy-start(bf16[4,2,256,256]{3,2,1,0:T(8,128)(2,1)} %constant.2.clone.refs_1_) | copy-start | bytes 3145732
  22.3 2.8 %collective-permute-start.5 = (f32[3,2,128,128]{3,2,1,0:T(8,128)S(1)}, f32[3,2,128,128]{3,2,1,0:T(8,128)S(1)}, u32[]{:S(2)}, u32[]{:S(2)}) collective-permute-start(f32[3,2,128,128]{3,2,1,0:T(8,128)S(1)} %hold.1.refs_6_), channel_id=1, source_target_pairs={{0,16},{1,17},{2,18},{3,19},{4,20},{5,21},{6,22},{7,23},{8,24},{9,... | collective-permute-start | bytes 1179656 | tf_op jit(solution)/shard_map/ppermute | solution.py:264
  31.4 1.9 %collective-permute-start.6 = (f32[3,2,128,128]{3,2,1,0:T(8,128)S(1)}, f32[3,2,128,128]{3,2,1,0:T(8,128)S(1)}, u32[]{:S(2)}, u32[]{:S(2)}) collective-permute-start(f32[3,2,128,128]{3,2,1,0:T(8,128)S(1)} %get-tuple-element.25), channel_id=1, source_target_pairs={{0,16},{16,0},{1,17},{17,1},{2,18},{18,2},{3,19},{19,3},{4,20},{20... | collective-permute-start | bytes 1179656 | tf_op jit(solution)/shard_map/ppermute | solution.py:294
  31.9 1.4 %collective-permute-start.7 = (f32[2,64,128]{2,1,0:T(8,128)S(1)}, f32[2,64,128]{2,1,0:T(8,128)S(1)}, u32[]{:S(2)}, u32[]{:S(2)}) collective-permute-start(f32[2,64,128]{2,1,0:T(8,128)S(1)} %get-tuple-element.27), channel_id=1, source_target_pairs={{0,16},{16,0},{1,17},{17,1},{2,18},{18,2},{3,19},{19,3},{4,20},{20... | collective-permute-start | bytes 196616 | tf_op jit(solution)/shard_map/ppermute | solution.py:293
  33.4 5.0 %collective-permute-start.9 = (f32[2,64,128]{2,1,0:T(8,128)S(1)}, f32[2,64,128]{2,1,0:T(8,128)S(1)}, u32[]{:S(2)}, u32[]{:S(2)}) collective-permute-start(f32[2,64,128]{2,1,0:T(8,128)S(1)} %get-tuple-element.29.refs_0_), channel_id=1, source_target_pairs={{0,1},{1,0},{2,3},{3,2},{4,5},{5,4},{6,7},{7,6},{8,9},{9,8},{10,11... | collective-permute-start | bytes 196616 | tf_op jit(solution)/shard_map/ppermute | solution.py:241
  33.4 9.6 %collective-permute-start.8 = (f32[1,2,128,128]{3,2,1,0:T(8,128)S(1)}, f32[1,2,128,128]{3,2,1,0:T(8,128)S(1)}, u32[]{:S(2)}, u32[]{:S(2)}) collective-permute-start(f32[1,2,128,128]{3,2,1,0:T(8,128)S(1)} %get-tuple-element.28), channel_id=1, source_target_pairs={{0,1},{1,2},{2,3},{3,4},{4,5},{5,6},{6,7},{7,8},{8,9},{9,10},{10,1... | collective-permute-start | bytes 393224 | tf_op jit(solution)/shard_map/ppermute | solution.py:331
  38.4 7.5 %collective-permute-start.11 = (f32[2,64,128]{2,1,0:T(8,128)S(1)}, f32[2,64,128]{2,1,0:T(8,128)S(1)}, u32[]{:S(2)}, u32[]{:S(2)}) collective-permute-start(f32[2,64,128]{2,1,0:T(8,128)S(1)} %get-tuple-element.33.refs_1_), channel_id=1, source_target_pairs={{0,2},{1,3},{2,0},{3,1},{4,6},{5,7},{6,4},{7,5},{8,10},{9,11},{10,... | collective-permute-start | bytes 196616 | tf_op jit(solution)/shard_map/ppermute | solution.py:241
  38.5 16.8 %collective-permute-start.10 = (f32[2,2,128,128]{3,2,1,0:T(8,128)S(1)}, f32[2,2,128,128]{3,2,1,0:T(8,128)S(1)}, u32[]{:S(2)}, u32[]{:S(2)}) collective-permute-start(f32[2,2,128,128]{3,2,1,0:T(8,128)S(1)} %get-tuple-element.30), channel_id=1, source_target_pairs={{0,1},{1,2},{2,3},{3,4},{4,5},{5,6},{6,7},{7,8},{8,9},{9,10},{10,1... | collective-permute-start | bytes 786440 | tf_op jit(solution)/shard_map/ppermute | solution.py:331
  46.0 4.3 %collective-permute-start.12 = (f32[2,64,128]{2,1,0:T(8,128)S(1)}, f32[2,64,128]{2,1,0:T(8,128)S(1)}, u32[]{:S(2)}, u32[]{:S(2)}) collective-permute-start(f32[2,64,128]{2,1,0:T(8,128)S(1)} %step.7.refs_1_), channel_id=1, source_target_pairs={{0,4},{1,5},{2,6},{3,7},{4,0},{5,1},{6,2},{7,3},{8,12},{9,13},{10,... | collective-permute-start | bytes 196616 | tf_op jit(solution)/shard_map/ppermute | solution.py:241
  50.3 7.2 %collective-permute-start.13 = (f32[2,64,128]{2,1,0:T(8,128)S(1)}, f32[2,64,128]{2,1,0:T(8,128)S(1)}, u32[]{:S(2)}, u32[]{:S(2)}) collective-permute-start(f32[2,64,128]{2,1,0:T(8,128)S(1)} %step.8.refs_1_), channel_id=1, source_target_pairs={{0,8},{1,9},{2,10},{3,11},{4,12},{5,13},{6,14},{7,15},{8,0},{9,1},... | collective-permute-start | bytes 196616 | tf_op jit(solution)/shard_map/ppermute | solution.py:241

commit v16 on v15

--- a/solution.py
+++ b/solution.py
@@ -236,7 +236,8 @@
     levels = scan_count.bit_length() - 1
     route = []
     for d in range(depth_count):
-        step = 1 << (1 + (level - 1 + d % 2) % (levels - 1) if level else 0)
+        middle = level + 1 if d % 2 else levels - level
+        step = 1 << (0 if level == 0 else 1 if level == levels - 1 else middle)
         route += [(d * scan_count + i, d * scan_count + (i ^ step)) for i in range(scan_count)]
     return lax.ppermute(x, ("depth", "scan"), route)
 

time: 58.8 us -> 54.5 us (0.927)
  starting transfers between devices: 21.3 us -> 18 us
  waiting for transfers between devices: 22.1 us -> 21.5 us
    ppermute x4, starting transfers between devices: 5.71 us -> 2.69 us  [sum_round(): return lax.ppermute(x, ('depth', 'scan'), route)]
    ppermute x4, waiting for transfers between devices: 9.21 us -> 6.91 us  [sum_round(): return lax.ppermute(x, ('depth', 'scan'), route)]
    ppermute x2, waiting for transfers between devices: 3.37 us -> 5.06 us  [body(): spill += [lax.ppermute(x, 'scan', ahead) for x in payload]]
where the time goes in v16:
time: 54.5 us; the launch traced here: 54.2 us
  waiting for transfers between devices  21.5 us (39%)
  starting transfers between devices  18 us (33%)
  Pallas kernels  12 us (22%)
  local copies, waits for them, and re-layouts  1.14 us (2%)
  between operations  0.79 us (1%)
  other arithmetic  0.75 us (1%)
    pallas_call x12, Pallas kernels, call(): pl.pallas_call(kernel, name=name, out_shape=outs, in_specs=[pl.BlockSpec(...  12 us
    ppermute x4, waiting for transfers between devices, sum_round(): return lax.ppermute(x, ('depth', 'scan'), route)  6.91 us
    ppermute x2, waiting for transfers between devices, body(): spill += [lax.ppermute(x, 'scan', ahead) for x in payload]  5.06 us
    ppermute x1, starting transfers between devices, across(): return lax.ppermute(x, ('depth', 'scan'), route)  4.85 us
    ppermute x3, starting transfers between devices, gathered(): lax.ppermute(x, 'depth', [((target - j) % depth_count, target)])  4.04 us
    ppermute x1, waiting for transfers between devices, body(): lax.ppermute(offsets, 'scan', [(i, (i + 1) % scan_count) for i in range(s...  3.67 us
    ppermute x1, waiting for transfers between devices, body(): lax.ppermute(halo, 'scan', [((i + 1) % scan_count, i) for i in range(scan...  3.25 us
    ppermute x2, starting transfers between devices, body(): spill += [lax.ppermute(x, 'scan', ahead) for x in payload]  2.99 us
  transfers between devices with their start and end apart: 14, of which 9 were waited for; matrix products, arithmetic and copies ran while one was open for 1% of the time, Pallas kernels for 7%

profile of v16, /device:TPU:0, one launch (start us, length us, event | category | flops | bytes accessed | tf_op | source)
XLA Modules:
  0.0 54.2 jit_solution(7598275836497315001)
XLA Ops:
  0.6 4.8 %collective-permute-start.1 = (f32[2,128,128]{2,1,0:T(8,128)}, f32[2,128,128]{2,1,0:T(8,128)S(1)}, u32[]{:S(2)}, u32[]{:S(2)}) collective-permute-start(f32[2,128,128]{2,1,0:T(8,128)} %intensity.1), channel_id=1, source_target_pairs={{0,1},{1,2},{2,3},{3,4},{4,5},{5,6},{6,7},{7,8},{8,9},{9,10},{10,1... | collective-permute-start | bytes 393224 | tf_op jit(solution)/shard_map/ppermute | solution.py:253
  5.5 0.7 %pad_add_fusion.offsets.refs_0_ = s32[4]{0:T(128)S(1)} fusion(s32[2]{0:T(128)} %param.9, s32[2]{0:T(128)} %param.8), kind=kLoop, calls=%fused_computation | loop fusion | flops 4 | bytes 32 | tf_op jit(solution)/shard_map/concatenate | solution.py:255
  6.2 1.5 %collective-permute-start = (s32[4]{0:T(128)S(1)}, s32[4]{0:T(128)S(1)}, u32[]{:S(2)}, u32[]{:S(2)}) collective-permute-start(s32[4]{0:T(128)S(1)} %pad_add_fusion.offsets.refs_0_), channel_id=1, source_target_pairs={{0,1},{1,2},{2,3},{3,4},{4,5},{5,6},{6,7},{7,8},{8,9},{9,10},{10,1... | collective-permute-start | bytes 56 | tf_op jit(solution)/shard_map/ppermute | solution.py:256
  7.7 0.0 copy-start
  7.7 1.1 %copy-done = f32[3,2,128,256]{3,2,1,0:T(8,128)S(1)} copy-done((f32[3,2,128,256]{3,2,1,0:T(8,128)S(1)}, f32[3,2,128,256]{3,2,1,0:T(8,128)}, u32[]{:S(2)}) %copy-start) | copy-done | bytes 786456
  8.9 0.8 %own.1 = (f32[3,2,128,256]{3,2,1,0:T(8,128)S(1)}, f32[3,2,128,128]{3,2,1,0:T(8,128)S(1)}) custom-call(s32[4]{0:T(128)S(1)} %pad_add_fusion.offsets.refs_0_, f32[3,2,128,256]{3,2,1,0:T(8,128)S(1)} %copy-done), custom_call_target="tpu_custom_call" | custom-call | flops 1000000000 | bytes 1966080 | tf_op jit(solution)/shard_map/own/pallas_call | solution.py:220
  9.7 3.7 %collective-permute-done.offsets_prev.refs_1_ = s32[4]{0:T(128)S(1)} collective-permute-done((s32[4]{0:T(128)S(1)}, s32[4]{0:T(128)S(1)}, u32[]{:S(2)}, u32[]{:S(2)}) %collective-permute-start) | collective-permute-done | bytes 48 | tf_op jit(solution)/shard_map/ppermute | solution.py:256
  13.4 0.0 collective-permute-done.1.far.after
  13.4 0.0 copy-start.1
  13.4 0.0 copy-start.2
  13.4 1.0 %prev.1 = (f32[3,2,128,128]{3,2,1,0:T(8,128)S(1)}, f32[3,2,128,128]{3,2,1,0:T(8,128)S(1)}) custom-call(s32[4]{0:T(128)S(1)} %collective-permute-done.offsets_prev.refs_1_, f32[2,128,128]{2,1,0:T(8,128)S(1)} %collective-permute-done.1.far.after, f32[3,2,128,256]{3,2,1,0:T(8,128)S(1)} %get-tuple-element.20.tiles), custom_call_target="tpu_custom_call" | custom-call | flops 1000000000 | bytes 1572864 | tf_op jit(solution)/shard_map/prev/pallas_call | solution.py:220
  14.4 1.4 %collective-permute-start.2 = (f32[3,2,128,128]{3,2,1,0:T(8,128)S(1)}, f32[3,2,128,128]{3,2,1,0:T(8,128)S(1)}, u32[]{:S(2)}, u32[]{:S(2)}) collective-permute-start(f32[3,2,128,128]{3,2,1,0:T(8,128)S(1)} %get-tuple-element.23), channel_id=1, source_target_pairs={{1,0},{2,1},{3,2},{4,3},{5,4},{6,5},{7,6},{8,7},{9,8},{10,9},{11,1... | collective-permute-start | bytes 1179656 | tf_op jit(solution)/shard_map/ppermute | solution.py:262
  15.8 1.3 %collective-permute-start.4 = (f32[3,2,128,128]{3,2,1,0:T(8,128)S(1)}, f32[3,2,128,128]{3,2,1,0:T(8,128)S(1)}, u32[]{:S(2)}, u32[]{:S(2)}) collective-permute-start(f32[3,2,128,128]{3,2,1,0:T(8,128)S(1)} %get-tuple-element.22.refs_5_), channel_id=1, source_target_pairs={{0,16},{1,17},{2,18},{3,19},{4,20},{5,21},{6,22},{7,23},{8,24},{9,... | collective-permute-start | bytes 1179656 | tf_op jit(solution)/shard_map/ppermute | solution.py:265
  17.1 1.3 %collective-permute-start.3 = (f32[3,2,128,128]{3,2,1,0:T(8,128)S(1)}, f32[3,2,128,128]{3,2,1,0:T(8,128)S(1)}, u32[]{:S(2)}, u32[]{:S(2)}) collective-permute-start(f32[3,2,128,128]{3,2,1,0:T(8,128)S(1)} %get-tuple-element.21.refs_4_), channel_id=1, source_target_pairs={{16,0},{17,1},{18,2},{19,3},{20,4},{21,5},{22,6},{23,7},{24,8},{25... | collective-permute-start | bytes 1179656 | tf_op jit(solution)/shard_map/ppermute | solution.py:265
  18.4 0.0 copy-done.1
  18.4 0.0 copy-done.2
  18.4 0.6 %load.1 = (f32[128,128]{1,0:T(8,128)S(1)}, f32[2,128,128]{2,1,0:T(8,128)S(1)}) custom-call(s32[4]{0:T(128)S(1)} %pad_add_fusion.offsets.refs_0_, s32[4]{0:T(128)S(1)} %collective-permute-done.offsets_prev.refs_1_, f32[2,128,128]{2,1,0:T(8,128)S(1)} %copy-done.1, f32[2,128,128]{2,1,0:T(8,128)S(1)} %collective-permute-done.1.far.after, ...), custom_call_target="tpu_custom_call" | custom-call | flops 1000000000 | bytes 589824 | tf_op jit(solution)/shard_map/load/pallas_call | solution.py:220
  19.0 3.2 %collective-permute-done.2.x = f32[3,2,128,128]{3,2,1,0:T(8,128)S(1)} collective-permute-done((f32[3,2,128,128]{3,2,1,0:T(8,128)S(1)}, f32[3,2,128,128]{3,2,1,0:T(8,128)S(1)}, u32[]{:S(2)}, u32[]{:S(2)}) %collective-permute-start.2) | collective-permute-done | bytes 393248 | tf_op jit(solution)/shard_map/ppermute | solution.py:262
  22.2 0.0 copy-start.3
  22.3 1.4 %collective-permute-start.5 = (f32[3,2,128,128]{3,2,1,0:T(8,128)S(1)}, f32[3,2,128,128]{3,2,1,0:T(8,128)S(1)}, u32[]{:S(2)}, u32[]{:S(2)}) collective-permute-start(f32[3,2,128,128]{3,2,1,0:T(8,128)S(1)} %hold.1.refs_6_), channel_id=1, source_target_pairs={{0,16},{1,17},{2,18},{3,19},{4,20},{5,21},{6,22},{7,23},{8,24},{9,... | collective-permute-start | bytes 1179656 | tf_op jit(solution)/shard_map/ppermute | solution.py:265
  23.7 0.0 collective-permute-done.4.refs_8_
  23.7 0.0 collective-permute-done.3.refs_7_
  23.7 1.3 %collective-permute-done.5.refs_9_ = f32[3,2,128,128]{3,2,1,0:T(8,128)S(1)} collective-permute-done((f32[3,2,128,128]{3,2,1,0:T(8,128)S(1)}, f32[3,2,128,128]{3,2,1,0:T(8,128)S(1)}, u32[]{:S(2)}, u32[]{:S(2)}) %collective-permute-start.5) | collective-permute-done | bytes 393248 | tf_op jit(solution)/shard_map/ppermute | solution.py:265
  25.0 0.0 copy-done.3
  25.0 6.4 %wave.1 = (f32[3,2,128,128]{3,2,1,0:T(8,128)S(1)}, f32[3,2,128,128]{3,2,1,0:T(8,128)S(1)}, f32[2,64,128]{2,1,0:T(8,128)S(1)}, f32[2,64,128]{2,1,0:T(8,128)S(1)}) custom-call(s32[4]{0:T(128)S(1)} %pad_add_fusion.offsets.refs_0_, bf16[4,2,256,256]{3,2,1,0:T(8,128)(2,1)S(1)} %copy-done.3, f32[2,128,128]{2,1,0:T(8,128)S(1)} %get-tuple-element.18.refs_2_, ...), custom_call_target="tpu_custom_call" | custom-call | flops 5000000000 | bytes 4521984 | tf_op jit(solution)/shard_map/wave/pallas_call | solution.py:220
  31.4 0.4 collective-permute-start.6
  31.9 0.1 collective-permute-start.7
  32.0 1.3 %collective-permute-done.7.refs_1_ = f32[2,64,128]{2,1,0:T(8,128)S(1)} collective-permute-done((f32[2,64,128]{2,1,0:T(8,128)S(1)}, f32[2,64,128]{2,1,0:T(8,128)S(1)}, u32[]{:S(2)}, u32[]{:S(2)}) %collective-permute-start.7) | collective-permute-done | bytes 65568 | tf_op jit(solution)/shard_map/ppermute | solution.py:294
  33.3 0.0 collective-permute-done.6.refs_3_
  33.4 0.1 collective-permute-start.9
  33.4 2.0 %collective-permute-start.8 = (f32[1,2,128,128]{3,2,1,0:T(8,128)S(1)}, f32[1,2,128,128]{3,2,1,0:T(8,128)S(1)}, u32[]{:S(2)}, u32[]{:S(2)}) collective-permute-start(f32[1,2,128,128]{3,2,1,0:T(8,128)S(1)} %get-tuple-element.28), channel_id=1, source_target_pairs={{0,1},{1,2},{2,3},{3,4},{4,5},{5,6},{6,7},{7,8},{8,9},{9,10},{10,1... | collective-permute-start | bytes 393224 | tf_op jit(solution)/shard_map/ppermute | solution.py:332
  35.5 2.9 %collective-permute-done.9.refs_1_ = f32[2,64,128]{2,1,0:T(8,128)S(1)} collective-permute-done((f32[2,64,128]{2,1,0:T(8,128)S(1)}, f32[2,64,128]{2,1,0:T(8,128)S(1)}, u32[]{:S(2)}, u32[]{:S(2)}) %collective-permute-start.9) | collective-permute-done | bytes 65568 | tf_op jit(solution)/shard_map/ppermute | solution.py:242
  38.4 0.3 collective-permute-start.11
  38.7 1.0 %collective-permute-start.10 = (f32[2,2,128,128]{3,2,1,0:T(8,128)S(1)}, f32[2,2,128,128]{3,2,1,0:T(8,128)S(1)}, u32[]{:S(2)}, u32[]{:S(2)}) collective-permute-start(f32[2,2,128,128]{3,2,1,0:T(8,128)S(1)} %get-tuple-element.30), channel_id=1, source_target_pairs={{0,1},{1,2},{2,3},{3,4},{4,5},{5,6},{6,7},{7,8},{8,9},{9,10},{10,1... | collective-permute-start | bytes 786440 | tf_op jit(solution)/shard_map/ppermute | solution.py:332
  39.7 3.3 %collective-permute-done.8.refs_0_ = f32[1,2,128,128]{3,2,1,0:T(8,128)S(1)} collective-permute-done((f32[1,2,128,128]{3,2,1,0:T(8,128)S(1)}, f32[1,2,128,128]{3,2,1,0:T(8,128)S(1)}, u32[]{:S(2)}, u32[]{:S(2)}) %collective-permute-start.8) | collective-permute-done | bytes 131104 | tf_op jit(solution)/shard_map/ppermute | solution.py:332
  43.0 0.7 %collective-permute-done.11.refs_2_ = f32[2,64,128]{2,1,0:T(8,128)S(1)} collective-permute-done((f32[2,64,128]{2,1,0:T(8,128)S(1)}, f32[2,64,128]{2,1,0:T(8,128)S(1)}, u32[]{:S(2)}, u32[]{:S(2)}) %collective-permute-start.11) | collective-permute-done | bytes 65568 | tf_op jit(solution)/shard_map/ppermute | solution.py:242
  43.6 0.1 collective-permute-start.12
  43.7 0.9 %place.1.before.refs_0_ = f32[3,2,128,256]{3,2,1,0:T(8,128)S(1)} custom-call(s32[4]{0:T(128)S(1)} %pad_add_fusion.offsets.refs_0_, s32[4]{0:T(128)S(1)} %collective-permute-done.offsets_prev.refs_1_, f32[3,2,128,128]{3,2,1,0:T(8,128)S(1)} %get-tuple-element.24.refs_2_, f32[3,2,128,128]{3,2,1,0:T(8,128)S(1)} %collective-permute-done.6.refs_3_), custom_call_target="tpu_custom_call" | custom-call | flops 2000000000 | bytes 1572864 | tf_op jit(solution)/shard_map/place/pallas_call | solution.py:220
  44.6 3.4 %collective-permute-done.12.refs_2_ = f32[2,64,128]{2,1,0:T(8,128)S(1)} collective-permute-done((f32[2,64,128]{2,1,0:T(8,128)S(1)}, f32[2,64,128]{2,1,0:T(8,128)S(1)}, u32[]{:S(2)}, u32[]{:S(2)}) %collective-permute-start.12) | collective-permute-done | bytes 65568 | tf_op jit(solution)/shard_map/ppermute | solution.py:242
  48.0 2.3 %collective-permute-start.13 = (f32[2,64,128]{2,1,0:T(8,128)S(1)}, f32[2,64,128]{2,1,0:T(8,128)S(1)}, u32[]{:S(2)}, u32[]{:S(2)}) collective-permute-start(f32[2,64,128]{2,1,0:T(8,128)S(1)} %step.8.refs_1_), channel_id=1, source_target_pairs={{0,2},{1,3},{2,0},{3,1},{4,6},{5,7},{6,4},{7,5},{8,10},{9,11},{10,... | collective-permute-start | bytes 196616 | tf_op jit(solution)/shard_map/ppermute | solution.py:242
  50.2 1.7 %collective-permute-done.10.refs_1_ = f32[2,2,128,128]{3,2,1,0:T(8,128)S(1)} collective-permute-done((f32[2,2,128,128]{3,2,1,0:T(8,128)S(1)}, f32[2,2,128,128]{3,2,1,0:T(8,128)S(1)}, u32[]{:S(2)}, u32[]{:S(2)}) %collective-permute-start.10) | collective-permute-done | bytes 262176 | tf_op jit(solution)/shard_map/ppermute | solution.py:332
  52.0 1.6 %spill.1 = (f32[3,2,128,256]{3,2,1,0:T(8,128)}, f32[8,128]{1,0:T(8,128)S(1)}) custom-call(s32[4]{0:T(128)S(1)} %collective-permute-done.offsets_prev.refs_1_, f32[3,2,128,256]{3,2,1,0:T(8,128)S(1)} %place.1.before.refs_0_, f32[1,2,128,128]{3,2,1,0:T(8,128)S(1)} %collective-permute-done.8.refs_0_, f32[2,2,128,128]{3,2,1,0:T(8,128)S(1)} %collective-permute-done.10.refs_1_), custom_call_target="tpu_custom_call" | custom-call | flops 1000000000 | bytes 1970176 | tf_op jit(solution)/shard_map/spill/pallas_call | solution.py:220
  53.6 0.0 collective-permute-done.13.refs_2_
  53.6 0.6 %step.9 = f32[2,64,128]{2,1,0:T(8,128)} custom-call(f32[8,128]{1,0:T(8,128)S(1)} %get-tuple-element.32.refs_0_, f32[2,64,128]{2,1,0:T(8,128)S(1)} %step.8.refs_1_, f32[2,64,128]{2,1,0:T(8,128)S(1)} %collective-permute-done.13.refs_2_), custom_call_target="tpu_custom_call" | custom-call | flops 1000000000 | bytes 196608 | tf_op jit(solution)/shard_map/step/pallas_call | solution.py:220
  (5 shorter events, 0.1 us)
Async XLA Ops:
  0.6 12.7 %collective-permute-start.1 = (f32[2,128,128]{2,1,0:T(8,128)}, f32[2,128,128]{2,1,0:T(8,128)S(1)}, u32[]{:S(2)}, u32[]{:S(2)}) collective-permute-start(f32[2,128,128]{2,1,0:T(8,128)} %intensity.1), channel_id=1, source_target_pairs={{0,1},{1,2},{2,3},{3,4},{4,5},{5,6},{6,7},{7,8},{8,9},{9,10},{10,1... | collective-permute-start | bytes 393224 | tf_op jit(solution)/shard_map/ppermute | solution.py:253
  6.2 7.1 %collective-permute-start = (s32[4]{0:T(128)S(1)}, s32[4]{0:T(128)S(1)}, u32[]{:S(2)}, u32[]{:S(2)}) collective-permute-start(s32[4]{0:T(128)S(1)} %pad_add_fusion.offsets.refs_0_), channel_id=1, source_target_pairs={{0,1},{1,2},{2,3},{3,4},{4,5},{5,6},{6,7},{7,8},{8,9},{9,10},{10,1... | collective-permute-start | bytes 56 | tf_op jit(solution)/shard_map/ppermute | solution.py:256
  7.7 1.1 %copy-start = (f32[3,2,128,256]{3,2,1,0:T(8,128)S(1)}, f32[3,2,128,256]{3,2,1,0:T(8,128)}, u32[]{:S(2)}) copy-start(f32[3,2,128,256]{3,2,1,0:T(8,128)} %objects.1) | copy-start | bytes 2359300
  13.4 5.0 %copy-start.1 = (f32[2,128,128]{2,1,0:T(8,128)S(1)}, f32[2,128,128]{2,1,0:T(8,128)}, u32[]{:S(2)}) copy-start(f32[2,128,128]{2,1,0:T(8,128)} %intensity.1) | copy-start | bytes 393220
  13.4 5.0 %copy-start.2 = (f32[2,128,128]{2,1,0:T(8,128)S(1)}, f32[2,128,128]{2,1,0:T(8,128)}, u32[]{:S(2)}) copy-start(f32[2,128,128]{2,1,0:T(8,128)} %probe.1) | copy-start | bytes 393220
  14.4 7.8 %collective-permute-start.2 = (f32[3,2,128,128]{3,2,1,0:T(8,128)S(1)}, f32[3,2,128,128]{3,2,1,0:T(8,128)S(1)}, u32[]{:S(2)}, u32[]{:S(2)}) collective-permute-start(f32[3,2,128,128]{3,2,1,0:T(8,128)S(1)} %get-tuple-element.23), channel_id=1, source_target_pairs={{1,0},{2,1},{3,2},{4,3},{5,4},{6,5},{7,6},{8,7},{9,8},{10,9},{11,1... | collective-permute-start | bytes 1179656 | tf_op jit(solution)/shard_map/ppermute | solution.py:262
  15.8 7.9 %collective-permute-start.4 = (f32[3,2,128,128]{3,2,1,0:T(8,128)S(1)}, f32[3,2,128,128]{3,2,1,0:T(8,128)S(1)}, u32[]{:S(2)}, u32[]{:S(2)}) collective-permute-start(f32[3,2,128,128]{3,2,1,0:T(8,128)S(1)} %get-tuple-element.22.refs_5_), channel_id=1, source_target_pairs={{0,16},{1,17},{2,18},{3,19},{4,20},{5,21},{6,22},{7,23},{8,24},{9,... | collective-permute-start | bytes 1179656 | tf_op jit(solution)/shard_map/ppermute | solution.py:265
  17.1 6.6 %collective-permute-start.3 = (f32[3,2,128,128]{3,2,1,0:T(8,128)S(1)}, f32[3,2,128,128]{3,2,1,0:T(8,128)S(1)}, u32[]{:S(2)}, u32[]{:S(2)}) collective-permute-start(f32[3,2,128,128]{3,2,1,0:T(8,128)S(1)} %get-tuple-element.21.refs_4_), channel_id=1, source_target_pairs={{16,0},{17,1},{18,2},{19,3},{20,4},{21,5},{22,6},{23,7},{24,8},{25... | collective-permute-start | bytes 1179656 | tf_op jit(solution)/shard_map/ppermute | solution.py:265
  22.2 2.8 %copy-start.3 = (bf16[4,2,256,256]{3,2,1,0:T(8,128)(2,1)S(1)}, bf16[4,2,256,256]{3,2,1,0:T(8,128)(2,1)}, u32[]{:S(2)}) copy-start(bf16[4,2,256,256]{3,2,1,0:T(8,128)(2,1)} %constant.2.clone.refs_1_) | copy-start | bytes 3145732
  22.3 2.8 %collective-permute-start.5 = (f32[3,2,128,128]{3,2,1,0:T(8,128)S(1)}, f32[3,2,128,128]{3,2,1,0:T(8,128)S(1)}, u32[]{:S(2)}, u32[]{:S(2)}) collective-permute-start(f32[3,2,128,128]{3,2,1,0:T(8,128)S(1)} %hold.1.refs_6_), channel_id=1, source_target_pairs={{0,16},{1,17},{2,18},{3,19},{4,20},{5,21},{6,22},{7,23},{8,24},{9,... | collective-permute-start | bytes 1179656 | tf_op jit(solution)/shard_map/ppermute | solution.py:265
  31.4 1.9 %collective-permute-start.6 = (f32[3,2,128,128]{3,2,1,0:T(8,128)S(1)}, f32[3,2,128,128]{3,2,1,0:T(8,128)S(1)}, u32[]{:S(2)}, u32[]{:S(2)}) collective-permute-start(f32[3,2,128,128]{3,2,1,0:T(8,128)S(1)} %get-tuple-element.25), channel_id=1, source_target_pairs={{0,16},{16,0},{1,17},{17,1},{2,18},{18,2},{3,19},{19,3},{4,20},{20... | collective-permute-start | bytes 1179656 | tf_op jit(solution)/shard_map/ppermute | solution.py:295
  31.9 1.4 %collective-permute-start.7 = (f32[2,64,128]{2,1,0:T(8,128)S(1)}, f32[2,64,128]{2,1,0:T(8,128)S(1)}, u32[]{:S(2)}, u32[]{:S(2)}) collective-permute-start(f32[2,64,128]{2,1,0:T(8,128)S(1)} %get-tuple-element.27), channel_id=1, source_target_pairs={{0,16},{16,0},{1,17},{17,1},{2,18},{18,2},{3,19},{19,3},{4,20},{20... | collective-permute-start | bytes 196616 | tf_op jit(solution)/shard_map/ppermute | solution.py:294
  33.4 5.0 %collective-permute-start.9 = (f32[2,64,128]{2,1,0:T(8,128)S(1)}, f32[2,64,128]{2,1,0:T(8,128)S(1)}, u32[]{:S(2)}, u32[]{:S(2)}) collective-permute-start(f32[2,64,128]{2,1,0:T(8,128)S(1)} %get-tuple-element.29.refs_0_), channel_id=1, source_target_pairs={{0,1},{1,0},{2,3},{3,2},{4,5},{5,4},{6,7},{7,6},{8,9},{9,8},{10,11... | collective-permute-start | bytes 196616 | tf_op jit(solution)/shard_map/ppermute | solution.py:242
  33.4 9.5 %collective-permute-start.8 = (f32[1,2,128,128]{3,2,1,0:T(8,128)S(1)}, f32[1,2,128,128]{3,2,1,0:T(8,128)S(1)}, u32[]{:S(2)}, u32[]{:S(2)}) collective-permute-start(f32[1,2,128,128]{3,2,1,0:T(8,128)S(1)} %get-tuple-element.28), channel_id=1, source_target_pairs={{0,1},{1,2},{2,3},{3,4},{4,5},{5,6},{6,7},{7,8},{8,9},{9,10},{10,1... | collective-permute-start | bytes 393224 | tf_op jit(solution)/shard_map/ppermute | solution.py:332
  38.4 5.2 %collective-permute-start.11 = (f32[2,64,128]{2,1,0:T(8,128)S(1)}, f32[2,64,128]{2,1,0:T(8,128)S(1)}, u32[]{:S(2)}, u32[]{:S(2)}) collective-permute-start(f32[2,64,128]{2,1,0:T(8,128)S(1)} %get-tuple-element.33.refs_1_), channel_id=1, source_target_pairs={{0,8},{1,9},{2,10},{3,11},{4,12},{5,13},{6,14},{7,15},{8,0},{9,1},... | collective-permute-start | bytes 196616 | tf_op jit(solution)/shard_map/ppermute | solution.py:242
  38.7 13.3 %collective-permute-start.10 = (f32[2,2,128,128]{3,2,1,0:T(8,128)S(1)}, f32[2,2,128,128]{3,2,1,0:T(8,128)S(1)}, u32[]{:S(2)}, u32[]{:S(2)}) collective-permute-start(f32[2,2,128,128]{3,2,1,0:T(8,128)S(1)} %get-tuple-element.30), channel_id=1, source_target_pairs={{0,1},{1,2},{2,3},{3,4},{4,5},{5,6},{6,7},{7,8},{8,9},{9,10},{10,1... | collective-permute-start | bytes 786440 | tf_op jit(solution)/shard_map/ppermute | solution.py:332
  43.6 4.3 %collective-permute-start.12 = (f32[2,64,128]{2,1,0:T(8,128)S(1)}, f32[2,64,128]{2,1,0:T(8,128)S(1)}, u32[]{:S(2)}, u32[]{:S(2)}) collective-permute-start(f32[2,64,128]{2,1,0:T(8,128)S(1)} %step.7.refs_1_), channel_id=1, source_target_pairs={{0,4},{1,5},{2,6},{3,7},{4,0},{5,1},{6,2},{7,3},{8,12},{9,13},{10,... | collective-permute-start | bytes 196616 | tf_op jit(solution)/shard_map/ppermute | solution.py:242
  48.0 5.6 %collective-permute-start.13 = (f32[2,64,128]{2,1,0:T(8,128)S(1)}, f32[2,64,128]{2,1,0:T(8,128)S(1)}, u32[]{:S(2)}, u32[]{:S(2)}) collective-permute-start(f32[2,64,128]{2,1,0:T(8,128)S(1)} %step.8.refs_1_), channel_id=1, source_target_pairs={{0,2},{1,3},{2,0},{3,1},{4,6},{5,7},{6,4},{7,5},{8,10},{9,11},{10,... | collective-permute-start | bytes 196616 | tf_op jit(solution)/shard_map/ppermute | solution.py:242

commit v17 on v13

--- a/solution.py
+++ b/solution.py
@@ -247,13 +247,9 @@
     depth_count, scan_count = lax.axis_size("depth"), lax.axis_size("scan")
     f32 = jnp.float32
 
-    def across(x, source, target, shift):
-        route = [(source * scan_count + i, target * scan_count + (i + shift) % scan_count) for i in range(scan_count)]
-        return lax.ppermute(x, ("depth", "scan"), route)
-
     offsets = jnp.concatenate([row_offsets, col_offsets])
     offsets_prev = lax.ppermute(offsets, "scan", [(i, (i + 1) % scan_count) for i in range(scan_count)])
-    far = across(intensity, 0, 0, 1)
+    far = lax.ppermute(intensity, "scan", [(i, (i + 1) % scan_count) for i in range(scan_count)])
     window = jax.ShapeDtypeStruct((slab, 2, n, n), f32)
     whole = jax.ShapeDtypeStruct(objects.shape, f32)
     tiles, window_b = call(own_kernel, "own", [offsets], [objects], [whole, window])

time: 54.3 us -> 54.8 us (level)
  waiting for transfers between devices: 21.2 us -> 22.8 us
  starting transfers between devices: 18.1 us -> 17.1 us
    ppermute x1, waiting for transfers between devices: 3.25 us -> 5.29 us  [body(): lax.ppermute(halo, 'scan', [((i + 1) % scan_count, i) for i in range(scan...]
    ppermute x1, starting transfers between devices: 4.85 us -> 2.99 us  [body(): lax.ppermute(intensity, 'scan', [(i, (i + 1) % scan_count) for i in range...]
where the time goes in v17:
time: 54.8 us; the launch traced here: 54.6 us
  waiting for transfers between devices  22.8 us (42%)
  starting transfers between devices  17.1 us (31%)
  Pallas kernels  12.1 us (22%)
  local copies, waits for them, and re-layouts  1.14 us (2%)
  between operations  0.79 us (1%)
  other arithmetic  0.75 us (1%)
    pallas_call x12, Pallas kernels, call(): pl.pallas_call(kernel, name=name, out_shape=outs, in_specs=[pl.BlockSpec(...  12.1 us
    ppermute x4, waiting for transfers between devices, sum_round(): return lax.ppermute(x, ('depth', 'scan'), route)  7.1 us
    ppermute x1, waiting for transfers between devices, body(): lax.ppermute(halo, 'scan', [((i + 1) % scan_count, i) for i in range(scan...  5.29 us
    ppermute x2, waiting for transfers between devices, body(): spill += [lax.ppermute(x, 'scan', ahead) for x in payload]  4.14 us
    ppermute x3, starting transfers between devices, gathered(): lax.ppermute(x, 'depth', [((target - j) % depth_count, target)])  4.04 us
    ppermute x1, waiting for transfers between devices, body(): lax.ppermute(offsets, 'scan', [(i, (i + 1) % scan_count) for i in range(s...  3.67 us
    ppermute x2, starting transfers between devices, body(): spill += [lax.ppermute(x, 'scan', ahead) for x in payload]  3.4 us
    ppermute x1, starting transfers between devices, body(): lax.ppermute(intensity, 'scan', [(i, (i + 1) % scan_count) for i in range...  2.99 us
  transfers between devices with their start and end apart: 14, of which 9 were waited for; matrix products, arithmetic and copies ran while one was open for 1% of the time, Pallas kernels for 7%

profile of v17, /device:TPU:0, one launch (start us, length us, event | category | flops | bytes accessed | tf_op | source)
XLA Modules:
  0.0 54.6 jit_solution(9222565992200723872)
XLA Ops:
  0.6 3.0 %collective-permute-start.1 = (f32[2,128,128]{2,1,0:T(8,128)}, f32[2,128,128]{2,1,0:T(8,128)S(1)}, u32[]{:S(2)}, u32[]{:S(2)}) collective-permute-start(f32[2,128,128]{2,1,0:T(8,128)} %intensity.1), channel_id=1, source_target_pairs={{0,1},{1,2},{2,3},{3,4},{4,5},{5,6},{6,7},{7,8},{8,9},{9,10},{10,1... | collective-permute-start | bytes 393224 | tf_op jit(solution)/shard_map/ppermute | solution.py:252
  3.6 0.7 %pad_add_fusion.offsets.refs_0_ = s32[4]{0:T(128)S(1)} fusion(s32[2]{0:T(128)} %param.9, s32[2]{0:T(128)} %param.8), kind=kLoop, calls=%fused_computation | loop fusion | flops 4 | bytes 32 | tf_op jit(solution)/shard_map/concatenate | solution.py:250
  4.4 1.5 %collective-permute-start = (s32[4]{0:T(128)S(1)}, s32[4]{0:T(128)S(1)}, u32[]{:S(2)}, u32[]{:S(2)}) collective-permute-start(s32[4]{0:T(128)S(1)} %pad_add_fusion.offsets.refs_0_), channel_id=1, source_target_pairs={{0,1},{1,2},{2,3},{3,4},{4,5},{5,6},{6,7},{7,8},{8,9},{9,10},{10,1... | collective-permute-start | bytes 56 | tf_op jit(solution)/shard_map/ppermute | solution.py:251
  5.9 0.0 copy-start
  5.9 1.1 %copy-done = f32[3,2,128,256]{3,2,1,0:T(8,128)S(1)} copy-done((f32[3,2,128,256]{3,2,1,0:T(8,128)S(1)}, f32[3,2,128,256]{3,2,1,0:T(8,128)}, u32[]{:S(2)}) %copy-start) | copy-done | bytes 786456
  7.0 0.8 %own.1 = (f32[3,2,128,256]{3,2,1,0:T(8,128)S(1)}, f32[3,2,128,128]{3,2,1,0:T(8,128)S(1)}) custom-call(s32[4]{0:T(128)S(1)} %pad_add_fusion.offsets.refs_0_, f32[3,2,128,256]{3,2,1,0:T(8,128)S(1)} %copy-done), custom_call_target="tpu_custom_call" | custom-call | flops 1000000000 | bytes 1966080 | tf_op jit(solution)/shard_map/own/pallas_call | solution.py:220
  7.8 3.7 %collective-permute-done.offsets_prev.refs_1_ = s32[4]{0:T(128)S(1)} collective-permute-done((s32[4]{0:T(128)S(1)}, s32[4]{0:T(128)S(1)}, u32[]{:S(2)}, u32[]{:S(2)}) %collective-permute-start) | collective-permute-done | bytes 48 | tf_op jit(solution)/shard_map/ppermute | solution.py:251
  11.5 0.0 collective-permute-done.1.far.after
  11.5 0.0 copy-start.1
  11.5 0.0 copy-start.2
  11.5 1.0 %prev.1 = (f32[3,2,128,128]{3,2,1,0:T(8,128)S(1)}, f32[3,2,128,128]{3,2,1,0:T(8,128)S(1)}) custom-call(s32[4]{0:T(128)S(1)} %collective-permute-done.offsets_prev.refs_1_, f32[2,128,128]{2,1,0:T(8,128)S(1)} %collective-permute-done.1.far.after, f32[3,2,128,256]{3,2,1,0:T(8,128)S(1)} %get-tuple-element.20.tiles), custom_call_target="tpu_custom_call" | custom-call | flops 1000000000 | bytes 1572864 | tf_op jit(solution)/shard_map/prev/pallas_call | solution.py:220
  12.5 1.7 %collective-permute-start.2 = (f32[3,2,128,128]{3,2,1,0:T(8,128)S(1)}, f32[3,2,128,128]{3,2,1,0:T(8,128)S(1)}, u32[]{:S(2)}, u32[]{:S(2)}) collective-permute-start(f32[3,2,128,128]{3,2,1,0:T(8,128)S(1)} %get-tuple-element.23), channel_id=1, source_target_pairs={{1,0},{2,1},{3,2},{4,3},{5,4},{6,5},{7,6},{8,7},{9,8},{10,9},{11,1... | collective-permute-start | bytes 1179656 | tf_op jit(solution)/shard_map/ppermute | solution.py:257
  14.2 1.3 %collective-permute-start.4 = (f32[3,2,128,128]{3,2,1,0:T(8,128)S(1)}, f32[3,2,128,128]{3,2,1,0:T(8,128)S(1)}, u32[]{:S(2)}, u32[]{:S(2)}) collective-permute-start(f32[3,2,128,128]{3,2,1,0:T(8,128)S(1)} %get-tuple-element.22.refs_5_), channel_id=1, source_target_pairs={{0,16},{1,17},{2,18},{3,19},{4,20},{5,21},{6,22},{7,23},{8,24},{9,... | collective-permute-start | bytes 1179656 | tf_op jit(solution)/shard_map/ppermute | solution.py:260
  15.5 1.3 %collective-permute-start.3 = (f32[3,2,128,128]{3,2,1,0:T(8,128)S(1)}, f32[3,2,128,128]{3,2,1,0:T(8,128)S(1)}, u32[]{:S(2)}, u32[]{:S(2)}) collective-permute-start(f32[3,2,128,128]{3,2,1,0:T(8,128)S(1)} %get-tuple-element.21.refs_4_), channel_id=1, source_target_pairs={{16,0},{17,1},{18,2},{19,3},{20,4},{21,5},{22,6},{23,7},{24,8},{25... | collective-permute-start | bytes 1179656 | tf_op jit(solution)/shard_map/ppermute | solution.py:260
  16.8 0.0 copy-done.1
  16.8 0.0 copy-done.2
  16.9 0.6 %load.1 = (f32[128,128]{1,0:T(8,128)S(1)}, f32[2,128,128]{2,1,0:T(8,128)S(1)}) custom-call(s32[4]{0:T(128)S(1)} %pad_add_fusion.offsets.refs_0_, s32[4]{0:T(128)S(1)} %collective-permute-done.offsets_prev.refs_1_, f32[2,128,128]{2,1,0:T(8,128)S(1)} %copy-done.1, f32[2,128,128]{2,1,0:T(8,128)S(1)} %collective-permute-done.1.far.after, ...), custom_call_target="tpu_custom_call" | custom-call | flops 1000000000 | bytes 589824 | tf_op jit(solution)/shard_map/load/pallas_call | solution.py:220
  17.4 5.3 %collective-permute-done.2.x = f32[3,2,128,128]{3,2,1,0:T(8,128)S(1)} collective-permute-done((f32[3,2,128,128]{3,2,1,0:T(8,128)S(1)}, f32[3,2,128,128]{3,2,1,0:T(8,128)S(1)}, u32[]{:S(2)}, u32[]{:S(2)}) %collective-permute-start.2) | collective-permute-done | bytes 393248 | tf_op jit(solution)/shard_map/ppermute | solution.py:257
  22.7 0.0 copy-start.3
  22.7 1.4 %collective-permute-start.5 = (f32[3,2,128,128]{3,2,1,0:T(8,128)S(1)}, f32[3,2,128,128]{3,2,1,0:T(8,128)S(1)}, u32[]{:S(2)}, u32[]{:S(2)}) collective-permute-start(f32[3,2,128,128]{3,2,1,0:T(8,128)S(1)} %hold.1.refs_6_), channel_id=1, source_target_pairs={{0,16},{1,17},{2,18},{3,19},{4,20},{5,21},{6,22},{7,23},{8,24},{9,... | collective-permute-start | bytes 1179656 | tf_op jit(solution)/shard_map/ppermute | solution.py:260
  24.2 0.0 collective-permute-done.4.refs_8_
  24.2 0.0 collective-permute-done.3.refs_7_
  24.2 1.3 %collective-permute-done.5.refs_9_ = f32[3,2,128,128]{3,2,1,0:T(8,128)S(1)} collective-permute-done((f32[3,2,128,128]{3,2,1,0:T(8,128)S(1)}, f32[3,2,128,128]{3,2,1,0:T(8,128)S(1)}, u32[]{:S(2)}, u32[]{:S(2)}) %collective-permute-start.5) | collective-permute-done | bytes 393248 | tf_op jit(solution)/shard_map/ppermute | solution.py:260
  25.5 0.0 copy-done.3
  25.5 6.4 %wave.1 = (f32[3,2,128,128]{3,2,1,0:T(8,128)S(1)}, f32[3,2,128,128]{3,2,1,0:T(8,128)S(1)}, f32[2,64,128]{2,1,0:T(8,128)S(1)}, f32[2,64,128]{2,1,0:T(8,128)S(1)}) custom-call(s32[4]{0:T(128)S(1)} %pad_add_fusion.offsets.refs_0_, bf16[4,2,256,256]{3,2,1,0:T(8,128)(2,1)S(1)} %copy-done.3, f32[2,128,128]{2,1,0:T(8,128)S(1)} %get-tuple-element.18.refs_2_, ...), custom_call_target="tpu_custom_call" | custom-call | flops 5000000000 | bytes 4521984 | tf_op jit(solution)/shard_map/wave/pallas_call | solution.py:220
  31.9 0.4 collective-permute-start.6
  32.4 0.1 collective-permute-start.7
  32.5 1.3 %collective-permute-done.7.refs_1_ = f32[2,64,128]{2,1,0:T(8,128)S(1)} collective-permute-done((f32[2,64,128]{2,1,0:T(8,128)S(1)}, f32[2,64,128]{2,1,0:T(8,128)S(1)}, u32[]{:S(2)}, u32[]{:S(2)}) %collective-permute-start.7) | collective-permute-done | bytes 65568 | tf_op jit(solution)/shard_map/ppermute | solution.py:289
  33.8 0.0 collective-permute-done.6.refs_3_
  33.8 0.1 collective-permute-start.9
  33.9 2.0 %collective-permute-start.8 = (f32[1,2,128,128]{3,2,1,0:T(8,128)S(1)}, f32[1,2,128,128]{3,2,1,0:T(8,128)S(1)}, u32[]{:S(2)}, u32[]{:S(2)}) collective-permute-start(f32[1,2,128,128]{3,2,1,0:T(8,128)S(1)} %get-tuple-element.28), channel_id=1, source_target_pairs={{0,1},{1,2},{2,3},{3,4},{4,5},{5,6},{6,7},{7,8},{8,9},{9,10},{10,1... | collective-permute-start | bytes 393224 | tf_op jit(solution)/shard_map/ppermute | solution.py:327
  35.9 2.2 %collective-permute-done.9.refs_1_ = f32[2,64,128]{2,1,0:T(8,128)S(1)} collective-permute-done((f32[2,64,128]{2,1,0:T(8,128)S(1)}, f32[2,64,128]{2,1,0:T(8,128)S(1)}, u32[]{:S(2)}, u32[]{:S(2)}) %collective-permute-start.9) | collective-permute-done | bytes 65568 | tf_op jit(solution)/shard_map/ppermute | solution.py:241
  38.2 0.1 collective-permute-start.11
  38.3 1.4 %collective-permute-start.10 = (f32[2,2,128,128]{3,2,1,0:T(8,128)S(1)}, f32[2,2,128,128]{3,2,1,0:T(8,128)S(1)}, u32[]{:S(2)}, u32[]{:S(2)}) collective-permute-start(f32[2,2,128,128]{3,2,1,0:T(8,128)S(1)} %get-tuple-element.30), channel_id=1, source_target_pairs={{0,1},{1,2},{2,3},{3,4},{4,5},{5,6},{6,7},{7,8},{8,9},{9,10},{10,1... | collective-permute-start | bytes 786440 | tf_op jit(solution)/shard_map/ppermute | solution.py:327
  39.7 4.1 %collective-permute-done.8.refs_0_ = f32[1,2,128,128]{3,2,1,0:T(8,128)S(1)} collective-permute-done((f32[1,2,128,128]{3,2,1,0:T(8,128)S(1)}, f32[1,2,128,128]{3,2,1,0:T(8,128)S(1)}, u32[]{:S(2)}, u32[]{:S(2)}) %collective-permute-start.8) | collective-permute-done | bytes 131104 | tf_op jit(solution)/shard_map/ppermute | solution.py:327
  43.8 0.5 collective-permute-done.11.refs_2_
  44.4 0.1 collective-permute-start.12
  44.5 0.9 %place.1.before.refs_0_ = f32[3,2,128,256]{3,2,1,0:T(8,128)S(1)} custom-call(s32[4]{0:T(128)S(1)} %pad_add_fusion.offsets.refs_0_, s32[4]{0:T(128)S(1)} %collective-permute-done.offsets_prev.refs_1_, f32[3,2,128,128]{3,2,1,0:T(8,128)S(1)} %get-tuple-element.24.refs_2_, f32[3,2,128,128]{3,2,1,0:T(8,128)S(1)} %collective-permute-done.6.refs_3_), custom_call_target="tpu_custom_call" | custom-call | flops 2000000000 | bytes 1572864 | tf_op jit(solution)/shard_map/place/pallas_call | solution.py:220
  45.3 3.4 %collective-permute-done.12.refs_2_ = f32[2,64,128]{2,1,0:T(8,128)S(1)} collective-permute-done((f32[2,64,128]{2,1,0:T(8,128)S(1)}, f32[2,64,128]{2,1,0:T(8,128)S(1)}, u32[]{:S(2)}, u32[]{:S(2)}) %collective-permute-start.12) | collective-permute-done | bytes 65568 | tf_op jit(solution)/shard_map/ppermute | solution.py:241
  48.7 2.7 %collective-permute-start.13 = (f32[2,64,128]{2,1,0:T(8,128)S(1)}, f32[2,64,128]{2,1,0:T(8,128)S(1)}, u32[]{:S(2)}, u32[]{:S(2)}) collective-permute-start(f32[2,64,128]{2,1,0:T(8,128)S(1)} %step.8.refs_1_), channel_id=1, source_target_pairs={{0,8},{1,9},{2,10},{3,11},{4,12},{5,13},{6,14},{7,15},{8,0},{9,1},... | collective-permute-start | bytes 196616 | tf_op jit(solution)/shard_map/ppermute | solution.py:241
  51.4 0.0 collective-permute-done.10.refs_1_
  51.4 1.6 %spill.1 = (f32[3,2,128,256]{3,2,1,0:T(8,128)}, f32[8,128]{1,0:T(8,128)S(1)}) custom-call(s32[4]{0:T(128)S(1)} %collective-permute-done.offsets_prev.refs_1_, f32[3,2,128,256]{3,2,1,0:T(8,128)S(1)} %place.1.before.refs_0_, f32[1,2,128,128]{3,2,1,0:T(8,128)S(1)} %collective-permute-done.8.refs_0_, f32[2,2,128,128]{3,2,1,0:T(8,128)S(1)} %collective-permute-done.10.refs_1_), custom_call_target="tpu_custom_call" | custom-call | flops 1000000000 | bytes 1970176 | tf_op jit(solution)/shard_map/spill/pallas_call | solution.py:220
  53.0 0.9 %collective-permute-done.13.refs_2_ = f32[2,64,128]{2,1,0:T(8,128)S(1)} collective-permute-done((f32[2,64,128]{2,1,0:T(8,128)S(1)}, f32[2,64,128]{2,1,0:T(8,128)S(1)}, u32[]{:S(2)}, u32[]{:S(2)}) %collective-permute-start.13) | collective-permute-done | bytes 65568 | tf_op jit(solution)/shard_map/ppermute | solution.py:241
  54.0 0.6 %step.9 = f32[2,64,128]{2,1,0:T(8,128)} custom-call(f32[8,128]{1,0:T(8,128)S(1)} %get-tuple-element.32.refs_0_, f32[2,64,128]{2,1,0:T(8,128)S(1)} %step.8.refs_1_, f32[2,64,128]{2,1,0:T(8,128)S(1)} %collective-permute-done.13.refs_2_), custom_call_target="tpu_custom_call" | custom-call | flops 1000000000 | bytes 196608 | tf_op jit(solution)/shard_map/step/pallas_call | solution.py:220
  (5 shorter events, 0.1 us)
Async XLA Ops:
  0.6 10.9 %collective-permute-start.1 = (f32[2,128,128]{2,1,0:T(8,128)}, f32[2,128,128]{2,1,0:T(8,128)S(1)}, u32[]{:S(2)}, u32[]{:S(2)}) collective-permute-start(f32[2,128,128]{2,1,0:T(8,128)} %intensity.1), channel_id=1, source_target_pairs={{0,1},{1,2},{2,3},{3,4},{4,5},{5,6},{6,7},{7,8},{8,9},{9,10},{10,1... | collective-permute-start | bytes 393224 | tf_op jit(solution)/shard_map/ppermute | solution.py:252
  4.4 7.1 %collective-permute-start = (s32[4]{0:T(128)S(1)}, s32[4]{0:T(128)S(1)}, u32[]{:S(2)}, u32[]{:S(2)}) collective-permute-start(s32[4]{0:T(128)S(1)} %pad_add_fusion.offsets.refs_0_), channel_id=1, source_target_pairs={{0,1},{1,2},{2,3},{3,4},{4,5},{5,6},{6,7},{7,8},{8,9},{9,10},{10,1... | collective-permute-start | bytes 56 | tf_op jit(solution)/shard_map/ppermute | solution.py:251
  5.9 1.1 %copy-start = (f32[3,2,128,256]{3,2,1,0:T(8,128)S(1)}, f32[3,2,128,256]{3,2,1,0:T(8,128)}, u32[]{:S(2)}) copy-start(f32[3,2,128,256]{3,2,1,0:T(8,128)} %objects.1) | copy-start | bytes 2359300
  11.5 5.3 %copy-start.1 = (f32[2,128,128]{2,1,0:T(8,128)S(1)}, f32[2,128,128]{2,1,0:T(8,128)}, u32[]{:S(2)}) copy-start(f32[2,128,128]{2,1,0:T(8,128)} %intensity.1) | copy-start | bytes 393220
  11.5 5.3 %copy-start.2 = (f32[2,128,128]{2,1,0:T(8,128)S(1)}, f32[2,128,128]{2,1,0:T(8,128)}, u32[]{:S(2)}) copy-start(f32[2,128,128]{2,1,0:T(8,128)} %probe.1) | copy-start | bytes 393220
  12.5 10.2 %collective-permute-start.2 = (f32[3,2,128,128]{3,2,1,0:T(8,128)S(1)}, f32[3,2,128,128]{3,2,1,0:T(8,128)S(1)}, u32[]{:S(2)}, u32[]{:S(2)}) collective-permute-start(f32[3,2,128,128]{3,2,1,0:T(8,128)S(1)} %get-tuple-element.23), channel_id=1, source_target_pairs={{1,0},{2,1},{3,2},{4,3},{5,4},{6,5},{7,6},{8,7},{9,8},{10,9},{11,1... | collective-permute-start | bytes 1179656 | tf_op jit(solution)/shard_map/ppermute | solution.py:257
  14.2 10.0 %collective-permute-start.4 = (f32[3,2,128,128]{3,2,1,0:T(8,128)S(1)}, f32[3,2,128,128]{3,2,1,0:T(8,128)S(1)}, u32[]{:S(2)}, u32[]{:S(2)}) collective-permute-start(f32[3,2,128,128]{3,2,1,0:T(8,128)S(1)} %get-tuple-element.22.refs_5_), channel_id=1, source_target_pairs={{0,16},{1,17},{2,18},{3,19},{4,20},{5,21},{6,22},{7,23},{8,24},{9,... | collective-permute-start | bytes 1179656 | tf_op jit(solution)/shard_map/ppermute | solution.py:260
  15.5 8.7 %collective-permute-start.3 = (f32[3,2,128,128]{3,2,1,0:T(8,128)S(1)}, f32[3,2,128,128]{3,2,1,0:T(8,128)S(1)}, u32[]{:S(2)}, u32[]{:S(2)}) collective-permute-start(f32[3,2,128,128]{3,2,1,0:T(8,128)S(1)} %get-tuple-element.21.refs_4_), channel_id=1, source_target_pairs={{16,0},{17,1},{18,2},{19,3},{20,4},{21,5},{22,6},{23,7},{24,8},{25... | collective-permute-start | bytes 1179656 | tf_op jit(solution)/shard_map/ppermute | solution.py:260
  22.7 2.8 %copy-start.3 = (bf16[4,2,256,256]{3,2,1,0:T(8,128)(2,1)S(1)}, bf16[4,2,256,256]{3,2,1,0:T(8,128)(2,1)}, u32[]{:S(2)}) copy-start(bf16[4,2,256,256]{3,2,1,0:T(8,128)(2,1)} %constant.2.clone.refs_1_) | copy-start | bytes 3145732
  22.7 2.8 %collective-permute-start.5 = (f32[3,2,128,128]{3,2,1,0:T(8,128)S(1)}, f32[3,2,128,128]{3,2,1,0:T(8,128)S(1)}, u32[]{:S(2)}, u32[]{:S(2)}) collective-permute-start(f32[3,2,128,128]{3,2,1,0:T(8,128)S(1)} %hold.1.refs_6_), channel_id=1, source_target_pairs={{0,16},{1,17},{2,18},{3,19},{4,20},{5,21},{6,22},{7,23},{8,24},{9,... | collective-permute-start | bytes 1179656 | tf_op jit(solution)/shard_map/ppermute | solution.py:260
  31.9 1.9 %collective-permute-start.6 = (f32[3,2,128,128]{3,2,1,0:T(8,128)S(1)}, f32[3,2,128,128]{3,2,1,0:T(8,128)S(1)}, u32[]{:S(2)}, u32[]{:S(2)}) collective-permute-start(f32[3,2,128,128]{3,2,1,0:T(8,128)S(1)} %get-tuple-element.25), channel_id=1, source_target_pairs={{0,16},{16,0},{1,17},{17,1},{2,18},{18,2},{3,19},{19,3},{4,20},{20... | collective-permute-start | bytes 1179656 | tf_op jit(solution)/shard_map/ppermute | solution.py:290
  32.4 1.4 %collective-permute-start.7 = (f32[2,64,128]{2,1,0:T(8,128)S(1)}, f32[2,64,128]{2,1,0:T(8,128)S(1)}, u32[]{:S(2)}, u32[]{:S(2)}) collective-permute-start(f32[2,64,128]{2,1,0:T(8,128)S(1)} %get-tuple-element.27), channel_id=1, source_target_pairs={{0,16},{16,0},{1,17},{17,1},{2,18},{18,2},{3,19},{19,3},{4,20},{20... | collective-permute-start | bytes 196616 | tf_op jit(solution)/shard_map/ppermute | solution.py:289
  33.8 4.3 %collective-permute-start.9 = (f32[2,64,128]{2,1,0:T(8,128)S(1)}, f32[2,64,128]{2,1,0:T(8,128)S(1)}, u32[]{:S(2)}, u32[]{:S(2)}) collective-permute-start(f32[2,64,128]{2,1,0:T(8,128)S(1)} %get-tuple-element.29.refs_0_), channel_id=1, source_target_pairs={{0,1},{1,0},{2,3},{3,2},{4,5},{5,4},{6,7},{7,6},{8,9},{9,8},{10,11... | collective-permute-start | bytes 196616 | tf_op jit(solution)/shard_map/ppermute | solution.py:241
  33.9 9.9 %collective-permute-start.8 = (f32[1,2,128,128]{3,2,1,0:T(8,128)S(1)}, f32[1,2,128,128]{3,2,1,0:T(8,128)S(1)}, u32[]{:S(2)}, u32[]{:S(2)}) collective-permute-start(f32[1,2,128,128]{3,2,1,0:T(8,128)S(1)} %get-tuple-element.28), channel_id=1, source_target_pairs={{0,1},{1,2},{2,3},{3,4},{4,5},{5,6},{6,7},{7,8},{8,9},{9,10},{10,1... | collective-permute-start | bytes 393224 | tf_op jit(solution)/shard_map/ppermute | solution.py:327
  38.2 6.2 %collective-permute-start.11 = (f32[2,64,128]{2,1,0:T(8,128)S(1)}, f32[2,64,128]{2,1,0:T(8,128)S(1)}, u32[]{:S(2)}, u32[]{:S(2)}) collective-permute-start(f32[2,64,128]{2,1,0:T(8,128)S(1)} %get-tuple-element.33.refs_1_), channel_id=1, source_target_pairs={{0,2},{1,3},{2,0},{3,1},{4,6},{5,7},{6,4},{7,5},{8,10},{9,11},{10,... | collective-permute-start | bytes 196616 | tf_op jit(solution)/shard_map/ppermute | solution.py:241
  38.3 13.1 %collective-permute-start.10 = (f32[2,2,128,128]{3,2,1,0:T(8,128)S(1)}, f32[2,2,128,128]{3,2,1,0:T(8,128)S(1)}, u32[]{:S(2)}, u32[]{:S(2)}) collective-permute-start(f32[2,2,128,128]{3,2,1,0:T(8,128)S(1)} %get-tuple-element.30), channel_id=1, source_target_pairs={{0,1},{1,2},{2,3},{3,4},{4,5},{5,6},{6,7},{7,8},{8,9},{9,10},{10,1... | collective-permute-start | bytes 786440 | tf_op jit(solution)/shard_map/ppermute | solution.py:327
  44.4 4.3 %collective-permute-start.12 = (f32[2,64,128]{2,1,0:T(8,128)S(1)}, f32[2,64,128]{2,1,0:T(8,128)S(1)}, u32[]{:S(2)}, u32[]{:S(2)}) collective-permute-start(f32[2,64,128]{2,1,0:T(8,128)S(1)} %step.7.refs_1_), channel_id=1, source_target_pairs={{0,4},{1,5},{2,6},{3,7},{4,0},{5,1},{6,2},{7,3},{8,12},{9,13},{10,... | collective-permute-start | bytes 196616 | tf_op jit(solution)/shard_map/ppermute | solution.py:241
  48.7 5.2 %collective-permute-start.13 = (f32[2,64,128]{2,1,0:T(8,128)S(1)}, f32[2,64,128]{2,1,0:T(8,128)S(1)}, u32[]{:S(2)}, u32[]{:S(2)}) collective-permute-start(f32[2,64,128]{2,1,0:T(8,128)S(1)} %step.8.refs_1_), channel_id=1, source_target_pairs={{0,8},{1,9},{2,10},{3,11},{4,12},{5,13},{6,14},{7,15},{8,0},{9,1},... | collective-permute-start | bytes 196616 | tf_op jit(solution)/shard_map/ppermute | solution.py:241

commit v18 on v16

--- a/solution.py
+++ b/solution.py
@@ -202,8 +202,9 @@
                 refs[-1][i] = part[s]
 
 
-def spill_kernel(offsets_prev, before, *refs):
-    *spills, out, token = refs
+def spill_kernel(offsets_prev, before, a, b, *refs):
+    *spills, out, total = refs
+    total[...] = a[...] + b[...]
     slab, _, rows, cols = out.shape
     _, _, row_p, col_p = share(offsets_prev, rows)
     mask = lax.broadcasted_iota(jnp.int32, (rows, spills[0].shape[-1]), 0) < row_p
@@ -211,7 +212,6 @@
     for s in range(slab):
         for p in range(2):
             out[s, p] = before[s, p] + placed(came[s][0][came[s][1], p], col_p, mask, cols)
-    token[...] = jnp.zeros_like(token)
 
 
 def call(kernel, name, scalars, arrays, outs, scratch=(), work=10**9, after=()):
@@ -333,12 +333,10 @@
     if paired:
         (total,) = step(total, other, (), [object_grad])
         other = sum_round(total, rounds - 1)
-    object_grad, token = call(
-        spill_kernel, "spill", [offsets_prev], [object_grad, *spill], [whole, jax.ShapeDtypeStruct((8, n), f32)]
+    object_grad, total = call(
+        spill_kernel, "spill", [offsets_prev], [object_grad, total, other, *spill], [whole, half]
     )
-    if paired:
-        (total,) = step(total, other, (), [token])
-    else:
+    if not paired:
         total = lax.psum(total, "scan")
     return object_grad, total
 

time: 54.5 us -> 55 us (level)
  waiting for transfers between devices: 21.5 us -> 22.2 us
  Pallas kernels: 12 us -> 11.4 us
    ppermute x4, waiting for transfers between devices: 6.91 us -> 9.39 us  [sum_round(): return lax.ppermute(x, ('depth', 'scan'), route)]
    ppermute x2, waiting for transfers between devices: 5.06 us -> 3.31 us  [body(): spill += [lax.ppermute(x, 'scan', ahead) for x in payload]]
    pallas_call x12 -> x11, Pallas kernels: 12 us -> 11.4 us  [call(): pl.pallas_call(kernel, name=name, out_shape=outs, in_specs=[pl.BlockSpec(...]
  transfers between devices with their start and end apart: 14 -> 14, of which waited for: 9 -> 9; matrix products, arithmetic and copies ran while one was open for 1% -> 1% of each run, Pallas kernels for 7% -> 4%
where the time goes in v18:
time: 55 us; the launch traced here: 54.3 us
  waiting for transfers between devices  22.2 us (40%)
  starting transfers between devices  18 us (33%)
  Pallas kernels  11.4 us (21%)
  local copies, waits for them, and re-layouts  1.14 us (2%)
  between operations  0.79 us (1%)
  other arithmetic  0.75 us (1%)
    pallas_call x11, Pallas kernels, call(): pl.pallas_call(kernel, name=name, out_shape=outs, in_specs=[pl.BlockSpec(...  11.4 us
    ppermute x4, waiting for transfers between devices, sum_round(): return lax.ppermute(x, ('depth', 'scan'), route)  9.39 us
    ppermute x1, starting transfers between devices, across(): return lax.ppermute(x, ('depth', 'scan'), route)  4.85 us
    ppermute x3, starting transfers between devices, gathered(): lax.ppermute(x, 'depth', [((target - j) % depth_count, target)])  4.04 us
    ppermute x1, waiting for transfers between devices, body(): lax.ppermute(offsets, 'scan', [(i, (i + 1) % scan_count) for i in range(s...  3.67 us
    ppermute x2, waiting for transfers between devices, body(): spill += [lax.ppermute(x, 'scan', ahead) for x in payload]  3.31 us
    ppermute x1, waiting for transfers between devices, body(): lax.ppermute(halo, 'scan', [((i + 1) % scan_count, i) for i in range(scan...  3.25 us
    ppermute x2, starting transfers between devices, body(): spill += [lax.ppermute(x, 'scan', ahead) for x in payload]  2.99 us
  transfers between devices with their start and end apart: 14, of which 9 were waited for; matrix products, arithmetic and copies ran while one was open for 1% of the time, Pallas kernels for 4%

profile of v18, /device:TPU:0, one launch (start us, length us, event | category | flops | bytes accessed | tf_op | source)
XLA Modules:
  0.0 54.3 jit_solution(1221191306929699275)
XLA Ops:
  0.6 4.8 %collective-permute-start.1 = (f32[2,128,128]{2,1,0:T(8,128)}, f32[2,128,128]{2,1,0:T(8,128)S(1)}, u32[]{:S(2)}, u32[]{:S(2)}) collective-permute-start(f32[2,128,128]{2,1,0:T(8,128)} %intensity.1), channel_id=1, source_target_pairs={{0,1},{1,2},{2,3},{3,4},{4,5},{5,6},{6,7},{7,8},{8,9},{9,10},{10,1... | collective-permute-start | bytes 393224 | tf_op jit(solution)/shard_map/ppermute | solution.py:253
  5.5 0.7 %pad_add_fusion.offsets.refs_0_ = s32[4]{0:T(128)S(1)} fusion(s32[2]{0:T(128)} %param.9, s32[2]{0:T(128)} %param.8), kind=kLoop, calls=%fused_computation | loop fusion | flops 4 | bytes 32 | tf_op jit(solution)/shard_map/concatenate | solution.py:255
  6.2 1.5 %collective-permute-start = (s32[4]{0:T(128)S(1)}, s32[4]{0:T(128)S(1)}, u32[]{:S(2)}, u32[]{:S(2)}) collective-permute-start(s32[4]{0:T(128)S(1)} %pad_add_fusion.offsets.refs_0_), channel_id=1, source_target_pairs={{0,1},{1,2},{2,3},{3,4},{4,5},{5,6},{6,7},{7,8},{8,9},{9,10},{10,1... | collective-permute-start | bytes 56 | tf_op jit(solution)/shard_map/ppermute | solution.py:256
  7.7 0.0 copy-start
  7.7 1.1 %copy-done = f32[3,2,128,256]{3,2,1,0:T(8,128)S(1)} copy-done((f32[3,2,128,256]{3,2,1,0:T(8,128)S(1)}, f32[3,2,128,256]{3,2,1,0:T(8,128)}, u32[]{:S(2)}) %copy-start) | copy-done | bytes 786456
  8.9 0.8 %own.1 = (f32[3,2,128,256]{3,2,1,0:T(8,128)S(1)}, f32[3,2,128,128]{3,2,1,0:T(8,128)S(1)}) custom-call(s32[4]{0:T(128)S(1)} %pad_add_fusion.offsets.refs_0_, f32[3,2,128,256]{3,2,1,0:T(8,128)S(1)} %copy-done), custom_call_target="tpu_custom_call" | custom-call | flops 1000000000 | bytes 1966080 | tf_op jit(solution)/shard_map/own/pallas_call | solution.py:220
  9.7 3.7 %collective-permute-done.offsets_prev.refs_1_ = s32[4]{0:T(128)S(1)} collective-permute-done((s32[4]{0:T(128)S(1)}, s32[4]{0:T(128)S(1)}, u32[]{:S(2)}, u32[]{:S(2)}) %collective-permute-start) | collective-permute-done | bytes 48 | tf_op jit(solution)/shard_map/ppermute | solution.py:256
  13.4 0.0 collective-permute-done.1.far.after
  13.4 0.0 copy-start.1
  13.4 0.0 copy-start.2
  13.4 1.0 %prev.1 = (f32[3,2,128,128]{3,2,1,0:T(8,128)S(1)}, f32[3,2,128,128]{3,2,1,0:T(8,128)S(1)}) custom-call(s32[4]{0:T(128)S(1)} %collective-permute-done.offsets_prev.refs_1_, f32[2,128,128]{2,1,0:T(8,128)S(1)} %collective-permute-done.1.far.after, f32[3,2,128,256]{3,2,1,0:T(8,128)S(1)} %get-tuple-element.18.tiles), custom_call_target="tpu_custom_call" | custom-call | flops 1000000000 | bytes 1572864 | tf_op jit(solution)/shard_map/prev/pallas_call | solution.py:220
  14.4 1.4 %collective-permute-start.2 = (f32[3,2,128,128]{3,2,1,0:T(8,128)S(1)}, f32[3,2,128,128]{3,2,1,0:T(8,128)S(1)}, u32[]{:S(2)}, u32[]{:S(2)}) collective-permute-start(f32[3,2,128,128]{3,2,1,0:T(8,128)S(1)} %get-tuple-element.21), channel_id=1, source_target_pairs={{1,0},{2,1},{3,2},{4,3},{5,4},{6,5},{7,6},{8,7},{9,8},{10,9},{11,1... | collective-permute-start | bytes 1179656 | tf_op jit(solution)/shard_map/ppermute | solution.py:262
  15.8 1.3 %collective-permute-start.4 = (f32[3,2,128,128]{3,2,1,0:T(8,128)S(1)}, f32[3,2,128,128]{3,2,1,0:T(8,128)S(1)}, u32[]{:S(2)}, u32[]{:S(2)}) collective-permute-start(f32[3,2,128,128]{3,2,1,0:T(8,128)S(1)} %get-tuple-element.20.refs_5_), channel_id=1, source_target_pairs={{0,16},{1,17},{2,18},{3,19},{4,20},{5,21},{6,22},{7,23},{8,24},{9,... | collective-permute-start | bytes 1179656 | tf_op jit(solution)/shard_map/ppermute | solution.py:265
  17.1 1.3 %collective-permute-start.3 = (f32[3,2,128,128]{3,2,1,0:T(8,128)S(1)}, f32[3,2,128,128]{3,2,1,0:T(8,128)S(1)}, u32[]{:S(2)}, u32[]{:S(2)}) collective-permute-start(f32[3,2,128,128]{3,2,1,0:T(8,128)S(1)} %get-tuple-element.19.refs_4_), channel_id=1, source_target_pairs={{16,0},{17,1},{18,2},{19,3},{20,4},{21,5},{22,6},{23,7},{24,8},{25... | collective-permute-start | bytes 1179656 | tf_op jit(solution)/shard_map/ppermute | solution.py:265
  18.4 0.0 copy-done.1
  18.4 0.0 copy-done.2
  18.4 0.6 %load.1 = (f32[128,128]{1,0:T(8,128)S(1)}, f32[2,128,128]{2,1,0:T(8,128)S(1)}) custom-call(s32[4]{0:T(128)S(1)} %pad_add_fusion.offsets.refs_0_, s32[4]{0:T(128)S(1)} %collective-permute-done.offsets_prev.refs_1_, f32[2,128,128]{2,1,0:T(8,128)S(1)} %copy-done.1, f32[2,128,128]{2,1,0:T(8,128)S(1)} %collective-permute-done.1.far.after, ...), custom_call_target="tpu_custom_call" | custom-call | flops 1000000000 | bytes 589824 | tf_op jit(solution)/shard_map/load/pallas_call | solution.py:220
  19.0 3.2 %collective-permute-done.2.x = f32[3,2,128,128]{3,2,1,0:T(8,128)S(1)} collective-permute-done((f32[3,2,128,128]{3,2,1,0:T(8,128)S(1)}, f32[3,2,128,128]{3,2,1,0:T(8,128)S(1)}, u32[]{:S(2)}, u32[]{:S(2)}) %collective-permute-start.2) | collective-permute-done | bytes 393248 | tf_op jit(solution)/shard_map/ppermute | solution.py:262
  22.2 0.0 copy-start.3
  22.3 1.4 %collective-permute-start.5 = (f32[3,2,128,128]{3,2,1,0:T(8,128)S(1)}, f32[3,2,128,128]{3,2,1,0:T(8,128)S(1)}, u32[]{:S(2)}, u32[]{:S(2)}) collective-permute-start(f32[3,2,128,128]{3,2,1,0:T(8,128)S(1)} %hold.1.refs_6_), channel_id=1, source_target_pairs={{0,16},{1,17},{2,18},{3,19},{4,20},{5,21},{6,22},{7,23},{8,24},{9,... | collective-permute-start | bytes 1179656 | tf_op jit(solution)/shard_map/ppermute | solution.py:265
  23.7 0.0 collective-permute-done.4.refs_8_
  23.7 0.0 collective-permute-done.3.refs_7_
  23.7 1.3 %collective-permute-done.5.refs_9_ = f32[3,2,128,128]{3,2,1,0:T(8,128)S(1)} collective-permute-done((f32[3,2,128,128]{3,2,1,0:T(8,128)S(1)}, f32[3,2,128,128]{3,2,1,0:T(8,128)S(1)}, u32[]{:S(2)}, u32[]{:S(2)}) %collective-permute-start.5) | collective-permute-done | bytes 393248 | tf_op jit(solution)/shard_map/ppermute | solution.py:265
  25.0 0.0 copy-done.3
  25.0 6.4 %wave.1 = (f32[3,2,128,128]{3,2,1,0:T(8,128)S(1)}, f32[3,2,128,128]{3,2,1,0:T(8,128)S(1)}, f32[2,64,128]{2,1,0:T(8,128)S(1)}, f32[2,64,128]{2,1,0:T(8,128)S(1)}) custom-call(s32[4]{0:T(128)S(1)} %pad_add_fusion.offsets.refs_0_, bf16[4,2,256,256]{3,2,1,0:T(8,128)(2,1)S(1)} %copy-done.3, f32[2,128,128]{2,1,0:T(8,128)S(1)} %get-tuple-element.16.refs_2_, ...), custom_call_target="tpu_custom_call" | custom-call | flops 5000000000 | bytes 4521984 | tf_op jit(solution)/shard_map/wave/pallas_call | solution.py:220
  31.4 0.4 collective-permute-start.6
  31.9 0.1 collective-permute-start.7
  32.0 1.3 %collective-permute-done.7.refs_1_ = f32[2,64,128]{2,1,0:T(8,128)S(1)} collective-permute-done((f32[2,64,128]{2,1,0:T(8,128)S(1)}, f32[2,64,128]{2,1,0:T(8,128)S(1)}, u32[]{:S(2)}, u32[]{:S(2)}) %collective-permute-start.7) | collective-permute-done | bytes 65568 | tf_op jit(solution)/shard_map/ppermute | solution.py:294
  33.3 0.0 collective-permute-done.6.refs_3_
  33.4 0.1 collective-permute-start.9
  33.4 2.0 %collective-permute-start.8 = (f32[1,2,128,128]{3,2,1,0:T(8,128)S(1)}, f32[1,2,128,128]{3,2,1,0:T(8,128)S(1)}, u32[]{:S(2)}, u32[]{:S(2)}) collective-permute-start(f32[1,2,128,128]{3,2,1,0:T(8,128)S(1)} %get-tuple-element.26), channel_id=1, source_target_pairs={{0,1},{1,2},{2,3},{3,4},{4,5},{5,6},{6,7},{7,8},{8,9},{9,10},{10,1... | collective-permute-start | bytes 393224 | tf_op jit(solution)/shard_map/ppermute | solution.py:332
  35.5 2.9 %collective-permute-done.9.refs_1_ = f32[2,64,128]{2,1,0:T(8,128)S(1)} collective-permute-done((f32[2,64,128]{2,1,0:T(8,128)S(1)}, f32[2,64,128]{2,1,0:T(8,128)S(1)}, u32[]{:S(2)}, u32[]{:S(2)}) %collective-permute-start.9) | collective-permute-done | bytes 65568 | tf_op jit(solution)/shard_map/ppermute | solution.py:242
  38.4 0.3 collective-permute-start.10
  38.7 1.0 %collective-permute-start.13 = (f32[2,2,128,128]{3,2,1,0:T(8,128)S(1)}, f32[2,2,128,128]{3,2,1,0:T(8,128)S(1)}, u32[]{:S(2)}, u32[]{:S(2)}) collective-permute-start(f32[2,2,128,128]{3,2,1,0:T(8,128)S(1)} %get-tuple-element.29), channel_id=1, source_target_pairs={{0,1},{1,2},{2,3},{3,4},{4,5},{5,6},{6,7},{7,8},{8,9},{9,10},{10,1... | collective-permute-start | bytes 786440 | tf_op jit(solution)/shard_map/ppermute | solution.py:332
  39.7 3.3 %collective-permute-done.8.refs_0_ = f32[1,2,128,128]{3,2,1,0:T(8,128)S(1)} collective-permute-done((f32[1,2,128,128]{3,2,1,0:T(8,128)S(1)}, f32[1,2,128,128]{3,2,1,0:T(8,128)S(1)}, u32[]{:S(2)}, u32[]{:S(2)}) %collective-permute-start.8) | collective-permute-done | bytes 131104 | tf_op jit(solution)/shard_map/ppermute | solution.py:332
  43.0 0.7 %collective-permute-done.10.refs_2_ = f32[2,64,128]{2,1,0:T(8,128)S(1)} collective-permute-done((f32[2,64,128]{2,1,0:T(8,128)S(1)}, f32[2,64,128]{2,1,0:T(8,128)S(1)}, u32[]{:S(2)}, u32[]{:S(2)}) %collective-permute-start.10) | collective-permute-done | bytes 65568 | tf_op jit(solution)/shard_map/ppermute | solution.py:242
  43.6 0.1 collective-permute-start.11
  43.7 0.9 %place.1.refs_0_.before = f32[3,2,128,256]{3,2,1,0:T(8,128)S(1)} custom-call(s32[4]{0:T(128)S(1)} %pad_add_fusion.offsets.refs_0_, s32[4]{0:T(128)S(1)} %collective-permute-done.offsets_prev.refs_1_, f32[3,2,128,128]{3,2,1,0:T(8,128)S(1)} %get-tuple-element.22.refs_2_, f32[3,2,128,128]{3,2,1,0:T(8,128)S(1)} %collective-permute-done.6.refs_3_), custom_call_target="tpu_custom_call" | custom-call | flops 2000000000 | bytes 1572864 | tf_op jit(solution)/shard_map/place/pallas_call | solution.py:220
  44.6 3.4 %collective-permute-done.11.refs_2_ = f32[2,64,128]{2,1,0:T(8,128)S(1)} collective-permute-done((f32[2,64,128]{2,1,0:T(8,128)S(1)}, f32[2,64,128]{2,1,0:T(8,128)S(1)}, u32[]{:S(2)}, u32[]{:S(2)}) %collective-permute-start.11) | collective-permute-done | bytes 65568 | tf_op jit(solution)/shard_map/ppermute | solution.py:242
  48.0 2.3 %collective-permute-start.12 = (f32[2,64,128]{2,1,0:T(8,128)S(1)}, f32[2,64,128]{2,1,0:T(8,128)S(1)}, u32[]{:S(2)}, u32[]{:S(2)}) collective-permute-start(f32[2,64,128]{2,1,0:T(8,128)S(1)} %step.7.a), channel_id=1, source_target_pairs={{0,2},{1,3},{2,0},{3,1},{4,6},{5,7},{6,4},{7,5},{8,10},{9,11},{10,... | collective-permute-start | bytes 196616 | tf_op jit(solution)/shard_map/ppermute | solution.py:242
  50.2 2.5 %collective-permute-done.12.b = f32[2,64,128]{2,1,0:T(8,128)S(1)} collective-permute-done((f32[2,64,128]{2,1,0:T(8,128)S(1)}, f32[2,64,128]{2,1,0:T(8,128)S(1)}, u32[]{:S(2)}, u32[]{:S(2)}) %collective-permute-start.12) | collective-permute-done | bytes 65568 | tf_op jit(solution)/shard_map/ppermute | solution.py:242
  52.7 0.0 collective-permute-done.13.refs_1_
  52.7 1.6 %spill.1 = (f32[3,2,128,256]{3,2,1,0:T(8,128)}, f32[2,64,128]{2,1,0:T(8,128)}) custom-call(s32[4]{0:T(128)S(1)} %collective-permute-done.offsets_prev.refs_1_, f32[3,2,128,256]{3,2,1,0:T(8,128)S(1)} %place.1.refs_0_.before, f32[2,64,128]{2,1,0:T(8,128)S(1)} %step.7.a, f32[2,64,128]{2,1,0:T(8,128)S(1)} %collective-permute-done.12.b, ...), custom_call_target="tpu_custom_call" | custom-call | flops 1000000000 | bytes 2162688 | tf_op jit(solution)/shard_map/spill/pallas_call | solution.py:220
  (5 shorter events, 0.1 us)
Async XLA Ops:
  0.6 12.7 %collective-permute-start.1 = (f32[2,128,128]{2,1,0:T(8,128)}, f32[2,128,128]{2,1,0:T(8,128)S(1)}, u32[]{:S(2)}, u32[]{:S(2)}) collective-permute-start(f32[2,128,128]{2,1,0:T(8,128)} %intensity.1), channel_id=1, source_target_pairs={{0,1},{1,2},{2,3},{3,4},{4,5},{5,6},{6,7},{7,8},{8,9},{9,10},{10,1... | collective-permute-start | bytes 393224 | tf_op jit(solution)/shard_map/ppermute | solution.py:253
  6.2 7.1 %collective-permute-start = (s32[4]{0:T(128)S(1)}, s32[4]{0:T(128)S(1)}, u32[]{:S(2)}, u32[]{:S(2)}) collective-permute-start(s32[4]{0:T(128)S(1)} %pad_add_fusion.offsets.refs_0_), channel_id=1, source_target_pairs={{0,1},{1,2},{2,3},{3,4},{4,5},{5,6},{6,7},{7,8},{8,9},{9,10},{10,1... | collective-permute-start | bytes 56 | tf_op jit(solution)/shard_map/ppermute | solution.py:256
  7.7 1.1 %copy-start = (f32[3,2,128,256]{3,2,1,0:T(8,128)S(1)}, f32[3,2,128,256]{3,2,1,0:T(8,128)}, u32[]{:S(2)}) copy-start(f32[3,2,128,256]{3,2,1,0:T(8,128)} %objects.1) | copy-start | bytes 2359300
  13.4 5.0 %copy-start.1 = (f32[2,128,128]{2,1,0:T(8,128)S(1)}, f32[2,128,128]{2,1,0:T(8,128)}, u32[]{:S(2)}) copy-start(f32[2,128,128]{2,1,0:T(8,128)} %intensity.1) | copy-start | bytes 393220
  13.4 5.0 %copy-start.2 = (f32[2,128,128]{2,1,0:T(8,128)S(1)}, f32[2,128,128]{2,1,0:T(8,128)}, u32[]{:S(2)}) copy-start(f32[2,128,128]{2,1,0:T(8,128)} %probe.1) | copy-start | bytes 393220
  14.4 7.8 %collective-permute-start.2 = (f32[3,2,128,128]{3,2,1,0:T(8,128)S(1)}, f32[3,2,128,128]{3,2,1,0:T(8,128)S(1)}, u32[]{:S(2)}, u32[]{:S(2)}) collective-permute-start(f32[3,2,128,128]{3,2,1,0:T(8,128)S(1)} %get-tuple-element.21), channel_id=1, source_target_pairs={{1,0},{2,1},{3,2},{4,3},{5,4},{6,5},{7,6},{8,7},{9,8},{10,9},{11,1... | collective-permute-start | bytes 1179656 | tf_op jit(solution)/shard_map/ppermute | solution.py:262
  15.8 7.9 %collective-permute-start.4 = (f32[3,2,128,128]{3,2,1,0:T(8,128)S(1)}, f32[3,2,128,128]{3,2,1,0:T(8,128)S(1)}, u32[]{:S(2)}, u32[]{:S(2)}) collective-permute-start(f32[3,2,128,128]{3,2,1,0:T(8,128)S(1)} %get-tuple-element.20.refs_5_), channel_id=1, source_target_pairs={{0,16},{1,17},{2,18},{3,19},{4,20},{5,21},{6,22},{7,23},{8,24},{9,... | collective-permute-start | bytes 1179656 | tf_op jit(solution)/shard_map/ppermute | solution.py:265
  17.1 6.6 %collective-permute-start.3 = (f32[3,2,128,128]{3,2,1,0:T(8,128)S(1)}, f32[3,2,128,128]{3,2,1,0:T(8,128)S(1)}, u32[]{:S(2)}, u32[]{:S(2)}) collective-permute-start(f32[3,2,128,128]{3,2,1,0:T(8,128)S(1)} %get-tuple-element.19.refs_4_), channel_id=1, source_target_pairs={{16,0},{17,1},{18,2},{19,3},{20,4},{21,5},{22,6},{23,7},{24,8},{25... | collective-permute-start | bytes 1179656 | tf_op jit(solution)/shard_map/ppermute | solution.py:265
  22.2 2.8 %copy-start.3 = (bf16[4,2,256,256]{3,2,1,0:T(8,128)(2,1)S(1)}, bf16[4,2,256,256]{3,2,1,0:T(8,128)(2,1)}, u32[]{:S(2)}) copy-start(bf16[4,2,256,256]{3,2,1,0:T(8,128)(2,1)} %constant.2.clone.refs_1_) | copy-start | bytes 3145732
  22.3 2.8 %collective-permute-start.5 = (f32[3,2,128,128]{3,2,1,0:T(8,128)S(1)}, f32[3,2,128,128]{3,2,1,0:T(8,128)S(1)}, u32[]{:S(2)}, u32[]{:S(2)}) collective-permute-start(f32[3,2,128,128]{3,2,1,0:T(8,128)S(1)} %hold.1.refs_6_), channel_id=1, source_target_pairs={{0,16},{1,17},{2,18},{3,19},{4,20},{5,21},{6,22},{7,23},{8,24},{9,... | collective-permute-start | bytes 1179656 | tf_op jit(solution)/shard_map/ppermute | solution.py:265
  31.4 1.9 %collective-permute-start.6 = (f32[3,2,128,128]{3,2,1,0:T(8,128)S(1)}, f32[3,2,128,128]{3,2,1,0:T(8,128)S(1)}, u32[]{:S(2)}, u32[]{:S(2)}) collective-permute-start(f32[3,2,128,128]{3,2,1,0:T(8,128)S(1)} %get-tuple-element.23), channel_id=1, source_target_pairs={{0,16},{16,0},{1,17},{17,1},{2,18},{18,2},{3,19},{19,3},{4,20},{20... | collective-permute-start | bytes 1179656 | tf_op jit(solution)/shard_map/ppermute | solution.py:295
  31.9 1.4 %collective-permute-start.7 = (f32[2,64,128]{2,1,0:T(8,128)S(1)}, f32[2,64,128]{2,1,0:T(8,128)S(1)}, u32[]{:S(2)}, u32[]{:S(2)}) collective-permute-start(f32[2,64,128]{2,1,0:T(8,128)S(1)} %get-tuple-element.25), channel_id=1, source_target_pairs={{0,16},{16,0},{1,17},{17,1},{2,18},{18,2},{3,19},{19,3},{4,20},{20... | collective-permute-start | bytes 196616 | tf_op jit(solution)/shard_map/ppermute | solution.py:294
  33.4 5.0 %collective-permute-start.9 = (f32[2,64,128]{2,1,0:T(8,128)S(1)}, f32[2,64,128]{2,1,0:T(8,128)S(1)}, u32[]{:S(2)}, u32[]{:S(2)}) collective-permute-start(f32[2,64,128]{2,1,0:T(8,128)S(1)} %get-tuple-element.27.refs_0_), channel_id=1, source_target_pairs={{0,1},{1,0},{2,3},{3,2},{4,5},{5,4},{6,7},{7,6},{8,9},{9,8},{10,11... | collective-permute-start | bytes 196616 | tf_op jit(solution)/shard_map/ppermute | solution.py:242
  33.4 9.5 %collective-permute-start.8 = (f32[1,2,128,128]{3,2,1,0:T(8,128)S(1)}, f32[1,2,128,128]{3,2,1,0:T(8,128)S(1)}, u32[]{:S(2)}, u32[]{:S(2)}) collective-permute-start(f32[1,2,128,128]{3,2,1,0:T(8,128)S(1)} %get-tuple-element.26), channel_id=1, source_target_pairs={{0,1},{1,2},{2,3},{3,4},{4,5},{5,6},{6,7},{7,8},{8,9},{9,10},{10,1... | collective-permute-start | bytes 393224 | tf_op jit(solution)/shard_map/ppermute | solution.py:332
  38.4 5.2 %collective-permute-start.10 = (f32[2,64,128]{2,1,0:T(8,128)S(1)}, f32[2,64,128]{2,1,0:T(8,128)S(1)}, u32[]{:S(2)}, u32[]{:S(2)}) collective-permute-start(f32[2,64,128]{2,1,0:T(8,128)S(1)} %get-tuple-element.28.refs_1_), channel_id=1, source_target_pairs={{0,8},{1,9},{2,10},{3,11},{4,12},{5,13},{6,14},{7,15},{8,0},{9,1},... | collective-permute-start | bytes 196616 | tf_op jit(solution)/shard_map/ppermute | solution.py:242
  38.7 14.0 %collective-permute-start.13 = (f32[2,2,128,128]{3,2,1,0:T(8,128)S(1)}, f32[2,2,128,128]{3,2,1,0:T(8,128)S(1)}, u32[]{:S(2)}, u32[]{:S(2)}) collective-permute-start(f32[2,2,128,128]{3,2,1,0:T(8,128)S(1)} %get-tuple-element.29), channel_id=1, source_target_pairs={{0,1},{1,2},{2,3},{3,4},{4,5},{5,6},{6,7},{7,8},{8,9},{9,10},{10,1... | collective-permute-start | bytes 786440 | tf_op jit(solution)/shard_map/ppermute | solution.py:332
  43.6 4.3 %collective-permute-start.11 = (f32[2,64,128]{2,1,0:T(8,128)S(1)}, f32[2,64,128]{2,1,0:T(8,128)S(1)}, u32[]{:S(2)}, u32[]{:S(2)}) collective-permute-start(f32[2,64,128]{2,1,0:T(8,128)S(1)} %step.6.refs_1_), channel_id=1, source_target_pairs={{0,4},{1,5},{2,6},{3,7},{4,0},{5,1},{6,2},{7,3},{8,12},{9,13},{10,... | collective-permute-start | bytes 196616 | tf_op jit(solution)/shard_map/ppermute | solution.py:242
  48.0 4.7 %collective-permute-start.12 = (f32[2,64,128]{2,1,0:T(8,128)S(1)}, f32[2,64,128]{2,1,0:T(8,128)S(1)}, u32[]{:S(2)}, u32[]{:S(2)}) collective-permute-start(f32[2,64,128]{2,1,0:T(8,128)S(1)} %step.7.a), channel_id=1, source_target_pairs={{0,2},{1,3},{2,0},{3,1},{4,6},{5,7},{6,4},{7,5},{8,10},{9,11},{10,... | collective-permute-start | bytes 196616 | tf_op jit(solution)/shard_map/ppermute | solution.py:242
